TPU v7x, 768 devices: a whole 4x8x12 slice. The times are simulated.
768 devices in a mesh: row: 16 (over x_lo, y), col: 48 (over x_hi, z, core).
Axes of the slice: x: 4 (x_hi: 2, x_lo: 2; x = x_hi * 2 + x_lo), y: 8, z: 12, core: 2. Of those that a mesh axis runs over, the one named last changes fastest.
Arguments:
- a_own_values: bfloat16 [16, 48, 16, 1, 128, 128], P('row', 'col'), may hold values from -1.5 to 1.5
- a_own_code: int32 [16, 48, 16, 1], P('row', 'col'), may hold values from -1 to 2303, as said below
- b_own_values: bfloat16 [16, 48, 16, 1, 128, 128], P('row', 'col'), may hold values from -0.5 to 0.5
- b_own_code: int32 [16, 48, 16, 1], P('row', 'col'), may hold values from -1 to 767, as said below
- c_code: int32 [16, 48, 12], P('row', 'col'), may hold values from 0 to 767, as said below
Outputs:
- product: bfloat16 [16, 48, 12, 128, 128], P('row', 'col')
Inputs may be any that keep to these rules, and one draw needn't show every extreme that they name: `a_own_code`: entry [r, c, s, q] is the code of the q-th block that owner c of block row group r holds for panel (r, s) of A: i * 48 + k for block (i, k), or -1 for an unused entry. Live codes of one panel are distinct. In every draw some panel has all 48 entries live. `b_own_code`: entry [r, c, s, q] is the code of the q-th block that owner r holds for panel (s, c) of B: k * 16 + j for block (k, j), or -1 for an unused entry. Live codes of one panel are distinct. No block row of a panel holds more than 2 live blocks; in every draw some panel has all 16 entries live and some block row holds exactly 2. `c_code`: each grid position keeps 12 distinct blocks (i, j), coded i * 16 + j, with i < 48. Every product of a live block (i, k) of A's panel (r, s) with a live block (k, j) of B's panel (s, c), for the panels that meet at (r, c) within the window, falls on a kept block.
All inputs are finite; a program needn't handle non-finite values.
Results may differ from a plain program's by a relative error of at most 0.001.
Values may be sent and summed in bfloat16 or wider, within the bound.
No kernel may reach another device: no remote copies, remote signals or barrier semaphores. Data moves between devices by JAX's collectives and lax.ppermute only.
A program may use at most 64 MiB of HBM per device.

v0:
```python
import jax
import jax.numpy as jnp
from jax import lax
from jax.sharding import PartitionSpec as P

BC = 16
STEPS = 3
BROW = 2


def passed_along(block, axis, distance):
    devices = range(lax.axis_size(axis))
    route = [((i - distance) % len(devices), i) for i in devices]
    return lax.ppermute(block, axis, route)


def panel_product(
    running, left_blocks, left_codes, right_blocks, right_codes, slot_codes, panel_width
):
    right_capacity = right_blocks.shape[0]
    left_live = left_codes >= 0
    right_live = right_codes >= 0
    left_rows = left_codes // panel_width
    left_inner = left_codes % panel_width
    right_inner = right_codes // BC
    right_cols = right_codes % BC
    entries = jnp.arange(right_capacity, dtype=jnp.int32)
    same_row = (
        (right_inner[:, None] == right_inner[None, :]) & right_live[:, None] & right_live[None, :]
    )
    earlier = entries[None, :] < entries[:, None]
    rank_in_row = jnp.sum((same_row & earlier).astype(jnp.int32), axis=1)
    place = jnp.where(right_live, right_inner * BROW + rank_in_row, panel_width * BROW)
    row_table = (
        jnp.full((panel_width * BROW,), right_capacity, jnp.int32)
        .at[place]
        .set(entries, mode="drop")
    )
    safe_inner = jnp.where(left_live, left_inner, 0)
    partner = row_table[safe_inner[:, None] * BROW + jnp.arange(BROW, dtype=jnp.int32)[None, :]]
    partner = jnp.where(left_live[:, None], partner, right_capacity)
    valid = partner < right_capacity
    safe_partner = jnp.where(valid, partner, 0)
    cell = jnp.where(left_live, left_rows, 0)[:, None] * BC + right_cols[safe_partner]
    landing = ((cell[:, :, None] == slot_codes[None, None, :]) & valid[:, :, None]).astype(
        jnp.float32
    )
    for rank_number in range(BROW):
        chosen = jnp.take(right_blocks, safe_partner[:, rank_number], axis=0)
        pieces = jnp.einsum("aij,ajk->aik", left_blocks, chosen, preferred_element_type=jnp.float32)
        running = running + jnp.einsum(
            "ap,aik->pik", landing[:, rank_number, :], pieces, precision=lax.Precision.HIGHEST
        )
    return running


def local(a_own_values, a_own_code, b_own_values, b_own_code, c_code):
    col_count = lax.axis_size("col")
    row_count = lax.axis_size("row")
    panel_width = BC * (col_count // row_count)
    grid_row = lax.axis_index("row")
    grid_col = lax.axis_index("col")
    block_size = a_own_values.shape[-1]
    left_order = (grid_row + jnp.arange(col_count, dtype=jnp.int32)) % row_count
    left_send = a_own_values[0, 0][left_order]
    left_code_send = a_own_code[0, 0][left_order]
    left_blocks, left_codes = (
        lax.all_to_all(left_send, "col", split_axis=0, concat_axis=0, tiled=True),
        lax.all_to_all(left_code_send, "col", split_axis=0, concat_axis=0, tiled=True),
    )
    left_blocks = left_blocks.reshape(-1, block_size, block_size)
    left_codes = left_codes.reshape(-1)
    right_order = (jnp.arange(row_count, dtype=jnp.int32) + grid_col) % row_count
    right_send = b_own_values[0, 0][right_order]
    right_code_send = b_own_code[0, 0][right_order]
    right_blocks, right_codes = (
        lax.all_to_all(right_send, "row", split_axis=0, concat_axis=0, tiled=True),
        lax.all_to_all(right_code_send, "row", split_axis=0, concat_axis=0, tiled=True),
    )
    right_blocks = right_blocks.reshape(-1, block_size, block_size)
    right_codes = right_codes.reshape(-1)
    slot_codes = c_code[0, 0]
    kept_count = slot_codes.shape[0]
    running = jnp.zeros((kept_count, block_size, block_size), jnp.float32)
    left_now, left_code_now = (left_blocks, left_codes)
    right_now, right_code_now = (right_blocks, right_codes)
    for step_number in range(STEPS):
        if step_number > 0:
            left_now, left_code_now = passed_along((left_now, left_code_now), "col", -1)
            right_now, right_code_now = passed_along((right_now, right_code_now), "row", -1)
        running = panel_product(
            running, left_now, left_code_now, right_now, right_code_now, slot_codes, panel_width
        )
    return running.astype(jnp.bfloat16)[None, None]


def solution(mesh):
    return jax.shard_map(
        local,
        mesh=mesh,
        in_specs=(
            P("row", "col", None, None, None, None),
            P("row", "col", None, None),
            P("row", "col", None, None, None, None),
            P("row", "col", None, None),
            P("row", "col", None),
        ),
        out_specs=P("row", "col", None, None, None),
        check_vma=False,
    )
```

profile of v0, /device:TPU:60, one launch (start us, length us, event | category | flops | bytes accessed | tf_op | source)
XLA Modules:
  0.0 224.5 jit_solution(5131886351422350530)
XLA Ops:
  2.1 7.5 %all-to-all-start.1 = ((s32[16,1,1]{2,1,0:T(1,128)}), s32[16,1,1]{2,1,0:T(1,128)S(1)}, u32[]{:S(2)}, u32[]{:S(2)}) async-start(s32[16,1,1]{2,1,0:T(1,128)} %copy.51), calls=%async_computation.1 | async-start | bytes 16384 | tf_op jit(solution)/shard_map/all_to_all | solution.py:78
  11.8 2.5 %gather_fusion.5 = bf16[16,128,128]{2,1,0:T(8,128)(2,1)} fusion(bf16[16,128,128]{2,1,0:T(8,128)(2,1)} %bitcast.88, s32[1024]{0:T(1024)S(1)} %pad_clamp_fusion.12), kind=kCustom, calls=%fused_computation.11 | custom fusion | bytes 1048640 | tf_op jit(solution)/shard_map/gather | solution.py:74
  16.2 18.5 %all-to-all-start = ((s32[48,1,1]{2,1,0:T(1,128)}), s32[48,1,1]{2,1,0:T(1,128)S(1)}, u32[]{:S(2)}, u32[]{:S(2)}) async-start(s32[48,1,1]{2,1,0:T(1,128)} %copy.50), calls=%async_computation | async-start | bytes 49152 | tf_op jit(solution)/shard_map/all_to_all | solution.py:69
  35.1 3.4 %collective-permute-start.1 = (s32[16]{0:T(128)S(1)}, s32[16]{0:T(128)S(1)}, u32[]{:S(2)}, u32[]{:S(2)}) collective-permute-start(s32[16]{0:T(128)S(1)} %reduce.1), channel_id=1, source_target_pairs={{48,0},{96,48},{144,96},{192,144},{240,192},{288,240},{336,288},{3... | collective-permute-start | bytes 200 | tf_op jit(solution)/shard_map/ppermute | solution.py:14
  39.3 3.3 %collective-permute-done.1 = s32[16]{0:T(128)S(1)} collective-permute-done((s32[16]{0:T(128)S(1)}, s32[16]{0:T(128)S(1)}, u32[]{:S(2)}, u32[]{:S(2)}) %collective-permute-start.1) | collective-permute-done | bytes 96 | tf_op jit(solution)/shard_map/ppermute | solution.py:14
  45.4 5.0 %collective-permute-done.5 = s32[16]{0:T(128)S(1)} collective-permute-done((s32[16]{0:T(128)S(1)}, s32[16]{0:T(128)S(1)}, u32[]{:S(2)}, u32[]{:S(2)}) %collective-permute-start.5) | collective-permute-done | bytes 96 | tf_op jit(solution)/shard_map/ppermute | solution.py:14
  51.2 5.4 %all-to-all-start.3 = ((bf16[16,1,128,128]{3,2,1,0:T(8,128)(2,1)}), bf16[16,1,128,128]{3,2,1,0:T(8,128)(2,1)S(1)}, u32[]{:S(2)}, u32[]{:S(2)}) async-start(bf16[16,1,128,128]{3,2,1,0:T(8,128)(2,1)} %bitcast.15), calls=%async_computation.3 | async-start | bytes 1048576 | tf_op jit(solution)/shard_map/all_to_all | solution.py:77
  63.5 6.2 %all-to-all-done.3 = bf16[16,1,128,128]{3,2,1,0:T(8,128)(2,1)S(1)} async-done(((bf16[16,1,128,128]{3,2,1,0:T(8,128)(2,1)}), bf16[16,1,128,128]{3,2,1,0:T(8,128)(2,1)S(1)}, u32[]{:S(2)}, u32[]{:S(2)}) %all-to-all-start.3) | async-done | bytes 524320 | tf_op jit(solution)/shard_map/all_to_all | solution.py:77
  69.7 12.6 %all-to-all-start.2 = ((bf16[48,1,128,128]{3,2,1,0:T(8,128)(2,1)}), bf16[48,1,128,128]{3,2,1,0:T(8,128)(2,1)}, u32[]{:S(2)}, u32[]{:S(2)}) async-start(bf16[48,1,128,128]{3,2,1,0:T(8,128)(2,1)} %bitcast.12), calls=%async_computation.2 | async-start | bytes 3145728 | tf_op jit(solution)/shard_map/all_to_all | solution.py:68
  85.6 4.3 %collective-permute-start.4 = (s32[48]{0:T(128)S(1)}, s32[48]{0:T(128)S(1)}, u32[]{:S(2)}, u32[]{:S(2)}) collective-permute-start(s32[48]{0:T(128)S(1)} %collective-permute-done), channel_id=1, source_target_pairs={{1,0},{2,1},{3,2},{4,3},{5,4},{6,5},{7,6},{8,7},{9,8},{10,9},{11,1... | collective-permute-start | bytes 584 | tf_op jit(solution)/shard_map/ppermute | solution.py:14
  90.6 41.3 %collective-permute-done.4 = s32[48]{0:T(128)S(1)} collective-permute-done((s32[48]{0:T(128)S(1)}, s32[48]{0:T(128)S(1)}, u32[]{:S(2)}, u32[]{:S(2)}) %collective-permute-start.4) | collective-permute-done | bytes 224 | tf_op jit(solution)/shard_map/ppermute | solution.py:14
  135.5 2.3 %collective-permute-start.3 = (bf16[16,128,128]{2,1,0:T(8,128)(2,1)S(1)}, bf16[16,128,128]{2,1,0:T(8,128)(2,1)S(1)}, u32[]{:S(2)}, u32[]{:S(2)}) collective-permute-start(bf16[16,128,128]{2,1,0:T(8,128)(2,1)S(1)} %bitcast.85), channel_id=1, source_target_pairs={{48,0},{96,48},{144,96},{192,144},{240,192},{288,240},{336,288},{3... | collective-permute-start | bytes 1572872 | tf_op jit(solution)/shard_map/ppermute | solution.py:14
  138.0 14.1 %collective-permute-done.3 = bf16[16,128,128]{2,1,0:T(8,128)(2,1)S(1)} collective-permute-done((bf16[16,128,128]{2,1,0:T(8,128)(2,1)S(1)}, bf16[16,128,128]{2,1,0:T(8,128)(2,1)S(1)}, u32[]{:S(2)}, u32[]{:S(2)}) %collective-permute-start.3) | collective-permute-done | bytes 524320 | tf_op jit(solution)/shard_map/ppermute | solution.py:14
  154.0 7.2 %collective-permute-start.2 = (bf16[48,128,128]{2,1,0:T(8,128)(2,1)}, bf16[48,128,128]{2,1,0:T(8,128)(2,1)}, u32[]{:S(2)}, u32[]{:S(2)}) collective-permute-start(bf16[48,128,128]{2,1,0:T(8,128)(2,1)} %bitcast.13), channel_id=1, source_target_pairs={{1,0},{2,1},{3,2},{4,3},{5,4},{6,5},{7,6},{8,7},{9,8},{10,9},{11,1... | collective-permute-start | bytes 4718600 | tf_op jit(solution)/shard_map/ppermute | solution.py:14
  173.7 2.5 %fusion.20 = f32[48,128,128]{2,1,0:T(8,128)S(1)} fusion(bf16[48,128,128]{2,1,0:T(8,128)(2,1)} %gather_fusion.11, pred[48]{0:T(512)(128)(4,1)S(1)} %compare_and_fusion.7, bf16[48,1,128,128]{3,2,1,0:T(8,128)(2,1)} %all-to-all-done.2), kind=kOutput, calls=%fused_computation.39 | convolution fusion | flops 202113024 | bytes 6291504 | tf_op jit(solution)/shard_map/aij,ajk->aik/dot_general | solution.py:50
  176.3 2.9 %fusion.8 = f32[12,128,128]{2,0,1:T(8,128)S(1)} fusion(f32[48,128,128]{2,1,0:T(8,128)S(1)} %fusion.20, pred[48,2,12]{0,2,1:T(8,128)(4,1)S(1)} %get-tuple-element.12), kind=kOutput, calls=%fused_computation.27 | convolution fusion | flops 113246208 | bytes 3934208 | tf_op jit(solution)/shard_map/ap,aik->pik/dot_general | solution.py:51
  181.4 3.9 %collective-permute-done.2 = bf16[48,128,128]{2,1,0:T(8,128)(2,1)} collective-permute-done((bf16[48,128,128]{2,1,0:T(8,128)(2,1)}, bf16[48,128,128]{2,1,0:T(8,128)(2,1)}, u32[]{:S(2)}, u32[]{:S(2)}) %collective-permute-start.2) | collective-permute-done | bytes 1572896 | tf_op jit(solution)/shard_map/ppermute | solution.py:14
  185.3 12.7 %collective-permute-start.6 = (bf16[48,128,128]{2,1,0:T(8,128)(2,1)}, bf16[48,128,128]{2,1,0:T(8,128)(2,1)S(1)}, u32[]{:S(2)}, u32[]{:S(2)}) collective-permute-start(bf16[48,128,128]{2,1,0:T(8,128)(2,1)} %collective-permute-done.2), channel_id=1, source_target_pairs={{1,0},{2,1},{3,2},{4,3},{5,4},{6,5},{7,6},{8,7},{9,8},{10,9},{11,1... | collective-permute-start | bytes 4718600 | tf_op jit(solution)/shard_map/ppermute | solution.py:14
  200.1 2.9 %fusion.4 = f32[12,128,128]{2,0,1:T(8,128)S(1)} fusion(f32[48,128,128]{2,1,0:T(8,128)S(1)} %fusion.16, pred[48,2,12]{0,2,1:T(8,128)(4,1)S(1)} %get-tuple-element.13), kind=kOutput, calls=%fused_computation.23 | convolution fusion | flops 113246208 | bytes 3934208 | tf_op jit(solution)/shard_map/ap,aik->pik/dot_general | solution.py:51
  205.2 2.9 %fusion.6 = f32[12,128,128]{2,0,1:T(8,128)S(1)} fusion(f32[48,128,128]{2,1,0:T(8,128)S(1)} %fusion.18, pred[48,2,12]{0,2,1:T(8,128)(4,1)S(1)} %get-tuple-element.13), kind=kOutput, calls=%fused_computation.25 | convolution fusion | flops 113246208 | bytes 3934208 | tf_op jit(solution)/shard_map/ap,aik->pik/dot_general | solution.py:51
  208.1 3.0 %fusion.36 = f32[12,128,128]{2,0,1:T(8,128)S(1)} fusion(f32[12,128,128]{2,0,1:T(8,128)S(1)} %fusion.4, f32[12,128,128]{2,0,1:T(8,128)S(1)} %fusion.6, f32[12,128,128]{2,0,1:T(8,128)S(1)} %fusion.8, f32[48,128,128]{2,1,0:T(8,128)S(1)} %fusion.22, pred[48,2,12]{0,2,1:T(8,128)(4,1)S(1)} %get-tuple-element.12), kind=kOutput, calls=%fused_computation.51 | convolution fusion | flops 113836032 | bytes 7079936 | tf_op jit(solution)/shard_map/ap,aik->pik/dot_general | solution.py:51
  211.2 4.9 %collective-permute-done.6 = bf16[48,128,128]{2,1,0:T(8,128)(2,1)S(1)} collective-permute-done((bf16[48,128,128]{2,1,0:T(8,128)(2,1)}, bf16[48,128,128]{2,1,0:T(8,128)(2,1)S(1)}, u32[]{:S(2)}, u32[]{:S(2)}) %collective-permute-start.6) | collective-permute-done | bytes 1572896 | tf_op jit(solution)/shard_map/ppermute | solution.py:14
  216.7 3.2 %fusion = f32[12,128,128]{2,0,1:T(8,128)S(1)} fusion(f32[48,128,128]{2,1,0:T(8,128)S(1)} %fusion.12, pred[48,2,12]{0,2,1:T(8,128)(4,1)S(1)} %get-tuple-element.14), kind=kOutput, calls=%fused_computation.19 | convolution fusion | flops 113246208 | bytes 3934208 | tf_op jit(solution)/shard_map/ap,aik->pik/dot_general | solution.py:51
  220.6 3.0 %fusion.48 = bf16[1,1,12,128,128]{4,2,3,1,0:T(8,128)(2,1)S(1)} fusion(f32[12,128,128]{2,0,1:T(8,128)S(1)} %fusion, f32[12,128,128]{2,0,1:T(8,128)S(1)} %fusion.36, f32[48,128,128]{2,1,0:T(8,128)S(1)} %fusion.14, pred[48,2,12]{0,2,1:T(8,128)(4,1)S(1)} %get-tuple-element.14), kind=kOutput, calls=%fused_computation.55 | convolution fusion | flops 113836032 | bytes 5638144 | tf_op jit(solution)/shard_map/ap,aik->pik/dot_general | solution.py:51
  (135 shorter events, 47.9 us)
Async XLA Ops:
  0.0 14.2 %copy-start = (bf16[1,1,16,1,128,128]{5,4,3,2,1,0:T(8,128)(2,1)S(1)}, bf16[1,1,16,1,128,128]{5,4,3,2,1,0:T(8,128)(2,1)}, u32[]{:S(2)}) copy-start(bf16[1,1,16,1,128,128]{5,4,3,2,1,0:T(8,128)(2,1)} %param.7) | copy-start | bytes 1572868
  2.1 14.1 %all-to-all-start.1 = ((s32[16,1,1]{2,1,0:T(1,128)}), s32[16,1,1]{2,1,0:T(1,128)S(1)}, u32[]{:S(2)}, u32[]{:S(2)}) async-start(s32[16,1,1]{2,1,0:T(1,128)} %copy.51), calls=%async_computation.1 | async-start | bytes 16384 | tf_op jit(solution)/shard_map/all_to_all | solution.py:78
  16.2 35.0 %all-to-all-start = ((s32[48,1,1]{2,1,0:T(1,128)}), s32[48,1,1]{2,1,0:T(1,128)S(1)}, u32[]{:S(2)}, u32[]{:S(2)}) async-start(s32[48,1,1]{2,1,0:T(1,128)} %copy.50), calls=%async_computation | async-start | bytes 49152 | tf_op jit(solution)/shard_map/all_to_all | solution.py:69
  35.1 7.5 %collective-permute-start.1 = (s32[16]{0:T(128)S(1)}, s32[16]{0:T(128)S(1)}, u32[]{:S(2)}, u32[]{:S(2)}) collective-permute-start(s32[16]{0:T(128)S(1)} %reduce.1), channel_id=1, source_target_pairs={{48,0},{96,48},{144,96},{192,144},{240,192},{288,240},{336,288},{3... | collective-permute-start | bytes 200 | tf_op jit(solution)/shard_map/ppermute | solution.py:14
  42.8 7.5 %collective-permute-start.5 = (s32[16]{0:T(128)S(1)}, s32[16]{0:T(128)S(1)}, u32[]{:S(2)}, u32[]{:S(2)}) collective-permute-start(s32[16]{0:T(128)S(1)} %collective-permute-done.1), channel_id=1, source_target_pairs={{48,0},{96,48},{144,96},{192,144},{240,192},{288,240},{336,288},{3... | collective-permute-start | bytes 200 | tf_op jit(solution)/shard_map/ppermute | solution.py:14
  51.2 18.5 %all-to-all-start.3 = ((bf16[16,1,128,128]{3,2,1,0:T(8,128)(2,1)}), bf16[16,1,128,128]{3,2,1,0:T(8,128)(2,1)S(1)}, u32[]{:S(2)}, u32[]{:S(2)}) async-start(bf16[16,1,128,128]{3,2,1,0:T(8,128)(2,1)} %bitcast.15), calls=%async_computation.3 | async-start | bytes 1048576 | tf_op jit(solution)/shard_map/all_to_all | solution.py:77
  57.6 5.9 %collective-permute-start = (s32[48]{0:T(128)S(1)}, s32[48]{0:T(128)S(1)}, u32[]{:S(2)}, u32[]{:S(2)}) collective-permute-start(s32[48]{0:T(128)S(1)} %reduce), channel_id=1, source_target_pairs={{1,0},{2,1},{3,2},{4,3},{5,4},{6,5},{7,6},{8,7},{9,8},{10,9},{11,1... | collective-permute-start | bytes 584 | tf_op jit(solution)/shard_map/ppermute | solution.py:14
  69.7 84.3 %all-to-all-start.2 = ((bf16[48,1,128,128]{3,2,1,0:T(8,128)(2,1)}), bf16[48,1,128,128]{3,2,1,0:T(8,128)(2,1)}, u32[]{:S(2)}, u32[]{:S(2)}) async-start(bf16[48,1,128,128]{3,2,1,0:T(8,128)(2,1)} %bitcast.12), calls=%async_computation.2 | async-start | bytes 3145728 | tf_op jit(solution)/shard_map/all_to_all | solution.py:68
  85.6 46.3 %collective-permute-start.4 = (s32[48]{0:T(128)S(1)}, s32[48]{0:T(128)S(1)}, u32[]{:S(2)}, u32[]{:S(2)}) collective-permute-start(s32[48]{0:T(128)S(1)} %collective-permute-done), channel_id=1, source_target_pairs={{1,0},{2,1},{3,2},{4,3},{5,4},{6,5},{7,6},{8,7},{9,8},{10,9},{11,1... | collective-permute-start | bytes 584 | tf_op jit(solution)/shard_map/ppermute | solution.py:14
  133.9 27.6 %copy-start.6 = (s32[1,1,12]{2,1,0:T(1,128)S(1)}, s32[1,1,12]{2,1,0:T(1,128)}, u32[]{:S(2)}) copy-start(s32[1,1,12]{2,1,0:T(1,128)} %param.11) | copy-start | bytes 148
  135.5 16.6 %collective-permute-start.3 = (bf16[16,128,128]{2,1,0:T(8,128)(2,1)S(1)}, bf16[16,128,128]{2,1,0:T(8,128)(2,1)S(1)}, u32[]{:S(2)}, u32[]{:S(2)}) collective-permute-start(bf16[16,128,128]{2,1,0:T(8,128)(2,1)S(1)} %bitcast.85), channel_id=1, source_target_pairs={{48,0},{96,48},{144,96},{192,144},{240,192},{288,240},{336,288},{3... | collective-permute-start | bytes 1572872 | tf_op jit(solution)/shard_map/ppermute | solution.py:14
  152.1 17.7 %collective-permute-start.7 = (bf16[16,128,128]{2,1,0:T(8,128)(2,1)S(1)}, bf16[16,128,128]{2,1,0:T(8,128)(2,1)S(1)}, u32[]{:S(2)}, u32[]{:S(2)}) collective-permute-start(bf16[16,128,128]{2,1,0:T(8,128)(2,1)S(1)} %collective-permute-done.3), channel_id=1, source_target_pairs={{48,0},{96,48},{144,96},{192,144},{240,192},{288,240},{336,288},{3... | collective-permute-start | bytes 1572872 | tf_op jit(solution)/shard_map/ppermute | solution.py:14
  154.0 31.3 %collective-permute-start.2 = (bf16[48,128,128]{2,1,0:T(8,128)(2,1)}, bf16[48,128,128]{2,1,0:T(8,128)(2,1)}, u32[]{:S(2)}, u32[]{:S(2)}) collective-permute-start(bf16[48,128,128]{2,1,0:T(8,128)(2,1)} %bitcast.13), channel_id=1, source_target_pairs={{1,0},{2,1},{3,2},{4,3},{5,4},{6,5},{7,6},{8,7},{9,8},{10,9},{11,1... | collective-permute-start | bytes 4718600 | tf_op jit(solution)/shard_map/ppermute | solution.py:14
  176.2 2.9 %copy-start.5 = (bf16[48,128,128]{2,1,0:T(8,128)(2,1)S(1)}, bf16[48,128,128]{2,1,0:T(8,128)(2,1)}, u32[]{:S(2)}) copy-start(bf16[48,128,128]{2,1,0:T(8,128)(2,1)} %gather_fusion.10) | copy-start | bytes 4718596
  179.2 18.9 %copy-start.4 = (bf16[48,128,128]{2,1,0:T(8,128)(2,1)S(1)}, bf16[48,128,128]{2,1,0:T(8,128)(2,1)}, u32[]{:S(2)}) copy-start(bf16[48,128,128]{2,1,0:T(8,128)(2,1)} %gather_fusion.13) | copy-start | bytes 4718596
  185.3 30.8 %collective-permute-start.6 = (bf16[48,128,128]{2,1,0:T(8,128)(2,1)}, bf16[48,128,128]{2,1,0:T(8,128)(2,1)S(1)}, u32[]{:S(2)}, u32[]{:S(2)}) collective-permute-start(bf16[48,128,128]{2,1,0:T(8,128)(2,1)} %collective-permute-done.2), channel_id=1, source_target_pairs={{1,0},{2,1},{3,2},{4,3},{5,4},{6,5},{7,6},{8,7},{9,8},{10,9},{11,1... | collective-permute-start | bytes 4718600 | tf_op jit(solution)/shard_map/ppermute | solution.py:14
  200.1 2.9 %copy-start.3 = (bf16[48,128,128]{2,1,0:T(8,128)(2,1)S(1)}, bf16[48,128,128]{2,1,0:T(8,128)(2,1)}, u32[]{:S(2)}) copy-start(bf16[48,128,128]{2,1,0:T(8,128)(2,1)} %gather_fusion.12) | copy-start | bytes 4718596
  208.1 8.0 %copy-start.2 = (bf16[48,128,128]{2,1,0:T(8,128)(2,1)S(1)}, bf16[48,128,128]{2,1,0:T(8,128)(2,1)}, u32[]{:S(2)}) copy-start(bf16[48,128,128]{2,1,0:T(8,128)(2,1)} %gather_fusion.15) | copy-start | bytes 4718596
  216.7 3.2 %copy-start.1 = (bf16[48,128,128]{2,1,0:T(8,128)(2,1)S(1)}, bf16[48,128,128]{2,1,0:T(8,128)(2,1)}, u32[]{:S(2)}) copy-start(bf16[48,128,128]{2,1,0:T(8,128)(2,1)} %gather_fusion.14) | copy-start | bytes 4718596
where the time goes:
time: 225 us; the launch traced here: 224 us
  starting transfers between devices  79.8 us (35%)
  waiting for transfers between devices  79.1 us (35%)
  local copies, waits for them, and re-layouts  33.3 us (15%)
  matrix products  28.1 us (12%)
  other arithmetic  3.41 us (2%)
    ppermute x8, waiting for transfers between devices, passed_along(): return lax.ppermute(block, axis, route)  72.9 us
    ppermute x8, starting transfers between devices, passed_along(): return lax.ppermute(block, axis, route)  35.7 us
    all_to_all x1, starting transfers between devices, local(): lax.all_to_all(left_code_send, 'col', split_axis=0, concat_axis=0, tiled=...  18.5 us
    dot_general x6, matrix products, panel_product(): jnp.einsum('ap,aik->pik', landing[:, rank_number, :], pieces, precision=l...  18 us
    all_to_all x1, starting transfers between devices, local(): lax.all_to_all(left_send, 'col', split_axis=0, concat_axis=0, tiled=True)  12.6 us
    gather x6, local copies, waits for them, and re-layouts, panel_product(): chosen = jnp.take(right_blocks, safe_partner[:, rank_number], axis=0)  11.8 us
    dot_general x6, matrix products, panel_product(): jnp.einsum('aij,ajk->aik', left_blocks, chosen, preferred_element_type=jn...  10.1 us
    all_to_all x1, starting transfers between devices, local(): lax.all_to_all(right_code_send, 'row', split_axis=0, concat_axis=0, tiled...  7.52 us
  transfers between devices with their start and end apart: 12, of which 8 were waited for; matrix products, arithmetic and copies ran while one was open for 24% of the time, Pallas kernels for 0%

commit v1 on v0

v1 whole, which is shorter than its diff:
```python
import functools

import jax
import jax.numpy as jnp
from jax import lax
from jax.experimental import pallas as pl
from jax.experimental.pallas import tpu as pltpu
from jax.sharding import Mesh
from jax.sharding import PartitionSpec as P

AXES = ("xl", "y", "xh", "z", "core")
ROW = ("xl", "y")
COL = ("xh", "z", "core")
SIZES = (2, 8, 2, 12, 2)
NZ = 12
BC = 16
PANEL = 48
STEPS = 3
KEPT = 12
BLK = 128

GROUPS = (
    (((0, 0), (1, 1), (3, -1), (2, -2)), ((1, 0), (2, 1), (3, 2), (0, -1))),
    (((2, 2), (3, 3), (1, -3)), ((0, 3), (3, -2), (2, -3))),
    (((0, -4), (3, -5)), ((1, 4), (2, 5))),
    (((1, 5), (2, 6), (0, 4)), ((1, -4), (3, -6), (0, -5))),
)


def rot(distance):
    return [(i, (i + distance) % NZ) for i in range(NZ)]


def shifted(block, distance):
    return lax.ppermute(block, "z", rot(distance))


def shifted_across(block, distance):
    route = [
        (h * NZ + i, (1 - h) * NZ + (i + distance) % NZ) for h in range(2) for i in range(NZ)
    ]
    return lax.ppermute(block, ("xh", "z"), route)


def copy_blocks_kernel(order, outs_of, index_ref, src_ref, *rest):
    outs, sems = rest[: len(outs_of)], rest[len(outs_of)]
    copies = []
    at = 0
    for out, count in zip(outs, outs_of, strict=True):
        for n in range(count):
            copies.append(
                pltpu.make_async_copy(
                    src_ref.at[pl.ds(index_ref[order[at]], 1)], out.at[pl.ds(n, 1)], sems.at[at]
                )
            )
            at += 1
    for copy in copies:
        copy.start()
    for copy in copies:
        copy.wait()


def copy_blocks(src, index, order, outs_of):
    total = sum(outs_of)
    return pl.pallas_call(
        functools.partial(copy_blocks_kernel, order, outs_of),
        out_shape=[jax.ShapeDtypeStruct((n, BLK, BLK), src.dtype) for n in outs_of],
        in_specs=[
            pl.BlockSpec(memory_space=pltpu.SMEM),
            pl.BlockSpec(memory_space=pl.ANY),
        ],
        out_specs=[pl.BlockSpec(memory_space=pl.ANY) for _ in outs_of],
        scratch_shapes=[pltpu.SemaphoreType.DMA((total,))],
        cost_estimate=pl.CostEstimate(
            flops=0, bytes_accessed=2 * total * BLK * BLK * 2, transcendentals=0
        ),
    )(index, src)


def product_kernel(counts, table_ref, b_ref, *rest):
    lefts, out_ref, acc = rest[: len(counts)], rest[len(counts)], rest[len(counts) + 1]
    acc[...] = jnp.zeros_like(acc)
    base = 0
    for left, count in zip(lefts, counts, strict=True):

        def body(n, carry, left=left, base=base):
            block = left[n]
            for rank in range(2):
                place = table_ref[2 * rank + 1, base + n]
                right = b_ref[table_ref[2 * rank, base + n]]
                acc[place] += jnp.dot(block, right, preferred_element_type=jnp.float32)
            return carry

        lax.fori_loop(0, count, body, 0, unroll=6)
        base += count
    out_ref[...] = acc[:KEPT].astype(out_ref.dtype)


def product(table, right, lefts):
    counts = tuple(left.shape[0] for left in lefts)
    total = sum(counts)
    return pl.pallas_call(
        functools.partial(product_kernel, counts),
        out_shape=jax.ShapeDtypeStruct((KEPT, BLK, BLK), jnp.bfloat16),
        in_specs=[pl.BlockSpec(memory_space=pltpu.SMEM)]
        + [pl.BlockSpec(memory_space=pltpu.VMEM)] * (1 + len(lefts)),
        out_specs=pl.BlockSpec(memory_space=pltpu.VMEM),
        scratch_shapes=[pltpu.VMEM((KEPT + 1, BLK, BLK), jnp.float32)],
        compiler_params=pltpu.CompilerParams(vmem_limit_bytes=32 << 20),
        cost_estimate=pl.CostEstimate(
            flops=total * 4 * BLK**3, bytes_accessed=total * BLK * BLK * 2, transcendentals=0
        ),
    )(table, right, *lefts)


def tables(a_code, b_code, c_code, r, z, h, core):
    a_all = lax.all_gather(a_code, COL).reshape(2, NZ, 2, 16)
    b_all = lax.all_gather(b_code, ROW)
    c = 24 * h + 2 * z + core
    a_cyc = jnp.concatenate([a_all, a_all], axis=3)
    mine = lax.dynamic_slice_in_dim(a_cyc, (r + 24 * h + 2 * z) % 16, 4, 3)
    mine = jnp.concatenate([mine, mine], axis=1)[:, ::-1]
    mine = lax.dynamic_slice_in_dim(mine, NZ - 1 - z, NZ, 1)
    mine = jnp.where(h == 0, mine, mine[::-1])
    mine = jnp.where(core == 0, mine, mine[:, :, ::-1])
    b_cyc = jnp.concatenate([b_all, b_all], axis=1)
    right = lax.dynamic_slice_in_dim(b_cyc, (r + c) % 16, STEPS, 1).T
    is0 = core == 0
    steps = jnp.stack(
        [jnp.where(is0, 1, 0), jnp.where(is0, 2, 1), jnp.where(is0, 0, 2)]
    )
    right = jnp.stack(
        [
            jnp.where(is0, right[1], right[0]),
            jnp.where(is0, right[2], right[1]),
            jnp.where(is0, right[0], right[2]),
        ]
    )
    codes, slots = [], []
    for low, high in GROUPS:
        for other in range(2):
            for half in range(2):

                def pick(items, panel):
                    return [mine[half, d % NZ, other, panel] for _, d in items]

                codes += pick(low, 1) + pick(high, 2)
                codes += [
                    jnp.where(is0, x, y) for x, y in zip(pick(low, 0), pick(high, 3), strict=True)
                ]
                slots += [0] * len(low) + [1] * len(low) + [2] * len(low)
    codes = jnp.stack(codes)
    count = codes.shape[0]
    which = jnp.array(slots, jnp.int32)
    one_hot = which[:, None] == jnp.arange(3)[None, :]
    right_live = right >= 0
    right_inner = jnp.where(right_live, right // BC, -1)
    right_col = right % BC
    owners = jnp.arange(16, dtype=jnp.int32)
    earlier = owners[None, :] < owners[:, None]
    rank = jnp.sum(
        ((right_inner[:, :, None] == right_inner[:, None, :]) & earlier[None]).astype(jnp.int32),
        axis=2,
    )
    packed = right_inner * 1024 + rank * 32 + right_col
    packed = jnp.where(right_live, packed, -1)

    def of_slot(x):
        return jnp.sum(jnp.where(one_hot[:, :, None], x[None], 0), axis=1)

    right_n = of_slot(packed)
    live_n = right_n >= 0
    step_n = jnp.sum(jnp.where(one_hot, steps[None, :], 0), axis=1)
    left_live = codes >= 0
    left_row = codes // PANEL
    left_inner = codes % PANEL
    match = live_n & left_live[:, None] & ((right_n // 1024) == left_inner[:, None])
    rows = []
    for rank_number in range(2):
        hit = match & ((right_n // 32) % 32 == rank_number)
        valid = jnp.any(hit, axis=1)
        owner = jnp.sum(jnp.where(hit, owners[None, :], 0), axis=1)
        column = jnp.sum(jnp.where(hit, right_n % 32, 0), axis=1)
        target = left_row * BC + column
        found = (target[:, None] == c_code[None, :]) & valid[:, None]
        place = jnp.sum(jnp.where(found, jnp.arange(KEPT)[None, :] - KEPT, 0), axis=1) + KEPT
        rows += [owner * STEPS + step_n, place]
    return jnp.stack(rows).astype(jnp.int32).reshape(4, count)


def local(a_own_values, a_own_code, b_own_values, b_own_code, c_code):
    r = lax.axis_index(ROW)
    h = lax.axis_index("xh")
    z = lax.axis_index("z")
    core = lax.axis_index("core")
    is0 = core == 0
    c = 24 * h + 2 * z + core
    a_own = a_own_values.reshape(16, BLK, BLK)
    b_own = b_own_values.reshape(16, BLK, BLK)

    cyc = (r + 2 * z + jnp.arange(8, dtype=jnp.int32)) % 8
    a_index = jnp.concatenate([cyc, cyc + 8])
    order = tuple(e * 8 + 2 * a + b for a in (1, 2, 3, 0) for b in range(2) for e in range(2))
    first, second = copy_blocks(a_own, a_index, order, (8, 8))
    b_index = (c + jnp.arange(18, dtype=jnp.int32)) % 16
    b_order = tuple(n + t for n in range(16) for t in range(STEPS))
    (b_send,) = copy_blocks(b_own, b_index, b_order, (48,))

    items = {}

    def keep(moved, names):
        moved = moved.reshape(len(names), 2, 2, BLK, BLK)
        for n, name in enumerate(names):
            items[name] = moved[n]

    def joined(names):
        return jnp.stack([items[name] for name in names])

    keep(first, ((1, 0), (2, 0)))
    keep(second, ((3, 0), (0, 0)))
    up1 = shifted(first, 1)
    down1 = shifted(second, -1)
    up2 = shifted(second, 2)
    down2 = shifted(first, -2)
    right = lax.all_to_all(b_send.reshape(16, STEPS, BLK, BLK), ROW, 0, 0, tiled=True)
    right = right.reshape(48, BLK, BLK)
    keep(up1, ((1, 1), (2, 1)))
    keep(down1, ((3, -1), (0, -1)))
    keep(up2, ((3, 2), (0, 2)))
    keep(down2, ((1, -2), (2, -2)))
    keep(shifted(joined(((2, 1), (3, 2), (0, 2))), 1), ((2, 2), (3, 3), (0, 3)))
    keep(shifted(joined(((3, -1), (2, -2), (1, -2))), -1), ((3, -2), (2, -3), (1, -3)))
    keep(shifted(joined(((1, 1), (2, 2))), 3), ((1, 4), (2, 5)))
    keep(shifted(joined(((0, -1), (3, -2))), -3), ((0, -4), (3, -5)))

    def half_of(place):
        return [(r + 24 * h + 2 * (place % NZ) + w) % 16 // 8 for w in range(4)]

    def chosen(names, e):
        return jnp.stack(
            [jnp.where(e[b] == 0, items[name][b, 0], items[name][b, 1]) for name in names for b in range(2)]
        )

    def flipped(e):
        return [1 - x for x in e]

    lefts = []
    for number, (low, high) in enumerate(GROUPS):
        n = len(low)
        if number < 3:
            e = half_of(z)
            own = jnp.concatenate([chosen(low, e[:2]), chosen(high, e[2:])])
            out = jnp.concatenate(
                [chosen(low, flipped(e[:2])), chosen(high, flipped(e[2:]))]
            )
            other = lax.ppermute(out, "xh", [(0, 1), (1, 0)])
        else:
            e = half_of(z + 1)[:2]
            before = ((1, 4), (2, 5), (0, 3))
            own_low = shifted(chosen(before, e), 1)
            other_low = shifted_across(chosen(before, flipped(e)), 1)
            e = half_of(z - 1)[2:]
            before = ((1, -3), (3, -5), (0, -4))
            own_high = shifted(chosen(before, e), -1)
            other_high = shifted_across(chosen(before, flipped(e)), -1)
            own = jnp.concatenate([own_low, own_high])
            other = jnp.concatenate([other_low, other_high])
        kept, sent = [], []
        for part in (own, other):
            part = part.reshape(2, n, 2, BLK, BLK)
            low0, low1, high2, high3 = part[0, :, 0], part[0, :, 1], part[1, :, 0], part[1, :, 1]
            kept += [low1, high2, jnp.where(is0, low0, high3)]
            sent += [low1, high2, jnp.where(is0, high3, low0)]
        kept, sent = jnp.concatenate(kept), jnp.concatenate(sent)
        lefts += [kept, lax.ppermute(sent, "core", [(0, 1), (1, 0)])]

    table = tables(a_own_code.reshape(16), b_own_code.reshape(16), c_code.reshape(KEPT), r, z, h, core)
    return product(table, right, lefts)[None, None]


def solution(mesh):
    fine = Mesh(mesh.devices.reshape(SIZES), AXES)
    return jax.shard_map(
        local,
        mesh=fine,
        in_specs=(
            P(ROW, COL, None, None, None, None),
            P(ROW, COL, None, None),
            P(ROW, COL, None, None, None, None),
            P(ROW, COL, None, None),
            P(ROW, COL, None),
        ),
        out_specs=P(ROW, COL, None, None, None),
        check_vma=False,
    )
```

time: 225 us -> 439 us (1.95)
  the two profiles are of different devices: /device:TPU:60 before, /device:TPU:1 now
where the time goes in v1:
time: 439 us; the launch traced here: 436 us
  starting transfers between devices  106 us (24%)
  blocking collectives  86.1 us (20%)
  local copies, waits for them, and re-layouts  81.8 us (19%)
  Pallas kernels  75.6 us (17%)
  between operations  61.1 us (14%)
  other arithmetic  14.3 us (3%)
  waiting for transfers between devices  11.8 us (3%)
    pallas_call x2, Pallas kernels, copy_blocks(): pl.pallas_call(functools.partial(copy_blocks_kernel, order, outs_of), out...  67.6 us
    another operation x1, local copies, waits for them, and re-layouts, tables(): codes = jnp.stack(codes)  61.5 us
    all_gather x1, blocking collectives, tables(): a_all = lax.all_gather(a_code, COL).reshape(2, NZ, 2, 16)  60.5 us
    ppermute x10, starting transfers between devices, shifted(): return lax.ppermute(block, 'z', rot(distance))  43.3 us
    ppermute x4, starting transfers between devices, local(): lefts += [kept, lax.ppermute(sent, 'core', [(0, 1), (1, 0)])]  36.4 us
    all_gather x1, blocking collectives, tables(): b_all = lax.all_gather(b_code, ROW)  25.6 us
    unnamed x52, local copies, waits for them, and re-layouts  10.7 us
    unnamed x46, other arithmetic  10.6 us
  transfers between devices with their start and end apart: 20, of which 4 were waited for; matrix products, arithmetic and copies ran while one was open for 20% of the time, Pallas kernels for 11%

profile of v1, /device:TPU:1, one launch (start us, length us, event | category | flops | bytes accessed | tf_op | source)
XLA Modules:
  0.0 436.5 jit_solution(185943334687012430)
XLA Ops:
  0.7 17.8 %shard_map.65 = (bf16[8,128,128]{2,1,0:T(8,128)(2,1)}, bf16[8,128,128]{2,1,0:T(8,128)(2,1)}) custom-call(s32[16]{0:T(128)} %pad_add_fusion.4.index_ref, bf16[16,128,128]{2,1,0:T(8,128)(2,1)} %bitcast.802), custom_call_target="tpu_custom_call" | custom-call | bytes 1048576 | tf_op jit(solution)/shard_map/pallas_call | solution.py:65
  18.5 4.8 %collective-permute-start = (bf16[8,128,128]{2,1,0:T(8,128)(2,1)}, bf16[8,128,128]{2,1,0:T(8,128)(2,1)S(1)}, u32[]{:S(2)}, u32[]{:S(2)}) collective-permute-start(bf16[8,128,128]{2,1,0:T(8,128)(2,1)} %get-tuple-element.8), channel_id=1, source_target_pairs={{0,2},{2,4},{4,6},{6,8},{8,10},{10,12},{12,14},{14,16},{16,18},{18... | collective-permute-start | bytes 786440 | tf_op jit(solution)/shard_map/ppermute | solution.py:35
  23.3 13.4 %collective-permute-start.2 = (bf16[8,128,128]{2,1,0:T(8,128)(2,1)}, bf16[8,128,128]{2,1,0:T(8,128)(2,1)S(1)}, u32[]{:S(2)}, u32[]{:S(2)}) collective-permute-start(bf16[8,128,128]{2,1,0:T(8,128)(2,1)} %get-tuple-element.8), channel_id=1, source_target_pairs={{0,20},{2,22},{4,0},{6,2},{8,4},{10,6},{12,8},{14,10},{16,12},{18,... | collective-permute-start | bytes 786440 | tf_op jit(solution)/shard_map/ppermute | solution.py:35
  36.7 2.2 collective-permute-start.1
  38.9 2.8 collective-permute-start.3
  42.3 49.8 %shard_map.64 = bf16[48,128,128]{2,1,0:T(8,128)(2,1)} custom-call(s32[18]{0:T(128)} %and_select_fusion.1.index_ref, bf16[16,128,128]{2,1,0:T(8,128)(2,1)} %bitcast.801), custom_call_target="tpu_custom_call" | custom-call | bytes 3145728 | tf_op jit(solution)/shard_map/pallas_call | solution.py:65
  92.1 8.0 %all-to-all-start = ((bf16[16,3,128,128]{3,2,1,0:T(8,128)(2,1)}), bf16[16,3,128,128]{3,2,1,0:T(8,128)(2,1)S(1)}, u32[]{:S(2)}, u32[]{:S(2)}) async-start(bf16[16,3,128,128]{3,2,1,0:T(8,128)(2,1)} %bitcast.750), calls=%async_computation | async-start | bytes 3145728 | tf_op jit(solution)/shard_map/all_to_all | solution.py:225
  100.3 60.5 %all-gather.1 = s32[48,1,16,1]{2,3,1,0:T(1,128)S(1)} all-gather(s32[1,1,16,1]{2,3,1,0:T(1,128)S(1)} %copy-done.13), channel_id=3, replica_groups=mesh['xl'=2,'y'=8,'xh'=2,'z'=12,'core'=2] {'xh','z','core'}, dimensions={0}, use_global_device_ids=true | all-gather | bytes 3136 | tf_op jit(solution)/shard_map/all_gather | solution.py:117
  229.0 61.5 %stack.629 = s32[144]{0:T(256)S(1)} concatenate(s32[1]{0:T(128)} %bitcast.3, s32[1]{0:T(128)} %bitcast.4, s32[1]{0:T(128)} %bitcast.5, s32[1]{0:T(128)} %bitcast.6, s32[1]{0:T(128)} %bitcast.7, s32[1]{0:T(128)} %bitcast.8, s32[1]{0:T(128)} %bitcast.9, s32[1]{0:T(128)} %bitcast.10, s32[1]{0:T(128)} %bitcast.13, s32[1]{0:T(128)} %bitcast.16, s32[1]{0:T(128)} %bitcast.19, ...), dimensions={0} | concatenate | bytes 1152 | tf_op jit(solution)/shard_map/stack | solution.py:152
  290.9 25.6 %all-gather = s32[16,1,16,1]{2,3,1,0:T(1,128)S(1)} all-gather(s32[1,1,16,1]{2,3,1,0:T(1,128)S(1)} %copy-done.14), channel_id=2, replica_groups=mesh['xl'=2,'y'=8,'xh'=2,'z'=12,'core'=2] {'xl','y'}, dimensions={0}, use_global_device_ids=true | all-gather | bytes 1088 | tf_op jit(solution)/shard_map/all_gather | solution.py:118
  330.1 3.5 collective-permute-start.4
  335.6 4.6 %collective-permute-start.7 = (bf16[3,2,2,128,128]{4,3,2,1,0:T(8,128)(2,1)S(1)}, bf16[3,2,2,128,128]{4,3,2,1,0:T(8,128)(2,1)S(1)}, u32[]{:S(2)}, u32[]{:S(2)}) collective-permute-start(bf16[3,2,2,128,128]{4,3,2,1,0:T(8,128)(2,1)S(1)} %pad_maximum_fusion.1), channel_id=1, source_target_pairs={{0,22},{2,0},{4,2},{6,4},{8,6},{10,8},{12,10},{14,12},{16,14},{18,... | collective-permute-start | bytes 1179656 | tf_op jit(solution)/shard_map/ppermute | solution.py:35
  340.4 3.0 collective-permute-done.6
  345.6 6.4 %collective-permute-start.10 = (bf16[2,2,2,128,128]{4,3,2,1,0:T(8,128)(2,1)S(1)}, bf16[2,2,2,128,128]{4,3,2,1,0:T(8,128)(2,1)S(1)}, u32[]{:S(2)}, u32[]{:S(2)}) collective-permute-start(bf16[2,2,2,128,128]{4,3,2,1,0:T(8,128)(2,1)S(1)} %pad_maximum_fusion.4), channel_id=1, source_target_pairs={{0,18},{2,20},{4,22},{6,0},{8,2},{10,4},{12,6},{14,8},{16,10},{18,... | collective-permute-start | bytes 786440 | tf_op jit(solution)/shard_map/ppermute | solution.py:35
  352.3 18.3 %collective-permute-start.5 = (bf16[24,128,128]{2,1,0:T(8,128)(2,1)S(1)}, bf16[24,128,128]{2,1,0:T(8,128)(2,1)S(1)}, u32[]{:S(2)}, u32[]{:S(2)}) collective-permute-start(bf16[24,128,128]{2,1,0:T(8,128)(2,1)S(1)} %get-tuple-element.23), channel_id=1, source_target_pairs={{0,1},{1,0},{2,3},{3,2},{4,5},{5,4},{6,7},{7,6},{8,9},{9,8},{10,11... | collective-permute-start | bytes 2359304 | tf_op jit(solution)/shard_map/ppermute | solution.py:275
  371.6 3.3 collective-permute-start.8
  375.0 3.5 collective-permute-start.12
  380.5 3.4 collective-permute-start.14
  385.3 3.9 collective-permute-start.17
  389.2 3.8 collective-permute-start.16
  394.8 5.8 %collective-permute-done.16 = bf16[6,128,128]{2,1,0:T(8,128)(2,1)S(1)} collective-permute-done((bf16[6,128,128]{2,1,0:T(8,128)(2,1)S(1)}, bf16[6,128,128]{2,1,0:T(8,128)(2,1)S(1)}, u32[]{:S(2)}, u32[]{:S(2)}) %collective-permute-start.16) | collective-permute-done | bytes 196640 | tf_op jit(solution)/shard_map/ppermute | solution.py:42
  400.8 13.7 %collective-permute-start.18 = (bf16[18,128,128]{2,1,0:T(8,128)(2,1)S(1)}, bf16[18,128,128]{2,1,0:T(8,128)(2,1)S(1)}, u32[]{:S(2)}, u32[]{:S(2)}) collective-permute-start(bf16[18,128,128]{2,1,0:T(8,128)(2,1)S(1)} %get-tuple-element.27), channel_id=1, source_target_pairs={{0,1},{1,0},{2,3},{3,2},{4,5},{5,4},{6,7},{7,6},{8,9},{9,8},{10,11... | collective-permute-start | bytes 1769480 | tf_op jit(solution)/shard_map/ppermute | solution.py:275
  416.7 2.4 collective-permute-start.13
  428.5 7.9 %shard_map.66 = bf16[12,128,128]{2,1,0:T(8,128)(2,1)} custom-call(s32[4,144]{1,0:T(4,128)S(1)} %pad_add_fusion.1.table_ref, bf16[48,128,128]{2,1,0:T(8,128)(2,1)S(1)} %bitcast.749, bf16[24,128,128]{2,1,0:T(8,128)(2,1)S(1)} %constant_dynamic-update-slice_fusion.32.rest_0_, bf16[24,128,128]{2,1,0:T(8,128)(2,1)S(1)} %copy-done.3, ...), custom_call_target="tpu_custom_call" | custom-call | flops 1207959552 | bytes 4718592 | tf_op jit(solution)/shard_map/pallas_call | solution.py:102
  (196 shorter events, 45.3 us)
Async XLA Ops:
  18.5 301.6 %collective-permute-start = (bf16[8,128,128]{2,1,0:T(8,128)(2,1)}, bf16[8,128,128]{2,1,0:T(8,128)(2,1)S(1)}, u32[]{:S(2)}, u32[]{:S(2)}) collective-permute-start(bf16[8,128,128]{2,1,0:T(8,128)(2,1)} %get-tuple-element.8), channel_id=1, source_target_pairs={{0,2},{2,4},{4,6},{6,8},{8,10},{10,12},{12,14},{14,16},{16,18},{18... | collective-permute-start | bytes 786440 | tf_op jit(solution)/shard_map/ppermute | solution.py:35
  23.3 299.3 %collective-permute-start.2 = (bf16[8,128,128]{2,1,0:T(8,128)(2,1)}, bf16[8,128,128]{2,1,0:T(8,128)(2,1)S(1)}, u32[]{:S(2)}, u32[]{:S(2)}) collective-permute-start(bf16[8,128,128]{2,1,0:T(8,128)(2,1)} %get-tuple-element.8), channel_id=1, source_target_pairs={{0,20},{2,22},{4,0},{6,2},{8,4},{10,6},{12,8},{14,10},{16,12},{18,... | collective-permute-start | bytes 786440 | tf_op jit(solution)/shard_map/ppermute | solution.py:35
  36.7 284.7 %collective-permute-start.1 = (bf16[8,128,128]{2,1,0:T(8,128)(2,1)}, bf16[8,128,128]{2,1,0:T(8,128)(2,1)S(1)}, u32[]{:S(2)}, u32[]{:S(2)}) collective-permute-start(bf16[8,128,128]{2,1,0:T(8,128)(2,1)} %get-tuple-element.7), channel_id=1, source_target_pairs={{0,22},{2,0},{4,2},{6,4},{8,6},{10,8},{12,10},{14,12},{16,14},{18,... | collective-permute-start | bytes 786440 | tf_op jit(solution)/shard_map/ppermute | solution.py:35
  38.9 287.6 %collective-permute-start.3 = (bf16[8,128,128]{2,1,0:T(8,128)(2,1)}, bf16[8,128,128]{2,1,0:T(8,128)(2,1)S(1)}, u32[]{:S(2)}, u32[]{:S(2)}) collective-permute-start(bf16[8,128,128]{2,1,0:T(8,128)(2,1)} %get-tuple-element.7), channel_id=1, source_target_pairs={{0,4},{2,6},{4,8},{6,10},{8,12},{10,14},{12,16},{14,18},{16,20},{1... | collective-permute-start | bytes 786440 | tf_op jit(solution)/shard_map/ppermute | solution.py:35
  92.1 198.5 %copy-start.10 = (bf16[8,128,128]{2,1,0:T(8,128)(2,1)S(1)}, bf16[8,128,128]{2,1,0:T(8,128)(2,1)}, u32[]{:S(2)}) copy-start(bf16[8,128,128]{2,1,0:T(8,128)(2,1)} %get-tuple-element.7) | copy-start | bytes 786436
  92.1 331.1 %all-to-all-start = ((bf16[16,3,128,128]{3,2,1,0:T(8,128)(2,1)}), bf16[16,3,128,128]{3,2,1,0:T(8,128)(2,1)S(1)}, u32[]{:S(2)}, u32[]{:S(2)}) async-start(bf16[16,3,128,128]{3,2,1,0:T(8,128)(2,1)} %bitcast.750), calls=%async_computation | async-start | bytes 3145728 | tf_op jit(solution)/shard_map/all_to_all | solution.py:225
  100.1 190.6 %copy-start.11 = (s32[144]{0:T(256)S(1)}, s32[144]{0:T(256)}, u32[]{:S(2)}) copy-start(s32[144]{0:T(256)} %constant.336.clone) | copy-start | bytes 1732
  100.2 190.7 %copy-start.14 = (s32[1,1,16,1]{2,3,1,0:T(1,128)S(1)}, s32[1,1,16,1]{2,3,1,0:T(1,128)}, u32[]{:S(2)}) copy-start(s32[1,1,16,1]{2,3,1,0:T(1,128)} %param.9) | copy-start | bytes 196
  100.2 217.2 %copy-start.15 = (s32[1,1,12]{2,1,0:T(1,128)S(1)}, s32[1,1,12]{2,1,0:T(1,128)}, u32[]{:S(2)}) copy-start(s32[1,1,12]{2,1,0:T(1,128)} %param.10) | copy-start | bytes 148
  330.1 22.1 %collective-permute-start.4 = (bf16[16,128,128]{2,1,0:T(8,128)(2,1)S(1)}, bf16[16,128,128]{2,1,0:T(8,128)(2,1)S(1)}, u32[]{:S(2)}, u32[]{:S(2)}) collective-permute-start(bf16[16,128,128]{2,1,0:T(8,128)(2,1)S(1)} %copy-done.12), channel_id=1, source_target_pairs={{0,24},{24,0},{1,25},{25,1},{2,26},{26,2},{3,27},{27,3},{4,28},{28... | collective-permute-start | bytes 1572872 | tf_op jit(solution)/shard_map/ppermute | solution.py:256
  333.7 9.7 %collective-permute-start.6 = (bf16[3,2,2,128,128]{4,3,2,1,0:T(8,128)(2,1)S(1)}, bf16[3,2,2,128,128]{4,3,2,1,0:T(8,128)(2,1)S(1)}, u32[]{:S(2)}, u32[]{:S(2)}) collective-permute-start(bf16[3,2,2,128,128]{4,3,2,1,0:T(8,128)(2,1)S(1)} %pad_maximum_fusion), channel_id=1, source_target_pairs={{0,2},{2,4},{4,6},{6,8},{8,10},{10,12},{12,14},{14,16},{16,18},{18... | collective-permute-start | bytes 1179656 | tf_op jit(solution)/shard_map/ppermute | solution.py:35
  335.6 9.8 %collective-permute-start.7 = (bf16[3,2,2,128,128]{4,3,2,1,0:T(8,128)(2,1)S(1)}, bf16[3,2,2,128,128]{4,3,2,1,0:T(8,128)(2,1)S(1)}, u32[]{:S(2)}, u32[]{:S(2)}) collective-permute-start(bf16[3,2,2,128,128]{4,3,2,1,0:T(8,128)(2,1)S(1)} %pad_maximum_fusion.1), channel_id=1, source_target_pairs={{0,22},{2,0},{4,2},{6,4},{8,6},{10,8},{12,10},{14,12},{16,14},{18,... | collective-permute-start | bytes 1179656 | tf_op jit(solution)/shard_map/ppermute | solution.py:35
  343.5 27.5 %collective-permute-start.11 = (bf16[2,2,2,128,128]{4,3,2,1,0:T(8,128)(2,1)S(1)}, bf16[2,2,2,128,128]{4,3,2,1,0:T(8,128)(2,1)S(1)}, u32[]{:S(2)}, u32[]{:S(2)}) collective-permute-start(bf16[2,2,2,128,128]{4,3,2,1,0:T(8,128)(2,1)S(1)} %pad_maximum_fusion.5), channel_id=1, source_target_pairs={{0,6},{2,8},{4,10},{6,12},{8,14},{10,16},{12,18},{14,20},{16,22},{... | collective-permute-start | bytes 786440 | tf_op jit(solution)/shard_map/ppermute | solution.py:35
  345.6 25.1 %collective-permute-start.10 = (bf16[2,2,2,128,128]{4,3,2,1,0:T(8,128)(2,1)S(1)}, bf16[2,2,2,128,128]{4,3,2,1,0:T(8,128)(2,1)S(1)}, u32[]{:S(2)}, u32[]{:S(2)}) collective-permute-start(bf16[2,2,2,128,128]{4,3,2,1,0:T(8,128)(2,1)S(1)} %pad_maximum_fusion.4), channel_id=1, source_target_pairs={{0,18},{2,20},{4,22},{6,0},{8,2},{10,4},{12,6},{14,8},{16,10},{18,... | collective-permute-start | bytes 786440 | tf_op jit(solution)/shard_map/ppermute | solution.py:35
  352.3 67.6 %collective-permute-start.5 = (bf16[24,128,128]{2,1,0:T(8,128)(2,1)S(1)}, bf16[24,128,128]{2,1,0:T(8,128)(2,1)S(1)}, u32[]{:S(2)}, u32[]{:S(2)}) collective-permute-start(bf16[24,128,128]{2,1,0:T(8,128)(2,1)S(1)} %get-tuple-element.23), channel_id=1, source_target_pairs={{0,1},{1,0},{2,3},{3,2},{4,5},{5,4},{6,7},{7,6},{8,9},{9,8},{10,11... | collective-permute-start | bytes 2359304 | tf_op jit(solution)/shard_map/ppermute | solution.py:275
  371.6 43.0 %collective-permute-start.8 = (bf16[12,128,128]{2,1,0:T(8,128)(2,1)S(1)}, bf16[12,128,128]{2,1,0:T(8,128)(2,1)S(1)}, u32[]{:S(2)}, u32[]{:S(2)}) collective-permute-start(bf16[12,128,128]{2,1,0:T(8,128)(2,1)S(1)} %get-tuple-element.100), channel_id=1, source_target_pairs={{0,24},{24,0},{1,25},{25,1},{2,26},{26,2},{3,27},{27,3},{4,28},{28... | collective-permute-start | bytes 1179656 | tf_op jit(solution)/shard_map/ppermute | solution.py:256
  375.0 39.6 %collective-permute-start.12 = (bf16[8,128,128]{2,1,0:T(8,128)(2,1)S(1)}, bf16[8,128,128]{2,1,0:T(8,128)(2,1)S(1)}, u32[]{:S(2)}, u32[]{:S(2)}) collective-permute-start(bf16[8,128,128]{2,1,0:T(8,128)(2,1)S(1)} %get-tuple-element.69), channel_id=1, source_target_pairs={{0,24},{24,0},{1,25},{25,1},{2,26},{26,2},{3,27},{27,3},{4,28},{28... | collective-permute-start | bytes 786440 | tf_op jit(solution)/shard_map/ppermute | solution.py:256
  378.6 6.7 %collective-permute-start.15 = (bf16[6,128,128]{2,1,0:T(8,128)(2,1)S(1)}, bf16[6,128,128]{2,1,0:T(8,128)(2,1)S(1)}, u32[]{:S(2)}, u32[]{:S(2)}) collective-permute-start(bf16[6,128,128]{2,1,0:T(8,128)(2,1)S(1)} %constant_dynamic-update-slice_fusion.114), channel_id=1, source_target_pairs={{0,22},{2,0},{4,2},{6,4},{8,6},{10,8},{12,10},{14,12},{16,14},{18,... | collective-permute-start | bytes 589832 | tf_op jit(solution)/shard_map/ppermute | solution.py:35
  380.5 8.7 %collective-permute-start.14 = (bf16[6,128,128]{2,1,0:T(8,128)(2,1)S(1)}, bf16[6,128,128]{2,1,0:T(8,128)(2,1)S(1)}, u32[]{:S(2)}, u32[]{:S(2)}) collective-permute-start(bf16[6,128,128]{2,1,0:T(8,128)(2,1)S(1)} %constant_dynamic-update-slice_fusion.108), channel_id=1, source_target_pairs={{0,2},{2,4},{4,6},{6,8},{8,10},{10,12},{12,14},{14,16},{16,18},{18... | collective-permute-start | bytes 589832 | tf_op jit(solution)/shard_map/ppermute | solution.py:35
  385.3 9.5 %collective-permute-start.17 = (bf16[6,128,128]{2,1,0:T(8,128)(2,1)S(1)}, bf16[6,128,128]{2,1,0:T(8,128)(2,1)S(1)}, u32[]{:S(2)}, u32[]{:S(2)}) collective-permute-start(bf16[6,128,128]{2,1,0:T(8,128)(2,1)S(1)} %get-tuple-element.80), channel_id=1, source_target_pairs={{0,46},{2,24},{4,26},{6,28},{8,30},{10,32},{12,34},{14,36},{16,38}... | collective-permute-start | bytes 589832 | tf_op jit(solution)/shard_map/ppermute | solution.py:42
  389.2 11.4 %collective-permute-start.16 = (bf16[6,128,128]{2,1,0:T(8,128)(2,1)S(1)}, bf16[6,128,128]{2,1,0:T(8,128)(2,1)S(1)}, u32[]{:S(2)}, u32[]{:S(2)}) collective-permute-start(bf16[6,128,128]{2,1,0:T(8,128)(2,1)S(1)} %get-tuple-element.59), channel_id=1, source_target_pairs={{0,26},{2,28},{4,30},{6,32},{8,34},{10,36},{12,38},{14,40},{16,42}... | collective-permute-start | bytes 589832 | tf_op jit(solution)/shard_map/ppermute | solution.py:42
  400.8 20.8 %collective-permute-start.18 = (bf16[18,128,128]{2,1,0:T(8,128)(2,1)S(1)}, bf16[18,128,128]{2,1,0:T(8,128)(2,1)S(1)}, u32[]{:S(2)}, u32[]{:S(2)}) collective-permute-start(bf16[18,128,128]{2,1,0:T(8,128)(2,1)S(1)} %get-tuple-element.27), channel_id=1, source_target_pairs={{0,1},{1,0},{2,3},{3,2},{4,5},{5,4},{6,7},{7,6},{8,9},{9,8},{10,11... | collective-permute-start | bytes 1769480 | tf_op jit(solution)/shard_map/ppermute | solution.py:275
  414.7 7.7 %collective-permute-start.9 = (bf16[18,128,128]{2,1,0:T(8,128)(2,1)S(1)}, bf16[18,128,128]{2,1,0:T(8,128)(2,1)S(1)}, u32[]{:S(2)}, u32[]{:S(2)}) collective-permute-start(bf16[18,128,128]{2,1,0:T(8,128)(2,1)S(1)} %get-tuple-element.39), channel_id=1, source_target_pairs={{0,1},{1,0},{2,3},{3,2},{4,5},{5,4},{6,7},{7,6},{8,9},{9,8},{10,11... | collective-permute-start | bytes 1769480 | tf_op jit(solution)/shard_map/ppermute | solution.py:275
  416.7 4.1 collective-permute-start.13
  (12 other events, 18.5 us)

commit v2 on v0

v2 whole, which is shorter than its diff:
```python
import functools

import jax
import jax.numpy as jnp
import numpy as np
from jax import lax
from jax.experimental import pallas as pl
from jax.experimental.pallas import tpu as pltpu
from jax.sharding import Mesh
from jax.sharding import PartitionSpec as P

AXES = ("xl", "y", "xh", "z", "core")
ROW = ("xl", "y")
COL = ("xh", "z", "core")
SIZES = (2, 8, 2, 12, 2)
NZ = 12
BC = 16
PANEL = 48
STEPS = 3
KEPT = 12
BLK = 128

GROUPS = (
    (((0, 0), (1, 1), (3, -1), (2, -2)), ((1, 0), (2, 1), (3, 2), (0, -1))),
    (((2, 2), (3, 3), (1, -3)), ((0, 3), (3, -2), (2, -3))),
    (((0, -4), (3, -5)), ((1, 4), (2, 5))),
    (((1, 5), (2, 6), (0, 4)), ((1, -4), (3, -6), (0, -5))),
)


def rot(distance):
    return [(i, (i + distance) % NZ) for i in range(NZ)]


def shifted(block, distance):
    return lax.ppermute(block, "z", rot(distance))


def shifted_across(block, distance):
    route = [
        (h * NZ + i, (1 - h) * NZ + (i + distance) % NZ) for h in range(2) for i in range(NZ)
    ]
    return lax.ppermute(block, ("xh", "z"), route)


VMEM = pltpu.VMEM
SMEM_SPEC = pl.BlockSpec(memory_space=pltpu.SMEM)
VMEM_SPEC = pl.BlockSpec(memory_space=pltpu.VMEM)
LIMIT = pltpu.CompilerParams(vmem_limit_bytes=40 << 20)


def moves(blocks):
    return pl.CostEstimate(flops=0, bytes_accessed=2 * blocks * BLK * BLK * 2, transcendentals=0)


def block_shape(blocks):
    return jax.ShapeDtypeStruct((blocks, BLK, BLK), jnp.bfloat16)


def ordered_kernel(orders, index_ref, src_ref, *outs):
    for out, order in zip(outs, orders, strict=True):
        for n, place in enumerate(order):
            out[n] = src_ref[index_ref[place]]


def ordered(src, index, orders):
    return pl.pallas_call(
        functools.partial(ordered_kernel, orders),
        out_shape=[block_shape(len(order)) for order in orders],
        in_specs=[SMEM_SPEC, VMEM_SPEC],
        out_specs=[VMEM_SPEC for _ in orders],
        compiler_params=LIMIT,
        cost_estimate=moves(sum(len(order) for order in orders)),
    )(index, src)


def right_kernel(index_ref, src_ref, code_ref, out):
    for n in range(16):
        for t in range(STEPS):
            out[n, pl.ds(t * BLK, BLK), :] = src_ref[index_ref[n + t]]
        out[n, pl.ds(STEPS * BLK, 16), :] = code_ref[n]


def right_packed(src, index, codes):
    return pl.pallas_call(
        right_kernel,
        out_shape=jax.ShapeDtypeStruct((16, STEPS * BLK + 16, BLK), jnp.bfloat16),
        in_specs=[SMEM_SPEC, VMEM_SPEC, VMEM_SPEC],
        out_specs=VMEM_SPEC,
        compiler_params=LIMIT,
        cost_estimate=moves(48),
    )(index, src, codes)


def pack_kernel(spec, count, pick_ref, *refs):
    sources, outs = refs[:count], refs[count:]

    def copy(out, n, entry):
        source, block, pick, sign = entry
        place = block if pick is None else block + sign * pick_ref[pick]
        out[n] = sources[source][place]

    for out, entries in zip(outs, spec, strict=True):
        for n, (zero, one) in enumerate(entries):
            if zero == one:
                copy(out, n, zero)
    differ = any(zero != one for entries in spec for zero, one in entries)
    if differ:
        for core in range(2):

            @pl.when(pick_ref[4] == core)
            def _(core=core):
                for out, entries in zip(outs, spec, strict=True):
                    for n, pair in enumerate(entries):
                        if pair[0] != pair[1]:
                            copy(out, n, pair[core])


def pack(pick, sources, spec):
    return pl.pallas_call(
        functools.partial(pack_kernel, spec, len(sources)),
        out_shape=[block_shape(len(entries)) for entries in spec],
        in_specs=[SMEM_SPEC] + [VMEM_SPEC] * len(sources),
        out_specs=[VMEM_SPEC for _ in spec],
        compiler_params=LIMIT,
        cost_estimate=moves(sum(len(entries) for entries in spec)),
    )(pick, *sources)


def product_kernel(counts, base, first, last, table_ref, right_ref, *rest):
    lefts, rest = rest[: len(counts)], rest[len(counts) :]
    if last:
        before, out_ref, acc = rest
        acc[...] = before[...]
    elif first:
        (acc,) = rest
        acc[...] = jnp.zeros_like(acc)
    else:
        before, acc = rest
        acc[...] = before[...]
    for left, count in zip(lefts, counts, strict=True):

        def body(n, carry, left=left, base=base):
            block = left[n]
            for rank in range(2):
                owner = table_ref[3 * rank, base + n]
                row = pl.multiple_of(table_ref[3 * rank + 1, base + n], BLK)
                place = table_ref[3 * rank + 2, base + n]
                right = right_ref[owner, pl.ds(row, BLK), :]
                acc[place] += jnp.dot(block, right, preferred_element_type=jnp.float32)
            return carry

        lax.fori_loop(0, count, body, 0, unroll=6)
        base += count
    if last:
        out_ref[...] = acc[:KEPT].astype(out_ref.dtype)


def product(table, right, lefts, base, before=None, last=False):
    counts = tuple(left.shape[0] for left in lefts)
    total = sum(counts)
    sums = jax.ShapeDtypeStruct((KEPT + 1, BLK, BLK), jnp.float32)
    return pl.pallas_call(
        functools.partial(product_kernel, counts, base, before is None, last),
        out_shape=block_shape(KEPT) if last else sums,
        in_specs=[SMEM_SPEC] + [VMEM_SPEC] * (1 + len(lefts) + (before is not None)),
        out_specs=VMEM_SPEC,
        scratch_shapes=[VMEM(sums.shape, jnp.float32)] if last else [],
        compiler_params=LIMIT,
        cost_estimate=pl.CostEstimate(
            flops=total * 16 * BLK**3, bytes_accessed=total * BLK * BLK * 2, transcendentals=0
        ),
    )(table, right, *lefts, *(() if before is None else (before,)))


def left_order():
    found = []
    for core in range(2):
        rows = []
        for low, high in GROUPS:
            for other_core in range(2):
                for other_half in range(2):
                    rows += [(other_half, other_core, d, 1) for _, d in low]
                    rows += [(other_half, other_core, d, 2) for _, d in high]
                    rows += [
                        (other_half, other_core, d, 3 * core) for _, d in (high if core else low)
                    ]
        found.append(rows)
    return np.array(found, np.int32)


def tables(a_all, right_codes, c_code, r, z, h, core):
    order = left_order()
    order = jnp.where(core == 0, order[0], order[1])
    other_half, other_core, distance, panel = (order[:, n] for n in range(4))
    count = order.shape[0]
    owner = 24 * (h ^ other_half) + 2 * ((z - distance) % NZ) + (core ^ other_core)
    place = owner * 16 + (r + 24 * h + 2 * z + panel) % 16
    flat = a_all.reshape(1, 768)
    codes = jnp.sum(jnp.where(place[:, None] == jnp.arange(768)[None, :], flat, 0), axis=1)
    step = panel - core
    right_live = right_codes >= 0
    right_inner = jnp.where(right_live, right_codes // BC, -1)
    owners = jnp.arange(16, dtype=jnp.int32)
    earlier = owners[None, :] < owners[:, None]
    rank = jnp.sum(
        ((right_inner[:, None, :] == right_inner[None, :, :]) & earlier[:, :, None]).astype(jnp.int32),
        axis=1,
    )
    packed = jnp.where(right_live, right_inner * 1024 + rank * 32 + right_codes % BC, -1)
    right_n = jnp.where(
        (step == 0)[:, None],
        packed[None, :, 0],
        jnp.where((step == 1)[:, None], packed[None, :, 1], packed[None, :, 2]),
    )
    match = (right_n >= 0) & (codes >= 0)[:, None] & ((right_n // 1024) == (codes % PANEL)[:, None])
    rows = []
    for rank_number in range(2):
        hit = match & ((right_n // 32) % 32 == rank_number)
        found = jnp.sum(jnp.where(hit, owners[None, :] * 32 + right_n % 32 + 1, 0), axis=1)
        partner = jnp.maximum(found - 1, 0)
        target = (codes // PANEL) * BC + partner % 32
        there = (target[:, None] == c_code[None, :]) & (found > 0)[:, None]
        slot = jnp.sum(jnp.where(there, jnp.arange(KEPT)[None, :] - KEPT, 0), axis=1) + KEPT
        rows += [partner // 32, step * BLK, slot]
    return jnp.stack(rows).astype(jnp.int32).reshape(6, count)


def local(a_own_values, a_own_code, b_own_values, b_own_code, c_code):
    r = lax.axis_index(ROW)
    h = lax.axis_index("xh")
    z = lax.axis_index("z")
    core = lax.axis_index("core")
    c = 24 * h + 2 * z + core
    a_own = a_own_values.reshape(16, BLK, BLK)
    b_own = b_own_values.reshape(16, BLK, BLK)

    cyc = (r + 2 * z + jnp.arange(8, dtype=jnp.int32)) % 8
    a_index = jnp.concatenate([cyc, cyc + 8])

    def class_order(classes):
        return tuple(e * 8 + 2 * a + b for a in classes for b in range(2) for e in range(2))

    first, second = ordered(a_own, a_index, (class_order((1, 2)), class_order((3, 0))))
    up1 = shifted(first, 1)
    down1 = shifted(second, -1)
    up2 = shifted(second, 2)
    down2 = shifted(first, -2)

    shift = (c + jnp.arange(16, dtype=jnp.int32)) % 16
    b_index = jnp.concatenate([shift, shift[:2]])
    b_code = b_own_code.reshape(16) + 1
    b_code = jnp.sum(jnp.where(b_index[:, None] == jnp.arange(16)[None, :], b_code[None, :], 0), axis=1)
    b_code = jnp.stack([b_code[t : t + 16] for t in range(STEPS)], axis=1)
    b_code = jnp.concatenate([b_code // 16, b_code % 16], axis=1).astype(jnp.bfloat16)
    b_code = jnp.broadcast_to(jnp.pad(b_code, ((0, 0), (0, BLK - 6)))[:, None, :], (16, 16, BLK))
    right = lax.all_to_all(right_packed(b_own, b_index, b_code), ROW, 0, 0, tiled=True)
    a_all = lax.all_to_all(
        jnp.broadcast_to(a_own_code.reshape(1, 16), (48, 16)), COL, 0, 0, tiled=True
    )

    here = [(r + 24 * h + 2 * z + w) % 16 // 8 for w in range(4)]
    above = [(r + 24 * h + 2 * ((z + 1) % NZ) + w) % 16 // 8 for w in range(2)]
    below = [(r + 24 * h + 2 * ((z + NZ - 1) % NZ) + w) % 16 // 8 for w in range(2, 4)]
    pick = jnp.stack(here + [core] + above + below).astype(jnp.int32)

    sources, at = [], {}

    def keep(array, names):
        for n, name in enumerate(names):
            at[name] = (len(sources), 4 * n)
        sources.append(array)

    def packed(spec):
        used = sorted({entry[0] for entries in spec for pair in entries for entry in pair})
        where = {source: n for n, source in enumerate(used)}
        spec = tuple(
            tuple(tuple((where[entry[0]],) + entry[1:] for entry in pair) for pair in entries)
            for entries in spec
        )
        return pack(pick, [sources[source] for source in used], spec)

    def same(entry):
        return (entry, entry)

    def whole(names):
        return [
            same((at[name][0], at[name][1] + n, None, 1)) for name in names for n in range(4)
        ]

    def wanted(name, b, picked, other=False):
        source, block = at[name]
        return (source, block + 2 * b + (1 if other else 0), picked, -1 if other else 1)

    keep(first, ((1, 0), (2, 0)))
    keep(second, ((3, 0), (0, 0)))
    keep(up1, ((1, 1), (2, 1)))
    keep(down1, ((3, -1), (0, -1)))
    keep(up2, ((3, 2), (0, 2)))
    keep(down2, ((1, -2), (2, -2)))
    up_in, down_in = packed(
        [whole(((2, 1), (3, 2), (0, 2))), whole(((3, -1), (2, -2), (1, -2)))]
    )
    keep(shifted(up_in, 1), ((2, 2), (3, 3), (0, 3)))
    keep(shifted(down_in, -1), ((3, -2), (2, -3), (1, -3)))
    up_in, down_in = packed([whole(((1, 1), (2, 2))), whole(((0, -1), (3, -2)))])
    keep(shifted(up_in, 3), ((1, 4), (2, 5)))
    keep(shifted(down_in, -3), ((0, -4), (3, -5)))
    low_from, high_from = ((1, 4), (2, 5), (0, 3)), ((1, -3), (3, -5), (0, -4))
    last_low, last_low_other, last_high, last_high_other = packed(
        [
            [
                same(wanted(name, b, start + b, other))
                for name in names
                for b in range(2)
            ]
            for names, start in ((low_from, 5), (high_from, 7))
            for other in (False, True)
        ]
    )
    last = (
        shifted(last_low, 1),
        shifted_across(last_low_other, 1),
        shifted(last_high, -1),
        shifted_across(last_high_other, -1),
    )

    lefts = []
    for number, (low, high) in enumerate(GROUPS):
        n = len(low)
        if number < 3:
            (out,) = packed(
                [
                    [same(wanted(name, b, b, True)) for name in low for b in range(2)]
                    + [same(wanted(name, b, 2 + b, True)) for name in high for b in range(2)]
                ]
            )
            sources.append(lax.ppermute(out, "xh", [(0, 1), (1, 0)]))
            crossed = len(sources) - 1

            def own_block(i, panel, low=low, high=high):
                return wanted((low if panel < 2 else high)[i], panel % 2, panel)

            def other_block(i, panel, n=n, crossed=crossed):
                return (crossed, (n if panel >= 2 else 0) * 2 + 2 * i + panel % 2, None, 1)
        else:
            sources.extend(last)
            base = len(sources) - 4

            def own_block(i, panel, base=base):
                return (base + (2 if panel >= 2 else 0), 2 * i + panel % 2, None, 1)

            def other_block(i, panel, base=base):
                return (base + 1 + (2 if panel >= 2 else 0), 2 * i + panel % 2, None, 1)

        spec = []
        for for_other_core in range(2):
            entries = []
            for block in (own_block, other_block):
                for panel in (1, 2):
                    entries += [same(block(i, panel)) for i in range(n)]
                pair = (3, 0) if for_other_core else (0, 3)
                entries += [(block(i, pair[0]), block(i, pair[1])) for i in range(n)]
            spec.append(entries)
        kept, sent = packed(spec)
        lefts.append((kept, lax.ppermute(sent, "core", [(0, 1), (1, 0)])))

    right_codes = right[:, STEPS * BLK, :6].astype(jnp.int32)
    right_codes = right_codes[:, :3] * 16 + right_codes[:, 3:] - 1
    table = tables(a_all, right_codes, c_code.reshape(KEPT), r, z, h, core)
    sums = product(table, right, lefts[0], 0)
    sums = product(table, right, lefts[1] + lefts[2], 48, sums)
    return product(table, right, lefts[3], 108, sums, last=True)[None, None]


def solution(mesh):
    fine = Mesh(mesh.devices.reshape(SIZES), AXES)
    return jax.shard_map(
        local,
        mesh=fine,
        in_specs=(
            P(ROW, COL, None, None, None, None),
            P(ROW, COL, None, None),
            P(ROW, COL, None, None, None, None),
            P(ROW, COL, None, None),
            P(ROW, COL, None),
        ),
        out_specs=P(ROW, COL, None, None, None),
        check_vma=False,
    )
```

time: 225 us -> 160 us (0.71)
  the two profiles are of different devices: /device:TPU:60 before, /device:TPU:1 now
where the time goes in v2:
time: 160 us; the launch traced here: 159 us
  starting transfers between devices  94.8 us (59%)
  waiting for transfers between devices  28.1 us (18%)
  Pallas kernels  26.7 us (17%)
  local copies, waits for them, and re-layouts  5.09 us (3%)
  other arithmetic  3.29 us (2%)
    ppermute x10, starting transfers between devices, shifted(): return lax.ppermute(block, 'z', rot(distance))  37 us
    ppermute x10, waiting for transfers between devices, shifted(): return lax.ppermute(block, 'z', rot(distance))  20.2 us
    all_to_all x1, starting transfers between devices, local(): lax.all_to_all(jnp.broadcast_to(a_own_code.reshape(1, 16), (48, 16)), COL...  19.4 us
    pallas_call x10, Pallas kernels, pack(): pl.pallas_call(functools.partial(pack_kernel, spec, len(sources)), out_sh...  12.2 us
    pallas_call x3, Pallas kernels, product(): pl.pallas_call(functools.partial(product_kernel, counts, base, before is...  12.1 us
    ppermute x3, starting transfers between devices, local(): sources.append(lax.ppermute(out, 'xh', [(0, 1), (1, 0)]))  10.8 us
    ppermute x4, starting transfers between devices, local(): lefts.append((kept, lax.ppermute(sent, 'core', [(0, 1), (1, 0)])))  10.8 us
    ppermute x2, starting transfers between devices, shifted_across(): return lax.ppermute(block, ('xh', 'z'), route)  9.76 us
  transfers between devices with their start and end apart: 21, of which 6 were waited for; matrix products, arithmetic and copies ran while one was open for 3% of the time, Pallas kernels for 14%

profile of v2, /device:TPU:1, one launch (start us, length us, event | category | flops | bytes accessed | tf_op | source)
XLA Modules:
  0.0 158.8 jit_solution(13192087441826757440)
XLA Ops:
  1.3 19.4 %all-to-all-start.1 = ((s32[48,1,16]{2,1,0:T(1,128)}), s32[48,1,16]{2,1,0:T(1,128)S(1)}, u32[]{:S(2)}, u32[]{:S(2)}) async-start(s32[48,1,16]{2,1,0:T(1,128)} %broadcast_in_dim.152), calls=%async_computation.1 | async-start | bytes 49152 | tf_op jit(solution)/shard_map/all_to_all | solution.py:258
  24.7 7.9 %all-to-all-done.1 = s32[48,1,16]{2,1,0:T(1,128)S(1)} async-done(((s32[48,1,16]{2,1,0:T(1,128)}), s32[48,1,16]{2,1,0:T(1,128)S(1)}, u32[]{:S(2)}, u32[]{:S(2)}) %all-to-all-start.1) | async-done | bytes 3104 | tf_op jit(solution)/shard_map/all_to_all | solution.py:258
  32.6 7.0 %all-to-all-start = ((bf16[16,400,128]{2,1,0:T(8,128)(2,1)}), bf16[16,400,128]{2,1,0:T(8,128)(2,1)}, u32[]{:S(2)}, u32[]{:S(2)}) async-start(bf16[16,400,128]{2,1,0:T(8,128)(2,1)} %shard_map.73), calls=%async_computation | async-start | bytes 3276800 | tf_op jit(solution)/shard_map/all_to_all | solution.py:257
  40.3 2.1 %collective-permute-start = (bf16[8,128,128]{2,1,0:T(8,128)(2,1)S(1)}, bf16[8,128,128]{2,1,0:T(8,128)(2,1)S(1)}, u32[]{:S(2)}, u32[]{:S(2)}) collective-permute-start(bf16[8,128,128]{2,1,0:T(8,128)(2,1)S(1)} %get-tuple-element.23.refs_0_), channel_id=1, source_target_pairs={{0,2},{2,4},{4,6},{6,8},{8,10},{10,12},{12,14},{14,16},{16,18},{18... | collective-permute-start | bytes 786440 | tf_op jit(solution)/shard_map/ppermute | solution.py:36
  42.3 4.4 %collective-permute-start.1 = (bf16[8,128,128]{2,1,0:T(8,128)(2,1)S(1)}, bf16[8,128,128]{2,1,0:T(8,128)(2,1)S(1)}, u32[]{:S(2)}, u32[]{:S(2)}) collective-permute-start(bf16[8,128,128]{2,1,0:T(8,128)(2,1)S(1)} %get-tuple-element.24.refs_1_), channel_id=1, source_target_pairs={{0,22},{2,0},{4,2},{6,4},{8,6},{10,8},{12,10},{14,12},{16,14},{18,... | collective-permute-start | bytes 786440 | tf_op jit(solution)/shard_map/ppermute | solution.py:36
  48.7 5.5 %collective-permute-start.3 = (bf16[8,128,128]{2,1,0:T(8,128)(2,1)S(1)}, bf16[8,128,128]{2,1,0:T(8,128)(2,1)S(1)}, u32[]{:S(2)}, u32[]{:S(2)}) collective-permute-start(bf16[8,128,128]{2,1,0:T(8,128)(2,1)S(1)} %get-tuple-element.23.refs_0_), channel_id=1, source_target_pairs={{0,20},{2,22},{4,0},{6,2},{8,4},{10,6},{12,8},{14,10},{16,12},{18,... | collective-permute-start | bytes 786440 | tf_op jit(solution)/shard_map/ppermute | solution.py:36
  54.6 8.1 %collective-permute-done.2.refs_2_.refs_4_ = bf16[8,128,128]{2,1,0:T(8,128)(2,1)S(1)} collective-permute-done((bf16[8,128,128]{2,1,0:T(8,128)(2,1)S(1)}, bf16[8,128,128]{2,1,0:T(8,128)(2,1)S(1)}, u32[]{:S(2)}, u32[]{:S(2)}) %collective-permute-start.2) | collective-permute-done | bytes 262176 | tf_op jit(solution)/shard_map/ppermute | solution.py:36
  67.1 4.6 %collective-permute-start.5 = (bf16[12,128,128]{2,1,0:T(8,128)(2,1)S(1)}, bf16[12,128,128]{2,1,0:T(8,128)(2,1)S(1)}, u32[]{:S(2)}, u32[]{:S(2)}) collective-permute-start(bf16[12,128,128]{2,1,0:T(8,128)(2,1)S(1)} %get-tuple-element.26), channel_id=1, source_target_pairs={{0,22},{2,0},{4,2},{6,4},{8,6},{10,8},{12,10},{14,12},{16,14},{18,... | collective-permute-start | bytes 1179656 | tf_op jit(solution)/shard_map/ppermute | solution.py:36
  73.2 2.8 %collective-permute-start.17 = (bf16[16,128,128]{2,1,0:T(8,128)(2,1)}, bf16[16,128,128]{2,1,0:T(8,128)(2,1)S(1)}, u32[]{:S(2)}, u32[]{:S(2)}) collective-permute-start(bf16[16,128,128]{2,1,0:T(8,128)(2,1)} %shard_map.83), channel_id=1, source_target_pairs={{0,24},{24,0},{1,25},{25,1},{2,26},{26,2},{3,27},{27,3},{4,28},{28... | collective-permute-start | bytes 1572872 | tf_op jit(solution)/shard_map/ppermute | solution.py:338
  76.0 2.2 %collective-permute-done.4.refs_2_.refs_0_ = bf16[12,128,128]{2,1,0:T(8,128)(2,1)S(1)} collective-permute-done((bf16[12,128,128]{2,1,0:T(8,128)(2,1)S(1)}, bf16[12,128,128]{2,1,0:T(8,128)(2,1)S(1)}, u32[]{:S(2)}, u32[]{:S(2)}) %collective-permute-start.4) | collective-permute-done | bytes 393248 | tf_op jit(solution)/shard_map/ppermute | solution.py:36
  81.2 4.1 %collective-permute-start.6 = (bf16[8,128,128]{2,1,0:T(8,128)(2,1)}, bf16[8,128,128]{2,1,0:T(8,128)(2,1)S(1)}, u32[]{:S(2)}, u32[]{:S(2)}) collective-permute-start(bf16[8,128,128]{2,1,0:T(8,128)(2,1)} %get-tuple-element.27), channel_id=1, source_target_pairs={{0,6},{2,8},{4,10},{6,12},{8,14},{10,16},{12,18},{14,20},{16,22},{... | collective-permute-start | bytes 786440 | tf_op jit(solution)/shard_map/ppermute | solution.py:36
  85.3 4.2 %collective-permute-start.7 = (bf16[8,128,128]{2,1,0:T(8,128)(2,1)}, bf16[8,128,128]{2,1,0:T(8,128)(2,1)S(1)}, u32[]{:S(2)}, u32[]{:S(2)}) collective-permute-start(bf16[8,128,128]{2,1,0:T(8,128)(2,1)} %get-tuple-element.28), channel_id=1, source_target_pairs={{0,18},{2,20},{4,22},{6,0},{8,2},{10,4},{12,6},{14,8},{16,10},{18,... | collective-permute-start | bytes 786440 | tf_op jit(solution)/shard_map/ppermute | solution.py:36
  90.8 3.6 %collective-permute-start.13 = (bf16[12,128,128]{2,1,0:T(8,128)(2,1)}, bf16[12,128,128]{2,1,0:T(8,128)(2,1)}, u32[]{:S(2)}, u32[]{:S(2)}) collective-permute-start(bf16[12,128,128]{2,1,0:T(8,128)(2,1)} %shard_map.79), channel_id=1, source_target_pairs={{0,24},{24,0},{1,25},{25,1},{2,26},{26,2},{3,27},{27,3},{4,28},{28... | collective-permute-start | bytes 1179656 | tf_op jit(solution)/shard_map/ppermute | solution.py:338
  96.1 6.4 %collective-permute-done.6.refs_2_.refs_0_ = bf16[8,128,128]{2,1,0:T(8,128)(2,1)S(1)} collective-permute-done((bf16[8,128,128]{2,1,0:T(8,128)(2,1)}, bf16[8,128,128]{2,1,0:T(8,128)(2,1)S(1)}, u32[]{:S(2)}, u32[]{:S(2)}) %collective-permute-start.6) | collective-permute-done | bytes 262176 | tf_op jit(solution)/shard_map/ppermute | solution.py:36
  103.0 4.4 %collective-permute-start.15 = (bf16[8,128,128]{2,1,0:T(8,128)(2,1)S(1)}, bf16[8,128,128]{2,1,0:T(8,128)(2,1)S(1)}, u32[]{:S(2)}, u32[]{:S(2)}) collective-permute-start(bf16[8,128,128]{2,1,0:T(8,128)(2,1)S(1)} %shard_map.81), channel_id=1, source_target_pairs={{0,24},{24,0},{1,25},{25,1},{2,26},{26,2},{3,27},{27,3},{4,28},{28... | collective-permute-start | bytes 786440 | tf_op jit(solution)/shard_map/ppermute | solution.py:338
  108.0 6.4 %collective-permute-start.10 = (bf16[6,128,128]{2,1,0:T(8,128)(2,1)S(1)}, bf16[6,128,128]{2,1,0:T(8,128)(2,1)S(1)}, u32[]{:S(2)}, u32[]{:S(2)}) collective-permute-start(bf16[6,128,128]{2,1,0:T(8,128)(2,1)S(1)} %get-tuple-element.31), channel_id=1, source_target_pairs={{0,22},{2,0},{4,2},{6,4},{8,6},{10,8},{12,10},{14,12},{16,14},{18,... | collective-permute-start | bytes 589832 | tf_op jit(solution)/shard_map/ppermute | solution.py:36
  114.4 7.5 %collective-permute-start.11 = (bf16[6,128,128]{2,1,0:T(8,128)(2,1)S(1)}, bf16[6,128,128]{2,1,0:T(8,128)(2,1)S(1)}, u32[]{:S(2)}, u32[]{:S(2)}) collective-permute-start(bf16[6,128,128]{2,1,0:T(8,128)(2,1)S(1)} %get-tuple-element.32), channel_id=1, source_target_pairs={{0,46},{2,24},{4,26},{6,28},{8,30},{10,32},{12,34},{14,36},{16,38}... | collective-permute-start | bytes 589832 | tf_op jit(solution)/shard_map/ppermute | solution.py:43
  123.8 2.3 %collective-permute-start.9 = (bf16[6,128,128]{2,1,0:T(8,128)(2,1)S(1)}, bf16[6,128,128]{2,1,0:T(8,128)(2,1)S(1)}, u32[]{:S(2)}, u32[]{:S(2)}) collective-permute-start(bf16[6,128,128]{2,1,0:T(8,128)(2,1)S(1)} %get-tuple-element.30), channel_id=1, source_target_pairs={{0,26},{2,28},{4,30},{6,32},{8,34},{10,36},{12,38},{14,40},{16,42}... | collective-permute-start | bytes 589832 | tf_op jit(solution)/shard_map/ppermute | solution.py:43
  128.6 1.9 %shard_map.80 = (bf16[18,128,128]{2,1,0:T(8,128)(2,1)S(1)}, bf16[18,128,128]{2,1,0:T(8,128)(2,1)}) custom-call(s32[9]{0:T(128)S(1)} %stack.65.pick_ref, bf16[12,128,128]{2,1,0:T(8,128)(2,1)S(1)} %collective-permute-done.4.refs_2_.refs_0_, bf16[12,128,128]{2,1,0:T(8,128)(2,1)S(1)} %collective-permute-done.5.refs_3_.refs_1_, ...), custom_call_target="tpu_custom_call" | custom-call | bytes 2359296 | tf_op jit(solution)/shard_map/pallas_call | solution.py:120
  130.5 4.6 %collective-permute-start.18 = (bf16[24,128,128]{2,1,0:T(8,128)(2,1)}, bf16[24,128,128]{2,1,0:T(8,128)(2,1)S(1)}, u32[]{:S(2)}, u32[]{:S(2)}) collective-permute-start(bf16[24,128,128]{2,1,0:T(8,128)(2,1)} %get-tuple-element.40), channel_id=1, source_target_pairs={{0,1},{1,0},{2,3},{3,2},{4,5},{5,4},{6,7},{7,6},{8,9},{9,8},{10,11... | collective-permute-start | bytes 2359304 | tf_op jit(solution)/shard_map/ppermute | solution.py:366
  139.4 2.4 %collective-permute-start.12 = (bf16[18,128,128]{2,1,0:T(8,128)(2,1)}, bf16[18,128,128]{2,1,0:T(8,128)(2,1)}, u32[]{:S(2)}, u32[]{:S(2)}) collective-permute-start(bf16[18,128,128]{2,1,0:T(8,128)(2,1)} %get-tuple-element.34), channel_id=1, source_target_pairs={{0,1},{1,0},{2,3},{3,2},{4,5},{5,4},{6,7},{7,6},{8,9},{9,8},{10,11... | collective-permute-start | bytes 1769480 | tf_op jit(solution)/shard_map/ppermute | solution.py:366
  146.6 3.7 %shard_map.85.rest_4_ = f32[13,128,128]{2,1,0:T(8,128)S(1)} custom-call(s32[6,144]{1,0:T(8,128)S(1)} %stack.55.table_ref, bf16[16,400,128]{2,1,0:T(8,128)(2,1)} %all-to-all-done.right_ref, bf16[24,128,128]{2,1,0:T(8,128)(2,1)S(1)} %copy-done.3, bf16[24,128,128]{2,1,0:T(8,128)(2,1)S(1)} %collective-permute-done.18.rest_1_), custom_call_target="tpu_custom_call" | custom-call | flops 1610612736 | bytes 1572864 | tf_op jit(solution)/shard_map/pallas_call | solution.py:163
  150.3 4.4 %shard_map.86.rest_2_ = f32[13,128,128]{2,1,0:T(8,128)S(1)} custom-call(s32[6,144]{1,0:T(8,128)S(1)} %stack.55.table_ref, bf16[16,400,128]{2,1,0:T(8,128)(2,1)} %all-to-all-done.right_ref, bf16[18,128,128]{2,1,0:T(8,128)(2,1)S(1)} %get-tuple-element.35.rest_0_, bf16[18,128,128]{2,1,0:T(8,128)(2,1)} %collective-permute-done.14.rest_1_, ...), custom_call_target="tpu_custom_call" | custom-call | flops 2013265920 | bytes 1966080 | tf_op jit(solution)/shard_map/pallas_call | solution.py:163
  154.8 4.0 %shard_map.87 = bf16[12,128,128]{2,1,0:T(8,128)(2,1)} custom-call(s32[6,144]{1,0:T(8,128)S(1)} %stack.55.table_ref, bf16[16,400,128]{2,1,0:T(8,128)(2,1)} %all-to-all-done.right_ref, bf16[18,128,128]{2,1,0:T(8,128)(2,1)S(1)} %copy-done.5, bf16[18,128,128]{2,1,0:T(8,128)(2,1)} %collective-permute-done.12.rest_1_, f32[13,128,128]{2,1,0:T(8,128)S(1)} %shard_map.86.rest_2_), custom_call_target="tpu_custom_call" | custom-call | flops 1207959552 | bytes 1179648 | tf_op jit(solution)/shard_map/pallas_call | solution.py:163
  (93 shorter events, 34.2 us)
Async XLA Ops:
  1.3 31.3 %all-to-all-start.1 = ((s32[48,1,16]{2,1,0:T(1,128)}), s32[48,1,16]{2,1,0:T(1,128)S(1)}, u32[]{:S(2)}, u32[]{:S(2)}) async-start(s32[48,1,16]{2,1,0:T(1,128)} %broadcast_in_dim.152), calls=%async_computation.1 | async-start | bytes 49152 | tf_op jit(solution)/shard_map/all_to_all | solution.py:258
  24.7 29.9 %copy-start.6 = (s32[144,4]{0,1:T(4,128)S(1)}, s32[144,4]{0,1:T(4,128)}, u32[]{:S(2)}) copy-start(s32[144,4]{0,1:T(4,128)} %constant.335.clone) | copy-start | bytes 6916
  24.7 29.9 %copy-start.7 = (s32[144,4]{0,1:T(4,128)S(1)}, s32[144,4]{0,1:T(4,128)}, u32[]{:S(2)}) copy-start(s32[144,4]{0,1:T(4,128)} %constant.336.clone) | copy-start | bytes 6916
  32.6 112.6 %all-to-all-start = ((bf16[16,400,128]{2,1,0:T(8,128)(2,1)}), bf16[16,400,128]{2,1,0:T(8,128)(2,1)}, u32[]{:S(2)}, u32[]{:S(2)}) async-start(bf16[16,400,128]{2,1,0:T(8,128)(2,1)} %shard_map.73), calls=%async_computation | async-start | bytes 3276800 | tf_op jit(solution)/shard_map/all_to_all | solution.py:257
  40.3 14.4 %collective-permute-start = (bf16[8,128,128]{2,1,0:T(8,128)(2,1)S(1)}, bf16[8,128,128]{2,1,0:T(8,128)(2,1)S(1)}, u32[]{:S(2)}, u32[]{:S(2)}) collective-permute-start(bf16[8,128,128]{2,1,0:T(8,128)(2,1)S(1)} %get-tuple-element.23.refs_0_), channel_id=1, source_target_pairs={{0,2},{2,4},{4,6},{6,8},{8,10},{10,12},{12,14},{14,16},{16,18},{18... | collective-permute-start | bytes 786440 | tf_op jit(solution)/shard_map/ppermute | solution.py:36
  42.3 12.3 %collective-permute-start.1 = (bf16[8,128,128]{2,1,0:T(8,128)(2,1)S(1)}, bf16[8,128,128]{2,1,0:T(8,128)(2,1)S(1)}, u32[]{:S(2)}, u32[]{:S(2)}) collective-permute-start(bf16[8,128,128]{2,1,0:T(8,128)(2,1)S(1)} %get-tuple-element.24.refs_1_), channel_id=1, source_target_pairs={{0,22},{2,0},{4,2},{6,4},{8,6},{10,8},{12,10},{14,12},{16,14},{18,... | collective-permute-start | bytes 786440 | tf_op jit(solution)/shard_map/ppermute | solution.py:36
  46.8 16.0 %collective-permute-start.2 = (bf16[8,128,128]{2,1,0:T(8,128)(2,1)S(1)}, bf16[8,128,128]{2,1,0:T(8,128)(2,1)S(1)}, u32[]{:S(2)}, u32[]{:S(2)}) collective-permute-start(bf16[8,128,128]{2,1,0:T(8,128)(2,1)S(1)} %get-tuple-element.24.refs_1_), channel_id=1, source_target_pairs={{0,4},{2,6},{4,8},{6,10},{8,12},{10,14},{12,16},{14,18},{16,20},{1... | collective-permute-start | bytes 786440 | tf_op jit(solution)/shard_map/ppermute | solution.py:36
  48.7 15.9 %collective-permute-start.3 = (bf16[8,128,128]{2,1,0:T(8,128)(2,1)S(1)}, bf16[8,128,128]{2,1,0:T(8,128)(2,1)S(1)}, u32[]{:S(2)}, u32[]{:S(2)}) collective-permute-start(bf16[8,128,128]{2,1,0:T(8,128)(2,1)S(1)} %get-tuple-element.23.refs_0_), channel_id=1, source_target_pairs={{0,20},{2,22},{4,0},{6,2},{8,4},{10,6},{12,8},{14,10},{16,12},{18,... | collective-permute-start | bytes 786440 | tf_op jit(solution)/shard_map/ppermute | solution.py:36
  65.2 12.9 %collective-permute-start.4 = (bf16[12,128,128]{2,1,0:T(8,128)(2,1)S(1)}, bf16[12,128,128]{2,1,0:T(8,128)(2,1)S(1)}, u32[]{:S(2)}, u32[]{:S(2)}) collective-permute-start(bf16[12,128,128]{2,1,0:T(8,128)(2,1)S(1)} %get-tuple-element.25), channel_id=1, source_target_pairs={{0,2},{2,4},{4,6},{6,8},{8,10},{10,12},{12,14},{14,16},{16,18},{18... | collective-permute-start | bytes 1179656 | tf_op jit(solution)/shard_map/ppermute | solution.py:36
  67.1 12.7 %collective-permute-start.5 = (bf16[12,128,128]{2,1,0:T(8,128)(2,1)S(1)}, bf16[12,128,128]{2,1,0:T(8,128)(2,1)S(1)}, u32[]{:S(2)}, u32[]{:S(2)}) collective-permute-start(bf16[12,128,128]{2,1,0:T(8,128)(2,1)S(1)} %get-tuple-element.26), channel_id=1, source_target_pairs={{0,22},{2,0},{4,2},{6,4},{8,6},{10,8},{12,10},{14,12},{16,14},{18,... | collective-permute-start | bytes 1179656 | tf_op jit(solution)/shard_map/ppermute | solution.py:36
  73.2 48.7 %collective-permute-start.17 = (bf16[16,128,128]{2,1,0:T(8,128)(2,1)}, bf16[16,128,128]{2,1,0:T(8,128)(2,1)S(1)}, u32[]{:S(2)}, u32[]{:S(2)}) collective-permute-start(bf16[16,128,128]{2,1,0:T(8,128)(2,1)} %shard_map.83), channel_id=1, source_target_pairs={{0,24},{24,0},{1,25},{25,1},{2,26},{26,2},{3,27},{27,3},{4,28},{28... | collective-permute-start | bytes 1572872 | tf_op jit(solution)/shard_map/ppermute | solution.py:338
  81.2 21.2 %collective-permute-start.6 = (bf16[8,128,128]{2,1,0:T(8,128)(2,1)}, bf16[8,128,128]{2,1,0:T(8,128)(2,1)S(1)}, u32[]{:S(2)}, u32[]{:S(2)}) collective-permute-start(bf16[8,128,128]{2,1,0:T(8,128)(2,1)} %get-tuple-element.27), channel_id=1, source_target_pairs={{0,6},{2,8},{4,10},{6,12},{8,14},{10,16},{12,18},{14,20},{16,22},{... | collective-permute-start | bytes 786440 | tf_op jit(solution)/shard_map/ppermute | solution.py:36
  85.3 17.2 %collective-permute-start.7 = (bf16[8,128,128]{2,1,0:T(8,128)(2,1)}, bf16[8,128,128]{2,1,0:T(8,128)(2,1)S(1)}, u32[]{:S(2)}, u32[]{:S(2)}) collective-permute-start(bf16[8,128,128]{2,1,0:T(8,128)(2,1)} %get-tuple-element.28), channel_id=1, source_target_pairs={{0,18},{2,20},{4,22},{6,0},{8,2},{10,4},{12,6},{14,8},{16,10},{18,... | collective-permute-start | bytes 786440 | tf_op jit(solution)/shard_map/ppermute | solution.py:36
  90.8 33.0 %collective-permute-start.13 = (bf16[12,128,128]{2,1,0:T(8,128)(2,1)}, bf16[12,128,128]{2,1,0:T(8,128)(2,1)}, u32[]{:S(2)}, u32[]{:S(2)}) collective-permute-start(bf16[12,128,128]{2,1,0:T(8,128)(2,1)} %shard_map.79), channel_id=1, source_target_pairs={{0,24},{24,0},{1,25},{25,1},{2,26},{26,2},{3,27},{27,3},{4,28},{28... | collective-permute-start | bytes 1179656 | tf_op jit(solution)/shard_map/ppermute | solution.py:338
  103.0 38.8 %collective-permute-start.15 = (bf16[8,128,128]{2,1,0:T(8,128)(2,1)S(1)}, bf16[8,128,128]{2,1,0:T(8,128)(2,1)S(1)}, u32[]{:S(2)}, u32[]{:S(2)}) collective-permute-start(bf16[8,128,128]{2,1,0:T(8,128)(2,1)S(1)} %shard_map.81), channel_id=1, source_target_pairs={{0,24},{24,0},{1,25},{25,1},{2,26},{26,2},{3,27},{27,3},{4,28},{28... | collective-permute-start | bytes 786440 | tf_op jit(solution)/shard_map/ppermute | solution.py:338
  108.0 22.5 %collective-permute-start.10 = (bf16[6,128,128]{2,1,0:T(8,128)(2,1)S(1)}, bf16[6,128,128]{2,1,0:T(8,128)(2,1)S(1)}, u32[]{:S(2)}, u32[]{:S(2)}) collective-permute-start(bf16[6,128,128]{2,1,0:T(8,128)(2,1)S(1)} %get-tuple-element.31), channel_id=1, source_target_pairs={{0,22},{2,0},{4,2},{6,4},{8,6},{10,8},{12,10},{14,12},{16,14},{18,... | collective-permute-start | bytes 589832 | tf_op jit(solution)/shard_map/ppermute | solution.py:36
  114.4 20.7 %collective-permute-start.11 = (bf16[6,128,128]{2,1,0:T(8,128)(2,1)S(1)}, bf16[6,128,128]{2,1,0:T(8,128)(2,1)S(1)}, u32[]{:S(2)}, u32[]{:S(2)}) collective-permute-start(bf16[6,128,128]{2,1,0:T(8,128)(2,1)S(1)} %get-tuple-element.32), channel_id=1, source_target_pairs={{0,46},{2,24},{4,26},{6,28},{8,30},{10,32},{12,34},{14,36},{16,38}... | collective-permute-start | bytes 589832 | tf_op jit(solution)/shard_map/ppermute | solution.py:43
  121.9 15.2 %collective-permute-start.8 = (bf16[6,128,128]{2,1,0:T(8,128)(2,1)S(1)}, bf16[6,128,128]{2,1,0:T(8,128)(2,1)S(1)}, u32[]{:S(2)}, u32[]{:S(2)}) collective-permute-start(bf16[6,128,128]{2,1,0:T(8,128)(2,1)S(1)} %get-tuple-element.29), channel_id=1, source_target_pairs={{0,2},{2,4},{4,6},{6,8},{8,10},{10,12},{12,14},{14,16},{16,18},{18... | collective-permute-start | bytes 589832 | tf_op jit(solution)/shard_map/ppermute | solution.py:36
  123.8 13.2 %collective-permute-start.9 = (bf16[6,128,128]{2,1,0:T(8,128)(2,1)S(1)}, bf16[6,128,128]{2,1,0:T(8,128)(2,1)S(1)}, u32[]{:S(2)}, u32[]{:S(2)}) collective-permute-start(bf16[6,128,128]{2,1,0:T(8,128)(2,1)S(1)} %get-tuple-element.30), channel_id=1, source_target_pairs={{0,26},{2,28},{4,30},{6,32},{8,34},{10,36},{12,38},{14,40},{16,42}... | collective-permute-start | bytes 589832 | tf_op jit(solution)/shard_map/ppermute | solution.py:43
  128.6 17.8 %copy-start.8 = (s32[1,1,12]{2,1,0:T(1,128)S(1)}, s32[1,1,12]{2,1,0:T(1,128)}, u32[]{:S(2)}) copy-start(s32[1,1,12]{2,1,0:T(1,128)} %param.11) | copy-start | bytes 148
  130.5 16.1 %collective-permute-start.18 = (bf16[24,128,128]{2,1,0:T(8,128)(2,1)}, bf16[24,128,128]{2,1,0:T(8,128)(2,1)S(1)}, u32[]{:S(2)}, u32[]{:S(2)}) collective-permute-start(bf16[24,128,128]{2,1,0:T(8,128)(2,1)} %get-tuple-element.40), channel_id=1, source_target_pairs={{0,1},{1,0},{2,3},{3,2},{4,5},{5,4},{6,7},{7,6},{8,9},{9,8},{10,11... | collective-permute-start | bytes 2359304 | tf_op jit(solution)/shard_map/ppermute | solution.py:366
  135.1 15.2 %collective-permute-start.14 = (bf16[18,128,128]{2,1,0:T(8,128)(2,1)}, bf16[18,128,128]{2,1,0:T(8,128)(2,1)}, u32[]{:S(2)}, u32[]{:S(2)}) collective-permute-start(bf16[18,128,128]{2,1,0:T(8,128)(2,1)} %get-tuple-element.36), channel_id=1, source_target_pairs={{0,1},{1,0},{2,3},{3,2},{4,5},{5,4},{6,7},{7,6},{8,9},{9,8},{10,11... | collective-permute-start | bytes 1769480 | tf_op jit(solution)/shard_map/ppermute | solution.py:366
  139.4 15.3 %collective-permute-start.12 = (bf16[18,128,128]{2,1,0:T(8,128)(2,1)}, bf16[18,128,128]{2,1,0:T(8,128)(2,1)}, u32[]{:S(2)}, u32[]{:S(2)}) collective-permute-start(bf16[18,128,128]{2,1,0:T(8,128)(2,1)} %get-tuple-element.34), channel_id=1, source_target_pairs={{0,1},{1,0},{2,3},{3,2},{4,5},{5,4},{6,7},{7,6},{8,9},{9,8},{10,11... | collective-permute-start | bytes 1769480 | tf_op jit(solution)/shard_map/ppermute | solution.py:366
  143.2 7.1 %collective-permute-start.16 = (bf16[12,128,128]{2,1,0:T(8,128)(2,1)}, bf16[12,128,128]{2,1,0:T(8,128)(2,1)S(1)}, u32[]{:S(2)}, u32[]{:S(2)}) collective-permute-start(bf16[12,128,128]{2,1,0:T(8,128)(2,1)} %get-tuple-element.38), channel_id=1, source_target_pairs={{0,1},{1,0},{2,3},{3,2},{4,5},{5,4},{6,7},{7,6},{8,9},{9,8},{10,11... | collective-permute-start | bytes 1179656 | tf_op jit(solution)/shard_map/ppermute | solution.py:366
  (6 other events, 38.3 us)

commit v3 on v2

v3 whole, which is shorter than its diff:
```python
import functools

import jax
import jax.numpy as jnp
import numpy as np
from jax import lax
from jax.experimental import pallas as pl
from jax.experimental.pallas import tpu as pltpu
from jax.sharding import Mesh
from jax.sharding import PartitionSpec as P

AXES = ("xl", "y", "xh", "z", "core")
ROW = ("xl", "y")
COL = ("xh", "z", "core")
RING = ("xh", "z")
SIZES = (2, 8, 2, 12, 2)
NQ = 24
BC = 16
PANEL = 48
STEPS = 3
KEPT = 12
BLK = 128

GROUPS = (
    (
        ((0, 0), (4, 12), (1, 1), (5, 13), (7, 23), (3, 11), (6, 22), (2, 10)),
        ((1, 0), (5, 12), (2, 1), (6, 13), (3, 2), (7, 14), (0, 23), (4, 11)),
    ),
    (
        ((2, 2), (6, 14), (3, 3), (7, 15), (1, 9), (5, 21), (0, 8), (4, 20), (3, 19), (7, 7)),
        ((0, 15), (4, 3), (3, 10), (7, 22), (2, 9), (6, 21), (1, 16), (5, 4), (2, 17), (6, 5)),
    ),
    (
        ((1, 17), (5, 5), (2, 18), (6, 6), (0, 16), (4, 4)),
        ((0, 7), (4, 19), (3, 18), (7, 6), (1, 8), (5, 20)),
    ),
)

VMEM = pltpu.VMEM
SMEM_SPEC = pl.BlockSpec(memory_space=pltpu.SMEM)
VMEM_SPEC = pl.BlockSpec(memory_space=pltpu.VMEM)
ANY_SPEC = pl.BlockSpec(memory_space=pl.ANY)
LIMIT = pltpu.CompilerParams(vmem_limit_bytes=40 << 20)


def moves(blocks):
    return pl.CostEstimate(flops=0, bytes_accessed=2 * blocks * BLK * BLK * 2, transcendentals=0)


def rows_shape(rows):
    return jax.ShapeDtypeStruct((rows, BLK), jnp.bfloat16)


def blk(n):
    return pl.ds(n * BLK, BLK)


def ordered_kernel(orders, index_ref, src_ref, note_ref, *outs):
    for out, order in zip(outs, orders, strict=True):
        for n, place in enumerate(order):
            out[blk(n), :] = src_ref[index_ref[place]]
        out[pl.ds(len(order) * BLK, 16), :] = note_ref[...]


def ordered(src, index, note, orders):
    return pl.pallas_call(
        functools.partial(ordered_kernel, orders),
        out_shape=[rows_shape(len(order) * BLK + 16) for order in orders],
        in_specs=[SMEM_SPEC, VMEM_SPEC, VMEM_SPEC],
        out_specs=[VMEM_SPEC for _ in orders],
        compiler_params=LIMIT,
        cost_estimate=moves(sum(len(order) for order in orders)),
    )(index, src, note)


def right_kernel(index_ref, src_ref, code_ref, after_ref, out):
    del after_ref
    for n in range(16):
        for t in range(STEPS):
            out[n, pl.ds(t * BLK, BLK), :] = src_ref[index_ref[n + t]]
        out[n, pl.ds(STEPS * BLK, 16), :] = code_ref[n]


def right_packed(src, index, codes, after):
    return pl.pallas_call(
        right_kernel,
        out_shape=jax.ShapeDtypeStruct((16, STEPS * BLK + 16, BLK), jnp.bfloat16),
        in_specs=[SMEM_SPEC, VMEM_SPEC, VMEM_SPEC, ANY_SPEC],
        out_specs=VMEM_SPEC,
        compiler_params=LIMIT,
        cost_estimate=moves(48),
    )(index, src, codes, after)


def pack_kernel(spec, notes, count, core_ref, *refs):
    sources, outs = refs[:count], refs[count:]
    if notes:
        merged = None
        for source, row, rows, turn in notes:
            note = sources[source][pl.ds(row, rows), :].astype(jnp.float32)
            if rows == 16:
                note = jnp.concatenate([note, jnp.zeros((8, BLK), jnp.float32)])
            else:
                note = note[:NQ]
            if turn:
                note = pltpu.roll(note, turn, 0)
            merged = note if merged is None else jnp.maximum(merged, note)
        merged = jnp.concatenate([merged, jnp.zeros((8, BLK), jnp.float32)]).astype(jnp.bfloat16)

    def copy(out, n, entry):
        out[blk(n), :] = sources[entry[0]][blk(entry[1]), :]

    for out, (entries, noted) in zip(outs, spec, strict=True):
        for n, (zero, one) in enumerate(entries):
            if zero == one:
                copy(out, n, zero)
        if noted:
            out[pl.ds(len(entries) * BLK, 32), :] = merged
    if any(zero != one for entries, _ in spec for zero, one in entries):
        for core in range(2):

            @pl.when(core_ref[0] == core)
            def _(core=core):
                for out, (entries, _) in zip(outs, spec, strict=True):
                    for n, pair in enumerate(entries):
                        if pair[0] != pair[1]:
                            copy(out, n, pair[core])


def pack(core, sources, spec, notes):
    used = sorted({e[0] for entries, _ in spec for pair in entries for e in pair} | {n[0] for n in notes})
    where = {source: n for n, source in enumerate(used)}
    spec = tuple(
        (tuple(tuple((where[e[0]], e[1]) for e in pair) for pair in entries), noted)
        for entries, noted in spec
    )
    notes = tuple((where[n[0]],) + tuple(n[1:]) for n in notes)
    return pl.pallas_call(
        functools.partial(pack_kernel, spec, notes, len(used)),
        out_shape=[rows_shape(len(entries) * BLK + 32 * noted) for entries, noted in spec],
        in_specs=[SMEM_SPEC] + [VMEM_SPEC] * len(used),
        out_specs=[VMEM_SPEC for _ in spec],
        compiler_params=LIMIT,
        cost_estimate=moves(sum(len(entries) for entries, _ in spec)),
    )(core, *[sources[source] for source in used])


def product_kernel(counts, base, first, last, table_ref, right_ref, *rest):
    lefts, rest = rest[: len(counts)], rest[len(counts) :]
    if last:
        before, out_ref, acc = rest
        acc[...] = before[...]
    elif first:
        (acc,) = rest
        acc[...] = jnp.zeros_like(acc)
    else:
        before, acc = rest
        acc[...] = before[...]
    for left, count in zip(lefts, counts, strict=True):

        def body(n, carry, left=left, base=base):
            block = left[pl.ds(pl.multiple_of(n * BLK, BLK), BLK), :]
            for rank in range(2):
                owner = table_ref[3 * rank, base + n]
                row = pl.multiple_of(table_ref[3 * rank + 1, base + n], BLK)
                place = table_ref[3 * rank + 2, base + n]
                right = right_ref[owner, pl.ds(row, BLK), :]
                acc[place] += jnp.dot(block, right, preferred_element_type=jnp.float32)
            return carry

        lax.fori_loop(0, count, body, 0, unroll=6)
        base += count
    if last:
        out_ref[...] = acc[:KEPT].astype(out_ref.dtype)


def product(table, right, lefts, base, before=None, last=False):
    counts = tuple(left.shape[0] // BLK for left in lefts)
    total = sum(counts)
    sums = jax.ShapeDtypeStruct((KEPT + 1, BLK, BLK), jnp.float32)
    return pl.pallas_call(
        functools.partial(product_kernel, counts, base, before is None, last),
        out_shape=jax.ShapeDtypeStruct((KEPT, BLK, BLK), jnp.bfloat16) if last else sums,
        in_specs=[SMEM_SPEC] + [VMEM_SPEC] * (1 + len(lefts) + (before is not None)),
        out_specs=VMEM_SPEC,
        scratch_shapes=[VMEM(sums.shape, jnp.float32)] if last else [],
        compiler_params=LIMIT,
        cost_estimate=pl.CostEstimate(
            flops=total * 16 * BLK**3, bytes_accessed=total * BLK * BLK * 2, transcendentals=0
        ),
    )(table, right, *lefts, *(() if before is None else (before,)))


def left_order(groups):
    found = []
    for core in range(2):
        rows = []
        for low, high in groups:
            for other_core in range(2):
                rows += [(other_core, d, 1) for _, d in low]
                rows += [(other_core, d, 2) for _, d in high]
                rows += [(other_core, d, 3 * core) for _, d in (high if core else low)]
        found.append(rows)
    return np.array(found, np.int32)


def tables(groups, notes, right_codes, c_code, start, core):
    order = left_order(groups)
    order = jnp.where(core == 0, order[0], order[1])
    other_core, distance, panel = (order[:, n] for n in range(3))
    count = order.shape[0]
    notes = jnp.stack(notes)[:, :NQ, :32].astype(jnp.int32)
    flat = (notes[:, :, :16] * 64 + notes[:, :, 16:] - 1).reshape(1, 2 * NQ * 16)
    place = (other_core * NQ + distance) * 16 + (start + panel) % 16
    codes = jnp.sum(jnp.where(place[:, None] == jnp.arange(2 * NQ * 16)[None, :], flat, 0), axis=1)
    step = panel - core
    right_live = right_codes >= 0
    right_inner = jnp.where(right_live, right_codes // BC, -1)
    owners = jnp.arange(16, dtype=jnp.int32)
    earlier = owners[None, :] < owners[:, None]
    rank = jnp.sum(
        ((right_inner[:, None, :] == right_inner[None, :, :]) & earlier[:, :, None]).astype(jnp.int32),
        axis=1,
    )
    packed = jnp.where(right_live, right_inner * 1024 + rank * 32 + right_codes % BC, -1)
    right_n = jnp.where(
        (step == 0)[:, None],
        packed[None, :, 0],
        jnp.where((step == 1)[:, None], packed[None, :, 1], packed[None, :, 2]),
    )
    match = (right_n >= 0) & (codes >= 0)[:, None] & ((right_n // 1024) == (codes % PANEL)[:, None])
    rows = []
    for rank_number in range(2):
        hit = match & ((right_n // 32) % 32 == rank_number)
        found = jnp.sum(jnp.where(hit, owners[None, :] * 32 + right_n % 32 + 1, 0), axis=1)
        partner = jnp.maximum(found - 1, 0)
        target = (codes // PANEL) * BC + partner % 32
        there = (target[:, None] == c_code[None, :]) & (found > 0)[:, None]
        slot = jnp.sum(jnp.where(there, jnp.arange(KEPT)[None, :] - KEPT, 0), axis=1) + KEPT
        rows += [partner // 32, step * BLK, slot]
    return jnp.stack(rows).astype(jnp.int32).reshape(6, count)


def moved(array, distance):
    route = [(i, (i + distance) % NQ) for i in range(NQ)]
    return lax.ppermute(array, RING, route)


def local(a_own_values, a_own_code, b_own_values, b_own_code, c_code):
    r = lax.axis_index(ROW)
    q = lax.axis_index(RING)
    core = lax.axis_index("core")
    start = (r + 2 * q) % 16
    a_own = a_own_values.reshape(16, BLK, BLK)
    b_own = b_own_values.reshape(16, BLK, BLK)
    core_1d = core.astype(jnp.int32).reshape(1)

    sources, at = [], {}

    def keep(array, names):
        for n, name in enumerate(names):
            at[name] = (len(sources), 2 * n)
        sources.append(array)
        return len(sources) - 1

    def send(array, names, distance):
        return keep(moved(array, distance), [(a, (d + distance) % NQ) for a, d in names])

    def both(entry):
        return (entry, entry)

    def blocks(names):
        return [both((at[name][0], at[name][1] + b)) for name in names for b in range(2)]

    def packed(spec, notes=()):
        return pack(core_1d, sources, spec, notes)

    def core_blocks(group):
        low, high = group

        def block(name, b):
            return (at[name][0], at[name][1] + b)

        spec = []
        for turned in (False, True):
            entries = [both(block(name, 1)) for name in low]
            entries += [both(block(name, 0)) for name in high]
            for x, y in zip(low, high, strict=True):
                pair = (block(x, 0), block(y, 1))
                entries.append(pair[::-1] if turned else pair)
            spec.append((entries, turned))
        return spec

    code = a_own_code.reshape(16) + 1
    note = jnp.concatenate([code // 64, code % 64]).astype(jnp.bfloat16).reshape(1, 32)
    note = jnp.pad(note, ((0, 15), (0, BLK - 32)))
    a_index = (start + jnp.arange(16, dtype=jnp.int32)) % 16

    def class_order(classes):
        return tuple(2 * a + b for a in classes for b in range(2))

    one, two = (1, 2, 5, 6), (3, 0, 7, 4)
    first, second = ordered(a_own, a_index, note, (class_order(one), class_order(two)))
    ones, twos = [(a, 0) for a in one], [(a, 0) for a in two]
    own = keep(first, ones)
    keep(second, twos)
    up2 = send(second, twos, 2)
    down2 = send(first, ones, -2)
    up1 = send(first, ones, 1)
    down1 = send(second, twos, -1)

    shift = (2 * q + core + jnp.arange(18, dtype=jnp.int32)) % 16
    b_code = b_own_code.reshape(16) + 1
    b_code = jnp.sum(jnp.where(shift[:, None] == jnp.arange(16)[None, :], b_code[None, :], 0), axis=1)
    b_code = jnp.stack([b_code[t : t + 16] for t in range(STEPS)], axis=1)
    b_code = jnp.concatenate([b_code // 16, b_code % 16], axis=1).astype(jnp.bfloat16)
    b_code = jnp.broadcast_to(jnp.pad(b_code, ((0, 0), (0, BLK - 6)))[:, None, :], (16, 16, BLK))
    right = right_packed(b_own, shift, b_code, sources[up1])
    right = lax.all_to_all(right, ROW, 0, 0, tiled=True)

    near = [(own, 8 * BLK, 16, 0)]
    near += [(up1, 8 * BLK, 16, 1), (up2, 8 * BLK, 16, 2), (down1, 8 * BLK, 16, 23), (down2, 8 * BLK, 16, 22)]
    up_names = [(2, 1), (6, 1), (3, 2), (7, 2), (0, 2), (4, 2)]
    down_names = [(3, 23), (7, 23), (2, 22), (6, 22), (1, 22), (5, 22)]
    up_in, down_in = packed([(blocks(up_names), True), (blocks(down_names), True)], near)
    mine = len(sources)
    sources.append(up_in)
    up3 = send(up_in, up_names, 1)
    down3 = send(down_in, down_names, -1)

    cross_names = [(5, 1), (6, 1), (7, 2), (4, 0), (5, 0), (4, 23), (3, 23), (2, 22)]
    (cross_in,) = packed([(blocks(cross_names), True)], near)
    sources.append(cross_in)
    crossed = send(cross_in, cross_names, 12)
    around = [(crossed - 1, 16 * BLK, 32, 0), (crossed, 16 * BLK, 32, 12)]

    near = [(mine, 12 * BLK, 32, 0), (up3, 12 * BLK, 32, 1), (down3, 12 * BLK, 32, 23)]
    plans = (([(1, 1), (2, 2)], 15), ([(5, 1), (6, 2)], 3), ([(0, 23), (7, 22)], 9), ([(4, 23), (3, 22)], -3))
    inputs = packed([(blocks(names), True) for names, _ in plans], near)
    far = [(len(sources), 4 * BLK, 32, 0)]
    sources.append(inputs[0])
    for array, (names, distance) in zip(inputs, plans, strict=True):
        far.append((send(array, names, distance), 4 * BLK, 32, distance % NQ))

    cross_names = [(6, 2), (7, 3), (0, 3), (3, 22), (2, 21), (1, 21)]
    (cross_in,) = packed([(blocks(cross_names), False)])
    send(cross_in, cross_names, 12)

    up_names = [(1, 16), (5, 4), (2, 17), (6, 5), (0, 15), (4, 3)]
    down_names = [(0, 8), (4, 20), (3, 19), (7, 7), (1, 9), (5, 21)]
    up_in, down_in = packed([(blocks(up_names), False), (blocks(down_names), False)])
    send(up_in, up_names, 1)
    send(down_in, down_names, -1)

    lefts, notes = [], []
    for number, group in enumerate(GROUPS):
        spec = core_blocks(group)
        if number == 2:
            spec = [(entries, False) for entries, _ in spec]
        kept, sent = packed(spec, (around, far, ())[number])
        received = lax.ppermute(sent, "core", [(0, 1), (1, 0)])
        count = len(spec[0][0])
        lefts.append((kept, received))
        notes.append((sent[count * BLK :], received[count * BLK :]))

    right_codes = right[:, STEPS * BLK, :6].astype(jnp.int32)
    right_codes = right_codes[:, :3] * 16 + right_codes[:, 3:] - 1
    c_code = c_code.reshape(KEPT)
    table = tables(GROUPS[:1], notes[0], right_codes, c_code, start, core)
    sums = product(table, right, lefts[0], 0)
    table = tables(GROUPS[1:], notes[1], right_codes, c_code, start, core)
    sums = product(table, right, lefts[1], 0, sums)
    return product(table, right, lefts[2], 60, sums, last=True)[None, None]


def solution(mesh):
    fine = Mesh(mesh.devices.reshape(SIZES), AXES)
    return jax.shard_map(
        local,
        mesh=fine,
        in_specs=(
            P(ROW, COL, None, None, None, None),
            P(ROW, COL, None, None),
            P(ROW, COL, None, None, None, None),
            P(ROW, COL, None, None),
            P(ROW, COL, None),
        ),
        out_specs=P(ROW, COL, None, None, None),
        check_vma=False,
    )
```

time: 160 us -> 147 us (0.919)
  the two profiles are of different devices: /device:TPU:1 before, /device:TPU:43 now
where the time goes in v3:
time: 147 us; the launch traced here: 146 us
  starting transfers between devices  91.4 us (62%)
  waiting for transfers between devices  25.4 us (17%)
  Pallas kernels  17.8 us (12%)
  local copies, waits for them, and re-layouts  5.55 us (4%)
  other arithmetic  5.11 us (3%)
    ppermute x14, starting transfers between devices, moved(): return lax.ppermute(array, RING, route)  71.6 us
    ppermute x14, waiting for transfers between devices, moved(): return lax.ppermute(array, RING, route)  25.4 us
    ppermute x3, starting transfers between devices, local(): received = lax.ppermute(sent, 'core', [(0, 1), (1, 0)])  12.3 us
    pallas_call x3, Pallas kernels, product(): pl.pallas_call(functools.partial(product_kernel, counts, base, before is...  12.1 us
    all_to_all x1, starting transfers between devices, local(): right = lax.all_to_all(right, ROW, 0, 0, tiled=True)  7.45 us
    unnamed x15, local copies, waits for them, and re-layouts  5.15 us
    pallas_call x8, Pallas kernels, pack(): pl.pallas_call(functools.partial(pack_kernel, spec, notes, len(used)), ou...  3.33 us
  transfers between devices with their start and end apart: 18, of which 6 were waited for; matrix products, arithmetic and copies ran while one was open for 3% of the time, Pallas kernels for 9%

profile of v3, /device:TPU:43, one launch (start us, length us, event | category | flops | bytes accessed | tf_op | source)
XLA Modules:
  0.0 145.8 jit_solution(10312122947538082333)
XLA Ops:
  2.4 4.0 %collective-permute-start = (bf16[1040,128]{1,0:T(8,128)(2,1)S(1)}, bf16[1040,128]{1,0:T(8,128)(2,1)S(1)}, u32[]{:S(2)}, u32[]{:S(2)}) collective-permute-start(bf16[1040,128]{1,0:T(8,128)(2,1)S(1)} %get-tuple-element.21.refs_0_), channel_id=1, source_target_pairs={{0,2},{2,4},{4,6},{6,8},{8,10},{10,12},{12,14},{14,16},{16,18},{18... | collective-permute-start | bytes 798728 | tf_op jit(solution)/shard_map/ppermute | solution.py:246
  6.4 15.0 %collective-permute-start.2 = (bf16[1040,128]{1,0:T(8,128)(2,1)S(1)}, bf16[1040,128]{1,0:T(8,128)(2,1)S(1)}, u32[]{:S(2)}, u32[]{:S(2)}) collective-permute-start(bf16[1040,128]{1,0:T(8,128)(2,1)S(1)} %get-tuple-element.21.refs_0_), channel_id=1, source_target_pairs={{0,44},{2,46},{4,0},{6,2},{8,4},{10,6},{12,8},{14,10},{16,12},{18,... | collective-permute-start | bytes 798728 | tf_op jit(solution)/shard_map/ppermute | solution.py:246
  21.4 1.9 %collective-permute-start.1 = (bf16[1040,128]{1,0:T(8,128)(2,1)S(1)}, bf16[1040,128]{1,0:T(8,128)(2,1)S(1)}, u32[]{:S(2)}, u32[]{:S(2)}) collective-permute-start(bf16[1040,128]{1,0:T(8,128)(2,1)S(1)} %get-tuple-element.22.refs_1_), channel_id=1, source_target_pairs={{0,4},{2,6},{4,8},{6,10},{8,12},{10,14},{12,16},{14,18},{16,20},{1... | collective-permute-start | bytes 798728 | tf_op jit(solution)/shard_map/ppermute | solution.py:246
  23.3 6.7 %collective-permute-start.3 = (bf16[1040,128]{1,0:T(8,128)(2,1)S(1)}, bf16[1040,128]{1,0:T(8,128)(2,1)S(1)}, u32[]{:S(2)}, u32[]{:S(2)}) collective-permute-start(bf16[1040,128]{1,0:T(8,128)(2,1)S(1)} %get-tuple-element.22.refs_1_), channel_id=1, source_target_pairs={{0,46},{2,0},{4,2},{6,4},{8,6},{10,8},{12,10},{14,12},{16,14},{18,... | collective-permute-start | bytes 798728 | tf_op jit(solution)/shard_map/ppermute | solution.py:246
  32.3 7.9 %collective-permute-done.1.refs_1_.refs_2_ = bf16[1040,128]{1,0:T(8,128)(2,1)S(1)} collective-permute-done((bf16[1040,128]{1,0:T(8,128)(2,1)S(1)}, bf16[1040,128]{1,0:T(8,128)(2,1)S(1)}, u32[]{:S(2)}, u32[]{:S(2)}) %collective-permute-start.1) | collective-permute-done | bytes 266272 | tf_op jit(solution)/shard_map/ppermute | solution.py:246
  40.2 3.0 %collective-permute-start.15 = (bf16[2080,128]{1,0:T(8,128)(2,1)S(1)}, bf16[2080,128]{1,0:T(8,128)(2,1)S(1)}, u32[]{:S(2)}, u32[]{:S(2)}) collective-permute-start(bf16[2080,128]{1,0:T(8,128)(2,1)S(1)} %shard_map.99.refs_6_), channel_id=1, source_target_pairs={{0,24},{2,26},{4,28},{6,30},{8,32},{10,34},{12,36},{14,38},{16,40}... | collective-permute-start | bytes 1597448 | tf_op jit(solution)/shard_map/ppermute | solution.py:246
  46.2 7.0 %collective-permute-start.5 = (bf16[1568,128]{1,0:T(8,128)(2,1)}, bf16[1568,128]{1,0:T(8,128)(2,1)S(1)}, u32[]{:S(2)}, u32[]{:S(2)}) collective-permute-start(bf16[1568,128]{1,0:T(8,128)(2,1)} %get-tuple-element.24), channel_id=1, source_target_pairs={{0,46},{2,0},{4,2},{6,4},{8,6},{10,8},{12,10},{14,12},{16,14},{18,... | collective-permute-start | bytes 1204232 | tf_op jit(solution)/shard_map/ppermute | solution.py:246
  56.1 7.5 %all-to-all-start = ((bf16[16,400,128]{2,1,0:T(8,128)(2,1)}), bf16[16,400,128]{2,1,0:T(8,128)(2,1)}, u32[]{:S(2)}, u32[]{:S(2)}) async-start(bf16[16,400,128]{2,1,0:T(8,128)(2,1)} %shard_map.92), calls=%async_computation | async-start | bytes 3276800 | tf_op jit(solution)/shard_map/all_to_all | solution.py:319
  63.6 4.0 %collective-permute-start.10 = (bf16[1536,128]{1,0:T(8,128)(2,1)S(1)}, bf16[1536,128]{1,0:T(8,128)(2,1)S(1)}, u32[]{:S(2)}, u32[]{:S(2)}) collective-permute-start(bf16[1536,128]{1,0:T(8,128)(2,1)S(1)} %shard_map.95), channel_id=1, source_target_pairs={{0,24},{2,26},{4,28},{6,30},{8,32},{10,34},{12,36},{14,38},{16,40}... | collective-permute-start | bytes 1179656 | tf_op jit(solution)/shard_map/ppermute | solution.py:246
  68.6 1.9 %collective-permute-start.6 = (bf16[544,128]{1,0:T(8,128)(2,1)S(1)}, bf16[544,128]{1,0:T(8,128)(2,1)S(1)}, u32[]{:S(2)}, u32[]{:S(2)}) collective-permute-start(bf16[544,128]{1,0:T(8,128)(2,1)S(1)} %get-tuple-element.25.refs_2_), channel_id=1, source_target_pairs={{0,30},{2,32},{4,34},{6,36},{8,38},{10,40},{12,42},{14,44},{16,46}... | collective-permute-start | bytes 417800 | tf_op jit(solution)/shard_map/ppermute | solution.py:246
  71.6 5.5 %collective-permute-start.16 = (bf16[3104,128]{1,0:T(8,128)(2,1)S(1)}, bf16[3104,128]{1,0:T(8,128)(2,1)S(1)}, u32[]{:S(2)}, u32[]{:S(2)}) collective-permute-start(bf16[3104,128]{1,0:T(8,128)(2,1)S(1)} %get-tuple-element.35), channel_id=1, source_target_pairs={{0,1},{1,0},{2,3},{3,2},{4,5},{5,4},{6,7},{7,6},{8,9},{9,8},{10,11... | collective-permute-start | bytes 2383880 | tf_op jit(solution)/shard_map/ppermute | solution.py:361
  77.1 1.9 %collective-permute-start.7 = (bf16[544,128]{1,0:T(8,128)(2,1)S(1)}, bf16[544,128]{1,0:T(8,128)(2,1)S(1)}, u32[]{:S(2)}, u32[]{:S(2)}) collective-permute-start(bf16[544,128]{1,0:T(8,128)(2,1)S(1)} %get-tuple-element.26), channel_id=1, source_target_pairs={{0,6},{2,8},{4,10},{6,12},{8,14},{10,16},{12,18},{14,20},{16,22},{... | collective-permute-start | bytes 417800 | tf_op jit(solution)/shard_map/ppermute | solution.py:246
  79.0 7.2 %collective-permute-start.8 = (bf16[544,128]{1,0:T(8,128)(2,1)S(1)}, bf16[544,128]{1,0:T(8,128)(2,1)S(1)}, u32[]{:S(2)}, u32[]{:S(2)}) collective-permute-start(bf16[544,128]{1,0:T(8,128)(2,1)S(1)} %get-tuple-element.27), channel_id=1, source_target_pairs={{0,18},{2,20},{4,22},{6,24},{8,26},{10,28},{12,30},{14,32},{16,34}... | collective-permute-start | bytes 417800 | tf_op jit(solution)/shard_map/ppermute | solution.py:246
  86.2 8.2 %collective-permute-start.9 = (bf16[544,128]{1,0:T(8,128)(2,1)S(1)}, bf16[544,128]{1,0:T(8,128)(2,1)S(1)}, u32[]{:S(2)}, u32[]{:S(2)}) collective-permute-start(bf16[544,128]{1,0:T(8,128)(2,1)S(1)} %get-tuple-element.28), channel_id=1, source_target_pairs={{0,42},{2,44},{4,46},{6,0},{8,2},{10,4},{12,6},{14,8},{16,10},{18,... | collective-permute-start | bytes 417800 | tf_op jit(solution)/shard_map/ppermute | solution.py:246
  94.5 2.2 %collective-permute-done.7.refs_4_.refs_3_ = bf16[544,128]{1,0:T(8,128)(2,1)S(1)} collective-permute-done((bf16[544,128]{1,0:T(8,128)(2,1)S(1)}, bf16[544,128]{1,0:T(8,128)(2,1)S(1)}, u32[]{:S(2)}, u32[]{:S(2)}) %collective-permute-start.7) | collective-permute-done | bytes 139296 | tf_op jit(solution)/shard_map/ppermute | solution.py:246
  96.7 5.6 %collective-permute-done.8.refs_5_.refs_4_ = bf16[544,128]{1,0:T(8,128)(2,1)S(1)} collective-permute-done((bf16[544,128]{1,0:T(8,128)(2,1)S(1)}, bf16[544,128]{1,0:T(8,128)(2,1)S(1)}, u32[]{:S(2)}, u32[]{:S(2)}) %collective-permute-start.8) | collective-permute-done | bytes 139296 | tf_op jit(solution)/shard_map/ppermute | solution.py:246
  102.4 6.4 %collective-permute-done.9.refs_6_.refs_5_ = bf16[544,128]{1,0:T(8,128)(2,1)S(1)} collective-permute-done((bf16[544,128]{1,0:T(8,128)(2,1)S(1)}, bf16[544,128]{1,0:T(8,128)(2,1)S(1)}, u32[]{:S(2)}, u32[]{:S(2)}) %collective-permute-start.9) | collective-permute-done | bytes 139296 | tf_op jit(solution)/shard_map/ppermute | solution.py:246
  110.8 7.0 %collective-permute-start.13 = (bf16[1536,128]{1,0:T(8,128)(2,1)S(1)}, bf16[1536,128]{1,0:T(8,128)(2,1)S(1)}, u32[]{:S(2)}, u32[]{:S(2)}) collective-permute-start(bf16[1536,128]{1,0:T(8,128)(2,1)S(1)} %get-tuple-element.31), channel_id=1, source_target_pairs={{0,46},{2,0},{4,2},{6,4},{8,6},{10,8},{12,10},{14,12},{16,14},{18,... | collective-permute-start | bytes 1179656 | tf_op jit(solution)/shard_map/ppermute | solution.py:246
  118.9 3.1 %collective-permute-start.11 = (bf16[3872,128]{1,0:T(8,128)(2,1)S(1)}, bf16[3872,128]{1,0:T(8,128)(2,1)S(1)}, u32[]{:S(2)}, u32[]{:S(2)}) collective-permute-start(bf16[3872,128]{1,0:T(8,128)(2,1)S(1)} %get-tuple-element.29), channel_id=1, source_target_pairs={{0,1},{1,0},{2,3},{3,2},{4,5},{5,4},{6,7},{7,6},{8,9},{9,8},{10,11... | collective-permute-start | bytes 2973704 | tf_op jit(solution)/shard_map/ppermute | solution.py:361
  122.0 2.3 %collective-permute-done.12.refs_0_ = bf16[1536,128]{1,0:T(8,128)(2,1)S(1)} collective-permute-done((bf16[1536,128]{1,0:T(8,128)(2,1)S(1)}, bf16[1536,128]{1,0:T(8,128)(2,1)S(1)}, u32[]{:S(2)}, u32[]{:S(2)}) %collective-permute-start.12) | collective-permute-done | bytes 393248 | tf_op jit(solution)/shard_map/ppermute | solution.py:246
  126.2 3.8 %collective-permute-start.14 = (bf16[2304,128]{1,0:T(8,128)(2,1)}, bf16[2304,128]{1,0:T(8,128)(2,1)}, u32[]{:S(2)}, u32[]{:S(2)}) collective-permute-start(bf16[2304,128]{1,0:T(8,128)(2,1)} %get-tuple-element.33), channel_id=1, source_target_pairs={{0,1},{1,0},{2,3},{3,2},{4,5},{5,4},{6,7},{7,6},{8,9},{9,8},{10,11... | collective-permute-start | bytes 1769480 | tf_op jit(solution)/shard_map/ppermute | solution.py:361
  133.7 3.8 %shard_map.101.rest_2_ = f32[13,128,128]{2,1,0:T(8,128)S(1)} custom-call(s32[6,48]{1,0:T(8,128)S(1)} %stack.59.table_ref, bf16[16,400,128]{2,1,0:T(8,128)(2,1)} %all-to-all-done.right_ref, bf16[3072,128]{1,0:T(8,128)(2,1)S(1)} %copy-done.5, bf16[3104,128]{1,0:T(8,128)(2,1)S(1)} %collective-permute-done.16.rest_1_), custom_call_target="tpu_custom_call" | custom-call | flops 1610612736 | bytes 1572864 | tf_op jit(solution)/shard_map/pallas_call | solution.py:181
  137.4 4.2 %shard_map.102.rest_2_ = f32[13,128,128]{2,1,0:T(8,128)S(1)} custom-call(s32[6,96]{1,0:T(8,128)S(1)} %stack.55.table_ref, bf16[16,400,128]{2,1,0:T(8,128)(2,1)} %all-to-all-done.right_ref, bf16[3840,128]{1,0:T(8,128)(2,1)S(1)} %copy-done.3, bf16[3872,128]{1,0:T(8,128)(2,1)S(1)} %collective-permute-done.11.rest_1_, f32[13,128,128]{2,1,0:T(8,128)S(1)} %shard_map.101.rest_2_), custom_call_target="tpu_custom_call" | custom-call | flops 2013265920 | bytes 1966080 | tf_op jit(solution)/shard_map/pallas_call | solution.py:181
  141.7 4.1 %shard_map.103 = bf16[12,128,128]{2,1,0:T(8,128)(2,1)} custom-call(s32[6,96]{1,0:T(8,128)S(1)} %stack.55.table_ref, bf16[16,400,128]{2,1,0:T(8,128)(2,1)} %all-to-all-done.right_ref, bf16[2304,128]{1,0:T(8,128)(2,1)S(1)} %get-tuple-element.32.rest_0_, bf16[2304,128]{1,0:T(8,128)(2,1)} %collective-permute-done.14.rest_1_, f32[13,128,128]{2,1,0:T(8,128)S(1)} %shard_map.102.rest_2_), custom_call_target="tpu_custom_call" | custom-call | flops 1207959552 | bytes 1179648 | tf_op jit(solution)/shard_map/pallas_call | solution.py:181
  (101 shorter events, 21.1 us)
Async XLA Ops:
  0.8 1.0 copy-start
  2.4 29.9 %collective-permute-start = (bf16[1040,128]{1,0:T(8,128)(2,1)S(1)}, bf16[1040,128]{1,0:T(8,128)(2,1)S(1)}, u32[]{:S(2)}, u32[]{:S(2)}) collective-permute-start(bf16[1040,128]{1,0:T(8,128)(2,1)S(1)} %get-tuple-element.21.refs_0_), channel_id=1, source_target_pairs={{0,2},{2,4},{4,6},{6,8},{8,10},{10,12},{12,14},{14,16},{16,18},{18... | collective-permute-start | bytes 798728 | tf_op jit(solution)/shard_map/ppermute | solution.py:246
  6.4 33.8 %collective-permute-start.2 = (bf16[1040,128]{1,0:T(8,128)(2,1)S(1)}, bf16[1040,128]{1,0:T(8,128)(2,1)S(1)}, u32[]{:S(2)}, u32[]{:S(2)}) collective-permute-start(bf16[1040,128]{1,0:T(8,128)(2,1)S(1)} %get-tuple-element.21.refs_0_), channel_id=1, source_target_pairs={{0,44},{2,46},{4,0},{6,2},{8,4},{10,6},{12,8},{14,10},{16,12},{18,... | collective-permute-start | bytes 798728 | tf_op jit(solution)/shard_map/ppermute | solution.py:246
  21.4 18.8 %collective-permute-start.1 = (bf16[1040,128]{1,0:T(8,128)(2,1)S(1)}, bf16[1040,128]{1,0:T(8,128)(2,1)S(1)}, u32[]{:S(2)}, u32[]{:S(2)}) collective-permute-start(bf16[1040,128]{1,0:T(8,128)(2,1)S(1)} %get-tuple-element.22.refs_1_), channel_id=1, source_target_pairs={{0,4},{2,6},{4,8},{6,10},{8,12},{10,14},{12,16},{14,18},{16,20},{1... | collective-permute-start | bytes 798728 | tf_op jit(solution)/shard_map/ppermute | solution.py:246
  23.3 16.9 %collective-permute-start.3 = (bf16[1040,128]{1,0:T(8,128)(2,1)S(1)}, bf16[1040,128]{1,0:T(8,128)(2,1)S(1)}, u32[]{:S(2)}, u32[]{:S(2)}) collective-permute-start(bf16[1040,128]{1,0:T(8,128)(2,1)S(1)} %get-tuple-element.22.refs_1_), channel_id=1, source_target_pairs={{0,46},{2,0},{4,2},{6,4},{8,6},{10,8},{12,10},{14,12},{16,14},{18,... | collective-permute-start | bytes 798728 | tf_op jit(solution)/shard_map/ppermute | solution.py:246
  40.2 30.3 %collective-permute-start.15 = (bf16[2080,128]{1,0:T(8,128)(2,1)S(1)}, bf16[2080,128]{1,0:T(8,128)(2,1)S(1)}, u32[]{:S(2)}, u32[]{:S(2)}) collective-permute-start(bf16[2080,128]{1,0:T(8,128)(2,1)S(1)} %shard_map.99.refs_6_), channel_id=1, source_target_pairs={{0,24},{2,26},{4,28},{6,30},{8,32},{10,34},{12,36},{14,38},{16,40}... | collective-permute-start | bytes 1597448 | tf_op jit(solution)/shard_map/ppermute | solution.py:246
  44.3 19.3 %collective-permute-start.4 = (bf16[1568,128]{1,0:T(8,128)(2,1)}, bf16[1568,128]{1,0:T(8,128)(2,1)S(1)}, u32[]{:S(2)}, u32[]{:S(2)}) collective-permute-start(bf16[1568,128]{1,0:T(8,128)(2,1)} %get-tuple-element.23.refs_2_), channel_id=1, source_target_pairs={{0,2},{2,4},{4,6},{6,8},{8,10},{10,12},{12,14},{14,16},{16,18},{18... | collective-permute-start | bytes 1204232 | tf_op jit(solution)/shard_map/ppermute | solution.py:246
  46.2 17.3 %collective-permute-start.5 = (bf16[1568,128]{1,0:T(8,128)(2,1)}, bf16[1568,128]{1,0:T(8,128)(2,1)S(1)}, u32[]{:S(2)}, u32[]{:S(2)}) collective-permute-start(bf16[1568,128]{1,0:T(8,128)(2,1)} %get-tuple-element.24), channel_id=1, source_target_pairs={{0,46},{2,0},{4,2},{6,4},{8,6},{10,8},{12,10},{14,12},{16,14},{18,... | collective-permute-start | bytes 1204232 | tf_op jit(solution)/shard_map/ppermute | solution.py:246
  53.2 1.0 copy-start.1
  56.1 74.7 %all-to-all-start = ((bf16[16,400,128]{2,1,0:T(8,128)(2,1)}), bf16[16,400,128]{2,1,0:T(8,128)(2,1)}, u32[]{:S(2)}, u32[]{:S(2)}) async-start(bf16[16,400,128]{2,1,0:T(8,128)(2,1)} %shard_map.92), calls=%async_computation | async-start | bytes 3276800 | tf_op jit(solution)/shard_map/all_to_all | solution.py:319
  63.6 45.2 %collective-permute-start.10 = (bf16[1536,128]{1,0:T(8,128)(2,1)S(1)}, bf16[1536,128]{1,0:T(8,128)(2,1)S(1)}, u32[]{:S(2)}, u32[]{:S(2)}) collective-permute-start(bf16[1536,128]{1,0:T(8,128)(2,1)S(1)} %shard_map.95), channel_id=1, source_target_pairs={{0,24},{2,26},{4,28},{6,30},{8,32},{10,34},{12,36},{14,38},{16,40}... | collective-permute-start | bytes 1179656 | tf_op jit(solution)/shard_map/ppermute | solution.py:246
  68.6 17.6 %collective-permute-start.6 = (bf16[544,128]{1,0:T(8,128)(2,1)S(1)}, bf16[544,128]{1,0:T(8,128)(2,1)S(1)}, u32[]{:S(2)}, u32[]{:S(2)}) collective-permute-start(bf16[544,128]{1,0:T(8,128)(2,1)S(1)} %get-tuple-element.25.refs_2_), channel_id=1, source_target_pairs={{0,30},{2,32},{4,34},{6,36},{8,38},{10,40},{12,42},{14,44},{16,46}... | collective-permute-start | bytes 417800 | tf_op jit(solution)/shard_map/ppermute | solution.py:246
  71.6 58.4 %collective-permute-start.16 = (bf16[3104,128]{1,0:T(8,128)(2,1)S(1)}, bf16[3104,128]{1,0:T(8,128)(2,1)S(1)}, u32[]{:S(2)}, u32[]{:S(2)}) collective-permute-start(bf16[3104,128]{1,0:T(8,128)(2,1)S(1)} %get-tuple-element.35), channel_id=1, source_target_pairs={{0,1},{1,0},{2,3},{3,2},{4,5},{5,4},{6,7},{7,6},{8,9},{9,8},{10,11... | collective-permute-start | bytes 2383880 | tf_op jit(solution)/shard_map/ppermute | solution.py:361
  77.1 19.6 %collective-permute-start.7 = (bf16[544,128]{1,0:T(8,128)(2,1)S(1)}, bf16[544,128]{1,0:T(8,128)(2,1)S(1)}, u32[]{:S(2)}, u32[]{:S(2)}) collective-permute-start(bf16[544,128]{1,0:T(8,128)(2,1)S(1)} %get-tuple-element.26), channel_id=1, source_target_pairs={{0,6},{2,8},{4,10},{6,12},{8,14},{10,16},{12,18},{14,20},{16,22},{... | collective-permute-start | bytes 417800 | tf_op jit(solution)/shard_map/ppermute | solution.py:246
  79.0 23.4 %collective-permute-start.8 = (bf16[544,128]{1,0:T(8,128)(2,1)S(1)}, bf16[544,128]{1,0:T(8,128)(2,1)S(1)}, u32[]{:S(2)}, u32[]{:S(2)}) collective-permute-start(bf16[544,128]{1,0:T(8,128)(2,1)S(1)} %get-tuple-element.27), channel_id=1, source_target_pairs={{0,18},{2,20},{4,22},{6,24},{8,26},{10,28},{12,30},{14,32},{16,34}... | collective-permute-start | bytes 417800 | tf_op jit(solution)/shard_map/ppermute | solution.py:246
  86.2 22.6 %collective-permute-start.9 = (bf16[544,128]{1,0:T(8,128)(2,1)S(1)}, bf16[544,128]{1,0:T(8,128)(2,1)S(1)}, u32[]{:S(2)}, u32[]{:S(2)}) collective-permute-start(bf16[544,128]{1,0:T(8,128)(2,1)S(1)} %get-tuple-element.28), channel_id=1, source_target_pairs={{0,42},{2,44},{4,46},{6,0},{8,2},{10,4},{12,6},{14,8},{16,10},{18,... | collective-permute-start | bytes 417800 | tf_op jit(solution)/shard_map/ppermute | solution.py:246
  108.9 23.2 %copy-start.6 = (s32[1,1,12]{2,1,0:T(1,128)S(1)}, s32[1,1,12]{2,1,0:T(1,128)}, u32[]{:S(2)}) copy-start(s32[1,1,12]{2,1,0:T(1,128)} %param.13) | copy-start | bytes 148
  108.9 15.5 %collective-permute-start.12 = (bf16[1536,128]{1,0:T(8,128)(2,1)S(1)}, bf16[1536,128]{1,0:T(8,128)(2,1)S(1)}, u32[]{:S(2)}, u32[]{:S(2)}) collective-permute-start(bf16[1536,128]{1,0:T(8,128)(2,1)S(1)} %get-tuple-element.30), channel_id=1, source_target_pairs={{0,2},{2,4},{4,6},{6,8},{8,10},{10,12},{12,14},{14,16},{16,18},{18... | collective-permute-start | bytes 1179656 | tf_op jit(solution)/shard_map/ppermute | solution.py:246
  110.8 14.4 %collective-permute-start.13 = (bf16[1536,128]{1,0:T(8,128)(2,1)S(1)}, bf16[1536,128]{1,0:T(8,128)(2,1)S(1)}, u32[]{:S(2)}, u32[]{:S(2)}) collective-permute-start(bf16[1536,128]{1,0:T(8,128)(2,1)S(1)} %get-tuple-element.31), channel_id=1, source_target_pairs={{0,46},{2,0},{4,2},{6,4},{8,6},{10,8},{12,10},{14,12},{16,14},{18,... | collective-permute-start | bytes 1179656 | tf_op jit(solution)/shard_map/ppermute | solution.py:246
  117.9 1.0 copy-start.2
  118.9 11.4 %collective-permute-start.11 = (bf16[3872,128]{1,0:T(8,128)(2,1)S(1)}, bf16[3872,128]{1,0:T(8,128)(2,1)S(1)}, u32[]{:S(2)}, u32[]{:S(2)}) collective-permute-start(bf16[3872,128]{1,0:T(8,128)(2,1)S(1)} %get-tuple-element.29), channel_id=1, source_target_pairs={{0,1},{1,0},{2,3},{3,2},{4,5},{5,4},{6,7},{7,6},{8,9},{9,8},{10,11... | collective-permute-start | bytes 2973704 | tf_op jit(solution)/shard_map/ppermute | solution.py:361
  126.2 15.5 %collective-permute-start.14 = (bf16[2304,128]{1,0:T(8,128)(2,1)}, bf16[2304,128]{1,0:T(8,128)(2,1)}, u32[]{:S(2)}, u32[]{:S(2)}) collective-permute-start(bf16[2304,128]{1,0:T(8,128)(2,1)} %get-tuple-element.33), channel_id=1, source_target_pairs={{0,1},{1,0},{2,3},{3,2},{4,5},{5,4},{6,7},{7,6},{8,9},{9,8},{10,11... | collective-permute-start | bytes 1769480 | tf_op jit(solution)/shard_map/ppermute | solution.py:361
  132.5 1.1 copy-start.5
  133.7 3.8 %copy-start.3 = (bf16[3840,128]{1,0:T(8,128)(2,1)S(1)}, bf16[3840,128]{1,0:T(8,128)(2,1)}, u32[]{:S(2)}) copy-start(bf16[3840,128]{1,0:T(8,128)(2,1)} %copy-done.2) | copy-start | bytes 2949124
  (1 other events, 0.9 us)

commit v4 on v3

v4 whole, which is shorter than its diff:
```python
import functools

import jax
import jax.numpy as jnp
import numpy as np
from jax import lax
from jax.experimental import pallas as pl
from jax.experimental.pallas import tpu as pltpu
from jax.sharding import Mesh
from jax.sharding import PartitionSpec as P

AXES = ("xl", "y", "xh", "z", "core")
ROW = ("xl", "y")
COL = ("xh", "z", "core")
SIZES = (2, 8, 2, 12, 2)
NQ = 24
NOTE = 2 * NQ
BC = 16
PANEL = 48
STEPS = 3
KEPT = 12
BLK = 128


def items(pairs):
    return [(a, d, k) for a, d in pairs for k in range(2)]


def wanted(name):
    a, d, _ = name
    return [(0, 0), (1, 1)] if (d - a) % 8 == 0 else [(0, 2)]


def passed_on(name):
    a, d, _ = name
    return [(1, 2)] if (d - a) % 8 == 0 else [(0, 1), (1, 0)]


VMEM = pltpu.VMEM
SMEM_SPEC = pl.BlockSpec(memory_space=pltpu.SMEM)
VMEM_SPEC = pl.BlockSpec(memory_space=pltpu.VMEM)
ANY_SPEC = pl.BlockSpec(memory_space=pl.ANY)
LIMIT = pltpu.CompilerParams(vmem_limit_bytes=40 << 20)


def moves(blocks):
    return pl.CostEstimate(flops=0, bytes_accessed=2 * blocks * BLK * BLK * 2, transcendentals=0)


def rows_shape(rows):
    return jax.ShapeDtypeStruct((rows, BLK), jnp.bfloat16)


def blk(n):
    return pl.ds(n * BLK, BLK)


def first_kernel(orders, index_ref, own_ref, other_ref, own_note, other_note, *outs):
    empty = jnp.zeros((8, BLK), jnp.float32)
    note = jnp.concatenate(
        [own_note[...].astype(jnp.float32), empty, other_note[...].astype(jnp.float32), empty]
    ).astype(jnp.bfloat16)
    for out, order in zip(outs, orders, strict=True):
        for n, (other, place) in enumerate(order):
            out[blk(n), :] = (other_ref if other else own_ref)[index_ref[place]]
        out[pl.ds(len(order) * BLK, NOTE), :] = note


def first_packed(index, own, other, own_note, other_note, orders):
    return pl.pallas_call(
        functools.partial(first_kernel, orders),
        out_shape=[rows_shape(len(order) * BLK + NOTE) for order in orders],
        in_specs=[SMEM_SPEC] + [VMEM_SPEC] * 4,
        out_specs=[VMEM_SPEC for _ in orders],
        compiler_params=LIMIT,
        cost_estimate=moves(sum(len(order) for order in orders)),
    )(index, own, other, own_note, other_note)


def right_kernel(index_ref, src_ref, code_ref, after_ref, out):
    del after_ref
    for n in range(16):
        for t in range(STEPS):
            out[n, pl.ds(t * BLK, BLK), :] = src_ref[index_ref[n + t]]
        out[n, pl.ds(STEPS * BLK, 16), :] = code_ref[n]


def right_packed(src, index, codes, after):
    return pl.pallas_call(
        right_kernel,
        out_shape=jax.ShapeDtypeStruct((16, STEPS * BLK + 16, BLK), jnp.bfloat16),
        in_specs=[SMEM_SPEC, VMEM_SPEC, VMEM_SPEC, ANY_SPEC],
        out_specs=VMEM_SPEC,
        compiler_params=LIMIT,
        cost_estimate=moves(48),
    )(index, src, codes, after)


def turned(note, distance):
    if distance == 0:
        return note
    return jnp.concatenate([pltpu.roll(note[n : n + NQ], distance, 0) for n in (0, NQ)])


def pack_kernel(spec, notes, count, *refs):
    sources, outs = refs[:count], refs[-len(spec) :]
    if notes:
        merged = None
        for source, row, distance in notes:
            note = sources[source][pl.ds(row, NOTE), :].astype(jnp.float32)
            note = turned(note, distance)
            merged = note if merged is None else jnp.maximum(merged, note)
        merged = merged.astype(jnp.bfloat16)
    for out, (entries, noted) in zip(outs, spec, strict=True):
        for n, (source, place) in enumerate(entries):
            out[blk(n), :] = sources[source][blk(place), :]
        if noted:
            out[pl.ds(len(entries) * BLK, NOTE), :] = merged


def pack(sources, spec, notes, after):
    used = sorted({e[0] for entries, _ in spec for e in entries} | {n[0] for n in notes})
    where = {source: n for n, source in enumerate(used)}
    spec = tuple((tuple((where[s], n) for s, n in entries), noted) for entries, noted in spec)
    notes = tuple((where[n[0]],) + tuple(n[1:]) for n in notes)
    return pl.pallas_call(
        functools.partial(pack_kernel, spec, notes, len(used)),
        out_shape=[rows_shape(len(entries) * BLK + NOTE * noted) for entries, noted in spec],
        in_specs=[VMEM_SPEC] * len(used) + [ANY_SPEC] * len(after),
        out_specs=[VMEM_SPEC for _ in spec],
        compiler_params=LIMIT,
        cost_estimate=moves(sum(len(entries) for entries, _ in spec)),
    )(*[sources[source] for source in used], *after)


def product_kernel(counts, base, first, last, table_ref, right_ref, *rest):
    lefts, rest = rest[: len(counts)], rest[len(counts) :]
    if last:
        before, out_ref, acc = rest
        acc[...] = before[...]
    elif first:
        (acc,) = rest
        acc[...] = jnp.zeros_like(acc)
    else:
        before, acc = rest
        acc[...] = before[...]
    for left, count in zip(lefts, counts, strict=True):

        def body(n, carry, left=left, base=base):
            block = left[pl.ds(pl.multiple_of(table_ref[6, base + n], BLK), BLK), :]
            for rank in range(2):
                owner = table_ref[3 * rank, base + n]
                row = pl.multiple_of(table_ref[3 * rank + 1, base + n], BLK)
                place = table_ref[3 * rank + 2, base + n]
                right = right_ref[owner, pl.ds(row, BLK), :]
                acc[place] += jnp.dot(block, right, preferred_element_type=jnp.float32)
            return carry

        unroll = max(n for n in (7, 6, 5, 4, 3, 2, 1) if count % n == 0)
        lax.fori_loop(0, count, body, 0, unroll=unroll)
        base += count
    if last:
        out_ref[...] = acc[:KEPT].astype(out_ref.dtype)


def product(table, right, lefts, counts, base, before=None, last=False):
    total = sum(counts)
    sums = jax.ShapeDtypeStruct((KEPT + 1, BLK, BLK), jnp.float32)
    return pl.pallas_call(
        functools.partial(product_kernel, counts, base, before is None, last),
        out_shape=jax.ShapeDtypeStruct((KEPT, BLK, BLK), jnp.bfloat16) if last else sums,
        in_specs=[SMEM_SPEC] + [VMEM_SPEC] * (1 + len(lefts) + (before is not None)),
        out_specs=VMEM_SPEC,
        scratch_shapes=[VMEM(sums.shape, jnp.float32)] if last else [],
        compiler_params=LIMIT,
        cost_estimate=pl.CostEstimate(
            flops=total * 16 * BLK**3, bytes_accessed=total * BLK * BLK * 2, transcendentals=0
        ),
    )(table, right, *lefts, *(() if before is None else (before,)))


def tables(order, notes, right_codes, c_code, start, core):
    order = np.array(order, np.int32)
    count = order.shape[0]
    row, other, k, distance, panel = (order[:, n] for n in range(5))
    notes = jnp.stack(notes)[:, :, :32].astype(jnp.int32)
    flat = (notes[:, :, :16] * 64 + notes[:, :, 16:] - 1).reshape(1, 2 * NOTE * 16)
    of = (start + panel + core * (3 - 2 * panel)) % 16
    place = (other * NOTE + k * NQ + distance) * 16 + of
    codes = jnp.sum(jnp.where(place[:, None] == jnp.arange(2 * NOTE * 16)[None, :], flat, 0), axis=1)
    step = panel + core * (2 - 2 * panel)
    right_live = right_codes >= 0
    right_inner = jnp.where(right_live, right_codes // BC, -1)
    owners = jnp.arange(16, dtype=jnp.int32)
    earlier = owners[None, :] < owners[:, None]
    rank = jnp.sum(
        ((right_inner[:, None, :] == right_inner[None, :, :]) & earlier[:, :, None]).astype(jnp.int32),
        axis=1,
    )
    packed = jnp.where(right_live, right_inner * 1024 + rank * 32 + right_codes % BC, -1)
    right_n = jnp.where(
        (step == 0)[:, None],
        packed[None, :, 0],
        jnp.where((step == 1)[:, None], packed[None, :, 1], packed[None, :, 2]),
    )
    match = (right_n >= 0) & (codes >= 0)[:, None] & ((right_n // 1024) == (codes % PANEL)[:, None])
    rows = []
    for rank_number in range(2):
        hit = match & ((right_n // 32) % 32 == rank_number)
        found = jnp.sum(jnp.where(hit, owners[None, :] * 32 + right_n % 32 + 1, 0), axis=1)
        partner = jnp.maximum(found - 1, 0)
        target = (codes // PANEL) * BC + partner % 32
        there = (target[:, None] == c_code[None, :]) & (found > 0)[:, None]
        slot = jnp.sum(jnp.where(there, jnp.arange(KEPT)[None, :] - KEPT, 0), axis=1) + KEPT
        rows += [partner // 32, step * BLK, slot]
    return jnp.stack(rows + [jnp.array(row)]).astype(jnp.int32).reshape(7, count)


def moved(array, distance):
    route = []
    for i in range(NQ):
        route.append((2 * i, 2 * ((i + distance) % NQ)))
        route.append((2 * i + 1, 2 * ((i - distance) % NQ) + 1))
    return lax.ppermute(array, COL, route)


def from_other_core(array):
    return lax.ppermute(array, "core", [(0, 1), (1, 0)])


def local(a_own_values, a_own_code, b_own_values, b_own_code, c_code):
    r = lax.axis_index(ROW)
    q = lax.axis_index(("xh", "z"))
    core = lax.axis_index("core")
    start = (r + 2 * q) % 16
    a_own = a_own_values.reshape(16, BLK, BLK)
    b_own = b_own_values.reshape(16, BLK, BLK)

    sources, at = [], {}

    def keep(array, names):
        for n, name in enumerate(names):
            at[name] = (len(sources), 2 * n)
        sources.append(array)
        return len(sources) - 1

    def send(array, names, distance):
        return keep(moved(array, distance), [(a, (d + distance) % NQ, k) for a, d, k in names])

    def blocks(names):
        return [(at[name][0], at[name][1] + b) for name in names for b in range(2)]

    def packed(spec, notes=(), after=()):
        return pack(sources, spec, notes, after)

    code = a_own_code.reshape(16) + 1
    note = jnp.concatenate([code // 64, code % 64]).astype(jnp.bfloat16).reshape(1, 32)
    note = jnp.pad(note, ((0, 15), (0, BLK - 32)))
    a_other, note_other = from_other_core(a_own), from_other_core(note)
    a_index = jnp.arange(16, dtype=jnp.int32)
    a_index = (start + jnp.where(core == 0, a_index, 3 - a_index)) % 16

    ones, twos = (items((a, 0) for a in classes) for classes in ((1, 2, 5, 6), (3, 0, 7, 4)))
    orders = tuple(
        tuple((k, 2 * a + b) for a, _, k in names for b in range(2)) for names in (ones, twos)
    )
    first, second = first_packed(a_index, a_own, a_other, note, note_other, orders)
    own = keep(first, ones)
    keep(second, twos)
    up2 = send(second, twos, 2)
    up1 = send(first, ones, 1)

    shift = (2 * q + core + jnp.arange(18, dtype=jnp.int32)) % 16
    b_code = b_own_code.reshape(16) + 1
    b_code = jnp.sum(jnp.where(shift[:, None] == jnp.arange(16)[None, :], b_code[None, :], 0), axis=1)
    b_code = jnp.stack([b_code[t : t + 16] for t in range(STEPS)], axis=1)
    b_code = jnp.concatenate([b_code // 16, b_code % 16], axis=1).astype(jnp.bfloat16)
    b_code = jnp.broadcast_to(jnp.pad(b_code, ((0, 0), (0, BLK - 6)))[:, None, :], (16, 16, BLK))
    right = right_packed(b_own, shift, b_code, sources[up2])
    right = lax.all_to_all(right, ROW, 0, 0, tiled=True)

    near = [(own, 16 * BLK, 0), (up1, 16 * BLK, 1), (up2, 16 * BLK, 2)]
    names = items([(2, 1), (6, 1), (3, 2), (7, 2), (0, 2), (4, 2)])
    (up_in,) = packed([(blocks(names), True)], near)
    sources.append(up_in)
    up3 = send(up_in, names, 1)

    names = items([(5, 1), (6, 1), (7, 2)]) + [(4, 0, 0), (5, 0, 0)]
    (cross_in,) = packed([(blocks(names), True)], near, (up_in,))
    crossed = send(cross_in, names, 12)
    far = [(crossed, 16 * BLK, 12)]

    near = [(up3 - 1, 24 * BLK, 0), (up3, 24 * BLK, 1)]
    plans = ((items([(1, 1), (2, 2)]), 15), (items([(5, 1), (6, 2)]), 3))
    inputs = packed([(blocks(names), True) for names, _ in plans], near)
    far.append((len(sources), 8 * BLK, 0))
    sources.append(inputs[0])
    for array, (names, distance) in zip(inputs, plans, strict=True):
        far.append((send(array, names, distance), 8 * BLK, distance))

    names = items([(6, 2), (7, 3), (0, 3)])
    (cross_in,) = packed([(blocks(names), False)], (), (inputs[0],))
    send(cross_in, names, 12)

    early = items([(1, 1), (5, 13), (2, 2), (6, 14), (3, 3), (7, 15)]) + [(4, 12, 0)]
    early += items([(2, 1), (6, 13), (3, 2), (7, 14), (0, 15), (4, 3)]) + [(5, 12, 0)]

    def pass_on(names, after=()):
        entries = [(at[name][0], at[name][1] + b) for name in names for b, _ in passed_on(name)]
        (array,) = packed([(entries, False)], (), after)
        return from_other_core(array)

    early_other = pass_on(early)

    names = items([(1, 16), (5, 4), (2, 17), (6, 5), (0, 15), (4, 3)])
    up_in, notes = packed([(blocks(names), False), ((), True)], far)
    send(up_in, names, 1)
    notes = (notes, from_other_core(notes))

    late = items([(1, 16), (5, 4), (2, 17), (6, 5)])
    late += items([(1, 17), (5, 5), (2, 18), (6, 6), (0, 16), (4, 4)])


    def part_of(names):
        by_source = {}
        for name in names:
            source, place = at[name]
            for b, panel in wanted(name):
                by_source.setdefault(source, []).append(((place + b) * BLK, 0, name[2], name[1], panel))
        found = sorted(by_source.items())
        return [(sources[source], rows) for source, rows in found]

    def received_of(array, names):
        rows = []
        for name in names:
            for _, panel in passed_on(name):
                rows.append((len(rows) * BLK, 1, name[2], name[1], panel))
        return [(array, rows)]

    parts = [
        part_of(items([(0, 0), (1, 0)]) + early) + received_of(early_other, early),
        part_of(late),
        received_of(None, late),
    ]
    order = [row for part in parts for _, rows in part for row in rows]
    right_codes = right[:, STEPS * BLK, :6].astype(jnp.int32)
    right_codes = right_codes[:, :3] * 16 + right_codes[:, 3:] - 1
    table = tables(order, notes, right_codes, c_code.reshape(KEPT), start, core)

    def product_of(part, base, before=None, last=False):
        lefts, counts = [array for array, _ in part], tuple(len(rows) for _, rows in part)
        return product(table, right, lefts, counts, base, before, last), base + sum(counts)

    sums, base = product_of(parts[0], 0)
    late_other = pass_on(late, (sums,))
    sums, base = product_of(parts[1], base, sums)
    parts[2] = received_of(late_other, late)
    out, base = product_of(parts[2], base, sums, last=True)
    return out[None, None]


def solution(mesh):
    fine = Mesh(mesh.devices.reshape(SIZES), AXES)
    return jax.shard_map(
        local,
        mesh=fine,
        in_specs=(
            P(ROW, COL, None, None, None, None),
            P(ROW, COL, None, None),
            P(ROW, COL, None, None, None, None),
            P(ROW, COL, None, None),
            P(ROW, COL, None),
        ),
        out_specs=P(ROW, COL, None, None, None),
        check_vma=False,
    )
```

time: 147 us -> 152 us (1.034)
  the two profiles are of different devices: /device:TPU:43 before, /device:TPU:1 now
where the time goes in v4:
time: 152 us; the launch traced here: 149 us
  starting transfers between devices  61.1 us (40%)
  waiting for transfers between devices  53 us (35%)
  Pallas kernels  17.3 us (11%)
  local copies, waits for them, and re-layouts  11.3 us (7%)
  other arithmetic  6.12 us (4%)
    ppermute x8, waiting for transfers between devices, moved(): return lax.ppermute(array, COL, route)  52.5 us
    ppermute x8, starting transfers between devices, moved(): return lax.ppermute(array, COL, route)  32.9 us
    ppermute x5, starting transfers between devices, from_other_core(): return lax.ppermute(array, 'core', [(0, 1), (1, 0)])  21.2 us
    pallas_call x3, Pallas kernels, product(): pl.pallas_call(functools.partial(product_kernel, counts, base, before is...  12.5 us
    unnamed x47, local copies, waits for them, and re-layouts  10.2 us
    all_to_all x1, starting transfers between devices, local(): right = lax.all_to_all(right, ROW, 0, 0, tiled=True)  6.95 us
    pallas_call x7, Pallas kernels, pack(): pl.pallas_call(functools.partial(pack_kernel, spec, notes, len(used)), ou...  3.53 us
  transfers between devices with their start and end apart: 14, of which 6 were waited for; matrix products, arithmetic and copies ran while one was open for 5% of the time, Pallas kernels for 8%

profile of v4, /device:TPU:1, one launch (start us, length us, event | category | flops | bytes accessed | tf_op | source)
XLA Modules:
  0.0 149.2 jit_solution(5291457621224390764)
XLA Ops:
  0.0 12.4 %collective-permute-start = (bf16[16,128,128]{2,1,0:T(8,128)(2,1)}, bf16[16,128,128]{2,1,0:T(8,128)(2,1)S(1)}, u32[]{:S(2)}, u32[]{:S(2)}) collective-permute-start(bf16[16,128,128]{2,1,0:T(8,128)(2,1)} %bitcast.44), channel_id=1, source_target_pairs={{0,1},{1,0},{2,3},{3,2},{4,5},{5,4},{6,7},{7,6},{8,9},{9,8},{10,11... | collective-permute-start | bytes 1572872 | tf_op jit(solution)/shard_map/ppermute | solution.py:228
  13.2 1.9 %collective-permute-start.1 = (bf16[16,128]{1,0:T(8,128)(2,1)S(1)}, bf16[16,128]{1,0:T(8,128)(2,1)S(1)}, u32[]{:S(2)}, u32[]{:S(2)}) collective-permute-start(bf16[16,128]{1,0:T(8,128)(2,1)S(1)} %fusion.18.own_note), channel_id=1, source_target_pairs={{0,1},{1,0},{2,3},{3,2},{4,5},{5,4},{6,7},{7,6},{8,9},{9,8},{10,11... | collective-permute-start | bytes 12296 | tf_op jit(solution)/shard_map/ppermute | solution.py:228
  17.9 7.7 %collective-permute-start.2 = (bf16[2096,128]{1,0:T(8,128)(2,1)S(1)}, bf16[2096,128]{1,0:T(8,128)(2,1)S(1)}, u32[]{:S(2)}, u32[]{:S(2)}) collective-permute-start(bf16[2096,128]{1,0:T(8,128)(2,1)S(1)} %get-tuple-element.11.refs_1_.rest_1_), channel_id=1, source_target_pairs={{0,4},{1,45},{2,6},{3,47},{4,8},{5,1},{6,10},{7,3},{8,12},{9,5},{1... | collective-permute-start | bytes 1609736 | tf_op jit(solution)/shard_map/ppermute | solution.py:224
  26.8 10.9 %collective-permute-done.2.after_ref.refs_1_.refs_2_.refs_0_.rest_2_ = bf16[2096,128]{1,0:T(8,128)(2,1)S(1)} collective-permute-done((bf16[2096,128]{1,0:T(8,128)(2,1)S(1)}, bf16[2096,128]{1,0:T(8,128)(2,1)S(1)}, u32[]{:S(2)}, u32[]{:S(2)}) %collective-permute-start.2) | collective-permute-done | bytes 536608 | tf_op jit(solution)/shard_map/ppermute | solution.py:224
  39.4 1.2 copy-done
  40.5 7.0 %all-to-all-start = ((bf16[16,400,128]{2,1,0:T(8,128)(2,1)}), bf16[16,400,128]{2,1,0:T(8,128)(2,1)S(1)}, u32[]{:S(2)}, u32[]{:S(2)}) async-start(bf16[16,400,128]{2,1,0:T(8,128)(2,1)} %copy-done), calls=%async_computation | async-start | bytes 3276800 | tf_op jit(solution)/shard_map/all_to_all | solution.py:280
  47.5 3.6 %collective-permute-start.3 = (bf16[2096,128]{1,0:T(8,128)(2,1)S(1)}, bf16[2096,128]{1,0:T(8,128)(2,1)S(1)}, u32[]{:S(2)}, u32[]{:S(2)}) collective-permute-start(bf16[2096,128]{1,0:T(8,128)(2,1)S(1)} %get-tuple-element.12.refs_0_.rest_0_), channel_id=1, source_target_pairs={{0,2},{1,47},{2,4},{3,1},{4,6},{5,3},{6,8},{7,5},{8,10},{9,7},{10,... | collective-permute-start | bytes 1609736 | tf_op jit(solution)/shard_map/ppermute | solution.py:224
  51.1 8.2 %collective-permute-done.3.refs_2_.refs_3_.refs_0_.refs_1_.rest_3_ = bf16[2096,128]{1,0:T(8,128)(2,1)S(1)} collective-permute-done((bf16[2096,128]{1,0:T(8,128)(2,1)S(1)}, bf16[2096,128]{1,0:T(8,128)(2,1)S(1)}, u32[]{:S(2)}, u32[]{:S(2)}) %collective-permute-start.3) | collective-permute-done | bytes 536608 | tf_op jit(solution)/shard_map/ppermute | solution.py:224
  59.4 8.2 %collective-permute-start.4 = (bf16[3120,128]{1,0:T(8,128)(2,1)S(1)}, bf16[3120,128]{1,0:T(8,128)(2,1)S(1)}, u32[]{:S(2)}, u32[]{:S(2)}) collective-permute-start(bf16[3120,128]{1,0:T(8,128)(2,1)S(1)} %shard_map.102.refs_4_.refs_1_), channel_id=1, source_target_pairs={{0,2},{1,47},{2,4},{3,1},{4,6},{5,3},{6,8},{7,5},{8,10},{9,7},{10,... | collective-permute-start | bytes 2396168 | tf_op jit(solution)/shard_map/ppermute | solution.py:224
  68.7 3.9 %collective-permute-start.5 = (bf16[2096,128]{1,0:T(8,128)(2,1)S(1)}, bf16[2096,128]{1,0:T(8,128)(2,1)S(1)}, u32[]{:S(2)}, u32[]{:S(2)}) collective-permute-start(bf16[2096,128]{1,0:T(8,128)(2,1)S(1)} %shard_map.103), channel_id=1, source_target_pairs={{0,24},{1,25},{2,26},{3,27},{4,28},{5,29},{6,30},{7,31},{8,32},{9,... | collective-permute-start | bytes 1609736 | tf_op jit(solution)/shard_map/ppermute | solution.py:224
  72.7 8.6 %collective-permute-done.4.refs_2_.refs_0_.rest_4_ = bf16[3120,128]{1,0:T(8,128)(2,1)S(1)} collective-permute-done((bf16[3120,128]{1,0:T(8,128)(2,1)S(1)}, bf16[3120,128]{1,0:T(8,128)(2,1)S(1)}, u32[]{:S(2)}, u32[]{:S(2)}) %collective-permute-start.4) | collective-permute-done | bytes 798752 | tf_op jit(solution)/shard_map/ppermute | solution.py:224
  81.4 3.6 %collective-permute-start.8 = (bf16[1536,128]{1,0:T(8,128)(2,1)S(1)}, bf16[1536,128]{1,0:T(8,128)(2,1)S(1)}, u32[]{:S(2)}, u32[]{:S(2)}) collective-permute-start(bf16[1536,128]{1,0:T(8,128)(2,1)S(1)} %shard_map.105), channel_id=1, source_target_pairs={{0,24},{1,25},{2,26},{3,27},{4,28},{5,29},{6,30},{7,31},{8,32},{9,... | collective-permute-start | bytes 1179656 | tf_op jit(solution)/shard_map/ppermute | solution.py:224
  84.9 1.9 %collective-permute-start.6 = (bf16[1072,128]{1,0:T(8,128)(2,1)S(1)}, bf16[1072,128]{1,0:T(8,128)(2,1)S(1)}, u32[]{:S(2)}, u32[]{:S(2)}) collective-permute-start(bf16[1072,128]{1,0:T(8,128)(2,1)S(1)} %get-tuple-element.13.refs_1_.refs_2_), channel_id=1, source_target_pairs={{0,30},{1,19},{2,32},{3,21},{4,34},{5,23},{6,36},{7,25},{8,38},{9,... | collective-permute-start | bytes 823304 | tf_op jit(solution)/shard_map/ppermute | solution.py:224
  86.9 1.9 %collective-permute-start.7 = (bf16[1072,128]{1,0:T(8,128)(2,1)S(1)}, bf16[1072,128]{1,0:T(8,128)(2,1)S(1)}, u32[]{:S(2)}, u32[]{:S(2)}) collective-permute-start(bf16[1072,128]{1,0:T(8,128)(2,1)S(1)} %get-tuple-element.14), channel_id=1, source_target_pairs={{0,6},{1,43},{2,8},{3,45},{4,10},{5,47},{6,12},{7,1},{8,14},{9,3},... | collective-permute-start | bytes 823304 | tf_op jit(solution)/shard_map/ppermute | solution.py:224
  89.4 13.6 %collective-permute-done.5.refs_1_.refs_3_.rest_5_ = bf16[2096,128]{1,0:T(8,128)(2,1)S(1)} collective-permute-done((bf16[2096,128]{1,0:T(8,128)(2,1)S(1)}, bf16[2096,128]{1,0:T(8,128)(2,1)S(1)}, u32[]{:S(2)}, u32[]{:S(2)}) %collective-permute-start.5) | collective-permute-done | bytes 536608 | tf_op jit(solution)/shard_map/ppermute | solution.py:224
  103.0 11.4 %collective-permute-done.8.refs_5_.refs_4_.rest_6_ = bf16[1536,128]{1,0:T(8,128)(2,1)S(1)} collective-permute-done((bf16[1536,128]{1,0:T(8,128)(2,1)S(1)}, bf16[1536,128]{1,0:T(8,128)(2,1)S(1)}, u32[]{:S(2)}, u32[]{:S(2)}) %collective-permute-start.8) | collective-permute-done | bytes 393248 | tf_op jit(solution)/shard_map/ppermute | solution.py:224
  116.1 2.5 %collective-permute-start.9 = (bf16[48,128]{1,0:T(8,128)(2,1)S(1)}, bf16[48,128]{1,0:T(8,128)(2,1)S(1)}, u32[]{:S(2)}, u32[]{:S(2)}) collective-permute-start(bf16[48,128]{1,0:T(8,128)(2,1)S(1)} %get-tuple-element.15), channel_id=1, source_target_pairs={{0,1},{1,0},{2,3},{3,2},{4,5},{5,4},{6,7},{7,6},{8,9},{9,8},{10,11... | collective-permute-start | bytes 36872 | tf_op jit(solution)/shard_map/ppermute | solution.py:228
  119.2 2.0 %collective-permute-start.10 = (bf16[3072,128]{1,0:T(8,128)(2,1)}, bf16[3072,128]{1,0:T(8,128)(2,1)}, u32[]{:S(2)}, u32[]{:S(2)}) collective-permute-start(bf16[3072,128]{1,0:T(8,128)(2,1)} %get-tuple-element.16), channel_id=1, source_target_pairs={{0,2},{1,47},{2,4},{3,1},{4,6},{5,3},{6,8},{7,5},{8,10},{9,7},{10,... | collective-permute-start | bytes 2359304 | tf_op jit(solution)/shard_map/ppermute | solution.py:224
  122.4 1.9 %collective-permute-start.11 = (bf16[4992,128]{1,0:T(8,128)(2,1)}, bf16[4992,128]{1,0:T(8,128)(2,1)}, u32[]{:S(2)}, u32[]{:S(2)}) collective-permute-start(bf16[4992,128]{1,0:T(8,128)(2,1)} %shard_map.107), channel_id=1, source_target_pairs={{0,1},{1,0},{2,3},{3,2},{4,5},{5,4},{6,7},{7,6},{8,9},{9,8},{10,11... | collective-permute-start | bytes 3833864 | tf_op jit(solution)/shard_map/ppermute | solution.py:228
  133.0 7.2 %shard_map.108.refs_3_.rest_3_ = f32[13,128,128]{2,1,0:T(8,128)S(1)} custom-call(s32[7,144]{1,0:T(8,128)S(1)} %stack.44.table_ref, bf16[16,400,128]{2,1,0:T(8,128)(2,1)S(1)} %all-to-all-done.right_ref, bf16[2096,128]{1,0:T(8,128)(2,1)S(1)} %copy-done.9, bf16[2096,128]{1,0:T(8,128)(2,1)S(1)} %copy-done.14, ...), custom_call_target="tpu_custom_call" | custom-call | flops 2818572288 | bytes 2752512 | tf_op jit(solution)/shard_map/pallas_call | solution.py:169
  140.3 1.2 shard_map.109
  141.5 2.4 %collective-permute-start.12 = (bf16[3584,128]{1,0:T(8,128)(2,1)S(1)}, bf16[3584,128]{1,0:T(8,128)(2,1)S(1)}, u32[]{:S(2)}, u32[]{:S(2)}) collective-permute-start(bf16[3584,128]{1,0:T(8,128)(2,1)S(1)} %shard_map.109), channel_id=1, source_target_pairs={{0,1},{1,0},{2,3},{3,2},{4,5},{5,4},{6,7},{7,6},{8,9},{9,8},{10,11... | collective-permute-start | bytes 2752520 | tf_op jit(solution)/shard_map/ppermute | solution.py:228
  143.9 2.5 %shard_map.110.rest_1_ = f32[13,128,128]{2,1,0:T(8,128)S(1)} custom-call(s32[7,144]{1,0:T(8,128)S(1)} %stack.44.table_ref, bf16[16,400,128]{2,1,0:T(8,128)(2,1)S(1)} %all-to-all-done.right_ref, bf16[1072,128]{1,0:T(8,128)(2,1)S(1)} %copy-done.2, bf16[1072,128]{1,0:T(8,128)(2,1)S(1)} %copy-done.4, bf16[3072,128]{1,0:T(8,128)(2,1)} %collective-permute-done.10.refs_2_.rest_2_, ...), custom_call_target="tpu_custom_call" | custom-call | flops 1073741824 | bytes 1048576 | tf_op jit(solution)/shard_map/pallas_call | solution.py:169
  146.5 2.7 %shard_map.111 = bf16[12,128,128]{2,1,0:T(8,128)(2,1)} custom-call(s32[7,144]{1,0:T(8,128)S(1)} %stack.44.table_ref, bf16[16,400,128]{2,1,0:T(8,128)(2,1)S(1)} %all-to-all-done.right_ref, bf16[3584,128]{1,0:T(8,128)(2,1)S(1)} %collective-permute-done.12.rest_0_, f32[13,128,128]{2,1,0:T(8,128)S(1)} %shard_map.110.rest_1_), custom_call_target="tpu_custom_call" | custom-call | flops 939524096 | bytes 917504 | tf_op jit(solution)/shard_map/pallas_call | solution.py:169
  (102 shorter events, 20.2 us)
Async XLA Ops:
  0.0 16.2 %collective-permute-start = (bf16[16,128,128]{2,1,0:T(8,128)(2,1)}, bf16[16,128,128]{2,1,0:T(8,128)(2,1)S(1)}, u32[]{:S(2)}, u32[]{:S(2)}) collective-permute-start(bf16[16,128,128]{2,1,0:T(8,128)(2,1)} %bitcast.44), channel_id=1, source_target_pairs={{0,1},{1,0},{2,3},{3,2},{4,5},{5,4},{6,7},{7,6},{8,9},{9,8},{10,11... | collective-permute-start | bytes 1572872 | tf_op jit(solution)/shard_map/ppermute | solution.py:228
  13.2 3.0 %collective-permute-start.1 = (bf16[16,128]{1,0:T(8,128)(2,1)S(1)}, bf16[16,128]{1,0:T(8,128)(2,1)S(1)}, u32[]{:S(2)}, u32[]{:S(2)}) collective-permute-start(bf16[16,128]{1,0:T(8,128)(2,1)S(1)} %fusion.18.own_note), channel_id=1, source_target_pairs={{0,1},{1,0},{2,3},{3,2},{4,5},{5,4},{6,7},{7,6},{8,9},{9,8},{10,11... | collective-permute-start | bytes 12296 | tf_op jit(solution)/shard_map/ppermute | solution.py:228
  17.9 41.4 %copy-start.7 = (bf16[2096,128]{1,0:T(8,128)(2,1)}, bf16[2096,128]{1,0:T(8,128)(2,1)S(1)}, u32[]{:S(2)}) copy-start(bf16[2096,128]{1,0:T(8,128)(2,1)S(1)} %get-tuple-element.12.refs_0_.rest_0_) | copy-start | bytes 1609732
  17.9 19.7 %collective-permute-start.2 = (bf16[2096,128]{1,0:T(8,128)(2,1)S(1)}, bf16[2096,128]{1,0:T(8,128)(2,1)S(1)}, u32[]{:S(2)}, u32[]{:S(2)}) collective-permute-start(bf16[2096,128]{1,0:T(8,128)(2,1)S(1)} %get-tuple-element.11.refs_1_.rest_1_), channel_id=1, source_target_pairs={{0,4},{1,45},{2,6},{3,47},{4,8},{5,1},{6,10},{7,3},{8,12},{9,5},{1... | collective-permute-start | bytes 1609736 | tf_op jit(solution)/shard_map/ppermute | solution.py:224
  40.5 86.2 %all-to-all-start = ((bf16[16,400,128]{2,1,0:T(8,128)(2,1)}), bf16[16,400,128]{2,1,0:T(8,128)(2,1)S(1)}, u32[]{:S(2)}, u32[]{:S(2)}) async-start(bf16[16,400,128]{2,1,0:T(8,128)(2,1)} %copy-done), calls=%async_computation | async-start | bytes 3276800 | tf_op jit(solution)/shard_map/all_to_all | solution.py:280
  47.5 20.1 %copy-start.13 = (bf16[2096,128]{1,0:T(8,128)(2,1)S(1)}, bf16[2096,128]{1,0:T(8,128)(2,1)}, u32[]{:S(2)}) copy-start(bf16[2096,128]{1,0:T(8,128)(2,1)} %copy-done.12) | copy-start | bytes 1609732
  47.5 11.8 %collective-permute-start.3 = (bf16[2096,128]{1,0:T(8,128)(2,1)S(1)}, bf16[2096,128]{1,0:T(8,128)(2,1)S(1)}, u32[]{:S(2)}, u32[]{:S(2)}) collective-permute-start(bf16[2096,128]{1,0:T(8,128)(2,1)S(1)} %get-tuple-element.12.refs_0_.rest_0_), channel_id=1, source_target_pairs={{0,2},{1,47},{2,4},{3,1},{4,6},{5,3},{6,8},{7,5},{8,10},{9,7},{10,... | collective-permute-start | bytes 1609736 | tf_op jit(solution)/shard_map/ppermute | solution.py:224
  59.4 21.9 %collective-permute-start.4 = (bf16[3120,128]{1,0:T(8,128)(2,1)S(1)}, bf16[3120,128]{1,0:T(8,128)(2,1)S(1)}, u32[]{:S(2)}, u32[]{:S(2)}) collective-permute-start(bf16[3120,128]{1,0:T(8,128)(2,1)S(1)} %shard_map.102.refs_4_.refs_1_), channel_id=1, source_target_pairs={{0,2},{1,47},{2,4},{3,1},{4,6},{5,3},{6,8},{7,5},{8,10},{9,7},{10,... | collective-permute-start | bytes 2396168 | tf_op jit(solution)/shard_map/ppermute | solution.py:224
  68.7 34.2 %collective-permute-start.5 = (bf16[2096,128]{1,0:T(8,128)(2,1)S(1)}, bf16[2096,128]{1,0:T(8,128)(2,1)S(1)}, u32[]{:S(2)}, u32[]{:S(2)}) collective-permute-start(bf16[2096,128]{1,0:T(8,128)(2,1)S(1)} %shard_map.103), channel_id=1, source_target_pairs={{0,24},{1,25},{2,26},{3,27},{4,28},{5,29},{6,30},{7,31},{8,32},{9,... | collective-permute-start | bytes 1609736 | tf_op jit(solution)/shard_map/ppermute | solution.py:224
  72.7 16.7 %copy-start.19 = (s32[144]{0:T(256)S(1)}, s32[144]{0:T(256)}, u32[]{:S(2)}) copy-start(s32[144]{0:T(256)} %constant.256.clone) | copy-start | bytes 1732
  72.7 16.7 %copy-start.20 = (s32[144]{0:T(256)S(1)}, s32[144]{0:T(256)}, u32[]{:S(2)}) copy-start(s32[144]{0:T(256)} %constant.255.clone) | copy-start | bytes 1732
  81.4 33.0 %collective-permute-start.8 = (bf16[1536,128]{1,0:T(8,128)(2,1)S(1)}, bf16[1536,128]{1,0:T(8,128)(2,1)S(1)}, u32[]{:S(2)}, u32[]{:S(2)}) collective-permute-start(bf16[1536,128]{1,0:T(8,128)(2,1)S(1)} %shard_map.105), channel_id=1, source_target_pairs={{0,24},{1,25},{2,26},{3,27},{4,28},{5,29},{6,30},{7,31},{8,32},{9,... | collective-permute-start | bytes 1179656 | tf_op jit(solution)/shard_map/ppermute | solution.py:224
  84.9 18.0 %collective-permute-start.6 = (bf16[1072,128]{1,0:T(8,128)(2,1)S(1)}, bf16[1072,128]{1,0:T(8,128)(2,1)S(1)}, u32[]{:S(2)}, u32[]{:S(2)}) collective-permute-start(bf16[1072,128]{1,0:T(8,128)(2,1)S(1)} %get-tuple-element.13.refs_1_.refs_2_), channel_id=1, source_target_pairs={{0,30},{1,19},{2,32},{3,21},{4,34},{5,23},{6,36},{7,25},{8,38},{9,... | collective-permute-start | bytes 823304 | tf_op jit(solution)/shard_map/ppermute | solution.py:224
  86.9 16.1 %collective-permute-start.7 = (bf16[1072,128]{1,0:T(8,128)(2,1)S(1)}, bf16[1072,128]{1,0:T(8,128)(2,1)S(1)}, u32[]{:S(2)}, u32[]{:S(2)}) collective-permute-start(bf16[1072,128]{1,0:T(8,128)(2,1)S(1)} %get-tuple-element.14), channel_id=1, source_target_pairs={{0,6},{1,43},{2,8},{3,45},{4,10},{5,47},{6,12},{7,1},{8,14},{9,3},... | collective-permute-start | bytes 823304 | tf_op jit(solution)/shard_map/ppermute | solution.py:224
  103.0 19.4 %copy-start.5 = (bf16[2096,128]{1,0:T(8,128)(2,1)}, bf16[2096,128]{1,0:T(8,128)(2,1)S(1)}, u32[]{:S(2)}) copy-start(bf16[2096,128]{1,0:T(8,128)(2,1)S(1)} %collective-permute-done.5.refs_1_.refs_3_.rest_5_) | copy-start | bytes 1609732
  103.0 19.4 %copy-start.1 = (bf16[1072,128]{1,0:T(8,128)(2,1)}, bf16[1072,128]{1,0:T(8,128)(2,1)S(1)}, u32[]{:S(2)}) copy-start(bf16[1072,128]{1,0:T(8,128)(2,1)S(1)} %collective-permute-done.6.refs_3_.refs_0_.rest_0_) | copy-start | bytes 823300
  116.1 8.2 %collective-permute-start.9 = (bf16[48,128]{1,0:T(8,128)(2,1)S(1)}, bf16[48,128]{1,0:T(8,128)(2,1)S(1)}, u32[]{:S(2)}, u32[]{:S(2)}) collective-permute-start(bf16[48,128]{1,0:T(8,128)(2,1)S(1)} %get-tuple-element.15), channel_id=1, source_target_pairs={{0,1},{1,0},{2,3},{3,2},{4,5},{5,4},{6,7},{7,6},{8,9},{9,8},{10,11... | collective-permute-start | bytes 36872 | tf_op jit(solution)/shard_map/ppermute | solution.py:228
  119.2 8.8 %copy-start.22 = (s32[1,1,12]{2,1,0:T(1,128)S(1)}, s32[1,1,12]{2,1,0:T(1,128)}, u32[]{:S(2)}) copy-start(s32[1,1,12]{2,1,0:T(1,128)} %param.14) | copy-start | bytes 148
  119.2 9.6 %copy-start.21 = (s32[1,144]{1,0:T(1,128)S(1)}, s32[1,144]{1,0:T(1,128)}, u32[]{:S(2)}) copy-start(s32[1,144]{1,0:T(1,128)} %constant.268) | copy-start | bytes 1732
  119.2 21.1 %collective-permute-start.10 = (bf16[3072,128]{1,0:T(8,128)(2,1)}, bf16[3072,128]{1,0:T(8,128)(2,1)}, u32[]{:S(2)}, u32[]{:S(2)}) collective-permute-start(bf16[3072,128]{1,0:T(8,128)(2,1)} %get-tuple-element.16), channel_id=1, source_target_pairs={{0,2},{1,47},{2,4},{3,1},{4,6},{5,3},{6,8},{7,5},{8,10},{9,7},{10,... | collective-permute-start | bytes 2359304 | tf_op jit(solution)/shard_map/ppermute | solution.py:224
  122.4 6.5 %collective-permute-start.11 = (bf16[4992,128]{1,0:T(8,128)(2,1)}, bf16[4992,128]{1,0:T(8,128)(2,1)}, u32[]{:S(2)}, u32[]{:S(2)}) collective-permute-start(bf16[4992,128]{1,0:T(8,128)(2,1)} %shard_map.107), channel_id=1, source_target_pairs={{0,1},{1,0},{2,3},{3,2},{4,5},{5,4},{6,7},{7,6},{8,9},{9,8},{10,11... | collective-permute-start | bytes 3833864 | tf_op jit(solution)/shard_map/ppermute | solution.py:228
  128.8 11.5 %copy-start.2 = (bf16[1072,128]{1,0:T(8,128)(2,1)S(1)}, bf16[1072,128]{1,0:T(8,128)(2,1)}, u32[]{:S(2)}) copy-start(bf16[1072,128]{1,0:T(8,128)(2,1)} %copy-done.1) | copy-start | bytes 823300
  128.8 11.5 %copy-start.4 = (bf16[1072,128]{1,0:T(8,128)(2,1)S(1)}, bf16[1072,128]{1,0:T(8,128)(2,1)}, u32[]{:S(2)}) copy-start(bf16[1072,128]{1,0:T(8,128)(2,1)} %copy-done.3) | copy-start | bytes 823300
  141.5 5.0 %collective-permute-start.12 = (bf16[3584,128]{1,0:T(8,128)(2,1)S(1)}, bf16[3584,128]{1,0:T(8,128)(2,1)S(1)}, u32[]{:S(2)}, u32[]{:S(2)}) collective-permute-start(bf16[3584,128]{1,0:T(8,128)(2,1)S(1)} %shard_map.109), channel_id=1, source_target_pairs={{0,1},{1,0},{2,3},{3,2},{4,5},{5,4},{6,7},{7,6},{8,9},{9,8},{10,11... | collective-permute-start | bytes 2752520 | tf_op jit(solution)/shard_map/ppermute | solution.py:228
  (13 other events, 26.1 us)

commit v5 on v4

--- a/solution.py
+++ b/solution.py
@@ -40,7 +40,7 @@
 SMEM_SPEC = pl.BlockSpec(memory_space=pltpu.SMEM)
 VMEM_SPEC = pl.BlockSpec(memory_space=pltpu.VMEM)
 ANY_SPEC = pl.BlockSpec(memory_space=pl.ANY)
-LIMIT = pltpu.CompilerParams(vmem_limit_bytes=40 << 20)
+LIMIT = pltpu.CompilerParams(vmem_limit_bytes=16 << 20)
 
 
 def moves(blocks):
@@ -55,45 +55,40 @@
     return pl.ds(n * BLK, BLK)
 
 
-def first_kernel(orders, index_ref, own_ref, other_ref, own_note, other_note, *outs):
-    empty = jnp.zeros((8, BLK), jnp.float32)
-    note = jnp.concatenate(
-        [own_note[...].astype(jnp.float32), empty, other_note[...].astype(jnp.float32), empty]
-    ).astype(jnp.bfloat16)
+def first_kernel(orders, index_ref, own_ref, other_ref, note_ref, *outs):
     for out, order in zip(outs, orders, strict=True):
         for n, (other, place) in enumerate(order):
             out[blk(n), :] = (other_ref if other else own_ref)[index_ref[place]]
-        out[pl.ds(len(order) * BLK, NOTE), :] = note
-
-
-def first_packed(index, own, other, own_note, other_note, orders):
+        out[pl.ds(len(order) * BLK, 16), :] = note_ref[...]
+
+
+def first_packed(index, own, other, note, orders):
     return pl.pallas_call(
         functools.partial(first_kernel, orders),
-        out_shape=[rows_shape(len(order) * BLK + NOTE) for order in orders],
-        in_specs=[SMEM_SPEC] + [VMEM_SPEC] * 4,
+        out_shape=[rows_shape(len(order) * BLK + 16) for order in orders],
+        in_specs=[SMEM_SPEC] + [VMEM_SPEC] * 3,
         out_specs=[VMEM_SPEC for _ in orders],
         compiler_params=LIMIT,
         cost_estimate=moves(sum(len(order) for order in orders)),
-    )(index, own, other, own_note, other_note)
-
-
-def right_kernel(index_ref, src_ref, code_ref, after_ref, out):
-    del after_ref
+    )(index, own, other, note)
+
+
+def right_kernel(index_ref, src_ref, code_ref, out):
     for n in range(16):
         for t in range(STEPS):
             out[n, pl.ds(t * BLK, BLK), :] = src_ref[index_ref[n + t]]
         out[n, pl.ds(STEPS * BLK, 16), :] = code_ref[n]
 
 
-def right_packed(src, index, codes, after):
+def right_packed(src, index, codes):
     return pl.pallas_call(
         right_kernel,
         out_shape=jax.ShapeDtypeStruct((16, STEPS * BLK + 16, BLK), jnp.bfloat16),
-        in_specs=[SMEM_SPEC, VMEM_SPEC, VMEM_SPEC, ANY_SPEC],
+        in_specs=[SMEM_SPEC, VMEM_SPEC, VMEM_SPEC],
         out_specs=VMEM_SPEC,
         compiler_params=LIMIT,
         cost_estimate=moves(48),
-    )(index, src, codes, after)
+    )(index, src, codes)
 
 
 def turned(note, distance):
@@ -106,9 +101,14 @@
     sources, outs = refs[:count], refs[-len(spec) :]
     if notes:
         merged = None
-        for source, row, distance in notes:
-            note = sources[source][pl.ds(row, NOTE), :].astype(jnp.float32)
-            note = turned(note, distance)
+        rows = lax.broadcasted_iota(jnp.int32, (NOTE, BLK), 0)
+        for source, row, distance, small in notes:
+            if small:
+                note = sources[source][pl.ds(row, 16), :].astype(jnp.float32)
+                other = jnp.where(rows == NQ + distance, note[1:2], 0.0)
+                note = jnp.where(rows == distance, note[0:1], other)
+            else:
+                note = turned(sources[source][pl.ds(row, NOTE), :].astype(jnp.float32), distance)
             merged = note if merged is None else jnp.maximum(merged, note)
         merged = merged.astype(jnp.bfloat16)
     for out, (entries, noted) in zip(outs, spec, strict=True):
@@ -148,12 +148,14 @@
 
         def body(n, carry, left=left, base=base):
             block = left[pl.ds(pl.multiple_of(table_ref[6, base + n], BLK), BLK), :]
+            pair = []
             for rank in range(2):
                 owner = table_ref[3 * rank, base + n]
                 row = pl.multiple_of(table_ref[3 * rank + 1, base + n], BLK)
-                place = table_ref[3 * rank + 2, base + n]
-                right = right_ref[owner, pl.ds(row, BLK), :]
-                acc[place] += jnp.dot(block, right, preferred_element_type=jnp.float32)
+                pair.append(right_ref[owner, pl.ds(row, BLK), :])
+            both = jnp.dot(block, jnp.concatenate(pair, axis=1), preferred_element_type=jnp.float32)
+            acc[table_ref[2, base + n]] += both[:, :BLK]
+            acc[table_ref[5, base + n]] += both[:, BLK:]
             return carry
 
         unroll = max(n for n in (7, 6, 5, 4, 3, 2, 1) if count % n == 0)
@@ -257,18 +259,28 @@
     note = jnp.concatenate([code // 64, code % 64]).astype(jnp.bfloat16).reshape(1, 32)
     note = jnp.pad(note, ((0, 15), (0, BLK - 32)))
     a_other, note_other = from_other_core(a_own), from_other_core(note)
+    note = jnp.concatenate([note[:1], note_other[:1], note[2:]])
     a_index = jnp.arange(16, dtype=jnp.int32)
     a_index = (start + jnp.where(core == 0, a_index, 3 - a_index)) % 16
 
-    ones, twos = (items((a, 0) for a in classes) for classes in ((1, 2, 5, 6), (3, 0, 7, 4)))
+    starts = [
+        (items([(3, 0), (4, 0)]), 2),
+        (items([(7, 0), (0, 0)]), 14),
+        (items([(1, 0), (2, 0)]), 1),
+        (items([(5, 0), (6, 0)]), 13),
+        ([(4, 0, 0), (5, 0, 0)], 12),
+    ]
     orders = tuple(
-        tuple((k, 2 * a + b) for a, _, k in names for b in range(2)) for names in (ones, twos)
+        tuple((k, 2 * a + b) for a, _, k in names for b in range(2)) for names, _ in starts
     )
-    first, second = first_packed(a_index, a_own, a_other, note, note_other, orders)
-    own = keep(first, ones)
-    keep(second, twos)
-    up2 = send(second, twos, 2)
-    up1 = send(first, ones, 1)
+    arrays = first_packed(a_index, a_own, a_other, note, orders)
+    near = []
+    for array, (names, _) in zip(arrays[:4], starts[:4], strict=True):
+        own = keep(array, names)
+    near.append((own, 8 * BLK, 0, True))
+    for array, (names, distance) in zip(arrays, starts, strict=True):
+        near.append((send(array, names, distance), 2 * len(names) * BLK, distance, True))
+    crossed = near.pop()
 
     shift = (2 * q + core + jnp.arange(18, dtype=jnp.int32)) % 16
     b_code = b_own_code.reshape(16) + 1
@@ -276,41 +288,32 @@
     b_code = jnp.stack([b_code[t : t + 16] for t in range(STEPS)], axis=1)
     b_code = jnp.concatenate([b_code // 16, b_code % 16], axis=1).astype(jnp.bfloat16)
     b_code = jnp.broadcast_to(jnp.pad(b_code, ((0, 0), (0, BLK - 6)))[:, None, :], (16, 16, BLK))
-    right = right_packed(b_own, shift, b_code, sources[up2])
+    right = right_packed(b_own, shift, b_code)
     right = lax.all_to_all(right, ROW, 0, 0, tiled=True)
 
-    near = [(own, 16 * BLK, 0), (up1, 16 * BLK, 1), (up2, 16 * BLK, 2)]
-    names = items([(2, 1), (6, 1), (3, 2), (7, 2), (0, 2), (4, 2)])
+    names = items([(2, 1), (6, 13), (3, 2), (7, 14), (0, 14), (4, 2)])
     (up_in,) = packed([(blocks(names), True)], near)
     sources.append(up_in)
     up3 = send(up_in, names, 1)
-
-    names = items([(5, 1), (6, 1), (7, 2)]) + [(4, 0, 0), (5, 0, 0)]
-    (cross_in,) = packed([(blocks(names), True)], near, (up_in,))
-    crossed = send(cross_in, names, 12)
-    far = [(crossed, 16 * BLK, 12)]
-
-    near = [(up3 - 1, 24 * BLK, 0), (up3, 24 * BLK, 1)]
-    plans = ((items([(1, 1), (2, 2)]), 15), (items([(5, 1), (6, 2)]), 3))
-    inputs = packed([(blocks(names), True) for names, _ in plans], near)
-    far.append((len(sources), 8 * BLK, 0))
-    sources.append(inputs[0])
-    for array, (names, distance) in zip(inputs, plans, strict=True):
-        far.append((send(array, names, distance), 8 * BLK, distance))
-
-    names = items([(6, 2), (7, 3), (0, 3)])
-    (cross_in,) = packed([(blocks(names), False)], (), (inputs[0],))
-    send(cross_in, names, 12)
+    middle = [(up3 - 1, 24 * BLK, 0, False), (up3, 24 * BLK, 1, False)]
+
+    names = items([(1, 1), (5, 13), (2, 2), (6, 14)])
+    (up_in,) = packed([(blocks(names), True)], middle)
+    up6 = send(up_in, names, 15)
+    middle.append(crossed)
+    far = middle + [(up6, 16 * BLK, 15, False)]
 
     early = items([(1, 1), (5, 13), (2, 2), (6, 14), (3, 3), (7, 15)]) + [(4, 12, 0)]
     early += items([(2, 1), (6, 13), (3, 2), (7, 14), (0, 15), (4, 3)]) + [(5, 12, 0)]
 
-    def pass_on(names, after=()):
+    def pass_on(names, noted, notes=(), after=()):
         entries = [(at[name][0], at[name][1] + b) for name in names for b, _ in passed_on(name)]
-        (array,) = packed([(entries, False)], (), after)
-        return from_other_core(array)
-
-    early_other = pass_on(early)
+        (array,) = packed([(entries, noted)], notes, after)
+        received = from_other_core(array)
+        end = len(entries) * BLK
+        return received, (array[end:], received[end:])
+
+    early_other, early_notes = pass_on(early, True, middle, (up_in,))
 
     names = items([(1, 16), (5, 4), (2, 17), (6, 5), (0, 15), (4, 3)])
     up_in, notes = packed([(blocks(names), False), ((), True)], far)
@@ -319,7 +322,6 @@
 
     late = items([(1, 16), (5, 4), (2, 17), (6, 5)])
     late += items([(1, 17), (5, 5), (2, 18), (6, 6), (0, 16), (4, 4)])
-
 
     def part_of(names):
         by_source = {}
@@ -327,8 +329,7 @@
             source, place = at[name]
             for b, panel in wanted(name):
                 by_source.setdefault(source, []).append(((place + b) * BLK, 0, name[2], name[1], panel))
-        found = sorted(by_source.items())
-        return [(sources[source], rows) for source, rows in found]
+        return [(sources[source], rows) for source, rows in sorted(by_source.items())]
 
     def received_of(array, names):
         rows = []
@@ -337,25 +338,25 @@
                 rows.append((len(rows) * BLK, 1, name[2], name[1], panel))
         return [(array, rows)]
 
-    parts = [
-        part_of(items([(0, 0), (1, 0)]) + early) + received_of(early_other, early),
-        part_of(late),
-        received_of(None, late),
-    ]
-    order = [row for part in parts for _, rows in part for row in rows]
     right_codes = right[:, STEPS * BLK, :6].astype(jnp.int32)
     right_codes = right_codes[:, :3] * 16 + right_codes[:, 3:] - 1
-    table = tables(order, notes, right_codes, c_code.reshape(KEPT), start, core)
-
-    def product_of(part, base, before=None, last=False):
+    c_code = c_code.reshape(KEPT)
+
+    def table_of(parts, notes):
+        order = [row for part in parts for _, rows in part for row in rows]
+        return tables(order, notes, right_codes, c_code, start, core)
+
+    def product_of(table, part, base, before=None, last=False):
         lefts, counts = [array for array, _ in part], tuple(len(rows) for _, rows in part)
         return product(table, right, lefts, counts, base, before, last), base + sum(counts)
 
-    sums, base = product_of(parts[0], 0)
-    late_other = pass_on(late, (sums,))
-    sums, base = product_of(parts[1], base, sums)
-    parts[2] = received_of(late_other, late)
-    out, base = product_of(parts[2], base, sums, last=True)
+    part = part_of(items([(0, 0), (1, 0)]) + early) + received_of(early_other, early)
+    sums, _ = product_of(table_of((part,), early_notes), part, 0)
+    parts = [part_of(late), received_of(None, late)]
+    table = table_of(parts, notes)
+    late_other, _ = pass_on(late, False, (), (sums,))
+    sums, base = product_of(table, parts[0], 0, sums)
+    out, _ = product_of(table, received_of(late_other, late), base, sums, last=True)
     return out[None, None]
 
 

time: 152 us -> 129 us (0.85)
  the two profiles are of different devices: /device:TPU:1 before, /device:TPU:201 now
where the time goes in v5:
time: 129 us; the launch traced here: 127 us
  starting transfers between devices  66 us (51%)
  waiting for transfers between devices  26 us (20%)
  Pallas kernels  18 us (14%)
  local copies, waits for them, and re-layouts  13.5 us (10%)
  other arithmetic  3.12 us (2%)
    ppermute x8, starting transfers between devices, moved(): return lax.ppermute(array, COL, route)  38.1 us
    ppermute x8, waiting for transfers between devices, moved(): return lax.ppermute(array, COL, route)  25.7 us
    ppermute x5, starting transfers between devices, from_other_core(): return lax.ppermute(array, 'core', [(0, 1), (1, 0)])  20.8 us
    pallas_call x3, Pallas kernels, product(): pl.pallas_call(functools.partial(product_kernel, counts, base, before is...  12 us
    unnamed x71, local copies, waits for them, and re-layouts  11.6 us
    all_to_all x1, starting transfers between devices, local(): right = lax.all_to_all(right, ROW, 0, 0, tiled=True)  7.17 us
    pallas_call x5, Pallas kernels, pack(): pl.pallas_call(functools.partial(pack_kernel, spec, notes, len(used)), ou...  4.73 us
  transfers between devices with their start and end apart: 14, of which 4 were waited for; matrix products, arithmetic and copies ran while one was open for 4% of the time, Pallas kernels for 9%

profile of v5, /device:TPU:201, one launch (start us, length us, event | category | flops | bytes accessed | tf_op | source)
XLA Modules:
  0.0 127.4 jit_solution(2840845399312814499)
XLA Ops:
  0.0 2.6 %collective-permute-start = (bf16[16,128,128]{2,1,0:T(8,128)(2,1)}, bf16[16,128,128]{2,1,0:T(8,128)(2,1)S(1)}, u32[]{:S(2)}, u32[]{:S(2)}) collective-permute-start(bf16[16,128,128]{2,1,0:T(8,128)(2,1)} %bitcast.72), channel_id=1, source_target_pairs={{0,1},{1,0},{2,3},{3,2},{4,5},{5,4},{6,7},{7,6},{8,9},{9,8},{10,11... | collective-permute-start | bytes 1572872 | tf_op jit(solution)/shard_map/ppermute | solution.py:230
  3.3 1.9 %collective-permute-start.1 = (bf16[16,128]{1,0:T(8,128)(2,1)S(1)}, bf16[16,128]{1,0:T(8,128)(2,1)S(1)}, u32[]{:S(2)}, u32[]{:S(2)}) collective-permute-start(bf16[16,128]{1,0:T(8,128)(2,1)S(1)} %fusion.31), channel_id=1, source_target_pairs={{0,1},{1,0},{2,3},{3,2},{4,5},{5,4},{6,7},{7,6},{8,9},{9,8},{10,11... | collective-permute-start | bytes 12296 | tf_op jit(solution)/shard_map/ppermute | solution.py:230
  8.8 2.0 %collective-permute-start.3 = (bf16[1040,128]{1,0:T(8,128)(2,1)S(1)}, bf16[1040,128]{1,0:T(8,128)(2,1)S(1)}, u32[]{:S(2)}, u32[]{:S(2)}) collective-permute-start(bf16[1040,128]{1,0:T(8,128)(2,1)S(1)} %get-tuple-element.14), channel_id=1, source_target_pairs={{0,4},{1,45},{2,6},{3,47},{4,8},{5,1},{6,10},{7,3},{8,12},{9,5},{1... | collective-permute-start | bytes 798728 | tf_op jit(solution)/shard_map/ppermute | solution.py:226
  10.8 14.3 %collective-permute-start.4 = (bf16[1040,128]{1,0:T(8,128)(2,1)S(1)}, bf16[1040,128]{1,0:T(8,128)(2,1)S(1)}, u32[]{:S(2)}, u32[]{:S(2)}) collective-permute-start(bf16[1040,128]{1,0:T(8,128)(2,1)S(1)} %get-tuple-element.15.rest_0_), channel_id=1, source_target_pairs={{0,28},{1,21},{2,30},{3,23},{4,32},{5,25},{6,34},{7,27},{8,36},{9,... | collective-permute-start | bytes 798728 | tf_op jit(solution)/shard_map/ppermute | solution.py:226
  25.1 2.2 %collective-permute-start.5 = (bf16[1040,128]{1,0:T(8,128)(2,1)S(1)}, bf16[1040,128]{1,0:T(8,128)(2,1)S(1)}, u32[]{:S(2)}, u32[]{:S(2)}) collective-permute-start(bf16[1040,128]{1,0:T(8,128)(2,1)S(1)} %get-tuple-element.16.rest_1_), channel_id=1, source_target_pairs={{0,2},{1,47},{2,4},{3,1},{4,6},{5,3},{6,8},{7,5},{8,10},{9,7},{10,... | collective-permute-start | bytes 798728 | tf_op jit(solution)/shard_map/ppermute | solution.py:226
  27.3 4.4 %collective-permute-start.6 = (bf16[1040,128]{1,0:T(8,128)(2,1)S(1)}, bf16[1040,128]{1,0:T(8,128)(2,1)S(1)}, u32[]{:S(2)}, u32[]{:S(2)}) collective-permute-start(bf16[1040,128]{1,0:T(8,128)(2,1)S(1)} %get-tuple-element.13.refs_0_), channel_id=1, source_target_pairs={{0,26},{1,23},{2,28},{3,25},{4,30},{5,27},{6,32},{7,29},{8,34},{9,... | collective-permute-start | bytes 798728 | tf_op jit(solution)/shard_map/ppermute | solution.py:226
  31.9 1.6 %collective-permute-done.5.refs_3_.refs_0_.refs_2_.rest_4_ = bf16[1040,128]{1,0:T(8,128)(2,1)S(1)} collective-permute-done((bf16[1040,128]{1,0:T(8,128)(2,1)S(1)}, bf16[1040,128]{1,0:T(8,128)(2,1)S(1)}, u32[]{:S(2)}, u32[]{:S(2)}) %collective-permute-start.5) | collective-permute-done | bytes 266272 | tf_op jit(solution)/shard_map/ppermute | solution.py:226
  33.5 7.5 %collective-permute-done.6.refs_4_.refs_1_.refs_3_.rest_5_ = bf16[1040,128]{1,0:T(8,128)(2,1)S(1)} collective-permute-done((bf16[1040,128]{1,0:T(8,128)(2,1)S(1)}, bf16[1040,128]{1,0:T(8,128)(2,1)S(1)}, u32[]{:S(2)}, u32[]{:S(2)}) %collective-permute-start.6) | collective-permute-done | bytes 266272 | tf_op jit(solution)/shard_map/ppermute | solution.py:226
  41.7 2.2 %collective-permute-start.7 = (bf16[3120,128]{1,0:T(8,128)(2,1)S(1)}, bf16[3120,128]{1,0:T(8,128)(2,1)S(1)}, u32[]{:S(2)}, u32[]{:S(2)}) collective-permute-start(bf16[3120,128]{1,0:T(8,128)(2,1)S(1)} %shard_map.147.refs_2_.refs_1_.refs_5_), channel_id=1, source_target_pairs={{0,2},{1,47},{2,4},{3,1},{4,6},{5,3},{6,8},{7,5},{8,10},{9,7},{10,... | collective-permute-start | bytes 2396168 | tf_op jit(solution)/shard_map/ppermute | solution.py:226
  44.8 1.2 copy-done
  46.1 7.2 %all-to-all-start = ((bf16[16,400,128]{2,1,0:T(8,128)(2,1)}), bf16[16,400,128]{2,1,0:T(8,128)(2,1)S(1)}, u32[]{:S(2)}, u32[]{:S(2)}) async-start(bf16[16,400,128]{2,1,0:T(8,128)(2,1)} %copy-done), calls=%async_computation | async-start | bytes 3276800 | tf_op jit(solution)/shard_map/all_to_all | solution.py:292
  53.4 3.6 %collective-permute-start.2 = (bf16[528,128]{1,0:T(8,128)(2,1)}, bf16[528,128]{1,0:T(8,128)(2,1)S(1)}, u32[]{:S(2)}, u32[]{:S(2)}) collective-permute-start(bf16[528,128]{1,0:T(8,128)(2,1)} %copy-done.23), channel_id=1, source_target_pairs={{0,24},{1,25},{2,26},{3,27},{4,28},{5,29},{6,30},{7,31},{8,32},{9,... | collective-permute-start | bytes 405512 | tf_op jit(solution)/shard_map/ppermute | solution.py:226
  58.0 7.5 %collective-permute-start.8 = (bf16[2096,128]{1,0:T(8,128)(2,1)S(1)}, bf16[2096,128]{1,0:T(8,128)(2,1)S(1)}, u32[]{:S(2)}, u32[]{:S(2)}) collective-permute-start(bf16[2096,128]{1,0:T(8,128)(2,1)S(1)} %shard_map.148.refs_7_), channel_id=1, source_target_pairs={{0,30},{1,19},{2,32},{3,21},{4,34},{5,23},{6,36},{7,25},{8,38},{9,... | collective-permute-start | bytes 1609736 | tf_op jit(solution)/shard_map/ppermute | solution.py:226
  65.6 1.1 shard_map.150
  66.7 3.3 %collective-permute-start.11 = (bf16[5040,128]{1,0:T(8,128)(2,1)}, bf16[5040,128]{1,0:T(8,128)(2,1)}, u32[]{:S(2)}, u32[]{:S(2)}) collective-permute-start(bf16[5040,128]{1,0:T(8,128)(2,1)} %shard_map.150), channel_id=1, source_target_pairs={{0,1},{1,0},{2,3},{3,2},{4,5},{5,4},{6,7},{7,6},{8,9},{9,8},{10,11... | collective-permute-start | bytes 3870728 | tf_op jit(solution)/shard_map/ppermute | solution.py:230
  70.0 16.6 %collective-permute-done.8.refs_3_.refs_0_.rest_0_ = bf16[2096,128]{1,0:T(8,128)(2,1)S(1)} collective-permute-done((bf16[2096,128]{1,0:T(8,128)(2,1)S(1)}, bf16[2096,128]{1,0:T(8,128)(2,1)S(1)}, u32[]{:S(2)}, u32[]{:S(2)}) %collective-permute-start.8) | collective-permute-done | bytes 536608 | tf_op jit(solution)/shard_map/ppermute | solution.py:226
  87.8 7.4 %collective-permute-start.9 = (bf16[48,128]{1,0:T(8,128)(2,1)S(1)}, bf16[48,128]{1,0:T(8,128)(2,1)S(1)}, u32[]{:S(2)}, u32[]{:S(2)}) collective-permute-start(bf16[48,128]{1,0:T(8,128)(2,1)S(1)} %get-tuple-element.17), channel_id=1, source_target_pairs={{0,1},{1,0},{2,3},{3,2},{4,5},{5,4},{6,7},{7,6},{8,9},{9,8},{10,11... | collective-permute-start | bytes 36872 | tf_op jit(solution)/shard_map/ppermute | solution.py:230
  95.9 1.9 %collective-permute-start.10 = (bf16[3072,128]{1,0:T(8,128)(2,1)}, bf16[3072,128]{1,0:T(8,128)(2,1)}, u32[]{:S(2)}, u32[]{:S(2)}) collective-permute-start(bf16[3072,128]{1,0:T(8,128)(2,1)} %get-tuple-element.18), channel_id=1, source_target_pairs={{0,2},{1,47},{2,4},{3,1},{4,6},{5,3},{6,8},{7,5},{8,10},{9,7},{10,... | collective-permute-start | bytes 2359304 | tf_op jit(solution)/shard_map/ppermute | solution.py:226
  105.9 5.9 %shard_map.151.refs_2_.rest_2_ = f32[13,128,128]{2,1,0:T(8,128)S(1)} custom-call(s32[7,84]{1,0:T(8,128)S(1)} %stack.73.table_ref, bf16[16,400,128]{2,1,0:T(8,128)(2,1)S(1)} %all-to-all-done.right_ref, bf16[1040,128]{1,0:T(8,128)(2,1)S(1)} %copy-done.20, bf16[1040,128]{1,0:T(8,128)(2,1)S(1)} %copy-done.22, bf16[1040,128]{1,0:T(8,128)(2,1)S(1)} %copy-done.11, ...), custom_call_target="tpu_custom_call" | custom-call | flops 2818572288 | bytes 2752512 | tf_op jit(solution)/shard_map/pallas_call | solution.py:171
  111.9 2.4 %shard_map.152 = bf16[3584,128]{1,0:T(8,128)(2,1)} custom-call(bf16[2096,128]{1,0:T(8,128)(2,1)S(1)} %copy-done.2, bf16[3072,128]{1,0:T(8,128)(2,1)} %collective-permute-done.10.refs_1_.rest_1_, f32[13,128,128]{2,1,0:T(8,128)S(1)} %shard_map.151.refs_2_.rest_2_), custom_call_target="tpu_custom_call" | custom-call | bytes 1835008 | tf_op jit(solution)/shard_map/pallas_call | solution.py:126
  114.3 5.7 %collective-permute-start.12 = (bf16[3584,128]{1,0:T(8,128)(2,1)}, bf16[3584,128]{1,0:T(8,128)(2,1)}, u32[]{:S(2)}, u32[]{:S(2)}) collective-permute-start(bf16[3584,128]{1,0:T(8,128)(2,1)} %shard_map.152), channel_id=1, source_target_pairs={{0,1},{1,0},{2,3},{3,2},{4,5},{5,4},{6,7},{7,6},{8,9},{9,8},{10,11... | collective-permute-start | bytes 2752520 | tf_op jit(solution)/shard_map/ppermute | solution.py:230
  120.2 1.1 copy-done.4
  121.4 2.8 %shard_map.153.rest_1_ = f32[13,128,128]{2,1,0:T(8,128)S(1)} custom-call(s32[7,60]{1,0:T(8,128)S(1)} %stack.67.table_ref, bf16[16,400,128]{2,1,0:T(8,128)(2,1)S(1)} %all-to-all-done.right_ref, bf16[2096,128]{1,0:T(8,128)(2,1)S(1)} %copy-done.2, bf16[3072,128]{1,0:T(8,128)(2,1)} %collective-permute-done.10.refs_1_.rest_1_, f32[13,128,128]{2,1,0:T(8,128)S(1)} %copy-done.4), custom_call_target="tpu_custom_call" | custom-call | flops 1073741824 | bytes 1048576 | tf_op jit(solution)/shard_map/pallas_call | solution.py:171
  124.2 3.2 %shard_map.154 = bf16[12,128,128]{2,1,0:T(8,128)(2,1)} custom-call(s32[7,60]{1,0:T(8,128)S(1)} %stack.67.table_ref, bf16[16,400,128]{2,1,0:T(8,128)(2,1)S(1)} %all-to-all-done.right_ref, bf16[3584,128]{1,0:T(8,128)(2,1)} %collective-permute-done.12.rest_0_, f32[13,128,128]{2,1,0:T(8,128)S(1)} %shard_map.153.rest_1_), custom_call_target="tpu_custom_call" | custom-call | flops 939524096 | bytes 917504 | tf_op jit(solution)/shard_map/pallas_call | solution.py:171
  (147 shorter events, 17.0 us)
Async XLA Ops:
  0.0 6.5 %collective-permute-start = (bf16[16,128,128]{2,1,0:T(8,128)(2,1)}, bf16[16,128,128]{2,1,0:T(8,128)(2,1)S(1)}, u32[]{:S(2)}, u32[]{:S(2)}) collective-permute-start(bf16[16,128,128]{2,1,0:T(8,128)(2,1)} %bitcast.72), channel_id=1, source_target_pairs={{0,1},{1,0},{2,3},{3,2},{4,5},{5,4},{6,7},{7,6},{8,9},{9,8},{10,11... | collective-permute-start | bytes 1572872 | tf_op jit(solution)/shard_map/ppermute | solution.py:230
  3.3 3.0 %collective-permute-start.1 = (bf16[16,128]{1,0:T(8,128)(2,1)S(1)}, bf16[16,128]{1,0:T(8,128)(2,1)S(1)}, u32[]{:S(2)}, u32[]{:S(2)}) collective-permute-start(bf16[16,128]{1,0:T(8,128)(2,1)S(1)} %fusion.31), channel_id=1, source_target_pairs={{0,1},{1,0},{2,3},{3,2},{4,5},{5,4},{6,7},{7,6},{8,9},{9,8},{10,11... | collective-permute-start | bytes 12296 | tf_op jit(solution)/shard_map/ppermute | solution.py:230
  8.8 35.1 %copy-start.19 = (bf16[1040,128]{1,0:T(8,128)(2,1)}, bf16[1040,128]{1,0:T(8,128)(2,1)S(1)}, u32[]{:S(2)}) copy-start(bf16[1040,128]{1,0:T(8,128)(2,1)S(1)} %get-tuple-element.15.rest_0_) | copy-start | bytes 798724
  8.8 35.1 %copy-start.21 = (bf16[1040,128]{1,0:T(8,128)(2,1)}, bf16[1040,128]{1,0:T(8,128)(2,1)S(1)}, u32[]{:S(2)}) copy-start(bf16[1040,128]{1,0:T(8,128)(2,1)S(1)} %get-tuple-element.16.rest_1_) | copy-start | bytes 798724
  8.8 35.3 %copy-start.17 = (bf16[1,1,16,1,128,128]{5,4,3,2,1,0:T(8,128)(2,1)S(1)}, bf16[1,1,16,1,128,128]{5,4,3,2,1,0:T(8,128)(2,1)}, u32[]{:S(2)}) copy-start(bf16[1,1,16,1,128,128]{5,4,3,2,1,0:T(8,128)(2,1)} %param.17) | copy-start | bytes 1572868
  8.8 23.1 %collective-permute-start.3 = (bf16[1040,128]{1,0:T(8,128)(2,1)S(1)}, bf16[1040,128]{1,0:T(8,128)(2,1)S(1)}, u32[]{:S(2)}, u32[]{:S(2)}) collective-permute-start(bf16[1040,128]{1,0:T(8,128)(2,1)S(1)} %get-tuple-element.14), channel_id=1, source_target_pairs={{0,4},{1,45},{2,6},{3,47},{4,8},{5,1},{6,10},{7,3},{8,12},{9,5},{1... | collective-permute-start | bytes 798728 | tf_op jit(solution)/shard_map/ppermute | solution.py:226
  10.8 21.0 %collective-permute-start.4 = (bf16[1040,128]{1,0:T(8,128)(2,1)S(1)}, bf16[1040,128]{1,0:T(8,128)(2,1)S(1)}, u32[]{:S(2)}, u32[]{:S(2)}) collective-permute-start(bf16[1040,128]{1,0:T(8,128)(2,1)S(1)} %get-tuple-element.15.rest_0_), channel_id=1, source_target_pairs={{0,28},{1,21},{2,30},{3,23},{4,32},{5,25},{6,34},{7,27},{8,36},{9,... | collective-permute-start | bytes 798728 | tf_op jit(solution)/shard_map/ppermute | solution.py:226
  25.1 8.4 %collective-permute-start.5 = (bf16[1040,128]{1,0:T(8,128)(2,1)S(1)}, bf16[1040,128]{1,0:T(8,128)(2,1)S(1)}, u32[]{:S(2)}, u32[]{:S(2)}) collective-permute-start(bf16[1040,128]{1,0:T(8,128)(2,1)S(1)} %get-tuple-element.16.rest_1_), channel_id=1, source_target_pairs={{0,2},{1,47},{2,4},{3,1},{4,6},{5,3},{6,8},{7,5},{8,10},{9,7},{10,... | collective-permute-start | bytes 798728 | tf_op jit(solution)/shard_map/ppermute | solution.py:226
  27.3 13.6 %collective-permute-start.6 = (bf16[1040,128]{1,0:T(8,128)(2,1)S(1)}, bf16[1040,128]{1,0:T(8,128)(2,1)S(1)}, u32[]{:S(2)}, u32[]{:S(2)}) collective-permute-start(bf16[1040,128]{1,0:T(8,128)(2,1)S(1)} %get-tuple-element.13.refs_0_), channel_id=1, source_target_pairs={{0,26},{1,23},{2,28},{3,25},{4,30},{5,27},{6,32},{7,29},{8,34},{9,... | collective-permute-start | bytes 798728 | tf_op jit(solution)/shard_map/ppermute | solution.py:226
  31.8 9.2 %copy-start.9 = (bf16[1040,128]{1,0:T(8,128)(2,1)}, bf16[1040,128]{1,0:T(8,128)(2,1)S(1)}, u32[]{:S(2)}) copy-start(bf16[1040,128]{1,0:T(8,128)(2,1)S(1)} %collective-permute-done.3.refs_1_.refs_0_.rest_2_) | copy-start | bytes 798724
  31.9 12.1 %copy-start.12 = (bf16[1040,128]{1,0:T(8,128)(2,1)}, bf16[1040,128]{1,0:T(8,128)(2,1)S(1)}, u32[]{:S(2)}) copy-start(bf16[1040,128]{1,0:T(8,128)(2,1)S(1)} %collective-permute-done.4.refs_2_.refs_1_.rest_3_) | copy-start | bytes 798724
  41.7 15.3 %collective-permute-start.7 = (bf16[3120,128]{1,0:T(8,128)(2,1)S(1)}, bf16[3120,128]{1,0:T(8,128)(2,1)S(1)}, u32[]{:S(2)}, u32[]{:S(2)}) collective-permute-start(bf16[3120,128]{1,0:T(8,128)(2,1)S(1)} %shard_map.147.refs_2_.refs_1_.refs_5_), channel_id=1, source_target_pairs={{0,2},{1,47},{2,4},{3,1},{4,6},{5,3},{6,8},{7,5},{8,10},{9,7},{10,... | collective-permute-start | bytes 2396168 | tf_op jit(solution)/shard_map/ppermute | solution.py:226
  46.1 53.3 %all-to-all-start = ((bf16[16,400,128]{2,1,0:T(8,128)(2,1)}), bf16[16,400,128]{2,1,0:T(8,128)(2,1)S(1)}, u32[]{:S(2)}, u32[]{:S(2)}) async-start(bf16[16,400,128]{2,1,0:T(8,128)(2,1)} %copy-done), calls=%async_computation | async-start | bytes 3276800 | tf_op jit(solution)/shard_map/all_to_all | solution.py:292
  53.4 12.2 %collective-permute-start.2 = (bf16[528,128]{1,0:T(8,128)(2,1)}, bf16[528,128]{1,0:T(8,128)(2,1)S(1)}, u32[]{:S(2)}, u32[]{:S(2)}) collective-permute-start(bf16[528,128]{1,0:T(8,128)(2,1)} %copy-done.23), channel_id=1, source_target_pairs={{0,24},{1,25},{2,26},{3,27},{4,28},{5,29},{6,30},{7,31},{8,32},{9,... | collective-permute-start | bytes 405512 | tf_op jit(solution)/shard_map/ppermute | solution.py:226
  58.0 7.6 %copy-start.13 = (bf16[1040,128]{1,0:T(8,128)(2,1)S(1)}, bf16[1040,128]{1,0:T(8,128)(2,1)}, u32[]{:S(2)}) copy-start(bf16[1040,128]{1,0:T(8,128)(2,1)} %copy-done.12) | copy-start | bytes 798724
  58.0 28.6 %collective-permute-start.8 = (bf16[2096,128]{1,0:T(8,128)(2,1)S(1)}, bf16[2096,128]{1,0:T(8,128)(2,1)S(1)}, u32[]{:S(2)}, u32[]{:S(2)}) collective-permute-start(bf16[2096,128]{1,0:T(8,128)(2,1)S(1)} %shard_map.148.refs_7_), channel_id=1, source_target_pairs={{0,30},{1,19},{2,32},{3,21},{4,34},{5,23},{6,36},{7,25},{8,38},{9,... | collective-permute-start | bytes 1609736 | tf_op jit(solution)/shard_map/ppermute | solution.py:226
  65.6 21.1 %copy-start.15 = (bf16[528,128]{1,0:T(8,128)(2,1)}, bf16[528,128]{1,0:T(8,128)(2,1)S(1)}, u32[]{:S(2)}) copy-start(bf16[528,128]{1,0:T(8,128)(2,1)S(1)} %collective-permute-done.2.refs_0_.refs_4_.rest_6_) | copy-start | bytes 405508
  66.7 31.5 %collective-permute-start.11 = (bf16[5040,128]{1,0:T(8,128)(2,1)}, bf16[5040,128]{1,0:T(8,128)(2,1)}, u32[]{:S(2)}, u32[]{:S(2)}) collective-permute-start(bf16[5040,128]{1,0:T(8,128)(2,1)} %shard_map.150), channel_id=1, source_target_pairs={{0,1},{1,0},{2,3},{3,2},{4,5},{5,4},{6,7},{7,6},{8,9},{9,8},{10,11... | collective-permute-start | bytes 3870728 | tf_op jit(solution)/shard_map/ppermute | solution.py:230
  70.0 29.9 %copy-start.28 = (s32[1,1,12]{2,1,0:T(1,128)S(1)}, s32[1,1,12]{2,1,0:T(1,128)}, u32[]{:S(2)}) copy-start(s32[1,1,12]{2,1,0:T(1,128)} %param.19) | copy-start | bytes 148
  70.0 30.0 %copy-start.34 = (s32[1,84]{1,0:T(1,128)S(1)}, s32[1,84]{1,0:T(1,128)}, u32[]{:S(2)}) copy-start(s32[1,84]{1,0:T(1,128)} %constant.384) | copy-start | bytes 1012
  87.8 10.0 %collective-permute-start.9 = (bf16[48,128]{1,0:T(8,128)(2,1)S(1)}, bf16[48,128]{1,0:T(8,128)(2,1)S(1)}, u32[]{:S(2)}, u32[]{:S(2)}) collective-permute-start(bf16[48,128]{1,0:T(8,128)(2,1)S(1)} %get-tuple-element.17), channel_id=1, source_target_pairs={{0,1},{1,0},{2,3},{3,2},{4,5},{5,4},{6,7},{7,6},{8,9},{9,8},{10,11... | collective-permute-start | bytes 36872 | tf_op jit(solution)/shard_map/ppermute | solution.py:230
  95.9 16.0 %collective-permute-start.10 = (bf16[3072,128]{1,0:T(8,128)(2,1)}, bf16[3072,128]{1,0:T(8,128)(2,1)}, u32[]{:S(2)}, u32[]{:S(2)}) collective-permute-start(bf16[3072,128]{1,0:T(8,128)(2,1)} %get-tuple-element.18), channel_id=1, source_target_pairs={{0,2},{1,47},{2,4},{3,1},{4,6},{5,3},{6,8},{7,5},{8,10},{9,7},{10,... | collective-permute-start | bytes 2359304 | tf_op jit(solution)/shard_map/ppermute | solution.py:226
  111.9 8.3 %copy-start.33 = (s32[1,60]{1,0:T(1,128)S(1)}, s32[1,60]{1,0:T(1,128)}, u32[]{:S(2)}) copy-start(s32[1,60]{1,0:T(1,128)} %constant.383) | copy-start | bytes 724
  114.3 9.9 %collective-permute-start.12 = (bf16[3584,128]{1,0:T(8,128)(2,1)}, bf16[3584,128]{1,0:T(8,128)(2,1)}, u32[]{:S(2)}, u32[]{:S(2)}) collective-permute-start(bf16[3584,128]{1,0:T(8,128)(2,1)} %shard_map.152), channel_id=1, source_target_pairs={{0,1},{1,0},{2,3},{3,2},{4,5},{5,4},{6,7},{7,6},{8,9},{9,8},{10,11... | collective-permute-start | bytes 2752520 | tf_op jit(solution)/shard_map/ppermute | solution.py:230
  (25 other events, 94.3 us)

commit v6 on v5

--- a/solution.py
+++ b/solution.py
@@ -19,6 +19,7 @@
 PANEL = 48
 STEPS = 3
 KEPT = 12
+SPAN = 8 + STEPS - 1
 BLK = 128
 
 
@@ -73,22 +74,52 @@
     )(index, own, other, note)
 
 
-def right_kernel(index_ref, src_ref, code_ref, out):
-    for n in range(16):
-        for t in range(STEPS):
-            out[n, pl.ds(t * BLK, BLK), :] = src_ref[index_ref[n + t]]
-        out[n, pl.ds(STEPS * BLK, 16), :] = code_ref[n]
-
-
-def right_packed(src, index, codes):
+def split_kernel(index_ref, src_ref, note_ref, *outs):
+    for half, out in enumerate(outs):
+        for n in range(SPAN):
+            out[blk(n), :] = src_ref[index_ref[SPAN * half + n]]
+        out[pl.ds(SPAN * BLK, 16), :] = note_ref[...]
+
+
+def split(index, src, note):
     return pl.pallas_call(
-        right_kernel,
-        out_shape=jax.ShapeDtypeStruct((16, STEPS * BLK + 16, BLK), jnp.bfloat16),
+        split_kernel,
+        out_shape=[rows_shape(SPAN * BLK + 16)] * 2,
         in_specs=[SMEM_SPEC, VMEM_SPEC, VMEM_SPEC],
+        out_specs=[VMEM_SPEC] * 2,
+        compiler_params=LIMIT,
+        cost_estimate=moves(2 * SPAN),
+    )(index, src, note)
+
+
+def chosen_kernel(index_ref, *rest):
+    sources, out, sems = rest[:2], rest[2], rest[3]
+    copies = []
+    for half, src in enumerate(sources):
+        for n in range(8):
+            for t in range(STEPS):
+                row = pl.multiple_of(index_ref[t] * BLK, BLK)
+                place = blk((half * STEPS + t) * 8 + n)
+                copies.append((src.at[n, pl.ds(row, BLK)], out.at[place]))
+            tail = pl.ds(STEPS * 16 * BLK + 16 * (8 * half + n), 16)
+            copies.append((src.at[n, pl.ds(SPAN * BLK, 16)], out.at[tail]))
+    copies = [pltpu.make_async_copy(a, b, sems.at[n]) for n, (a, b) in enumerate(copies)]
+    for copy in copies:
+        copy.start()
+    for copy in copies:
+        copy.wait()
+
+
+def chosen(index, sources):
+    return pl.pallas_call(
+        chosen_kernel,
+        out_shape=rows_shape(STEPS * 16 * BLK + 16 * 16),
+        in_specs=[SMEM_SPEC, ANY_SPEC, ANY_SPEC],
         out_specs=VMEM_SPEC,
+        scratch_shapes=[pltpu.SemaphoreType.DMA((2 * 8 * (STEPS + 1),))],
         compiler_params=LIMIT,
         cost_estimate=moves(48),
-    )(index, src, codes)
+    )(index, *sources)
 
 
 def turned(note, distance):
@@ -147,15 +178,14 @@
     for left, count in zip(lefts, counts, strict=True):
 
         def body(n, carry, left=left, base=base):
-            block = left[pl.ds(pl.multiple_of(table_ref[6, base + n], BLK), BLK), :]
+            block = left[pl.ds(pl.multiple_of(table_ref[4, base + n], BLK), BLK), :]
             pair = []
             for rank in range(2):
-                owner = table_ref[3 * rank, base + n]
-                row = pl.multiple_of(table_ref[3 * rank + 1, base + n], BLK)
-                pair.append(right_ref[owner, pl.ds(row, BLK), :])
+                row = pl.multiple_of(table_ref[2 * rank, base + n], BLK)
+                pair.append(right_ref[pl.ds(row, BLK), :])
             both = jnp.dot(block, jnp.concatenate(pair, axis=1), preferred_element_type=jnp.float32)
-            acc[table_ref[2, base + n]] += both[:, :BLK]
-            acc[table_ref[5, base + n]] += both[:, BLK:]
+            acc[table_ref[1, base + n]] += both[:, :BLK]
+            acc[table_ref[3, base + n]] += both[:, BLK:]
             return carry
 
         unroll = max(n for n in (7, 6, 5, 4, 3, 2, 1) if count % n == 0)
@@ -214,8 +244,9 @@
         target = (codes // PANEL) * BC + partner % 32
         there = (target[:, None] == c_code[None, :]) & (found > 0)[:, None]
         slot = jnp.sum(jnp.where(there, jnp.arange(KEPT)[None, :] - KEPT, 0), axis=1) + KEPT
-        rows += [partner // 32, step * BLK, slot]
-    return jnp.stack(rows + [jnp.array(row)]).astype(jnp.int32).reshape(7, count)
+        owner = partner // 32
+        rows += [(owner // 8 * (8 * STEPS) + step * 8 + owner % 8) * BLK, slot]
+    return jnp.stack(rows + [jnp.array(row)]).astype(jnp.int32).reshape(5, count)
 
 
 def moved(array, distance):
@@ -238,6 +269,17 @@
     a_own = a_own_values.reshape(16, BLK, BLK)
     b_own = b_own_values.reshape(16, BLK, BLK)
 
+    def note_of(code):
+        code = code.reshape(16) + 1
+        digits = jnp.concatenate([code // 64, code % 64]).astype(jnp.bfloat16).reshape(1, 32)
+        return jnp.pad(digits, ((0, 15), (0, BLK - 32)))
+
+    spans = 2 * q + core + 8 * lax.axis_index("xl") + jnp.arange(SPAN, dtype=jnp.int32)
+    spans = jnp.concatenate([spans, spans + 8]) % 16
+    b_kept, b_sent = split(spans, b_own, note_of(b_own_code))
+    b_all = [lax.all_gather(b_kept, "y")]
+    b_other = lax.ppermute(b_sent, "xl", [(0, 1), (1, 0)])
+
     sources, at = [], {}
 
     def keep(array, names):
@@ -255,9 +297,7 @@
     def packed(spec, notes=(), after=()):
         return pack(sources, spec, notes, after)
 
-    code = a_own_code.reshape(16) + 1
-    note = jnp.concatenate([code // 64, code % 64]).astype(jnp.bfloat16).reshape(1, 32)
-    note = jnp.pad(note, ((0, 15), (0, BLK - 32)))
+    note = note_of(a_own_code)
     a_other, note_other = from_other_core(a_own), from_other_core(note)
     note = jnp.concatenate([note[:1], note_other[:1], note[2:]])
     a_index = jnp.arange(16, dtype=jnp.int32)
@@ -280,16 +320,9 @@
     near.append((own, 8 * BLK, 0, True))
     for array, (names, distance) in zip(arrays, starts, strict=True):
         near.append((send(array, names, distance), 2 * len(names) * BLK, distance, True))
-    crossed = near.pop()
-
-    shift = (2 * q + core + jnp.arange(18, dtype=jnp.int32)) % 16
-    b_code = b_own_code.reshape(16) + 1
-    b_code = jnp.sum(jnp.where(shift[:, None] == jnp.arange(16)[None, :], b_code[None, :], 0), axis=1)
-    b_code = jnp.stack([b_code[t : t + 16] for t in range(STEPS)], axis=1)
-    b_code = jnp.concatenate([b_code // 16, b_code % 16], axis=1).astype(jnp.bfloat16)
-    b_code = jnp.broadcast_to(jnp.pad(b_code, ((0, 0), (0, BLK - 6)))[:, None, :], (16, 16, BLK))
-    right = right_packed(b_own, shift, b_code)
-    right = lax.all_to_all(right, ROW, 0, 0, tiled=True)
+
+    b_other, _ = lax.optimization_barrier((b_other, sources[near[1][0]]))
+    b_all.append(lax.all_gather(b_other, "y"))
 
     names = items([(2, 1), (6, 13), (3, 2), (7, 14), (0, 14), (4, 2)])
     (up_in,) = packed([(blocks(names), True)], near)
@@ -300,20 +333,23 @@
     names = items([(1, 1), (5, 13), (2, 2), (6, 14)])
     (up_in,) = packed([(blocks(names), True)], middle)
     up6 = send(up_in, names, 15)
-    middle.append(crossed)
     far = middle + [(up6, 16 * BLK, 15, False)]
 
     early = items([(1, 1), (5, 13), (2, 2), (6, 14), (3, 3), (7, 15)]) + [(4, 12, 0)]
     early += items([(2, 1), (6, 13), (3, 2), (7, 14), (0, 15), (4, 3)]) + [(5, 12, 0)]
 
-    def pass_on(names, noted, notes=(), after=()):
+    def pass_on(names, kept=None, notes=(), after=()):
         entries = [(at[name][0], at[name][1] + b) for name in names for b, _ in passed_on(name)]
-        (array,) = packed([(entries, noted)], notes, after)
+        spec = [(entries, bool(notes))]
+        if kept:
+            spec.append(([(at[name][0], at[name][1] + b) for name in kept for b, _ in wanted(name)], False))
+        array, *own_part = packed(spec, notes, after)
         received = from_other_core(array)
         end = len(entries) * BLK
-        return received, (array[end:], received[end:])
-
-    early_other, early_notes = pass_on(early, True, middle, (up_in,))
+        return received, own_part, (array[end:], received[end:])
+
+    mine = items([(0, 0), (1, 0)]) + early
+    early_other, early_own, early_notes = pass_on(early, mine, middle, (up_in,))
 
     names = items([(1, 16), (5, 4), (2, 17), (6, 5), (0, 15), (4, 3)])
     up_in, notes = packed([(blocks(names), False), ((), True)], far)
@@ -338,8 +374,13 @@
                 rows.append((len(rows) * BLK, 1, name[2], name[1], panel))
         return [(array, rows)]
 
-    right_codes = right[:, STEPS * BLK, :6].astype(jnp.int32)
-    right_codes = right_codes[:, :3] * 16 + right_codes[:, 3:] - 1
+    panels = (start + core + jnp.arange(STEPS, dtype=jnp.int32)) % 16
+    right = chosen(lax.axis_index("y") + jnp.arange(STEPS, dtype=jnp.int32), b_all)
+    digits = right[STEPS * 16 * BLK :].reshape(16, 16, BLK)[:, 0, :32].astype(jnp.int32)
+    right_codes = (digits[:, :16] * 64 + digits[:, 16:] - 1)[:, None, :]
+    right_codes = jnp.sum(
+        jnp.where(panels[:, None] == jnp.arange(16)[None, :], right_codes, 0), axis=2
+    )
     c_code = c_code.reshape(KEPT)
 
     def table_of(parts, notes):
@@ -350,11 +391,14 @@
         lefts, counts = [array for array, _ in part], tuple(len(rows) for _, rows in part)
         return product(table, right, lefts, counts, base, before, last), base + sum(counts)
 
-    part = part_of(items([(0, 0), (1, 0)]) + early) + received_of(early_other, early)
+    rows = []
+    for name in mine:
+        rows += [(len(rows) * BLK + n * BLK, 0, name[2], name[1], w) for n, (_, w) in enumerate(wanted(name))]
+    part = [(early_own[0], rows)] + received_of(early_other, early)
     sums, _ = product_of(table_of((part,), early_notes), part, 0)
     parts = [part_of(late), received_of(None, late)]
     table = table_of(parts, notes)
-    late_other, _ = pass_on(late, False, (), (sums,))
+    late_other, _, _ = pass_on(late, None, (), (sums,))
     sums, base = product_of(table, parts[0], 0, sums)
     out, _ = product_of(table, received_of(late_other, late), base, sums, last=True)
     return out[None, None]

time: 129 us -> 151 us (1.17)
  the two profiles are of different devices: /device:TPU:201 before, /device:TPU:1 now
where the time goes in v6:
time: 151 us; the launch traced here: 150 us
  starting transfers between devices  68 us (45%)
  waiting for transfers between devices  29.8 us (20%)
  Pallas kernels  22.4 us (15%)
  between operations  14 us (9%)
  local copies, waits for them, and re-layouts  12.4 us (8%)
  other arithmetic  3.48 us (2%)
    ppermute x8, starting transfers between devices, moved(): return lax.ppermute(array, COL, route)  38.6 us
    ppermute x8, waiting for transfers between devices, moved(): return lax.ppermute(array, COL, route)  28.7 us
    ppermute x5, starting transfers between devices, from_other_core(): return lax.ppermute(array, 'core', [(0, 1), (1, 0)])  25.3 us
    pallas_call x3, Pallas kernels, product(): pl.pallas_call(functools.partial(product_kernel, counts, base, before is...  12.6 us
    unnamed x44, local copies, waits for them, and re-layouts  10.7 us
    pallas_call x5, Pallas kernels, pack(): pl.pallas_call(functools.partial(pack_kernel, spec, notes, len(used)), ou...  4.49 us
    ppermute x1, starting transfers between devices, local(): b_other = lax.ppermute(b_sent, 'xl', [(0, 1), (1, 0)])  3.95 us
    pallas_call x1, Pallas kernels, chosen(): pl.pallas_call(chosen_kernel, out_shape=rows_shape(STEPS * 16 * BLK + 16...  3.36 us
  transfers between devices with their start and end apart: 16, of which 5 were waited for; matrix products, arithmetic and copies ran while one was open for 3% of the time, Pallas kernels for 10%

profile of v6, /device:TPU:1, one launch (start us, length us, event | category | flops | bytes accessed | tf_op | source)
XLA Modules:
  0.0 150.1 jit_solution(5397357795174222758)
XLA Ops:
  9.8 3.9 %collective-permute-start = (bf16[1296,128]{1,0:T(8,128)(2,1)S(1)}, bf16[1296,128]{1,0:T(8,128)(2,1)S(1)}, u32[]{:S(2)}, u32[]{:S(2)}) collective-permute-start(bf16[1296,128]{1,0:T(8,128)(2,1)S(1)} %get-tuple-element.18), channel_id=1, source_target_pairs={{0,384},{384,0},{1,385},{385,1},{2,386},{386,2},{3,387},{387,3},{4... | collective-permute-start | bytes 995336 | tf_op jit(solution)/shard_map/ppermute | solution.py:281
  13.8 10.4 %collective-permute-start.1 = (bf16[16,128,128]{2,1,0:T(8,128)(2,1)}, bf16[16,128,128]{2,1,0:T(8,128)(2,1)S(1)}, u32[]{:S(2)}, u32[]{:S(2)}) collective-permute-start(bf16[16,128,128]{2,1,0:T(8,128)(2,1)} %bitcast.75), channel_id=1, source_target_pairs={{0,1},{1,0},{2,3},{3,2},{4,5},{5,4},{6,7},{7,6},{8,9},{9,8},{10,11... | collective-permute-start | bytes 1572872 | tf_op jit(solution)/shard_map/ppermute | solution.py:261
  24.9 1.9 %collective-permute-start.2 = (bf16[16,128]{1,0:T(8,128)(2,1)S(1)}, bf16[16,128]{1,0:T(8,128)(2,1)S(1)}, u32[]{:S(2)}, u32[]{:S(2)}) collective-permute-start(bf16[16,128]{1,0:T(8,128)(2,1)S(1)} %fusion.37), channel_id=1, source_target_pairs={{0,1},{1,0},{2,3},{3,2},{4,5},{5,4},{6,7},{7,6},{8,9},{9,8},{10,11... | collective-permute-start | bytes 12296 | tf_op jit(solution)/shard_map/ppermute | solution.py:261
  29.8 9.1 %collective-permute-start.3 = (bf16[1040,128]{1,0:T(8,128)(2,1)S(1)}, bf16[1040,128]{1,0:T(8,128)(2,1)S(1)}, u32[]{:S(2)}, u32[]{:S(2)}) collective-permute-start(bf16[1040,128]{1,0:T(8,128)(2,1)S(1)} %get-tuple-element.19), channel_id=1, source_target_pairs={{0,4},{1,45},{2,6},{3,47},{4,8},{5,1},{6,10},{7,3},{8,12},{9,5},{1... | collective-permute-start | bytes 798728 | tf_op jit(solution)/shard_map/ppermute | solution.py:257
  38.9 6.2 %collective-permute-done.3.refs_1_.refs_2_ = bf16[1040,128]{1,0:T(8,128)(2,1)S(1)} collective-permute-done((bf16[1040,128]{1,0:T(8,128)(2,1)S(1)}, bf16[1040,128]{1,0:T(8,128)(2,1)S(1)}, u32[]{:S(2)}, u32[]{:S(2)}) %collective-permute-start.3) | collective-permute-done | bytes 266272 | tf_op jit(solution)/shard_map/ppermute | solution.py:257
  45.1 6.2 %collective-permute-start.4 = (bf16[1040,128]{1,0:T(8,128)(2,1)S(1)}, bf16[1040,128]{1,0:T(8,128)(2,1)S(1)}, u32[]{:S(2)}, u32[]{:S(2)}) collective-permute-start(bf16[1040,128]{1,0:T(8,128)(2,1)S(1)} %get-tuple-element.22.refs_0_), channel_id=1, source_target_pairs={{0,28},{1,21},{2,30},{3,23},{4,32},{5,25},{6,34},{7,27},{8,36},{9,... | collective-permute-start | bytes 798728 | tf_op jit(solution)/shard_map/ppermute | solution.py:257
  51.2 1.9 %collective-permute-start.5 = (bf16[1040,128]{1,0:T(8,128)(2,1)S(1)}, bf16[1040,128]{1,0:T(8,128)(2,1)S(1)}, u32[]{:S(2)}, u32[]{:S(2)}) collective-permute-start(bf16[1040,128]{1,0:T(8,128)(2,1)S(1)} %get-tuple-element.23.refs_1_), channel_id=1, source_target_pairs={{0,2},{1,47},{2,4},{3,1},{4,6},{5,3},{6,8},{7,5},{8,10},{9,7},{10,... | collective-permute-start | bytes 798728 | tf_op jit(solution)/shard_map/ppermute | solution.py:257
  53.9 2.2 %collective-permute-start.6 = (bf16[1040,128]{1,0:T(8,128)(2,1)S(1)}, bf16[1040,128]{1,0:T(8,128)(2,1)S(1)}, u32[]{:S(2)}, u32[]{:S(2)}) collective-permute-start(bf16[1040,128]{1,0:T(8,128)(2,1)S(1)} %get-tuple-element.21.refs_0_), channel_id=1, source_target_pairs={{0,26},{1,23},{2,28},{3,25},{4,30},{5,27},{6,32},{7,29},{8,34},{9,... | collective-permute-start | bytes 798728 | tf_op jit(solution)/shard_map/ppermute | solution.py:257
  56.1 4.4 %collective-permute-start.7 = (bf16[528,128]{1,0:T(8,128)(2,1)S(1)}, bf16[528,128]{1,0:T(8,128)(2,1)S(1)}, u32[]{:S(2)}, u32[]{:S(2)}) collective-permute-start(bf16[528,128]{1,0:T(8,128)(2,1)S(1)} %get-tuple-element.24), channel_id=1, source_target_pairs={{0,24},{1,25},{2,26},{3,27},{4,28},{5,29},{6,30},{7,31},{8,32},{9,... | collective-permute-start | bytes 405512 | tf_op jit(solution)/shard_map/ppermute | solution.py:257
  60.4 6.3 %collective-permute-done.7.refs_5_.refs_6_ = bf16[528,128]{1,0:T(8,128)(2,1)S(1)} collective-permute-done((bf16[528,128]{1,0:T(8,128)(2,1)S(1)}, bf16[528,128]{1,0:T(8,128)(2,1)S(1)}, u32[]{:S(2)}, u32[]{:S(2)}) %collective-permute-start.7) | collective-permute-done | bytes 135200 | tf_op jit(solution)/shard_map/ppermute | solution.py:257
  66.9 6.2 %collective-permute-start.8 = (bf16[3120,128]{1,0:T(8,128)(2,1)S(1)}, bf16[3120,128]{1,0:T(8,128)(2,1)S(1)}, u32[]{:S(2)}, u32[]{:S(2)}) collective-permute-start(bf16[3120,128]{1,0:T(8,128)(2,1)S(1)} %shard_map.148.refs_2_.refs_0_.refs_7_), channel_id=1, source_target_pairs={{0,2},{1,47},{2,4},{3,1},{4,6},{5,3},{6,8},{7,5},{8,10},{9,7},{10,... | collective-permute-start | bytes 2396168 | tf_op jit(solution)/shard_map/ppermute | solution.py:257
  73.2 8.9 %collective-permute-done.8.refs_3_.refs_1_.refs_8_ = bf16[3120,128]{1,0:T(8,128)(2,1)S(1)} collective-permute-done((bf16[3120,128]{1,0:T(8,128)(2,1)S(1)}, bf16[3120,128]{1,0:T(8,128)(2,1)S(1)}, u32[]{:S(2)}, u32[]{:S(2)}) %collective-permute-start.8) | collective-permute-done | bytes 798752 | tf_op jit(solution)/shard_map/ppermute | solution.py:257
  82.2 4.4 %collective-permute-start.9 = (bf16[2096,128]{1,0:T(8,128)(2,1)S(1)}, bf16[2096,128]{1,0:T(8,128)(2,1)S(1)}, u32[]{:S(2)}, u32[]{:S(2)}) collective-permute-start(bf16[2096,128]{1,0:T(8,128)(2,1)S(1)} %shard_map.149.refs_9_), channel_id=1, source_target_pairs={{0,30},{1,19},{2,32},{3,21},{4,34},{5,23},{6,36},{7,25},{8,38},{9,... | collective-permute-start | bytes 1609736 | tf_op jit(solution)/shard_map/ppermute | solution.py:257
  91.0 3.7 %collective-permute-start.12 = (bf16[5040,128]{1,0:T(8,128)(2,1)}, bf16[5040,128]{1,0:T(8,128)(2,1)}, u32[]{:S(2)}, u32[]{:S(2)}) collective-permute-start(bf16[5040,128]{1,0:T(8,128)(2,1)} %get-tuple-element.27), channel_id=1, source_target_pairs={{0,1},{1,0},{2,3},{3,2},{4,5},{5,4},{6,7},{7,6},{8,9},{9,8},{10,11... | collective-permute-start | bytes 3870728 | tf_op jit(solution)/shard_map/ppermute | solution.py:261
  94.6 7.3 %collective-permute-done.9.refs_2_.refs_0_.rest_0_ = bf16[2096,128]{1,0:T(8,128)(2,1)S(1)} collective-permute-done((bf16[2096,128]{1,0:T(8,128)(2,1)S(1)}, bf16[2096,128]{1,0:T(8,128)(2,1)S(1)}, u32[]{:S(2)}, u32[]{:S(2)}) %collective-permute-start.9) | collective-permute-done | bytes 536608 | tf_op jit(solution)/shard_map/ppermute | solution.py:257
  102.9 6.7 %collective-permute-start.10 = (bf16[48,128]{1,0:T(8,128)(2,1)S(1)}, bf16[48,128]{1,0:T(8,128)(2,1)S(1)}, u32[]{:S(2)}, u32[]{:S(2)}) collective-permute-start(bf16[48,128]{1,0:T(8,128)(2,1)S(1)} %get-tuple-element.25), channel_id=1, source_target_pairs={{0,1},{1,0},{2,3},{3,2},{4,5},{5,4},{6,7},{7,6},{8,9},{9,8},{10,11... | collective-permute-start | bytes 36872 | tf_op jit(solution)/shard_map/ppermute | solution.py:261
  110.3 4.4 %collective-permute-start.11 = (bf16[3072,128]{1,0:T(8,128)(2,1)}, bf16[3072,128]{1,0:T(8,128)(2,1)}, u32[]{:S(2)}, u32[]{:S(2)}) collective-permute-start(bf16[3072,128]{1,0:T(8,128)(2,1)} %get-tuple-element.26), channel_id=1, source_target_pairs={{0,2},{1,47},{2,4},{3,1},{4,6},{5,3},{6,8},{7,5},{8,10},{9,7},{10,... | collective-permute-start | bytes 2359304 | tf_op jit(solution)/shard_map/ppermute | solution.py:257
  118.1 1.7 %copy-done.1 = bf16[10368,128]{1,0:T(8,128)(2,1)S(1)} copy-done((bf16[10368,128]{1,0:T(8,128)(2,1)S(1)}, bf16[10368,128]{1,0:T(8,128)(2,1)}, u32[]{:S(2)}) %copy-start.1) | copy-done | bytes 2654232
  119.8 3.4 %shard_map.147.right_ref = bf16[6400,128]{1,0:T(8,128)(2,1)S(1)} custom-call(s32[3]{0:T(128)S(1)} %iota_add_fusion.2.index_ref, bf16[8,1296,128]{2,1,0:T(8,128)(2,1)S(1)} %bitcast.72, bf16[8,1296,128]{2,1,0:T(8,128)(2,1)S(1)} %bitcast.73), custom_call_target="tpu_custom_call" | custom-call | bytes 3145728 | tf_op jit(solution)/shard_map/pallas_call | solution.py:114
  125.6 6.6 %shard_map.152.refs_2_.rest_2_ = f32[13,128,128]{2,1,0:T(8,128)S(1)} custom-call(s32[5,84]{1,0:T(8,128)S(1)} %stack.59.table_ref, bf16[6400,128]{1,0:T(8,128)(2,1)S(1)} %shard_map.147.right_ref, bf16[5760,128]{1,0:T(8,128)(2,1)S(1)} %copy-done.9, bf16[5040,128]{1,0:T(8,128)(2,1)} %collective-permute-done.12.rest_1_), custom_call_target="tpu_custom_call" | custom-call | flops 2818572288 | bytes 2752512 | tf_op jit(solution)/shard_map/pallas_call | solution.py:201
  132.2 2.1 %shard_map.153 = bf16[3584,128]{1,0:T(8,128)(2,1)} custom-call(bf16[2096,128]{1,0:T(8,128)(2,1)S(1)} %collective-permute-done.9.refs_2_.refs_0_.rest_0_, bf16[3072,128]{1,0:T(8,128)(2,1)} %collective-permute-done.11.refs_1_.rest_1_, f32[13,128,128]{2,1,0:T(8,128)S(1)} %shard_map.152.refs_2_.rest_2_), custom_call_target="tpu_custom_call" | custom-call | bytes 1835008 | tf_op jit(solution)/shard_map/pallas_call | solution.py:157
  134.4 2.7 %collective-permute-start.13 = (bf16[3584,128]{1,0:T(8,128)(2,1)}, bf16[3584,128]{1,0:T(8,128)(2,1)}, u32[]{:S(2)}, u32[]{:S(2)}) collective-permute-start(bf16[3584,128]{1,0:T(8,128)(2,1)} %shard_map.153), channel_id=1, source_target_pairs={{0,1},{1,0},{2,3},{3,2},{4,5},{5,4},{6,7},{7,6},{8,9},{9,8},{10,11... | collective-permute-start | bytes 2752520 | tf_op jit(solution)/shard_map/ppermute | solution.py:261
  137.2 2.8 %shard_map.154.rest_1_ = f32[13,128,128]{2,1,0:T(8,128)S(1)} custom-call(s32[5,60]{1,0:T(8,128)S(1)} %stack.52.table_ref, bf16[6400,128]{1,0:T(8,128)(2,1)S(1)} %shard_map.147.right_ref, bf16[2096,128]{1,0:T(8,128)(2,1)S(1)} %collective-permute-done.9.refs_2_.refs_0_.rest_0_, bf16[3072,128]{1,0:T(8,128)(2,1)} %collective-permute-done.11.refs_1_.rest_1_, ...), custom_call_target="tpu_custom_call" | custom-call | flops 1073741824 | bytes 1048576 | tf_op jit(solution)/shard_map/pallas_call | solution.py:201
  140.0 3.2 %shard_map.155 = bf16[12,128,128]{2,1,0:T(8,128)(2,1)} custom-call(s32[5,60]{1,0:T(8,128)S(1)} %stack.52.table_ref, bf16[6400,128]{1,0:T(8,128)(2,1)S(1)} %shard_map.147.right_ref, bf16[3584,128]{1,0:T(8,128)(2,1)} %collective-permute-done.13.rest_0_, f32[13,128,128]{2,1,0:T(8,128)S(1)} %shard_map.154.rest_1_), custom_call_target="tpu_custom_call" | custom-call | flops 939524096 | bytes 917504 | tf_op jit(solution)/shard_map/pallas_call | solution.py:201
  (127 shorter events, 19.6 us)
Async XLA Ops:
  6.5 109.8 %all-gather.5.cloned.1.call-start = ((), (), s32[]{:S(2)}) async-start(), calls=%async_computation | async-start | bytes 2985984 | tf_op jit(solution)/shard_map/all_gather | solution.py:280
  9.8 106.6 %all-gather.7.cloned.1.call-start = ((), (), s32[]{:S(2)}) async-start(), calls=%async_computation.1 | async-start | bytes 2985984 | tf_op jit(solution)/shard_map/all_gather | solution.py:325
  9.8 29.0 %collective-permute-start = (bf16[1296,128]{1,0:T(8,128)(2,1)S(1)}, bf16[1296,128]{1,0:T(8,128)(2,1)S(1)}, u32[]{:S(2)}, u32[]{:S(2)}) collective-permute-start(bf16[1296,128]{1,0:T(8,128)(2,1)S(1)} %get-tuple-element.18), channel_id=1, source_target_pairs={{0,384},{384,0},{1,385},{385,1},{2,386},{386,2},{3,387},{387,3},{4... | collective-permute-start | bytes 995336 | tf_op jit(solution)/shard_map/ppermute | solution.py:281
  13.8 14.3 %collective-permute-start.1 = (bf16[16,128,128]{2,1,0:T(8,128)(2,1)}, bf16[16,128,128]{2,1,0:T(8,128)(2,1)S(1)}, u32[]{:S(2)}, u32[]{:S(2)}) collective-permute-start(bf16[16,128,128]{2,1,0:T(8,128)(2,1)} %bitcast.75), channel_id=1, source_target_pairs={{0,1},{1,0},{2,3},{3,2},{4,5},{5,4},{6,7},{7,6},{8,9},{9,8},{10,11... | collective-permute-start | bytes 1572872 | tf_op jit(solution)/shard_map/ppermute | solution.py:261
  24.9 3.0 %collective-permute-start.2 = (bf16[16,128]{1,0:T(8,128)(2,1)S(1)}, bf16[16,128]{1,0:T(8,128)(2,1)S(1)}, u32[]{:S(2)}, u32[]{:S(2)}) collective-permute-start(bf16[16,128]{1,0:T(8,128)(2,1)S(1)} %fusion.37), channel_id=1, source_target_pairs={{0,1},{1,0},{2,3},{3,2},{4,5},{5,4},{6,7},{7,6},{8,9},{9,8},{10,11... | collective-permute-start | bytes 12296 | tf_op jit(solution)/shard_map/ppermute | solution.py:261
  29.7 37.0 %copy-start.4 = (bf16[1040,128]{1,0:T(8,128)(2,1)}, bf16[1040,128]{1,0:T(8,128)(2,1)S(1)}, u32[]{:S(2)}) copy-start(bf16[1040,128]{1,0:T(8,128)(2,1)S(1)} %get-tuple-element.22.refs_0_) | copy-start | bytes 798724
  29.7 43.5 %copy-start.11 = (s32[60]{0:T(128)S(1)}, s32[60]{0:T(128)}, u32[]{:S(2)}) copy-start(s32[60]{0:T(128)} %constant.434.clone) | copy-start | bytes 724
  29.7 43.5 %copy-start.18 = (s32[60]{0:T(128)S(1)}, s32[60]{0:T(128)}, u32[]{:S(2)}) copy-start(s32[60]{0:T(128)} %constant.436.clone) | copy-start | bytes 724
  29.8 43.5 %copy-start.19 = (s32[60]{0:T(128)S(1)}, s32[60]{0:T(128)}, u32[]{:S(2)}) copy-start(s32[60]{0:T(128)} %constant.435.clone) | copy-start | bytes 724
  29.8 15.3 %collective-permute-start.3 = (bf16[1040,128]{1,0:T(8,128)(2,1)S(1)}, bf16[1040,128]{1,0:T(8,128)(2,1)S(1)}, u32[]{:S(2)}, u32[]{:S(2)}) collective-permute-start(bf16[1040,128]{1,0:T(8,128)(2,1)S(1)} %get-tuple-element.19), channel_id=1, source_target_pairs={{0,4},{1,45},{2,6},{3,47},{4,8},{5,1},{6,10},{7,3},{8,12},{9,5},{1... | collective-permute-start | bytes 798728 | tf_op jit(solution)/shard_map/ppermute | solution.py:257
  45.1 21.7 %collective-permute-start.4 = (bf16[1040,128]{1,0:T(8,128)(2,1)S(1)}, bf16[1040,128]{1,0:T(8,128)(2,1)S(1)}, u32[]{:S(2)}, u32[]{:S(2)}) collective-permute-start(bf16[1040,128]{1,0:T(8,128)(2,1)S(1)} %get-tuple-element.22.refs_0_), channel_id=1, source_target_pairs={{0,28},{1,21},{2,30},{3,23},{4,32},{5,25},{6,34},{7,27},{8,36},{9,... | collective-permute-start | bytes 798728 | tf_op jit(solution)/shard_map/ppermute | solution.py:257
  51.2 15.5 %collective-permute-start.5 = (bf16[1040,128]{1,0:T(8,128)(2,1)S(1)}, bf16[1040,128]{1,0:T(8,128)(2,1)S(1)}, u32[]{:S(2)}, u32[]{:S(2)}) collective-permute-start(bf16[1040,128]{1,0:T(8,128)(2,1)S(1)} %get-tuple-element.23.refs_1_), channel_id=1, source_target_pairs={{0,2},{1,47},{2,4},{3,1},{4,6},{5,3},{6,8},{7,5},{8,10},{9,7},{10,... | collective-permute-start | bytes 798728 | tf_op jit(solution)/shard_map/ppermute | solution.py:257
  53.9 12.9 %collective-permute-start.6 = (bf16[1040,128]{1,0:T(8,128)(2,1)S(1)}, bf16[1040,128]{1,0:T(8,128)(2,1)S(1)}, u32[]{:S(2)}, u32[]{:S(2)}) collective-permute-start(bf16[1040,128]{1,0:T(8,128)(2,1)S(1)} %get-tuple-element.21.refs_0_), channel_id=1, source_target_pairs={{0,26},{1,23},{2,28},{3,25},{4,30},{5,27},{6,32},{7,29},{8,34},{9,... | collective-permute-start | bytes 798728 | tf_op jit(solution)/shard_map/ppermute | solution.py:257
  56.1 10.7 %collective-permute-start.7 = (bf16[528,128]{1,0:T(8,128)(2,1)S(1)}, bf16[528,128]{1,0:T(8,128)(2,1)S(1)}, u32[]{:S(2)}, u32[]{:S(2)}) collective-permute-start(bf16[528,128]{1,0:T(8,128)(2,1)S(1)} %get-tuple-element.24), channel_id=1, source_target_pairs={{0,24},{1,25},{2,26},{3,27},{4,28},{5,29},{6,30},{7,31},{8,32},{9,... | collective-permute-start | bytes 405512 | tf_op jit(solution)/shard_map/ppermute | solution.py:257
  66.8 19.7 %copy-start.12 = (s32[84]{0:T(128)S(1)}, s32[84]{0:T(128)}, u32[]{:S(2)}) copy-start(s32[84]{0:T(128)} %constant.429.clone) | copy-start | bytes 1012
  66.9 19.7 %copy-start.16 = (s32[84]{0:T(128)S(1)}, s32[84]{0:T(128)}, u32[]{:S(2)}) copy-start(s32[84]{0:T(128)} %constant.431.clone) | copy-start | bytes 1012
  66.9 15.3 %collective-permute-start.8 = (bf16[3120,128]{1,0:T(8,128)(2,1)S(1)}, bf16[3120,128]{1,0:T(8,128)(2,1)S(1)}, u32[]{:S(2)}, u32[]{:S(2)}) collective-permute-start(bf16[3120,128]{1,0:T(8,128)(2,1)S(1)} %shard_map.148.refs_2_.refs_0_.refs_7_), channel_id=1, source_target_pairs={{0,2},{1,47},{2,4},{3,1},{4,6},{5,3},{6,8},{7,5},{8,10},{9,7},{10,... | collective-permute-start | bytes 2396168 | tf_op jit(solution)/shard_map/ppermute | solution.py:257
  82.2 19.7 %collective-permute-start.9 = (bf16[2096,128]{1,0:T(8,128)(2,1)S(1)}, bf16[2096,128]{1,0:T(8,128)(2,1)S(1)}, u32[]{:S(2)}, u32[]{:S(2)}) collective-permute-start(bf16[2096,128]{1,0:T(8,128)(2,1)S(1)} %shard_map.149.refs_9_), channel_id=1, source_target_pairs={{0,30},{1,19},{2,32},{3,21},{4,34},{5,23},{6,36},{7,25},{8,38},{9,... | collective-permute-start | bytes 1609736 | tf_op jit(solution)/shard_map/ppermute | solution.py:257
  91.0 24.2 %copy-start.13 = (s32[60]{0:T(128)S(1)}, s32[60]{0:T(128)}, u32[]{:S(2)}) copy-start(s32[60]{0:T(128)} %constant.437.clone) | copy-start | bytes 724
  91.0 25.3 %copy-start.14 = (s32[84]{0:T(128)S(1)}, s32[84]{0:T(128)}, u32[]{:S(2)}) copy-start(s32[84]{0:T(128)} %constant.432.clone) | copy-start | bytes 1012
  91.0 24.2 %collective-permute-start.12 = (bf16[5040,128]{1,0:T(8,128)(2,1)}, bf16[5040,128]{1,0:T(8,128)(2,1)}, u32[]{:S(2)}, u32[]{:S(2)}) collective-permute-start(bf16[5040,128]{1,0:T(8,128)(2,1)} %get-tuple-element.27), channel_id=1, source_target_pairs={{0,1},{1,0},{2,3},{3,2},{4,5},{5,4},{6,7},{7,6},{8,9},{9,8},{10,11... | collective-permute-start | bytes 3870728 | tf_op jit(solution)/shard_map/ppermute | solution.py:261
  102.9 11.8 %collective-permute-start.10 = (bf16[48,128]{1,0:T(8,128)(2,1)S(1)}, bf16[48,128]{1,0:T(8,128)(2,1)S(1)}, u32[]{:S(2)}, u32[]{:S(2)}) collective-permute-start(bf16[48,128]{1,0:T(8,128)(2,1)S(1)} %get-tuple-element.25), channel_id=1, source_target_pairs={{0,1},{1,0},{2,3},{3,2},{4,5},{5,4},{6,7},{7,6},{8,9},{9,8},{10,11... | collective-permute-start | bytes 36872 | tf_op jit(solution)/shard_map/ppermute | solution.py:261
  110.3 21.9 %collective-permute-start.11 = (bf16[3072,128]{1,0:T(8,128)(2,1)}, bf16[3072,128]{1,0:T(8,128)(2,1)}, u32[]{:S(2)}, u32[]{:S(2)}) collective-permute-start(bf16[3072,128]{1,0:T(8,128)(2,1)} %get-tuple-element.26), channel_id=1, source_target_pairs={{0,2},{1,47},{2,4},{3,1},{4,6},{5,3},{6,8},{7,5},{8,10},{9,7},{10,... | collective-permute-start | bytes 2359304 | tf_op jit(solution)/shard_map/ppermute | solution.py:257
  134.4 5.6 %collective-permute-start.13 = (bf16[3584,128]{1,0:T(8,128)(2,1)}, bf16[3584,128]{1,0:T(8,128)(2,1)}, u32[]{:S(2)}, u32[]{:S(2)}) collective-permute-start(bf16[3584,128]{1,0:T(8,128)(2,1)} %shard_map.153), channel_id=1, source_target_pairs={{0,1},{1,0},{2,3},{3,2},{4,5},{5,4},{6,7},{7,6},{8,9},{9,8},{10,11... | collective-permute-start | bytes 2752520 | tf_op jit(solution)/shard_map/ppermute | solution.py:261
  (14 other events, 49.9 us)
Sparse Core Ops, SparseCore 0:
  9.9 52.3 all-gather.4
  64.7 46.7 all-gather.6

commit v7 on v5

--- a/solution.py
+++ b/solution.py
@@ -280,7 +280,6 @@
     near.append((own, 8 * BLK, 0, True))
     for array, (names, distance) in zip(arrays, starts, strict=True):
         near.append((send(array, names, distance), 2 * len(names) * BLK, distance, True))
-    crossed = near.pop()
 
     shift = (2 * q + core + jnp.arange(18, dtype=jnp.int32)) % 16
     b_code = b_own_code.reshape(16) + 1
@@ -292,36 +291,40 @@
     right = lax.all_to_all(right, ROW, 0, 0, tiled=True)
 
     names = items([(2, 1), (6, 13), (3, 2), (7, 14), (0, 14), (4, 2)])
-    (up_in,) = packed([(blocks(names), True)], near)
+    long_names = items([(1, 1), (5, 13)])
+    up_in, long_in = packed([(blocks(names), True), (blocks(long_names), False)], near)
     sources.append(up_in)
     up3 = send(up_in, names, 1)
+    send(long_in, long_names, 15)
     middle = [(up3 - 1, 24 * BLK, 0, False), (up3, 24 * BLK, 1, False)]
 
-    names = items([(1, 1), (5, 13), (2, 2), (6, 14)])
-    (up_in,) = packed([(blocks(names), True)], middle)
-    up6 = send(up_in, names, 15)
-    middle.append(crossed)
-    far = middle + [(up6, 16 * BLK, 15, False)]
+    names = items([(0, 15), (4, 3), (1, 16), (5, 4)])
+    long_names = items([(2, 2), (6, 14)])
+    long_in, up_in = packed([(blocks(long_names), True), (blocks(names), False)], middle)
+    long = send(long_in, long_names, 15)
+    far = middle + [(long, 8 * BLK, 15, False)]
+    up7 = send(up_in, names, 1)
+    send(sources[long], items([(2, 17), (6, 5)]), 1)
 
     early = items([(1, 1), (5, 13), (2, 2), (6, 14), (3, 3), (7, 15)]) + [(4, 12, 0)]
     early += items([(2, 1), (6, 13), (3, 2), (7, 14), (0, 15), (4, 3)]) + [(5, 12, 0)]
-
-    def pass_on(names, noted, notes=(), after=()):
+    mine = items([(0, 0), (1, 0)]) + early
+    late = items([(1, 16), (5, 4), (2, 17), (6, 5), (0, 16), (4, 4), (1, 17), (5, 5)])
+    last = items([(2, 18), (6, 6)])
+
+    def pass_on(names, kept=None, notes=(), after=()):
         entries = [(at[name][0], at[name][1] + b) for name in names for b, _ in passed_on(name)]
-        (array,) = packed([(entries, noted)], notes, after)
+        spec = [(entries, bool(notes))]
+        if kept:
+            spec.append(([(at[name][0], at[name][1] + b) for name in kept for b, _ in wanted(name)], False))
+        array, *own_part = packed(spec, notes, after)
         received = from_other_core(array)
         end = len(entries) * BLK
-        return received, (array[end:], received[end:])
-
-    early_other, early_notes = pass_on(early, True, middle, (up_in,))
-
-    names = items([(1, 16), (5, 4), (2, 17), (6, 5), (0, 15), (4, 3)])
-    up_in, notes = packed([(blocks(names), False), ((), True)], far)
-    send(up_in, names, 1)
-    notes = (notes, from_other_core(notes))
-
-    late = items([(1, 16), (5, 4), (2, 17), (6, 5)])
-    late += items([(1, 17), (5, 5), (2, 18), (6, 6), (0, 16), (4, 4)])
+        return received, own_part, (array[end:], received[end:])
+
+    early_other, early_own, early_notes = pass_on(early, mine, middle, (sources[up7],))
+    late_other, _, notes = pass_on(late, None, far)
+    last_other, _, _ = pass_on(last)
 
     def part_of(names):
         by_source = {}
@@ -350,13 +353,13 @@
         lefts, counts = [array for array, _ in part], tuple(len(rows) for _, rows in part)
         return product(table, right, lefts, counts, base, before, last), base + sum(counts)
 
-    part = part_of(items([(0, 0), (1, 0)]) + early) + received_of(early_other, early)
+    rows = []
+    for name in mine:
+        rows += [(len(rows) * BLK + n * BLK, 0, name[2], name[1], w) for n, (_, w) in enumerate(wanted(name))]
+    part = [(early_own[0], rows)] + received_of(early_other, early)
     sums, _ = product_of(table_of((part,), early_notes), part, 0)
-    parts = [part_of(late), received_of(None, late)]
-    table = table_of(parts, notes)
-    late_other, _ = pass_on(late, False, (), (sums,))
-    sums, base = product_of(table, parts[0], 0, sums)
-    out, _ = product_of(table, received_of(late_other, late), base, sums, last=True)
+    part = part_of(late + last) + received_of(late_other, late) + received_of(last_other, last)
+    out, _ = product_of(table_of((part,), notes), part, 0, sums, last=True)
     return out[None, None]
 
 

time: 129 us -> 138 us (1.070)
  the two profiles are of different devices: /device:TPU:201 before, /device:TPU:1 now
where the time goes in v7:
time: 138 us; the launch traced here: 136 us
  starting transfers between devices  68.6 us (50%)
  waiting for transfers between devices  38.6 us (28%)
  Pallas kernels  16.2 us (12%)
  local copies, waits for them, and re-layouts  8.45 us (6%)
  other arithmetic  3.87 us (3%)
    ppermute x10, waiting for transfers between devices, moved(): return lax.ppermute(array, COL, route)  37.6 us
    ppermute x10, starting transfers between devices, moved(): return lax.ppermute(array, COL, route)  33.6 us
    ppermute x5, starting transfers between devices, from_other_core(): return lax.ppermute(array, 'core', [(0, 1), (1, 0)])  27.4 us
    pallas_call x2, Pallas kernels, product(): pl.pallas_call(functools.partial(product_kernel, counts, base, before is...  12.2 us
    all_to_all x1, starting transfers between devices, local(): right = lax.all_to_all(right, ROW, 0, 0, tiled=True)  7.58 us
    unnamed x59, local copies, waits for them, and re-layouts  7.25 us
  transfers between devices with their start and end apart: 16, of which 5 were waited for; matrix products, arithmetic and copies ran while one was open for 4% of the time, Pallas kernels for 7%

profile of v7, /device:TPU:1, one launch (start us, length us, event | category | flops | bytes accessed | tf_op | source)
XLA Modules:
  0.0 136.4 jit_solution(6794409588183930383)
XLA Ops:
  0.0 12.5 %collective-permute-start = (bf16[16,128,128]{2,1,0:T(8,128)(2,1)}, bf16[16,128,128]{2,1,0:T(8,128)(2,1)S(1)}, u32[]{:S(2)}, u32[]{:S(2)}) collective-permute-start(bf16[16,128,128]{2,1,0:T(8,128)(2,1)} %bitcast.74), channel_id=1, source_target_pairs={{0,1},{1,0},{2,3},{3,2},{4,5},{5,4},{6,7},{7,6},{8,9},{9,8},{10,11... | collective-permute-start | bytes 1572872 | tf_op jit(solution)/shard_map/ppermute | solution.py:230
  13.3 1.9 %collective-permute-start.1 = (bf16[16,128]{1,0:T(8,128)(2,1)S(1)}, bf16[16,128]{1,0:T(8,128)(2,1)S(1)}, u32[]{:S(2)}, u32[]{:S(2)}) collective-permute-start(bf16[16,128]{1,0:T(8,128)(2,1)S(1)} %fusion.31), channel_id=1, source_target_pairs={{0,1},{1,0},{2,3},{3,2},{4,5},{5,4},{6,7},{7,6},{8,9},{9,8},{10,11... | collective-permute-start | bytes 12296 | tf_op jit(solution)/shard_map/ppermute | solution.py:230
  18.1 7.7 %collective-permute-start.2 = (bf16[1040,128]{1,0:T(8,128)(2,1)S(1)}, bf16[1040,128]{1,0:T(8,128)(2,1)S(1)}, u32[]{:S(2)}, u32[]{:S(2)}) collective-permute-start(bf16[1040,128]{1,0:T(8,128)(2,1)S(1)} %get-tuple-element.17), channel_id=1, source_target_pairs={{0,4},{1,45},{2,6},{3,47},{4,8},{5,1},{6,10},{7,3},{8,12},{9,5},{1... | collective-permute-start | bytes 798728 | tf_op jit(solution)/shard_map/ppermute | solution.py:226
  25.9 1.9 %collective-permute-start.5 = (bf16[1040,128]{1,0:T(8,128)(2,1)S(1)}, bf16[1040,128]{1,0:T(8,128)(2,1)S(1)}, u32[]{:S(2)}, u32[]{:S(2)}) collective-permute-start(bf16[1040,128]{1,0:T(8,128)(2,1)S(1)} %get-tuple-element.16.refs_0_), channel_id=1, source_target_pairs={{0,26},{1,23},{2,28},{3,25},{4,30},{5,27},{6,32},{7,29},{8,34},{9,... | collective-permute-start | bytes 798728 | tf_op jit(solution)/shard_map/ppermute | solution.py:226
  27.8 3.6 %collective-permute-start.3 = (bf16[1040,128]{1,0:T(8,128)(2,1)S(1)}, bf16[1040,128]{1,0:T(8,128)(2,1)S(1)}, u32[]{:S(2)}, u32[]{:S(2)}) collective-permute-start(bf16[1040,128]{1,0:T(8,128)(2,1)S(1)} %get-tuple-element.18.refs_0_), channel_id=1, source_target_pairs={{0,28},{1,21},{2,30},{3,23},{4,32},{5,25},{6,34},{7,27},{8,36},{9,... | collective-permute-start | bytes 798728 | tf_op jit(solution)/shard_map/ppermute | solution.py:226
  32.1 4.0 %collective-permute-start.4 = (bf16[1040,128]{1,0:T(8,128)(2,1)S(1)}, bf16[1040,128]{1,0:T(8,128)(2,1)S(1)}, u32[]{:S(2)}, u32[]{:S(2)}) collective-permute-start(bf16[1040,128]{1,0:T(8,128)(2,1)S(1)} %get-tuple-element.19.refs_1_), channel_id=1, source_target_pairs={{0,2},{1,47},{2,4},{3,1},{4,6},{5,3},{6,8},{7,5},{8,10},{9,7},{10,... | collective-permute-start | bytes 798728 | tf_op jit(solution)/shard_map/ppermute | solution.py:226
  37.5 2.5 %collective-permute-start.6 = (bf16[528,128]{1,0:T(8,128)(2,1)S(1)}, bf16[528,128]{1,0:T(8,128)(2,1)S(1)}, u32[]{:S(2)}, u32[]{:S(2)}) collective-permute-start(bf16[528,128]{1,0:T(8,128)(2,1)S(1)} %get-tuple-element.20), channel_id=1, source_target_pairs={{0,24},{1,25},{2,26},{3,27},{4,28},{5,29},{6,30},{7,31},{8,32},{9,... | collective-permute-start | bytes 405512 | tf_op jit(solution)/shard_map/ppermute | solution.py:226
  40.1 7.7 %collective-permute-done.6.refs_5_.refs_6_ = bf16[528,128]{1,0:T(8,128)(2,1)S(1)} collective-permute-done((bf16[528,128]{1,0:T(8,128)(2,1)S(1)}, bf16[528,128]{1,0:T(8,128)(2,1)S(1)}, u32[]{:S(2)}, u32[]{:S(2)}) %collective-permute-start.6) | collective-permute-done | bytes 135200 | tf_op jit(solution)/shard_map/ppermute | solution.py:226
  49.1 5.3 %collective-permute-start.7 = (bf16[3120,128]{1,0:T(8,128)(2,1)S(1)}, bf16[3120,128]{1,0:T(8,128)(2,1)S(1)}, u32[]{:S(2)}, u32[]{:S(2)}) collective-permute-start(bf16[3120,128]{1,0:T(8,128)(2,1)S(1)} %get-tuple-element.21.refs_0_.refs_7_), channel_id=1, source_target_pairs={{0,2},{1,47},{2,4},{3,1},{4,6},{5,3},{6,8},{7,5},{8,10},{9,7},{10,... | collective-permute-start | bytes 2396168 | tf_op jit(solution)/shard_map/ppermute | solution.py:226
  54.7 1.8 %shard_map.145 = bf16[16,400,128]{2,1,0:T(8,128)(2,1)} custom-call(s32[18]{0:T(128)S(1)} %and_select_fusion.13.index_ref, bf16[16,128,128]{2,1,0:T(8,128)(2,1)S(1)} %bitcast.73, bf16[16,16,128]{2,1,0:T(8,128)(2,1)S(1)} %broadcast_in_dim.226.code_ref), custom_call_target="tpu_custom_call" | custom-call | bytes 3145728 | tf_op jit(solution)/shard_map/pallas_call | solution.py:84
  56.5 7.6 %all-to-all-start = ((bf16[16,400,128]{2,1,0:T(8,128)(2,1)}), bf16[16,400,128]{2,1,0:T(8,128)(2,1)}, u32[]{:S(2)}, u32[]{:S(2)}) async-start(bf16[16,400,128]{2,1,0:T(8,128)(2,1)} %shard_map.145), calls=%async_computation | async-start | bytes 3276800 | tf_op jit(solution)/shard_map/all_to_all | solution.py:291
  64.1 1.9 %collective-permute-start.8 = (bf16[1024,128]{1,0:T(8,128)(2,1)S(1)}, bf16[1024,128]{1,0:T(8,128)(2,1)S(1)}, u32[]{:S(2)}, u32[]{:S(2)}) collective-permute-start(bf16[1024,128]{1,0:T(8,128)(2,1)S(1)} %copy-done.17), channel_id=1, source_target_pairs={{0,30},{1,19},{2,32},{3,21},{4,34},{5,23},{6,36},{7,25},{8,38},{9,... | collective-permute-start | bytes 786440 | tf_op jit(solution)/shard_map/ppermute | solution.py:226
  66.1 13.0 %collective-permute-done.8.refs_2_.rest_0_ = bf16[1024,128]{1,0:T(8,128)(2,1)S(1)} collective-permute-done((bf16[1024,128]{1,0:T(8,128)(2,1)S(1)}, bf16[1024,128]{1,0:T(8,128)(2,1)S(1)}, u32[]{:S(2)}, u32[]{:S(2)}) %collective-permute-start.8) | collective-permute-done | bytes 262176 | tf_op jit(solution)/shard_map/ppermute | solution.py:226
  79.1 1.9 %collective-permute-start.10 = (bf16[2048,128]{1,0:T(8,128)(2,1)S(1)}, bf16[2048,128]{1,0:T(8,128)(2,1)S(1)}, u32[]{:S(2)}, u32[]{:S(2)}) collective-permute-start(bf16[2048,128]{1,0:T(8,128)(2,1)S(1)} %get-tuple-element.24), channel_id=1, source_target_pairs={{0,2},{1,47},{2,4},{3,1},{4,6},{5,3},{6,8},{7,5},{8,10},{9,7},{10,... | collective-permute-start | bytes 1572872 | tf_op jit(solution)/shard_map/ppermute | solution.py:226
  81.1 2.6 %collective-permute-start.9 = (bf16[1072,128]{1,0:T(8,128)(2,1)S(1)}, bf16[1072,128]{1,0:T(8,128)(2,1)S(1)}, u32[]{:S(2)}, u32[]{:S(2)}) collective-permute-start(bf16[1072,128]{1,0:T(8,128)(2,1)S(1)} %get-tuple-element.23), channel_id=1, source_target_pairs={{0,30},{1,19},{2,32},{3,21},{4,34},{5,23},{6,36},{7,25},{8,38},{9,... | collective-permute-start | bytes 823304 | tf_op jit(solution)/shard_map/ppermute | solution.py:226
  83.8 16.7 %collective-permute-done.9.refs_3_.rest_1_ = bf16[1072,128]{1,0:T(8,128)(2,1)S(1)} collective-permute-done((bf16[1072,128]{1,0:T(8,128)(2,1)S(1)}, bf16[1072,128]{1,0:T(8,128)(2,1)S(1)}, u32[]{:S(2)}, u32[]{:S(2)}) %collective-permute-start.9) | collective-permute-done | bytes 274464 | tf_op jit(solution)/shard_map/ppermute | solution.py:226
  100.6 4.4 %collective-permute-start.11 = (bf16[3120,128]{1,0:T(8,128)(2,1)S(1)}, bf16[3120,128]{1,0:T(8,128)(2,1)S(1)}, u32[]{:S(2)}, u32[]{:S(2)}) collective-permute-start(bf16[3120,128]{1,0:T(8,128)(2,1)S(1)} %shard_map.149), channel_id=1, source_target_pairs={{0,1},{1,0},{2,3},{3,2},{4,5},{5,4},{6,7},{7,6},{8,9},{9,8},{10,11... | collective-permute-start | bytes 2396168 | tf_op jit(solution)/shard_map/ppermute | solution.py:230
  105.1 2.1 %collective-permute-start.12 = (bf16[1072,128]{1,0:T(8,128)(2,1)S(1)}, bf16[1072,128]{1,0:T(8,128)(2,1)S(1)}, u32[]{:S(2)}, u32[]{:S(2)}) collective-permute-start(bf16[1072,128]{1,0:T(8,128)(2,1)S(1)} %collective-permute-done.9.refs_3_.rest_1_), channel_id=1, source_target_pairs={{0,2},{1,47},{2,4},{3,1},{4,6},{5,3},{6,8},{7,5},{8,10},{9,7},{10,... | collective-permute-start | bytes 823304 | tf_op jit(solution)/shard_map/ppermute | solution.py:226
  107.2 1.3 shard_map.151
  110.3 1.9 %collective-permute-start.14 = (bf16[5040,128]{1,0:T(8,128)(2,1)}, bf16[5040,128]{1,0:T(8,128)(2,1)S(1)}, u32[]{:S(2)}, u32[]{:S(2)}) collective-permute-start(bf16[5040,128]{1,0:T(8,128)(2,1)} %get-tuple-element.25), channel_id=1, source_target_pairs={{0,1},{1,0},{2,3},{3,2},{4,5},{5,4},{6,7},{7,6},{8,9},{9,8},{10,11... | collective-permute-start | bytes 3870728 | tf_op jit(solution)/shard_map/ppermute | solution.py:230
  112.5 6.7 %collective-permute-start.13 = (bf16[512,128]{1,0:T(8,128)(2,1)S(1)}, bf16[512,128]{1,0:T(8,128)(2,1)S(1)}, u32[]{:S(2)}, u32[]{:S(2)}) collective-permute-start(bf16[512,128]{1,0:T(8,128)(2,1)S(1)} %shard_map.150), channel_id=1, source_target_pairs={{0,1},{1,0},{2,3},{3,2},{4,5},{5,4},{6,7},{7,6},{8,9},{9,8},{10,11... | collective-permute-start | bytes 393224 | tf_op jit(solution)/shard_map/ppermute | solution.py:230
  122.8 1.4 copy-done.15
  124.2 6.8 %shard_map.152.rest_6_ = f32[13,128,128]{2,1,0:T(8,128)S(1)} custom-call(s32[7,84]{1,0:T(8,128)S(1)} %stack.73.table_ref, bf16[16,400,128]{2,1,0:T(8,128)(2,1)} %all-to-all-done.right_ref, bf16[5760,128]{1,0:T(8,128)(2,1)S(1)} %copy-done.15, bf16[5040,128]{1,0:T(8,128)(2,1)S(1)} %collective-permute-done.14.rest_1_), custom_call_target="tpu_custom_call" | custom-call | flops 2818572288 | bytes 2752512 | tf_op jit(solution)/shard_map/pallas_call | solution.py:171
  131.0 5.4 %shard_map.153 = bf16[12,128,128]{2,1,0:T(8,128)(2,1)} custom-call(s32[7,60]{1,0:T(8,128)S(1)} %stack.67.table_ref, bf16[16,400,128]{2,1,0:T(8,128)(2,1)} %all-to-all-done.right_ref, bf16[1024,128]{1,0:T(8,128)(2,1)S(1)} %collective-permute-done.8.refs_2_.rest_0_, bf16[1072,128]{1,0:T(8,128)(2,1)S(1)} %copy-done.7, ...), custom_call_target="tpu_custom_call" | custom-call | flops 2013265920 | bytes 1966080 | tf_op jit(solution)/shard_map/pallas_call | solution.py:171
  (140 shorter events, 13.0 us)
Async XLA Ops:
  0.0 54.7 %copy-start.2 = (bf16[1,1,16,1,128,128]{5,4,3,2,1,0:T(8,128)(2,1)S(1)}, bf16[1,1,16,1,128,128]{5,4,3,2,1,0:T(8,128)(2,1)}, u32[]{:S(2)}) copy-start(bf16[1,1,16,1,128,128]{5,4,3,2,1,0:T(8,128)(2,1)} %param.17) | copy-start | bytes 1572868
  0.0 16.4 %collective-permute-start = (bf16[16,128,128]{2,1,0:T(8,128)(2,1)}, bf16[16,128,128]{2,1,0:T(8,128)(2,1)S(1)}, u32[]{:S(2)}, u32[]{:S(2)}) collective-permute-start(bf16[16,128,128]{2,1,0:T(8,128)(2,1)} %bitcast.74), channel_id=1, source_target_pairs={{0,1},{1,0},{2,3},{3,2},{4,5},{5,4},{6,7},{7,6},{8,9},{9,8},{10,11... | collective-permute-start | bytes 1572872 | tf_op jit(solution)/shard_map/ppermute | solution.py:230
  13.3 3.0 %collective-permute-start.1 = (bf16[16,128]{1,0:T(8,128)(2,1)S(1)}, bf16[16,128]{1,0:T(8,128)(2,1)S(1)}, u32[]{:S(2)}, u32[]{:S(2)}) collective-permute-start(bf16[16,128]{1,0:T(8,128)(2,1)S(1)} %fusion.31), channel_id=1, source_target_pairs={{0,1},{1,0},{2,3},{3,2},{4,5},{5,4},{6,7},{7,6},{8,9},{9,8},{10,11... | collective-permute-start | bytes 12296 | tf_op jit(solution)/shard_map/ppermute | solution.py:230
  18.1 29.7 %collective-permute-start.2 = (bf16[1040,128]{1,0:T(8,128)(2,1)S(1)}, bf16[1040,128]{1,0:T(8,128)(2,1)S(1)}, u32[]{:S(2)}, u32[]{:S(2)}) collective-permute-start(bf16[1040,128]{1,0:T(8,128)(2,1)S(1)} %get-tuple-element.17), channel_id=1, source_target_pairs={{0,4},{1,45},{2,6},{3,47},{4,8},{5,1},{6,10},{7,3},{8,12},{9,5},{1... | collective-permute-start | bytes 798728 | tf_op jit(solution)/shard_map/ppermute | solution.py:226
  25.9 21.9 %collective-permute-start.5 = (bf16[1040,128]{1,0:T(8,128)(2,1)S(1)}, bf16[1040,128]{1,0:T(8,128)(2,1)S(1)}, u32[]{:S(2)}, u32[]{:S(2)}) collective-permute-start(bf16[1040,128]{1,0:T(8,128)(2,1)S(1)} %get-tuple-element.16.refs_0_), channel_id=1, source_target_pairs={{0,26},{1,23},{2,28},{3,25},{4,30},{5,27},{6,32},{7,29},{8,34},{9,... | collective-permute-start | bytes 798728 | tf_op jit(solution)/shard_map/ppermute | solution.py:226
  27.8 20.0 %collective-permute-start.3 = (bf16[1040,128]{1,0:T(8,128)(2,1)S(1)}, bf16[1040,128]{1,0:T(8,128)(2,1)S(1)}, u32[]{:S(2)}, u32[]{:S(2)}) collective-permute-start(bf16[1040,128]{1,0:T(8,128)(2,1)S(1)} %get-tuple-element.18.refs_0_), channel_id=1, source_target_pairs={{0,28},{1,21},{2,30},{3,23},{4,32},{5,25},{6,34},{7,27},{8,36},{9,... | collective-permute-start | bytes 798728 | tf_op jit(solution)/shard_map/ppermute | solution.py:226
  32.1 15.7 %collective-permute-start.4 = (bf16[1040,128]{1,0:T(8,128)(2,1)S(1)}, bf16[1040,128]{1,0:T(8,128)(2,1)S(1)}, u32[]{:S(2)}, u32[]{:S(2)}) collective-permute-start(bf16[1040,128]{1,0:T(8,128)(2,1)S(1)} %get-tuple-element.19.refs_1_), channel_id=1, source_target_pairs={{0,2},{1,47},{2,4},{3,1},{4,6},{5,3},{6,8},{7,5},{8,10},{9,7},{10,... | collective-permute-start | bytes 798728 | tf_op jit(solution)/shard_map/ppermute | solution.py:226
  37.5 10.3 %collective-permute-start.6 = (bf16[528,128]{1,0:T(8,128)(2,1)S(1)}, bf16[528,128]{1,0:T(8,128)(2,1)S(1)}, u32[]{:S(2)}, u32[]{:S(2)}) collective-permute-start(bf16[528,128]{1,0:T(8,128)(2,1)S(1)} %get-tuple-element.20), channel_id=1, source_target_pairs={{0,24},{1,25},{2,26},{3,27},{4,28},{5,29},{6,30},{7,31},{8,32},{9,... | collective-permute-start | bytes 405512 | tf_op jit(solution)/shard_map/ppermute | solution.py:226
  49.1 29.9 %collective-permute-start.7 = (bf16[3120,128]{1,0:T(8,128)(2,1)S(1)}, bf16[3120,128]{1,0:T(8,128)(2,1)S(1)}, u32[]{:S(2)}, u32[]{:S(2)}) collective-permute-start(bf16[3120,128]{1,0:T(8,128)(2,1)S(1)} %get-tuple-element.21.refs_0_.refs_7_), channel_id=1, source_target_pairs={{0,2},{1,47},{2,4},{3,1},{4,6},{5,3},{6,8},{7,5},{8,10},{9,7},{10,... | collective-permute-start | bytes 2396168 | tf_op jit(solution)/shard_map/ppermute | solution.py:226
  56.5 64.0 %all-to-all-start = ((bf16[16,400,128]{2,1,0:T(8,128)(2,1)}), bf16[16,400,128]{2,1,0:T(8,128)(2,1)}, u32[]{:S(2)}, u32[]{:S(2)}) async-start(bf16[16,400,128]{2,1,0:T(8,128)(2,1)} %shard_map.145), calls=%async_computation | async-start | bytes 3276800 | tf_op jit(solution)/shard_map/all_to_all | solution.py:291
  64.1 19.6 %copy-start.25 = (s32[84]{0:T(128)S(1)}, s32[84]{0:T(128)}, u32[]{:S(2)}) copy-start(s32[84]{0:T(128)} %constant.366.clone) | copy-start | bytes 1012
  64.1 19.6 %copy-start.26 = (s32[84]{0:T(128)S(1)}, s32[84]{0:T(128)}, u32[]{:S(2)}) copy-start(s32[84]{0:T(128)} %constant.365.clone) | copy-start | bytes 1012
  64.1 14.9 %collective-permute-start.8 = (bf16[1024,128]{1,0:T(8,128)(2,1)S(1)}, bf16[1024,128]{1,0:T(8,128)(2,1)S(1)}, u32[]{:S(2)}, u32[]{:S(2)}) collective-permute-start(bf16[1024,128]{1,0:T(8,128)(2,1)S(1)} %copy-done.17), channel_id=1, source_target_pairs={{0,30},{1,19},{2,32},{3,21},{4,34},{5,23},{6,36},{7,25},{8,38},{9,... | collective-permute-start | bytes 786440 | tf_op jit(solution)/shard_map/ppermute | solution.py:226
  79.1 21.4 %collective-permute-start.10 = (bf16[2048,128]{1,0:T(8,128)(2,1)S(1)}, bf16[2048,128]{1,0:T(8,128)(2,1)S(1)}, u32[]{:S(2)}, u32[]{:S(2)}) collective-permute-start(bf16[2048,128]{1,0:T(8,128)(2,1)S(1)} %get-tuple-element.24), channel_id=1, source_target_pairs={{0,2},{1,47},{2,4},{3,1},{4,6},{5,3},{6,8},{7,5},{8,10},{9,7},{10,... | collective-permute-start | bytes 1572872 | tf_op jit(solution)/shard_map/ppermute | solution.py:226
  81.1 19.4 %collective-permute-start.9 = (bf16[1072,128]{1,0:T(8,128)(2,1)S(1)}, bf16[1072,128]{1,0:T(8,128)(2,1)S(1)}, u32[]{:S(2)}, u32[]{:S(2)}) collective-permute-start(bf16[1072,128]{1,0:T(8,128)(2,1)S(1)} %get-tuple-element.23), channel_id=1, source_target_pairs={{0,30},{1,19},{2,32},{3,21},{4,34},{5,23},{6,36},{7,25},{8,38},{9,... | collective-permute-start | bytes 823304 | tf_op jit(solution)/shard_map/ppermute | solution.py:226
  83.8 21.2 %copy-start.23 = (s32[60]{0:T(128)S(1)}, s32[60]{0:T(128)}, u32[]{:S(2)}) copy-start(s32[60]{0:T(128)} %constant.371.clone) | copy-start | bytes 724
  83.8 21.2 %copy-start.24 = (s32[60]{0:T(128)S(1)}, s32[60]{0:T(128)}, u32[]{:S(2)}) copy-start(s32[60]{0:T(128)} %constant.370.clone) | copy-start | bytes 724
  83.8 23.3 %copy-start.1 = (bf16[528,128]{1,0:T(8,128)(2,1)S(1)}, bf16[528,128]{1,0:T(8,128)(2,1)}, u32[]{:S(2)}) copy-start(bf16[528,128]{1,0:T(8,128)(2,1)} %copy-done) | copy-start | bytes 405508
  83.8 23.3 %copy-start.9 = (bf16[1040,128]{1,0:T(8,128)(2,1)S(1)}, bf16[1040,128]{1,0:T(8,128)(2,1)}, u32[]{:S(2)}) copy-start(bf16[1040,128]{1,0:T(8,128)(2,1)} %copy-done.8) | copy-start | bytes 798724
  83.8 23.3 %copy-start.11 = (bf16[1040,128]{1,0:T(8,128)(2,1)S(1)}, bf16[1040,128]{1,0:T(8,128)(2,1)}, u32[]{:S(2)}) copy-start(bf16[1040,128]{1,0:T(8,128)(2,1)} %copy-done.10) | copy-start | bytes 798724
  100.6 18.6 %collective-permute-start.11 = (bf16[3120,128]{1,0:T(8,128)(2,1)S(1)}, bf16[3120,128]{1,0:T(8,128)(2,1)S(1)}, u32[]{:S(2)}, u32[]{:S(2)}) collective-permute-start(bf16[3120,128]{1,0:T(8,128)(2,1)S(1)} %shard_map.149), channel_id=1, source_target_pairs={{0,1},{1,0},{2,3},{3,2},{4,5},{5,4},{6,7},{7,6},{8,9},{9,8},{10,11... | collective-permute-start | bytes 2396168 | tf_op jit(solution)/shard_map/ppermute | solution.py:230
  105.1 7.4 %collective-permute-start.12 = (bf16[1072,128]{1,0:T(8,128)(2,1)S(1)}, bf16[1072,128]{1,0:T(8,128)(2,1)S(1)}, u32[]{:S(2)}, u32[]{:S(2)}) collective-permute-start(bf16[1072,128]{1,0:T(8,128)(2,1)S(1)} %collective-permute-done.9.refs_3_.rest_1_), channel_id=1, source_target_pairs={{0,2},{1,47},{2,4},{3,1},{4,6},{5,3},{6,8},{7,5},{8,10},{9,7},{10,... | collective-permute-start | bytes 823304 | tf_op jit(solution)/shard_map/ppermute | solution.py:226
  110.3 11.7 %collective-permute-start.14 = (bf16[5040,128]{1,0:T(8,128)(2,1)}, bf16[5040,128]{1,0:T(8,128)(2,1)S(1)}, u32[]{:S(2)}, u32[]{:S(2)}) collective-permute-start(bf16[5040,128]{1,0:T(8,128)(2,1)} %get-tuple-element.25), channel_id=1, source_target_pairs={{0,1},{1,0},{2,3},{3,2},{4,5},{5,4},{6,7},{7,6},{8,9},{9,8},{10,11... | collective-permute-start | bytes 3870728 | tf_op jit(solution)/shard_map/ppermute | solution.py:230
  112.5 18.5 %collective-permute-start.13 = (bf16[512,128]{1,0:T(8,128)(2,1)S(1)}, bf16[512,128]{1,0:T(8,128)(2,1)S(1)}, u32[]{:S(2)}, u32[]{:S(2)}) collective-permute-start(bf16[512,128]{1,0:T(8,128)(2,1)S(1)} %shard_map.150), channel_id=1, source_target_pairs={{0,1},{1,0},{2,3},{3,2},{4,5},{5,4},{6,7},{7,6},{8,9},{9,8},{10,11... | collective-permute-start | bytes 393224 | tf_op jit(solution)/shard_map/ppermute | solution.py:230
  (21 other events, 151.2 us)

commit v8 on v6

--- a/solution.py
+++ b/solution.py
@@ -20,6 +20,7 @@
 STEPS = 3
 KEPT = 12
 SPAN = 8 + STEPS - 1
+HALF = STEPS * 128 + 16
 BLK = 128
 
 
@@ -92,34 +93,24 @@
     )(index, src, note)
 
 
-def chosen_kernel(index_ref, *rest):
-    sources, out, sems = rest[:2], rest[2], rest[3]
-    copies = []
-    for half, src in enumerate(sources):
-        for n in range(8):
-            for t in range(STEPS):
-                row = pl.multiple_of(index_ref[t] * BLK, BLK)
-                place = blk((half * STEPS + t) * 8 + n)
-                copies.append((src.at[n, pl.ds(row, BLK)], out.at[place]))
-            tail = pl.ds(STEPS * 16 * BLK + 16 * (8 * half + n), 16)
-            copies.append((src.at[n, pl.ds(SPAN * BLK, 16)], out.at[tail]))
-    copies = [pltpu.make_async_copy(a, b, sems.at[n]) for n, (a, b) in enumerate(copies)]
-    for copy in copies:
-        copy.start()
-    for copy in copies:
-        copy.wait()
-
-
-def chosen(index, sources):
+def right_kernel(*refs):
+    sources, out = refs[:2], refs[-1]
+    for n in range(8):
+        for half, source in enumerate(sources):
+            out[n, pl.ds(half * HALF, STEPS * BLK), :] = source[pl.ds(n * BLK, STEPS * BLK), :]
+            note = source[pl.ds(SPAN * BLK, 16), :]
+            out[n, pl.ds(half * HALF + STEPS * BLK, 16), :] = note
+
+
+def right_packed(kept, other, after):
     return pl.pallas_call(
-        chosen_kernel,
-        out_shape=rows_shape(STEPS * 16 * BLK + 16 * 16),
-        in_specs=[SMEM_SPEC, ANY_SPEC, ANY_SPEC],
+        right_kernel,
+        out_shape=jax.ShapeDtypeStruct((8, 2 * HALF, BLK), jnp.bfloat16),
+        in_specs=[VMEM_SPEC, VMEM_SPEC, ANY_SPEC],
         out_specs=VMEM_SPEC,
-        scratch_shapes=[pltpu.SemaphoreType.DMA((2 * 8 * (STEPS + 1),))],
         compiler_params=LIMIT,
         cost_estimate=moves(48),
-    )(index, *sources)
+    )(kept, other, after)
 
 
 def turned(note, distance):
@@ -181,7 +172,7 @@
             block = left[pl.ds(pl.multiple_of(table_ref[4, base + n], BLK), BLK), :]
             pair = []
             for rank in range(2):
-                row = pl.multiple_of(table_ref[2 * rank, base + n], BLK)
+                row = pl.multiple_of(table_ref[2 * rank, base + n], 16)
                 pair.append(right_ref[pl.ds(row, BLK), :])
             both = jnp.dot(block, jnp.concatenate(pair, axis=1), preferred_element_type=jnp.float32)
             acc[table_ref[1, base + n]] += both[:, :BLK]
@@ -244,8 +235,7 @@
         target = (codes // PANEL) * BC + partner % 32
         there = (target[:, None] == c_code[None, :]) & (found > 0)[:, None]
         slot = jnp.sum(jnp.where(there, jnp.arange(KEPT)[None, :] - KEPT, 0), axis=1) + KEPT
-        owner = partner // 32
-        rows += [(owner // 8 * (8 * STEPS) + step * 8 + owner % 8) * BLK, slot]
+        rows += [partner // 32 * HALF + step * BLK, slot]
     return jnp.stack(rows + [jnp.array(row)]).astype(jnp.int32).reshape(5, count)
 
 
@@ -275,9 +265,7 @@
         return jnp.pad(digits, ((0, 15), (0, BLK - 32)))
 
     spans = 2 * q + core + 8 * lax.axis_index("xl") + jnp.arange(SPAN, dtype=jnp.int32)
-    spans = jnp.concatenate([spans, spans + 8]) % 16
-    b_kept, b_sent = split(spans, b_own, note_of(b_own_code))
-    b_all = [lax.all_gather(b_kept, "y")]
+    b_kept, b_sent = split(jnp.concatenate([spans, spans + 8]) % 16, b_own, note_of(b_own_code))
     b_other = lax.ppermute(b_sent, "xl", [(0, 1), (1, 0)])
 
     sources, at = [], {}
@@ -318,21 +306,22 @@
     for array, (names, _) in zip(arrays[:4], starts[:4], strict=True):
         own = keep(array, names)
     near.append((own, 8 * BLK, 0, True))
-    for array, (names, distance) in zip(arrays, starts, strict=True):
+    for array, (names, distance) in zip(arrays[:4], starts[:4], strict=True):
         near.append((send(array, names, distance), 2 * len(names) * BLK, distance, True))
 
-    b_other, _ = lax.optimization_barrier((b_other, sources[near[1][0]]))
-    b_all.append(lax.all_gather(b_other, "y"))
-
     names = items([(2, 1), (6, 13), (3, 2), (7, 14), (0, 14), (4, 2)])
-    (up_in,) = packed([(blocks(names), True)], near)
+    (up_in,) = packed([(blocks(names), True)], near, (b_other,))
     sources.append(up_in)
     up3 = send(up_in, names, 1)
+    right = lax.all_to_all(right_packed(b_kept, b_other, up_in), "y", 0, 0, tiled=True)
+    right = right.reshape(16 * HALF, BLK)
     middle = [(up3 - 1, 24 * BLK, 0, False), (up3, 24 * BLK, 1, False)]
 
     names = items([(1, 1), (5, 13), (2, 2), (6, 14)])
     (up_in,) = packed([(blocks(names), True)], middle)
     up6 = send(up_in, names, 15)
+    across, _ = lax.optimization_barrier((arrays[4], up_in))
+    middle.append((send(across, *starts[4]), 4 * BLK, starts[4][1], True))
     far = middle + [(up6, 16 * BLK, 15, False)]
 
     early = items([(1, 1), (5, 13), (2, 2), (6, 14), (3, 3), (7, 15)]) + [(4, 12, 0)]
@@ -375,8 +364,7 @@
         return [(array, rows)]
 
     panels = (start + core + jnp.arange(STEPS, dtype=jnp.int32)) % 16
-    right = chosen(lax.axis_index("y") + jnp.arange(STEPS, dtype=jnp.int32), b_all)
-    digits = right[STEPS * 16 * BLK :].reshape(16, 16, BLK)[:, 0, :32].astype(jnp.int32)
+    digits = right.reshape(16, HALF, BLK)[:, STEPS * BLK, :32].astype(jnp.int32)
     right_codes = (digits[:, :16] * 64 + digits[:, 16:] - 1)[:, None, :]
     right_codes = jnp.sum(
         jnp.where(panels[:, None] == jnp.arange(16)[None, :], right_codes, 0), axis=2

time: 151 us -> 126 us (0.83)
  between operations: 14 us -> 0.74 us
  waiting for transfers between devices: 29.8 us -> 21.3 us
  Pallas kernels: 22.4 us -> 18.7 us
  starting transfers between devices: 68 us -> 71.1 us
  local copies, waits for them, and re-layouts: 12.4 us -> 9.92 us
    ppermute x8, waiting for transfers between devices: 28.7 us -> 16.1 us  [moved(): return lax.ppermute(array, COL, route)]
    all_to_all x0 -> x1, starting transfers between devices: none -> 6.86 us  [local(): lax.all_to_all(right_packed(b_kept, b_other, up_in), 'y', 0, 0, tiled=True)]
    all_to_all x0 -> x1, waiting for transfers between devices: none -> 5.26 us  [local(): lax.all_to_all(right_packed(b_kept, b_other, up_in), 'y', 0, 0, tiled=True)]
    ppermute x8, starting transfers between devices: 38.6 us -> 33.6 us  [moved(): return lax.ppermute(array, COL, route)]
    ppermute x5, starting transfers between devices: 25.3 us -> 28.7 us  [from_other_core(): return lax.ppermute(array, 'core', [(0, 1), (1, 0)])]
    pallas_call x1, Pallas kernels: 3.36 us -> 0.21 us  [right_packed(): pl.pallas_call(right_kernel, out_shape=jax.ShapeDtypeStruct((8, 2 * HALF,...]
    unnamed x44 -> x62, local copies, waits for them, and re-layouts: 10.7 us -> 8.2 us
    ppermute x1, starting transfers between devices: 3.95 us -> 1.92 us  [local(): b_other = lax.ppermute(b_sent, 'xl', [(0, 1), (1, 0)])]
  transfers between devices with their start and end apart: 16 -> 15, of which waited for: 5 -> 7; matrix products, arithmetic and copies ran while one was open for 3% -> 4% of each run, Pallas kernels for 10% -> 11%
where the time goes in v8:
time: 126 us; the launch traced here: 125 us
  starting transfers between devices  71.1 us (56%)
  waiting for transfers between devices  21.3 us (17%)
  Pallas kernels  18.7 us (15%)
  local copies, waits for them, and re-layouts  9.92 us (8%)
  other arithmetic  3.47 us (3%)
    ppermute x8, starting transfers between devices, moved(): return lax.ppermute(array, COL, route)  33.6 us
    ppermute x5, starting transfers between devices, from_other_core(): return lax.ppermute(array, 'core', [(0, 1), (1, 0)])  28.7 us
    ppermute x8, waiting for transfers between devices, moved(): return lax.ppermute(array, COL, route)  16.1 us
    pallas_call x3, Pallas kernels, product(): pl.pallas_call(functools.partial(product_kernel, counts, base, before is...  12.7 us
    unnamed x62, local copies, waits for them, and re-layouts  8.2 us
    all_to_all x1, starting transfers between devices, local(): lax.all_to_all(right_packed(b_kept, b_other, up_in), 'y', 0, 0, tiled=True)  6.86 us
    all_to_all x1, waiting for transfers between devices, local(): lax.all_to_all(right_packed(b_kept, b_other, up_in), 'y', 0, 0, tiled=True)  5.26 us
    pallas_call x5, Pallas kernels, pack(): pl.pallas_call(functools.partial(pack_kernel, spec, notes, len(used)), ou...  4.53 us
  transfers between devices with their start and end apart: 15, of which 7 were waited for; matrix products, arithmetic and copies ran while one was open for 4% of the time, Pallas kernels for 11%

profile of v8, /device:TPU:1, one launch (start us, length us, event | category | flops | bytes accessed | tf_op | source)
XLA Modules:
  0.0 125.3 jit_solution(9232633932884572670)
XLA Ops:
  0.8 12.4 %collective-permute-start.2 = (bf16[16,128]{1,0:T(8,128)(2,1)S(1)}, bf16[16,128]{1,0:T(8,128)(2,1)S(1)}, u32[]{:S(2)}, u32[]{:S(2)}) collective-permute-start(bf16[16,128]{1,0:T(8,128)(2,1)S(1)} %fusion.37), channel_id=1, source_target_pairs={{0,1},{1,0},{2,3},{3,2},{4,5},{5,4},{6,7},{7,6},{8,9},{9,8},{10,11... | collective-permute-start | bytes 12296 | tf_op jit(solution)/shard_map/ppermute | solution.py:251
  13.2 1.9 %collective-permute-start.1 = (bf16[16,128,128]{2,1,0:T(8,128)(2,1)}, bf16[16,128,128]{2,1,0:T(8,128)(2,1)S(1)}, u32[]{:S(2)}, u32[]{:S(2)}) collective-permute-start(bf16[16,128,128]{2,1,0:T(8,128)(2,1)} %bitcast.76), channel_id=1, source_target_pairs={{0,1},{1,0},{2,3},{3,2},{4,5},{5,4},{6,7},{7,6},{8,9},{9,8},{10,11... | collective-permute-start | bytes 1572872 | tf_op jit(solution)/shard_map/ppermute | solution.py:251
  17.6 1.9 %collective-permute-start = (bf16[1296,128]{1,0:T(8,128)(2,1)S(1)}, bf16[1296,128]{1,0:T(8,128)(2,1)S(1)}, u32[]{:S(2)}, u32[]{:S(2)}) collective-permute-start(bf16[1296,128]{1,0:T(8,128)(2,1)S(1)} %get-tuple-element.18), channel_id=1, source_target_pairs={{0,384},{384,0},{1,385},{385,1},{2,386},{386,2},{3,387},{387,3},{4... | collective-permute-start | bytes 995336 | tf_op jit(solution)/shard_map/ppermute | solution.py:269
  22.2 8.8 %collective-permute-start.3 = (bf16[1040,128]{1,0:T(8,128)(2,1)S(1)}, bf16[1040,128]{1,0:T(8,128)(2,1)S(1)}, u32[]{:S(2)}, u32[]{:S(2)}) collective-permute-start(bf16[1040,128]{1,0:T(8,128)(2,1)S(1)} %get-tuple-element.20), channel_id=1, source_target_pairs={{0,4},{1,45},{2,6},{3,47},{4,8},{5,1},{6,10},{7,3},{8,12},{9,5},{1... | collective-permute-start | bytes 798728 | tf_op jit(solution)/shard_map/ppermute | solution.py:247
  31.0 1.9 %collective-permute-start.4 = (bf16[1040,128]{1,0:T(8,128)(2,1)S(1)}, bf16[1040,128]{1,0:T(8,128)(2,1)S(1)}, u32[]{:S(2)}, u32[]{:S(2)}) collective-permute-start(bf16[1040,128]{1,0:T(8,128)(2,1)S(1)} %get-tuple-element.21.refs_0_), channel_id=1, source_target_pairs={{0,28},{1,21},{2,30},{3,23},{4,32},{5,25},{6,34},{7,27},{8,36},{9,... | collective-permute-start | bytes 798728 | tf_op jit(solution)/shard_map/ppermute | solution.py:247
  32.9 3.9 %collective-permute-start.5 = (bf16[1040,128]{1,0:T(8,128)(2,1)S(1)}, bf16[1040,128]{1,0:T(8,128)(2,1)S(1)}, u32[]{:S(2)}, u32[]{:S(2)}) collective-permute-start(bf16[1040,128]{1,0:T(8,128)(2,1)S(1)} %get-tuple-element.22.refs_1_), channel_id=1, source_target_pairs={{0,2},{1,47},{2,4},{3,1},{4,6},{5,3},{6,8},{7,5},{8,10},{9,7},{10,... | collective-permute-start | bytes 798728 | tf_op jit(solution)/shard_map/ppermute | solution.py:247
  36.8 1.9 %collective-permute-start.6 = (bf16[1040,128]{1,0:T(8,128)(2,1)S(1)}, bf16[1040,128]{1,0:T(8,128)(2,1)S(1)}, u32[]{:S(2)}, u32[]{:S(2)}) collective-permute-start(bf16[1040,128]{1,0:T(8,128)(2,1)S(1)} %get-tuple-element.19.refs_0_), channel_id=1, source_target_pairs={{0,26},{1,23},{2,28},{3,25},{4,30},{5,27},{6,32},{7,29},{8,34},{9,... | collective-permute-start | bytes 798728 | tf_op jit(solution)/shard_map/ppermute | solution.py:247
  39.4 5.2 %collective-permute-done.4.refs_2_.refs_3_ = bf16[1040,128]{1,0:T(8,128)(2,1)S(1)} collective-permute-done((bf16[1040,128]{1,0:T(8,128)(2,1)S(1)}, bf16[1040,128]{1,0:T(8,128)(2,1)S(1)}, u32[]{:S(2)}, u32[]{:S(2)}) %collective-permute-start.4) | collective-permute-done | bytes 266272 | tf_op jit(solution)/shard_map/ppermute | solution.py:247
  44.6 1.7 %collective-permute-done.5.refs_3_.refs_0_.refs_4_ = bf16[1040,128]{1,0:T(8,128)(2,1)S(1)} collective-permute-done((bf16[1040,128]{1,0:T(8,128)(2,1)S(1)}, bf16[1040,128]{1,0:T(8,128)(2,1)S(1)}, u32[]{:S(2)}, u32[]{:S(2)}) %collective-permute-start.5) | collective-permute-done | bytes 266272 | tf_op jit(solution)/shard_map/ppermute | solution.py:247
  46.3 3.7 %collective-permute-done.6.refs_4_.refs_1_.refs_5_ = bf16[1040,128]{1,0:T(8,128)(2,1)S(1)} collective-permute-done((bf16[1040,128]{1,0:T(8,128)(2,1)S(1)}, bf16[1040,128]{1,0:T(8,128)(2,1)S(1)}, u32[]{:S(2)}, u32[]{:S(2)}) %collective-permute-start.6) | collective-permute-done | bytes 266272 | tf_op jit(solution)/shard_map/ppermute | solution.py:247
  50.9 5.2 %collective-permute-start.7 = (bf16[3120,128]{1,0:T(8,128)(2,1)S(1)}, bf16[3120,128]{1,0:T(8,128)(2,1)S(1)}, u32[]{:S(2)}, u32[]{:S(2)}) collective-permute-start(bf16[3120,128]{1,0:T(8,128)(2,1)S(1)} %shard_map.147.refs_2_.refs_0_.refs_6_), channel_id=1, source_target_pairs={{0,2},{1,47},{2,4},{3,1},{4,6},{5,3},{6,8},{7,5},{8,10},{9,7},{10,... | collective-permute-start | bytes 2396168 | tf_op jit(solution)/shard_map/ppermute | solution.py:247
  57.7 6.9 %all-to-all-start = ((bf16[8,800,128]{2,1,0:T(8,128)(2,1)}), bf16[8,800,128]{2,1,0:T(8,128)(2,1)S(1)}, u32[]{:S(2)}, u32[]{:S(2)}) async-start(bf16[8,800,128]{2,1,0:T(8,128)(2,1)} %copy-done), calls=%async_computation | async-start | bytes 3276800 | tf_op jit(solution)/shard_map/all_to_all | solution.py:316
  66.1 2.8 %collective-permute-start.8 = (bf16[2096,128]{1,0:T(8,128)(2,1)S(1)}, bf16[2096,128]{1,0:T(8,128)(2,1)S(1)}, u32[]{:S(2)}, u32[]{:S(2)}) collective-permute-start(bf16[2096,128]{1,0:T(8,128)(2,1)S(1)} %shard_map.149.refs_9_), channel_id=1, source_target_pairs={{0,30},{1,19},{2,32},{3,21},{4,34},{5,23},{6,36},{7,25},{8,38},{9,... | collective-permute-start | bytes 1609736 | tf_op jit(solution)/shard_map/ppermute | solution.py:247
  69.0 4.8 %collective-permute-start.9 = (bf16[528,128]{1,0:T(8,128)(2,1)S(1)}, bf16[528,128]{1,0:T(8,128)(2,1)S(1)}, u32[]{:S(2)}, u32[]{:S(2)}) collective-permute-start(bf16[528,128]{1,0:T(8,128)(2,1)S(1)} %copy-done.19), channel_id=1, source_target_pairs={{0,24},{1,25},{2,26},{3,27},{4,28},{5,29},{6,30},{7,31},{8,32},{9,... | collective-permute-start | bytes 405512 | tf_op jit(solution)/shard_map/ppermute | solution.py:247
  73.8 4.1 %collective-permute-done.9.refs_3_.refs_8_ = bf16[528,128]{1,0:T(8,128)(2,1)S(1)} collective-permute-done((bf16[528,128]{1,0:T(8,128)(2,1)S(1)}, bf16[528,128]{1,0:T(8,128)(2,1)S(1)}, u32[]{:S(2)}, u32[]{:S(2)}) %collective-permute-start.9) | collective-permute-done | bytes 135200 | tf_op jit(solution)/shard_map/ppermute | solution.py:247
  80.4 7.0 %collective-permute-start.12 = (bf16[5040,128]{1,0:T(8,128)(2,1)}, bf16[5040,128]{1,0:T(8,128)(2,1)}, u32[]{:S(2)}, u32[]{:S(2)}) collective-permute-start(bf16[5040,128]{1,0:T(8,128)(2,1)} %get-tuple-element.27), channel_id=1, source_target_pairs={{0,1},{1,0},{2,3},{3,2},{4,5},{5,4},{6,7},{7,6},{8,9},{9,8},{10,11... | collective-permute-start | bytes 3870728 | tf_op jit(solution)/shard_map/ppermute | solution.py:251
  88.5 5.2 %collective-permute-start.10 = (bf16[48,128]{1,0:T(8,128)(2,1)S(1)}, bf16[48,128]{1,0:T(8,128)(2,1)S(1)}, u32[]{:S(2)}, u32[]{:S(2)}) collective-permute-start(bf16[48,128]{1,0:T(8,128)(2,1)S(1)} %get-tuple-element.25), channel_id=1, source_target_pairs={{0,1},{1,0},{2,3},{3,2},{4,5},{5,4},{6,7},{7,6},{8,9},{9,8},{10,11... | collective-permute-start | bytes 36872 | tf_op jit(solution)/shard_map/ppermute | solution.py:251
  94.5 4.4 %collective-permute-start.11 = (bf16[3072,128]{1,0:T(8,128)(2,1)}, bf16[3072,128]{1,0:T(8,128)(2,1)}, u32[]{:S(2)}, u32[]{:S(2)}) collective-permute-start(bf16[3072,128]{1,0:T(8,128)(2,1)} %get-tuple-element.26), channel_id=1, source_target_pairs={{0,2},{1,47},{2,4},{3,1},{4,6},{5,3},{6,8},{7,5},{8,10},{9,7},{10,... | collective-permute-start | bytes 2359304 | tf_op jit(solution)/shard_map/ppermute | solution.py:247
  100.5 5.3 %all-to-all-done = bf16[8,800,128]{2,1,0:T(8,128)(2,1)S(1)} async-done(((bf16[8,800,128]{2,1,0:T(8,128)(2,1)}), bf16[8,800,128]{2,1,0:T(8,128)(2,1)S(1)}, u32[]{:S(2)}, u32[]{:S(2)}) %all-to-all-start) | async-done | bytes 1638432 | tf_op jit(solution)/shard_map/all_to_all | solution.py:316
  108.1 6.7 %shard_map.152.refs_2_.rest_2_ = f32[13,128,128]{2,1,0:T(8,128)S(1)} custom-call(s32[5,84]{1,0:T(8,128)S(1)} %stack.59.table_ref, bf16[6400,128]{1,0:T(8,128)(2,1)S(1)} %bitcast.72, bf16[5760,128]{1,0:T(8,128)(2,1)S(1)} %copy-done.17, bf16[5040,128]{1,0:T(8,128)(2,1)} %collective-permute-done.12.rest_1_), custom_call_target="tpu_custom_call" | custom-call | flops 2818572288 | bytes 2752512 | tf_op jit(solution)/shard_map/pallas_call | solution.py:192
  114.8 2.1 %shard_map.153 = bf16[3584,128]{1,0:T(8,128)(2,1)} custom-call(bf16[2096,128]{1,0:T(8,128)(2,1)S(1)} %copy-done.2, bf16[3072,128]{1,0:T(8,128)(2,1)} %collective-permute-done.11.refs_1_.rest_1_, f32[13,128,128]{2,1,0:T(8,128)S(1)} %shard_map.152.refs_2_.rest_2_), custom_call_target="tpu_custom_call" | custom-call | bytes 1835008 | tf_op jit(solution)/shard_map/pallas_call | solution.py:148
  116.9 2.1 %collective-permute-start.13 = (bf16[3584,128]{1,0:T(8,128)(2,1)}, bf16[3584,128]{1,0:T(8,128)(2,1)}, u32[]{:S(2)}, u32[]{:S(2)}) collective-permute-start(bf16[3584,128]{1,0:T(8,128)(2,1)} %shard_map.153), channel_id=1, source_target_pairs={{0,1},{1,0},{2,3},{3,2},{4,5},{5,4},{6,7},{7,6},{8,9},{9,8},{10,11... | collective-permute-start | bytes 2752520 | tf_op jit(solution)/shard_map/ppermute | solution.py:251
  119.2 2.8 %shard_map.154.rest_1_ = f32[13,128,128]{2,1,0:T(8,128)S(1)} custom-call(s32[5,60]{1,0:T(8,128)S(1)} %stack.52.table_ref, bf16[6400,128]{1,0:T(8,128)(2,1)S(1)} %bitcast.73, bf16[2096,128]{1,0:T(8,128)(2,1)S(1)} %copy-done.2, bf16[3072,128]{1,0:T(8,128)(2,1)} %collective-permute-done.11.refs_1_.rest_1_, f32[13,128,128]{2,1,0:T(8,128)S(1)} %shard_map.152.refs_2_.rest_2_), custom_call_target="tpu_custom_call" | custom-call | flops 1073741824 | bytes 1048576 | tf_op jit(solution)/shard_map/pallas_call | solution.py:192
  122.0 3.2 %shard_map.155 = bf16[12,128,128]{2,1,0:T(8,128)(2,1)} custom-call(s32[5,60]{1,0:T(8,128)S(1)} %stack.52.table_ref, bf16[6400,128]{1,0:T(8,128)(2,1)S(1)} %bitcast.74, bf16[3584,128]{1,0:T(8,128)(2,1)} %collective-permute-done.13.rest_0_, f32[13,128,128]{2,1,0:T(8,128)S(1)} %shard_map.154.rest_1_), custom_call_target="tpu_custom_call" | custom-call | flops 939524096 | bytes 917504 | tf_op jit(solution)/shard_map/pallas_call | solution.py:192
  (141 shorter events, 18.5 us)
Async XLA Ops:
  0.8 18.9 %collective-permute-start.2 = (bf16[16,128]{1,0:T(8,128)(2,1)S(1)}, bf16[16,128]{1,0:T(8,128)(2,1)S(1)}, u32[]{:S(2)}, u32[]{:S(2)}) collective-permute-start(bf16[16,128]{1,0:T(8,128)(2,1)S(1)} %fusion.37), channel_id=1, source_target_pairs={{0,1},{1,0},{2,3},{3,2},{4,5},{5,4},{6,7},{7,6},{8,9},{9,8},{10,11... | collective-permute-start | bytes 12296 | tf_op jit(solution)/shard_map/ppermute | solution.py:251
  13.2 6.6 %collective-permute-start.1 = (bf16[16,128,128]{2,1,0:T(8,128)(2,1)}, bf16[16,128,128]{2,1,0:T(8,128)(2,1)S(1)}, u32[]{:S(2)}, u32[]{:S(2)}) collective-permute-start(bf16[16,128,128]{2,1,0:T(8,128)(2,1)} %bitcast.76), channel_id=1, source_target_pairs={{0,1},{1,0},{2,3},{3,2},{4,5},{5,4},{6,7},{7,6},{8,9},{9,8},{10,11... | collective-permute-start | bytes 1572872 | tf_op jit(solution)/shard_map/ppermute | solution.py:251
  17.6 21.1 %collective-permute-start = (bf16[1296,128]{1,0:T(8,128)(2,1)S(1)}, bf16[1296,128]{1,0:T(8,128)(2,1)S(1)}, u32[]{:S(2)}, u32[]{:S(2)}) collective-permute-start(bf16[1296,128]{1,0:T(8,128)(2,1)S(1)} %get-tuple-element.18), channel_id=1, source_target_pairs={{0,384},{384,0},{1,385},{385,1},{2,386},{386,2},{3,387},{387,3},{4... | collective-permute-start | bytes 995336 | tf_op jit(solution)/shard_map/ppermute | solution.py:269
  22.1 34.4 %copy-start.12 = (bf16[1040,128]{1,0:T(8,128)(2,1)}, bf16[1040,128]{1,0:T(8,128)(2,1)S(1)}, u32[]{:S(2)}) copy-start(bf16[1040,128]{1,0:T(8,128)(2,1)S(1)} %get-tuple-element.21.refs_0_) | copy-start | bytes 798724
  22.1 34.0 %copy-start.21 = (s32[84]{0:T(128)S(1)}, s32[84]{0:T(128)}, u32[]{:S(2)}) copy-start(s32[84]{0:T(128)} %constant.374.clone) | copy-start | bytes 1012
  22.1 34.0 %copy-start.23 = (s32[84]{0:T(128)S(1)}, s32[84]{0:T(128)}, u32[]{:S(2)}) copy-start(s32[84]{0:T(128)} %constant.377.clone) | copy-start | bytes 1012
  22.1 34.0 %copy-start.27 = (s32[84]{0:T(128)S(1)}, s32[84]{0:T(128)}, u32[]{:S(2)}) copy-start(s32[84]{0:T(128)} %constant.375.clone) | copy-start | bytes 1012
  22.1 34.0 %copy-start.28 = (s32[84]{0:T(128)S(1)}, s32[84]{0:T(128)}, u32[]{:S(2)}) copy-start(s32[84]{0:T(128)} %constant.376.clone) | copy-start | bytes 1012
  22.1 34.0 %copy-start.20 = (s32[60]{0:T(128)S(1)}, s32[60]{0:T(128)}, u32[]{:S(2)}) copy-start(s32[60]{0:T(128)} %constant.379.clone) | copy-start | bytes 724
  22.1 34.0 %copy-start.22 = (s32[60]{0:T(128)S(1)}, s32[60]{0:T(128)}, u32[]{:S(2)}) copy-start(s32[60]{0:T(128)} %constant.382.clone) | copy-start | bytes 724
  22.1 34.1 %copy-start.25 = (s32[60]{0:T(128)S(1)}, s32[60]{0:T(128)}, u32[]{:S(2)}) copy-start(s32[60]{0:T(128)} %constant.380.clone) | copy-start | bytes 724
  22.2 34.0 %copy-start.26 = (s32[60]{0:T(128)S(1)}, s32[60]{0:T(128)}, u32[]{:S(2)}) copy-start(s32[60]{0:T(128)} %constant.381.clone) | copy-start | bytes 724
  22.2 17.2 %collective-permute-start.3 = (bf16[1040,128]{1,0:T(8,128)(2,1)S(1)}, bf16[1040,128]{1,0:T(8,128)(2,1)S(1)}, u32[]{:S(2)}, u32[]{:S(2)}) collective-permute-start(bf16[1040,128]{1,0:T(8,128)(2,1)S(1)} %get-tuple-element.20), channel_id=1, source_target_pairs={{0,4},{1,45},{2,6},{3,47},{4,8},{5,1},{6,10},{7,3},{8,12},{9,5},{1... | collective-permute-start | bytes 798728 | tf_op jit(solution)/shard_map/ppermute | solution.py:247
  31.0 13.7 %collective-permute-start.4 = (bf16[1040,128]{1,0:T(8,128)(2,1)S(1)}, bf16[1040,128]{1,0:T(8,128)(2,1)S(1)}, u32[]{:S(2)}, u32[]{:S(2)}) collective-permute-start(bf16[1040,128]{1,0:T(8,128)(2,1)S(1)} %get-tuple-element.21.refs_0_), channel_id=1, source_target_pairs={{0,28},{1,21},{2,30},{3,23},{4,32},{5,25},{6,34},{7,27},{8,36},{9,... | collective-permute-start | bytes 798728 | tf_op jit(solution)/shard_map/ppermute | solution.py:247
  32.9 13.4 %collective-permute-start.5 = (bf16[1040,128]{1,0:T(8,128)(2,1)S(1)}, bf16[1040,128]{1,0:T(8,128)(2,1)S(1)}, u32[]{:S(2)}, u32[]{:S(2)}) collective-permute-start(bf16[1040,128]{1,0:T(8,128)(2,1)S(1)} %get-tuple-element.22.refs_1_), channel_id=1, source_target_pairs={{0,2},{1,47},{2,4},{3,1},{4,6},{5,3},{6,8},{7,5},{8,10},{9,7},{10,... | collective-permute-start | bytes 798728 | tf_op jit(solution)/shard_map/ppermute | solution.py:247
  36.8 13.3 %collective-permute-start.6 = (bf16[1040,128]{1,0:T(8,128)(2,1)S(1)}, bf16[1040,128]{1,0:T(8,128)(2,1)S(1)}, u32[]{:S(2)}, u32[]{:S(2)}) collective-permute-start(bf16[1040,128]{1,0:T(8,128)(2,1)S(1)} %get-tuple-element.19.refs_0_), channel_id=1, source_target_pairs={{0,26},{1,23},{2,28},{3,25},{4,30},{5,27},{6,32},{7,29},{8,34},{9,... | collective-permute-start | bytes 798728 | tf_op jit(solution)/shard_map/ppermute | solution.py:247
  50.9 14.2 %collective-permute-start.7 = (bf16[3120,128]{1,0:T(8,128)(2,1)S(1)}, bf16[3120,128]{1,0:T(8,128)(2,1)S(1)}, u32[]{:S(2)}, u32[]{:S(2)}) collective-permute-start(bf16[3120,128]{1,0:T(8,128)(2,1)S(1)} %shard_map.147.refs_2_.refs_0_.refs_6_), channel_id=1, source_target_pairs={{0,2},{1,47},{2,4},{3,1},{4,6},{5,3},{6,8},{7,5},{8,10},{9,7},{10,... | collective-permute-start | bytes 2396168 | tf_op jit(solution)/shard_map/ppermute | solution.py:247
  57.7 48.0 %all-to-all-start = ((bf16[8,800,128]{2,1,0:T(8,128)(2,1)}), bf16[8,800,128]{2,1,0:T(8,128)(2,1)S(1)}, u32[]{:S(2)}, u32[]{:S(2)}) async-start(bf16[8,800,128]{2,1,0:T(8,128)(2,1)} %copy-done), calls=%async_computation | async-start | bytes 3276800 | tf_op jit(solution)/shard_map/all_to_all | solution.py:316
  66.1 21.3 %collective-permute-start.8 = (bf16[2096,128]{1,0:T(8,128)(2,1)S(1)}, bf16[2096,128]{1,0:T(8,128)(2,1)S(1)}, u32[]{:S(2)}, u32[]{:S(2)}) collective-permute-start(bf16[2096,128]{1,0:T(8,128)(2,1)S(1)} %shard_map.149.refs_9_), channel_id=1, source_target_pairs={{0,30},{1,19},{2,32},{3,21},{4,34},{5,23},{6,36},{7,25},{8,38},{9,... | collective-permute-start | bytes 1609736 | tf_op jit(solution)/shard_map/ppermute | solution.py:247
  69.0 9.0 %collective-permute-start.9 = (bf16[528,128]{1,0:T(8,128)(2,1)S(1)}, bf16[528,128]{1,0:T(8,128)(2,1)S(1)}, u32[]{:S(2)}, u32[]{:S(2)}) collective-permute-start(bf16[528,128]{1,0:T(8,128)(2,1)S(1)} %copy-done.19), channel_id=1, source_target_pairs={{0,24},{1,25},{2,26},{3,27},{4,28},{5,29},{6,30},{7,31},{8,32},{9,... | collective-permute-start | bytes 405512 | tf_op jit(solution)/shard_map/ppermute | solution.py:247
  80.4 18.9 %collective-permute-start.12 = (bf16[5040,128]{1,0:T(8,128)(2,1)}, bf16[5040,128]{1,0:T(8,128)(2,1)}, u32[]{:S(2)}, u32[]{:S(2)}) collective-permute-start(bf16[5040,128]{1,0:T(8,128)(2,1)} %get-tuple-element.27), channel_id=1, source_target_pairs={{0,1},{1,0},{2,3},{3,2},{4,5},{5,4},{6,7},{7,6},{8,9},{9,8},{10,11... | collective-permute-start | bytes 3870728 | tf_op jit(solution)/shard_map/ppermute | solution.py:251
  88.5 10.3 %collective-permute-start.10 = (bf16[48,128]{1,0:T(8,128)(2,1)S(1)}, bf16[48,128]{1,0:T(8,128)(2,1)S(1)}, u32[]{:S(2)}, u32[]{:S(2)}) collective-permute-start(bf16[48,128]{1,0:T(8,128)(2,1)S(1)} %get-tuple-element.25), channel_id=1, source_target_pairs={{0,1},{1,0},{2,3},{3,2},{4,5},{5,4},{6,7},{7,6},{8,9},{9,8},{10,11... | collective-permute-start | bytes 36872 | tf_op jit(solution)/shard_map/ppermute | solution.py:251
  94.5 20.3 %collective-permute-start.11 = (bf16[3072,128]{1,0:T(8,128)(2,1)}, bf16[3072,128]{1,0:T(8,128)(2,1)}, u32[]{:S(2)}, u32[]{:S(2)}) collective-permute-start(bf16[3072,128]{1,0:T(8,128)(2,1)} %get-tuple-element.26), channel_id=1, source_target_pairs={{0,2},{1,47},{2,4},{3,1},{4,6},{5,3},{6,8},{7,5},{8,10},{9,7},{10,... | collective-permute-start | bytes 2359304 | tf_op jit(solution)/shard_map/ppermute | solution.py:247
  116.9 5.1 %collective-permute-start.13 = (bf16[3584,128]{1,0:T(8,128)(2,1)}, bf16[3584,128]{1,0:T(8,128)(2,1)}, u32[]{:S(2)}, u32[]{:S(2)}) collective-permute-start(bf16[3584,128]{1,0:T(8,128)(2,1)} %shard_map.153), channel_id=1, source_target_pairs={{0,1},{1,0},{2,3},{3,2},{4,5},{5,4},{6,7},{7,6},{8,9},{9,8},{10,11... | collective-permute-start | bytes 2752520 | tf_op jit(solution)/shard_map/ppermute | solution.py:251
  (22 other events, 176.8 us)

commit v9 on v8

--- a/solution.py
+++ b/solution.py
@@ -179,7 +179,7 @@
             acc[table_ref[3, base + n]] += both[:, BLK:]
             return carry
 
-        unroll = max(n for n in (7, 6, 5, 4, 3, 2, 1) if count % n == 0)
+        unroll = max(n for n in range(1, 17) if count % n == 0)
         lax.fori_loop(0, count, body, 0, unroll=unroll)
         base += count
     if last:
@@ -327,22 +327,25 @@
     early = items([(1, 1), (5, 13), (2, 2), (6, 14), (3, 3), (7, 15)]) + [(4, 12, 0)]
     early += items([(2, 1), (6, 13), (3, 2), (7, 14), (0, 15), (4, 3)]) + [(5, 12, 0)]
 
-    def pass_on(names, kept=None, notes=(), after=()):
+    def pass_on(names, pieces, kept=None, notes=(), after=()):
         entries = [(at[name][0], at[name][1] + b) for name in names for b, _ in passed_on(name)]
-        spec = [(entries, bool(notes))]
+        size = len(entries) // pieces
+        assert size * pieces == len(entries)
+        spec = [(entries[n * size : (n + 1) * size], bool(notes) and n == 0) for n in range(pieces)]
         if kept:
             spec.append(([(at[name][0], at[name][1] + b) for name in kept for b, _ in wanted(name)], False))
-        array, *own_part = packed(spec, notes, after)
-        received = from_other_core(array)
-        end = len(entries) * BLK
-        return received, own_part, (array[end:], received[end:])
+        arrays = packed(spec, notes, after)
+        received = [from_other_core(array) for array in arrays[:pieces]]
+        end = size * BLK
+        return received, arrays[pieces:], (arrays[0][end:], received[0][end:])
 
     mine = items([(0, 0), (1, 0)]) + early
-    early_other, early_own, early_notes = pass_on(early, mine, middle, (up_in,))
+    early_other, early_own, early_notes = pass_on(early, 3, mine, middle, (up_in,))
 
     names = items([(1, 16), (5, 4), (2, 17), (6, 5), (0, 15), (4, 3)])
     up_in, notes = packed([(blocks(names), False), ((), True)], far)
     send(up_in, names, 1)
+    notes, _ = lax.optimization_barrier((notes, early_other[2]))
     notes = (notes, from_other_core(notes))
 
     late = items([(1, 16), (5, 4), (2, 17), (6, 5)])
@@ -356,12 +359,13 @@
                 by_source.setdefault(source, []).append(((place + b) * BLK, 0, name[2], name[1], panel))
         return [(sources[source], rows) for source, rows in sorted(by_source.items())]
 
-    def received_of(array, names):
-        rows = []
-        for name in names:
-            for _, panel in passed_on(name):
-                rows.append((len(rows) * BLK, 1, name[2], name[1], panel))
-        return [(array, rows)]
+    def received_of(arrays, names):
+        found = [(name, panel) for name in names for _, panel in passed_on(name)]
+        size = len(found) // len(arrays)
+        return [
+            (array, [(m * BLK, 1, name[2], name[1], panel) for m, (name, panel) in enumerate(found[n * size : (n + 1) * size])])
+            for n, array in enumerate(arrays)
+        ]
 
     panels = (start + core + jnp.arange(STEPS, dtype=jnp.int32)) % 16
     digits = right.reshape(16, HALF, BLK)[:, STEPS * BLK, :32].astype(jnp.int32)
@@ -384,9 +388,9 @@
         rows += [(len(rows) * BLK + n * BLK, 0, name[2], name[1], w) for n, (_, w) in enumerate(wanted(name))]
     part = [(early_own[0], rows)] + received_of(early_other, early)
     sums, _ = product_of(table_of((part,), early_notes), part, 0)
-    parts = [part_of(late), received_of(None, late)]
+    parts = [part_of(late), received_of([None], late)]
     table = table_of(parts, notes)
-    late_other, _, _ = pass_on(late, None, (), (sums,))
+    late_other, _, _ = pass_on(late, 1, None, (), (sums,))
     sums, base = product_of(table, parts[0], 0, sums)
     out, _ = product_of(table, received_of(late_other, late), base, sums, last=True)
     return out[None, None]

time: 126 us -> 129 us (1.024); the launches traced: 125 us -> 127 us
  local copies, waits for them, and re-layouts: 9.92 us -> 18 us
  waiting for transfers between devices: 21.3 us -> 15.5 us
  Pallas kernels: 18.7 us -> 16.5 us
  starting transfers between devices: 71.1 us -> 72.8 us
    unnamed x62 -> x70, local copies, waits for them, and re-layouts: 8.2 us -> 17.7 us
    all_to_all x1, waiting for transfers between devices: 5.26 us -> 0.01 us  [local(): lax.all_to_all(right_packed(b_kept, b_other, up_in), 'y', 0, 0, tiled=True)]
    pallas_call x3, Pallas kernels: 12.7 us -> 8.49 us  [product(): pl.pallas_call(functools.partial(product_kernel, counts, base, before is...]
    pallas_call x5, Pallas kernels: 4.53 us -> 5.98 us  [pack(): pl.pallas_call(functools.partial(pack_kernel, spec, notes, len(used)), ou...]
    another operation x2, local copies, waits for them, and re-layouts: 1.42 us -> 0.01 us  [tables(): notes = jnp.stack(notes)[:, :, :32].astype(jnp.int32)]
    ppermute x8, starting transfers between devices: 33.6 us -> 35 us  [moved(): return lax.ppermute(array, COL, route)]
    ppermute x5 -> x7, starting transfers between devices: 28.7 us -> 29 us  [from_other_core(): return lax.ppermute(array, 'core', [(0, 1), (1, 0)])]
  transfers between devices with their start and end apart: 15 -> 17, of which waited for: 7 -> 8; matrix products, arithmetic and copies ran while one was open for 4% -> 2% of each run, Pallas kernels for 11% -> 9%
where the time goes in v9:
time: 129 us; the launch traced here: 127 us
  starting transfers between devices  72.8 us (56%)
  local copies, waits for them, and re-layouts  18 us (14%)
  Pallas kernels  16.5 us (13%)
  waiting for transfers between devices  15.5 us (12%)
  other arithmetic  3.48 us (3%)
    ppermute x8, starting transfers between devices, moved(): return lax.ppermute(array, COL, route)  35 us
    ppermute x7, starting transfers between devices, from_other_core(): return lax.ppermute(array, 'core', [(0, 1), (1, 0)])  29 us
    unnamed x70, local copies, waits for them, and re-layouts  17.7 us
    ppermute x8, waiting for transfers between devices, moved(): return lax.ppermute(array, COL, route)  15.3 us
    pallas_call x3, Pallas kernels, product(): pl.pallas_call(functools.partial(product_kernel, counts, base, before is...  8.49 us
    all_to_all x1, starting transfers between devices, local(): lax.all_to_all(right_packed(b_kept, b_other, up_in), 'y', 0, 0, tiled=True)  6.86 us
    pallas_call x5, Pallas kernels, pack(): pl.pallas_call(functools.partial(pack_kernel, spec, notes, len(used)), ou...  5.98 us
  transfers between devices with their start and end apart: 17, of which 8 were waited for; matrix products, arithmetic and copies ran while one was open for 2% of the time, Pallas kernels for 9%

profile of v9, /device:TPU:1, one launch (start us, length us, event | category | flops | bytes accessed | tf_op | source)
XLA Modules:
  0.0 126.9 jit_solution(13066783437543065591)
XLA Ops:
  0.8 12.4 %collective-permute-start.2 = (bf16[16,128]{1,0:T(8,128)(2,1)S(1)}, bf16[16,128]{1,0:T(8,128)(2,1)S(1)}, u32[]{:S(2)}, u32[]{:S(2)}) collective-permute-start(bf16[16,128]{1,0:T(8,128)(2,1)S(1)} %fusion.37), channel_id=1, source_target_pairs={{0,1},{1,0},{2,3},{3,2},{4,5},{5,4},{6,7},{7,6},{8,9},{9,8},{10,11... | collective-permute-start | bytes 12296 | tf_op jit(solution)/shard_map/ppermute | solution.py:251
  13.2 1.9 %collective-permute-start.1 = (bf16[16,128,128]{2,1,0:T(8,128)(2,1)}, bf16[16,128,128]{2,1,0:T(8,128)(2,1)S(1)}, u32[]{:S(2)}, u32[]{:S(2)}) collective-permute-start(bf16[16,128,128]{2,1,0:T(8,128)(2,1)} %bitcast.76), channel_id=1, source_target_pairs={{0,1},{1,0},{2,3},{3,2},{4,5},{5,4},{6,7},{7,6},{8,9},{9,8},{10,11... | collective-permute-start | bytes 1572872 | tf_op jit(solution)/shard_map/ppermute | solution.py:251
  17.6 1.9 %collective-permute-start = (bf16[1296,128]{1,0:T(8,128)(2,1)S(1)}, bf16[1296,128]{1,0:T(8,128)(2,1)S(1)}, u32[]{:S(2)}, u32[]{:S(2)}) collective-permute-start(bf16[1296,128]{1,0:T(8,128)(2,1)S(1)} %get-tuple-element.21), channel_id=1, source_target_pairs={{0,384},{384,0},{1,385},{385,1},{2,386},{386,2},{3,387},{387,3},{4... | collective-permute-start | bytes 995336 | tf_op jit(solution)/shard_map/ppermute | solution.py:269
  22.2 8.6 %collective-permute-start.3 = (bf16[1040,128]{1,0:T(8,128)(2,1)S(1)}, bf16[1040,128]{1,0:T(8,128)(2,1)S(1)}, u32[]{:S(2)}, u32[]{:S(2)}) collective-permute-start(bf16[1040,128]{1,0:T(8,128)(2,1)S(1)} %get-tuple-element.23), channel_id=1, source_target_pairs={{0,4},{1,45},{2,6},{3,47},{4,8},{5,1},{6,10},{7,3},{8,12},{9,5},{1... | collective-permute-start | bytes 798728 | tf_op jit(solution)/shard_map/ppermute | solution.py:247
  30.8 1.9 %collective-permute-start.4 = (bf16[1040,128]{1,0:T(8,128)(2,1)S(1)}, bf16[1040,128]{1,0:T(8,128)(2,1)S(1)}, u32[]{:S(2)}, u32[]{:S(2)}) collective-permute-start(bf16[1040,128]{1,0:T(8,128)(2,1)S(1)} %get-tuple-element.24.refs_0_), channel_id=1, source_target_pairs={{0,28},{1,21},{2,30},{3,23},{4,32},{5,25},{6,34},{7,27},{8,36},{9,... | collective-permute-start | bytes 798728 | tf_op jit(solution)/shard_map/ppermute | solution.py:247
  32.7 3.9 %collective-permute-start.5 = (bf16[1040,128]{1,0:T(8,128)(2,1)S(1)}, bf16[1040,128]{1,0:T(8,128)(2,1)S(1)}, u32[]{:S(2)}, u32[]{:S(2)}) collective-permute-start(bf16[1040,128]{1,0:T(8,128)(2,1)S(1)} %get-tuple-element.25.refs_1_), channel_id=1, source_target_pairs={{0,2},{1,47},{2,4},{3,1},{4,6},{5,3},{6,8},{7,5},{8,10},{9,7},{10,... | collective-permute-start | bytes 798728 | tf_op jit(solution)/shard_map/ppermute | solution.py:247
  36.6 1.9 %collective-permute-start.6 = (bf16[1040,128]{1,0:T(8,128)(2,1)S(1)}, bf16[1040,128]{1,0:T(8,128)(2,1)S(1)}, u32[]{:S(2)}, u32[]{:S(2)}) collective-permute-start(bf16[1040,128]{1,0:T(8,128)(2,1)S(1)} %get-tuple-element.22.refs_0_), channel_id=1, source_target_pairs={{0,26},{1,23},{2,28},{3,25},{4,30},{5,27},{6,32},{7,29},{8,34},{9,... | collective-permute-start | bytes 798728 | tf_op jit(solution)/shard_map/ppermute | solution.py:247
  39.3 5.2 %collective-permute-done.4.refs_2_.refs_3_ = bf16[1040,128]{1,0:T(8,128)(2,1)S(1)} collective-permute-done((bf16[1040,128]{1,0:T(8,128)(2,1)S(1)}, bf16[1040,128]{1,0:T(8,128)(2,1)S(1)}, u32[]{:S(2)}, u32[]{:S(2)}) %collective-permute-start.4) | collective-permute-done | bytes 266272 | tf_op jit(solution)/shard_map/ppermute | solution.py:247
  46.2 3.7 %collective-permute-done.6.refs_4_.refs_1_.refs_5_ = bf16[1040,128]{1,0:T(8,128)(2,1)S(1)} collective-permute-done((bf16[1040,128]{1,0:T(8,128)(2,1)S(1)}, bf16[1040,128]{1,0:T(8,128)(2,1)S(1)}, u32[]{:S(2)}, u32[]{:S(2)}) %collective-permute-start.6) | collective-permute-done | bytes 266272 | tf_op jit(solution)/shard_map/ppermute | solution.py:247
  50.7 5.2 %collective-permute-start.7 = (bf16[3120,128]{1,0:T(8,128)(2,1)S(1)}, bf16[3120,128]{1,0:T(8,128)(2,1)S(1)}, u32[]{:S(2)}, u32[]{:S(2)}) collective-permute-start(bf16[3120,128]{1,0:T(8,128)(2,1)S(1)} %shard_map.147.refs_2_.refs_0_.refs_6_), channel_id=1, source_target_pairs={{0,2},{1,47},{2,4},{3,1},{4,6},{5,3},{6,8},{7,5},{8,10},{9,7},{10,... | collective-permute-start | bytes 2396168 | tf_op jit(solution)/shard_map/ppermute | solution.py:247
  57.5 6.9 %all-to-all-start = ((bf16[8,800,128]{2,1,0:T(8,128)(2,1)}), bf16[8,800,128]{2,1,0:T(8,128)(2,1)S(1)}, u32[]{:S(2)}, u32[]{:S(2)}) async-start(bf16[8,800,128]{2,1,0:T(8,128)(2,1)} %copy-done), calls=%async_computation | async-start | bytes 3276800 | tf_op jit(solution)/shard_map/all_to_all | solution.py:316
  66.8 3.8 %collective-permute-start.9 = (bf16[528,128]{1,0:T(8,128)(2,1)}, bf16[528,128]{1,0:T(8,128)(2,1)}, u32[]{:S(2)}, u32[]{:S(2)}) collective-permute-start(bf16[528,128]{1,0:T(8,128)(2,1)} %get-tuple-element.27), channel_id=1, source_target_pairs={{0,24},{1,25},{2,26},{3,27},{4,28},{5,29},{6,30},{7,31},{8,32},{9,... | collective-permute-start | bytes 405512 | tf_op jit(solution)/shard_map/ppermute | solution.py:247
  70.6 3.6 %collective-permute-start.8 = (bf16[2096,128]{1,0:T(8,128)(2,1)}, bf16[2096,128]{1,0:T(8,128)(2,1)S(1)}, u32[]{:S(2)}, u32[]{:S(2)}) collective-permute-start(bf16[2096,128]{1,0:T(8,128)(2,1)} %copy-done.6), channel_id=1, source_target_pairs={{0,30},{1,19},{2,32},{3,21},{4,34},{5,23},{6,36},{7,25},{8,38},{9,... | collective-permute-start | bytes 1609736 | tf_op jit(solution)/shard_map/ppermute | solution.py:247
  83.2 6.0 %collective-permute-start.13 = (bf16[1712,128]{1,0:T(8,128)(2,1)S(1)}, bf16[1712,128]{1,0:T(8,128)(2,1)S(1)}, u32[]{:S(2)}, u32[]{:S(2)}) collective-permute-start(bf16[1712,128]{1,0:T(8,128)(2,1)S(1)} %get-tuple-element.32), channel_id=1, source_target_pairs={{0,1},{1,0},{2,3},{3,2},{4,5},{5,4},{6,7},{7,6},{8,9},{9,8},{10,11... | collective-permute-start | bytes 1314824 | tf_op jit(solution)/shard_map/ppermute | solution.py:251
  89.2 1.9 %collective-permute-start.10 = (bf16[1664,128]{1,0:T(8,128)(2,1)S(1)}, bf16[1664,128]{1,0:T(8,128)(2,1)S(1)}, u32[]{:S(2)}, u32[]{:S(2)}) collective-permute-start(bf16[1664,128]{1,0:T(8,128)(2,1)S(1)} %get-tuple-element.29), channel_id=1, source_target_pairs={{0,1},{1,0},{2,3},{3,2},{4,5},{5,4},{6,7},{7,6},{8,9},{9,8},{10,11... | collective-permute-start | bytes 1277960 | tf_op jit(solution)/shard_map/ppermute | solution.py:251
  91.2 2.4 %collective-permute-start.14 = (bf16[1664,128]{1,0:T(8,128)(2,1)}, bf16[1664,128]{1,0:T(8,128)(2,1)}, u32[]{:S(2)}, u32[]{:S(2)}) collective-permute-start(bf16[1664,128]{1,0:T(8,128)(2,1)} %get-tuple-element.34), channel_id=1, source_target_pairs={{0,1},{1,0},{2,3},{3,2},{4,5},{5,4},{6,7},{7,6},{8,9},{9,8},{10,11... | collective-permute-start | bytes 1277960 | tf_op jit(solution)/shard_map/ppermute | solution.py:251
  93.6 3.1 %collective-permute-done.8.refs_2_.refs_0_.rest_0_ = bf16[2096,128]{1,0:T(8,128)(2,1)S(1)} collective-permute-done((bf16[2096,128]{1,0:T(8,128)(2,1)}, bf16[2096,128]{1,0:T(8,128)(2,1)S(1)}, u32[]{:S(2)}, u32[]{:S(2)}) %collective-permute-start.8) | collective-permute-done | bytes 536608 | tf_op jit(solution)/shard_map/ppermute | solution.py:247
  96.7 2.0 %shard_map.150 = (bf16[3072,128]{1,0:T(8,128)(2,1)}, bf16[48,128]{1,0:T(8,128)(2,1)S(1)}) custom-call(bf16[3120,128]{1,0:T(8,128)(2,1)S(1)} %shard_map.147.refs_2_.refs_0_.refs_6_, bf16[3120,128]{1,0:T(8,128)(2,1)S(1)} %collective-permute-done.7.refs_3_.refs_1_.refs_7_, bf16[2096,128]{1,0:T(8,128)(2,1)S(1)} %collective-permute-done.8.refs_2_.refs_0_.rest_0_, ...), custom_call_target="tpu_custom_call" | custom-call | bytes 1572864 | tf_op jit(solution)/shard_map/pallas_call | solution.py:148
  98.7 6.0 %collective-permute-start.12 = (bf16[3072,128]{1,0:T(8,128)(2,1)}, bf16[3072,128]{1,0:T(8,128)(2,1)}, u32[]{:S(2)}, u32[]{:S(2)}) collective-permute-start(bf16[3072,128]{1,0:T(8,128)(2,1)} %get-tuple-element.31), channel_id=1, source_target_pairs={{0,2},{1,47},{2,4},{3,1},{4,6},{5,3},{6,8},{7,5},{8,10},{9,7},{10,... | collective-permute-start | bytes 2359304 | tf_op jit(solution)/shard_map/ppermute | solution.py:247
  113.6 3.4 %shard_map.152.refs_2_.rest_2_ = f32[13,128,128]{2,1,0:T(8,128)S(1)} custom-call(s32[5,84]{1,0:T(8,128)S(1)} %stack.59.table_ref, bf16[6400,128]{1,0:T(8,128)(2,1)S(1)} %bitcast.72, bf16[5760,128]{1,0:T(8,128)(2,1)S(1)} %copy-done.21, bf16[1712,128]{1,0:T(8,128)(2,1)S(1)} %copy-done.19, bf16[1664,128]{1,0:T(8,128)(2,1)} %collective-permute-done.14.rest_2_, ...), custom_call_target="tpu_custom_call" | custom-call | flops 2818572288 | bytes 2752512 | tf_op jit(solution)/shard_map/pallas_call | solution.py:192
  117.0 2.1 %shard_map.153 = bf16[3584,128]{1,0:T(8,128)(2,1)} custom-call(bf16[2096,128]{1,0:T(8,128)(2,1)S(1)} %copy-done.2, bf16[3072,128]{1,0:T(8,128)(2,1)} %collective-permute-done.12.refs_1_.rest_1_, f32[13,128,128]{2,1,0:T(8,128)S(1)} %shard_map.152.refs_2_.rest_2_), custom_call_target="tpu_custom_call" | custom-call | bytes 1835008 | tf_op jit(solution)/shard_map/pallas_call | solution.py:148
  119.1 2.5 %collective-permute-start.15 = (bf16[3584,128]{1,0:T(8,128)(2,1)}, bf16[3584,128]{1,0:T(8,128)(2,1)}, u32[]{:S(2)}, u32[]{:S(2)}) collective-permute-start(bf16[3584,128]{1,0:T(8,128)(2,1)} %shard_map.153), channel_id=1, source_target_pairs={{0,1},{1,0},{2,3},{3,2},{4,5},{5,4},{6,7},{7,6},{8,9},{9,8},{10,11... | collective-permute-start | bytes 2752520 | tf_op jit(solution)/shard_map/ppermute | solution.py:251
  121.8 2.2 %shard_map.154.rest_1_ = f32[13,128,128]{2,1,0:T(8,128)S(1)} custom-call(s32[5,60]{1,0:T(8,128)S(1)} %stack.52.table_ref, bf16[6400,128]{1,0:T(8,128)(2,1)S(1)} %bitcast.73, bf16[2096,128]{1,0:T(8,128)(2,1)S(1)} %copy-done.2, bf16[3072,128]{1,0:T(8,128)(2,1)} %collective-permute-done.12.refs_1_.rest_1_, f32[13,128,128]{2,1,0:T(8,128)S(1)} %shard_map.152.refs_2_.rest_2_), custom_call_target="tpu_custom_call" | custom-call | flops 1073741824 | bytes 1048576 | tf_op jit(solution)/shard_map/pallas_call | solution.py:192
  124.0 2.9 %shard_map.155 = bf16[12,128,128]{2,1,0:T(8,128)(2,1)} custom-call(s32[5,60]{1,0:T(8,128)S(1)} %stack.52.table_ref, bf16[6400,128]{1,0:T(8,128)(2,1)S(1)} %bitcast.74, bf16[3584,128]{1,0:T(8,128)(2,1)} %collective-permute-done.15.rest_0_, f32[13,128,128]{2,1,0:T(8,128)S(1)} %shard_map.154.rest_1_), custom_call_target="tpu_custom_call" | custom-call | flops 939524096 | bytes 917504 | tf_op jit(solution)/shard_map/pallas_call | solution.py:192
  (153 shorter events, 30.7 us)
Async XLA Ops:
  0.0 38.5 %copy-start.25 = (s32[84]{0:T(128)S(1)}, s32[84]{0:T(128)}, u32[]{:S(2)}) copy-start(s32[84]{0:T(128)} %constant.374.clone) | copy-start | bytes 1012
  0.0 38.6 %copy-start.27 = (s32[84]{0:T(128)S(1)}, s32[84]{0:T(128)}, u32[]{:S(2)}) copy-start(s32[84]{0:T(128)} %constant.377.clone) | copy-start | bytes 1012
  0.8 18.9 %collective-permute-start.2 = (bf16[16,128]{1,0:T(8,128)(2,1)S(1)}, bf16[16,128]{1,0:T(8,128)(2,1)S(1)}, u32[]{:S(2)}, u32[]{:S(2)}) collective-permute-start(bf16[16,128]{1,0:T(8,128)(2,1)S(1)} %fusion.37), channel_id=1, source_target_pairs={{0,1},{1,0},{2,3},{3,2},{4,5},{5,4},{6,7},{7,6},{8,9},{9,8},{10,11... | collective-permute-start | bytes 12296 | tf_op jit(solution)/shard_map/ppermute | solution.py:251
  13.2 6.6 %collective-permute-start.1 = (bf16[16,128,128]{2,1,0:T(8,128)(2,1)}, bf16[16,128,128]{2,1,0:T(8,128)(2,1)S(1)}, u32[]{:S(2)}, u32[]{:S(2)}) collective-permute-start(bf16[16,128,128]{2,1,0:T(8,128)(2,1)} %bitcast.76), channel_id=1, source_target_pairs={{0,1},{1,0},{2,3},{3,2},{4,5},{5,4},{6,7},{7,6},{8,9},{9,8},{10,11... | collective-permute-start | bytes 1572872 | tf_op jit(solution)/shard_map/ppermute | solution.py:251
  17.6 20.9 %collective-permute-start = (bf16[1296,128]{1,0:T(8,128)(2,1)S(1)}, bf16[1296,128]{1,0:T(8,128)(2,1)S(1)}, u32[]{:S(2)}, u32[]{:S(2)}) collective-permute-start(bf16[1296,128]{1,0:T(8,128)(2,1)S(1)} %get-tuple-element.21), channel_id=1, source_target_pairs={{0,384},{384,0},{1,385},{385,1},{2,386},{386,2},{3,387},{387,3},{4... | collective-permute-start | bytes 995336 | tf_op jit(solution)/shard_map/ppermute | solution.py:269
  20.9 35.1 %copy-start.32 = (s32[84]{0:T(128)S(1)}, s32[84]{0:T(128)}, u32[]{:S(2)}) copy-start(s32[84]{0:T(128)} %constant.376.clone) | copy-start | bytes 1012
  20.9 35.1 %copy-start.24 = (s32[60]{0:T(128)S(1)}, s32[60]{0:T(128)}, u32[]{:S(2)}) copy-start(s32[60]{0:T(128)} %constant.379.clone) | copy-start | bytes 724
  20.9 35.1 %copy-start.26 = (s32[60]{0:T(128)S(1)}, s32[60]{0:T(128)}, u32[]{:S(2)}) copy-start(s32[60]{0:T(128)} %constant.382.clone) | copy-start | bytes 724
  20.9 35.1 %copy-start.29 = (s32[60]{0:T(128)S(1)}, s32[60]{0:T(128)}, u32[]{:S(2)}) copy-start(s32[60]{0:T(128)} %constant.380.clone) | copy-start | bytes 724
  20.9 35.1 %copy-start.30 = (s32[60]{0:T(128)S(1)}, s32[60]{0:T(128)}, u32[]{:S(2)}) copy-start(s32[60]{0:T(128)} %constant.381.clone) | copy-start | bytes 724
  22.2 17.1 %collective-permute-start.3 = (bf16[1040,128]{1,0:T(8,128)(2,1)S(1)}, bf16[1040,128]{1,0:T(8,128)(2,1)S(1)}, u32[]{:S(2)}, u32[]{:S(2)}) collective-permute-start(bf16[1040,128]{1,0:T(8,128)(2,1)S(1)} %get-tuple-element.23), channel_id=1, source_target_pairs={{0,4},{1,45},{2,6},{3,47},{4,8},{5,1},{6,10},{7,3},{8,12},{9,5},{1... | collective-permute-start | bytes 798728 | tf_op jit(solution)/shard_map/ppermute | solution.py:247
  30.8 13.7 %collective-permute-start.4 = (bf16[1040,128]{1,0:T(8,128)(2,1)S(1)}, bf16[1040,128]{1,0:T(8,128)(2,1)S(1)}, u32[]{:S(2)}, u32[]{:S(2)}) collective-permute-start(bf16[1040,128]{1,0:T(8,128)(2,1)S(1)} %get-tuple-element.24.refs_0_), channel_id=1, source_target_pairs={{0,28},{1,21},{2,30},{3,23},{4,32},{5,25},{6,34},{7,27},{8,36},{9,... | collective-permute-start | bytes 798728 | tf_op jit(solution)/shard_map/ppermute | solution.py:247
  32.7 13.4 %collective-permute-start.5 = (bf16[1040,128]{1,0:T(8,128)(2,1)S(1)}, bf16[1040,128]{1,0:T(8,128)(2,1)S(1)}, u32[]{:S(2)}, u32[]{:S(2)}) collective-permute-start(bf16[1040,128]{1,0:T(8,128)(2,1)S(1)} %get-tuple-element.25.refs_1_), channel_id=1, source_target_pairs={{0,2},{1,47},{2,4},{3,1},{4,6},{5,3},{6,8},{7,5},{8,10},{9,7},{10,... | collective-permute-start | bytes 798728 | tf_op jit(solution)/shard_map/ppermute | solution.py:247
  36.6 13.3 %collective-permute-start.6 = (bf16[1040,128]{1,0:T(8,128)(2,1)S(1)}, bf16[1040,128]{1,0:T(8,128)(2,1)S(1)}, u32[]{:S(2)}, u32[]{:S(2)}) collective-permute-start(bf16[1040,128]{1,0:T(8,128)(2,1)S(1)} %get-tuple-element.22.refs_0_), channel_id=1, source_target_pairs={{0,26},{1,23},{2,28},{3,25},{4,30},{5,27},{6,32},{7,29},{8,34},{9,... | collective-permute-start | bytes 798728 | tf_op jit(solution)/shard_map/ppermute | solution.py:247
  50.7 14.2 %collective-permute-start.7 = (bf16[3120,128]{1,0:T(8,128)(2,1)S(1)}, bf16[3120,128]{1,0:T(8,128)(2,1)S(1)}, u32[]{:S(2)}, u32[]{:S(2)}) collective-permute-start(bf16[3120,128]{1,0:T(8,128)(2,1)S(1)} %shard_map.147.refs_2_.refs_0_.refs_6_), channel_id=1, source_target_pairs={{0,2},{1,47},{2,4},{3,1},{4,6},{5,3},{6,8},{7,5},{8,10},{9,7},{10,... | collective-permute-start | bytes 2396168 | tf_op jit(solution)/shard_map/ppermute | solution.py:247
  57.5 51.7 %all-to-all-start = ((bf16[8,800,128]{2,1,0:T(8,128)(2,1)}), bf16[8,800,128]{2,1,0:T(8,128)(2,1)S(1)}, u32[]{:S(2)}, u32[]{:S(2)}) async-start(bf16[8,800,128]{2,1,0:T(8,128)(2,1)} %copy-done), calls=%async_computation | async-start | bytes 3276800 | tf_op jit(solution)/shard_map/all_to_all | solution.py:316
  66.8 7.8 %collective-permute-start.9 = (bf16[528,128]{1,0:T(8,128)(2,1)}, bf16[528,128]{1,0:T(8,128)(2,1)}, u32[]{:S(2)}, u32[]{:S(2)}) collective-permute-start(bf16[528,128]{1,0:T(8,128)(2,1)} %get-tuple-element.27), channel_id=1, source_target_pairs={{0,24},{1,25},{2,26},{3,27},{4,28},{5,29},{6,30},{7,31},{8,32},{9,... | collective-permute-start | bytes 405512 | tf_op jit(solution)/shard_map/ppermute | solution.py:247
  70.6 26.1 %collective-permute-start.8 = (bf16[2096,128]{1,0:T(8,128)(2,1)}, bf16[2096,128]{1,0:T(8,128)(2,1)S(1)}, u32[]{:S(2)}, u32[]{:S(2)}) collective-permute-start(bf16[2096,128]{1,0:T(8,128)(2,1)} %copy-done.6), channel_id=1, source_target_pairs={{0,30},{1,19},{2,32},{3,21},{4,34},{5,23},{6,36},{7,25},{8,38},{9,... | collective-permute-start | bytes 1609736 | tf_op jit(solution)/shard_map/ppermute | solution.py:247
  83.2 24.2 %collective-permute-start.13 = (bf16[1712,128]{1,0:T(8,128)(2,1)S(1)}, bf16[1712,128]{1,0:T(8,128)(2,1)S(1)}, u32[]{:S(2)}, u32[]{:S(2)}) collective-permute-start(bf16[1712,128]{1,0:T(8,128)(2,1)S(1)} %get-tuple-element.32), channel_id=1, source_target_pairs={{0,1},{1,0},{2,3},{3,2},{4,5},{5,4},{6,7},{7,6},{8,9},{9,8},{10,11... | collective-permute-start | bytes 1314824 | tf_op jit(solution)/shard_map/ppermute | solution.py:251
  89.2 15.5 %collective-permute-start.10 = (bf16[1664,128]{1,0:T(8,128)(2,1)S(1)}, bf16[1664,128]{1,0:T(8,128)(2,1)S(1)}, u32[]{:S(2)}, u32[]{:S(2)}) collective-permute-start(bf16[1664,128]{1,0:T(8,128)(2,1)S(1)} %get-tuple-element.29), channel_id=1, source_target_pairs={{0,1},{1,0},{2,3},{3,2},{4,5},{5,4},{6,7},{7,6},{8,9},{9,8},{10,11... | collective-permute-start | bytes 1277960 | tf_op jit(solution)/shard_map/ppermute | solution.py:251
  91.2 19.0 %collective-permute-start.14 = (bf16[1664,128]{1,0:T(8,128)(2,1)}, bf16[1664,128]{1,0:T(8,128)(2,1)}, u32[]{:S(2)}, u32[]{:S(2)}) collective-permute-start(bf16[1664,128]{1,0:T(8,128)(2,1)} %get-tuple-element.34), channel_id=1, source_target_pairs={{0,1},{1,0},{2,3},{3,2},{4,5},{5,4},{6,7},{7,6},{8,9},{9,8},{10,11... | collective-permute-start | bytes 1277960 | tf_op jit(solution)/shard_map/ppermute | solution.py:251
  98.7 18.3 %collective-permute-start.12 = (bf16[3072,128]{1,0:T(8,128)(2,1)}, bf16[3072,128]{1,0:T(8,128)(2,1)}, u32[]{:S(2)}, u32[]{:S(2)}) collective-permute-start(bf16[3072,128]{1,0:T(8,128)(2,1)} %get-tuple-element.31), channel_id=1, source_target_pairs={{0,2},{1,47},{2,4},{3,1},{4,6},{5,3},{6,8},{7,5},{8,10},{9,7},{10,... | collective-permute-start | bytes 2359304 | tf_op jit(solution)/shard_map/ppermute | solution.py:247
  105.5 3.1 %collective-permute-start.11 = (bf16[48,128]{1,0:T(8,128)(2,1)S(1)}, bf16[48,128]{1,0:T(8,128)(2,1)S(1)}, u32[]{:S(2)}, u32[]{:S(2)}) collective-permute-start(bf16[48,128]{1,0:T(8,128)(2,1)S(1)} %get-tuple-element.30), channel_id=1, source_target_pairs={{0,1},{1,0},{2,3},{3,2},{4,5},{5,4},{6,7},{7,6},{8,9},{9,8},{10,11... | collective-permute-start | bytes 36872 | tf_op jit(solution)/shard_map/ppermute | solution.py:251
  119.1 4.9 %collective-permute-start.15 = (bf16[3584,128]{1,0:T(8,128)(2,1)}, bf16[3584,128]{1,0:T(8,128)(2,1)}, u32[]{:S(2)}, u32[]{:S(2)}) collective-permute-start(bf16[3584,128]{1,0:T(8,128)(2,1)} %shard_map.153), channel_id=1, source_target_pairs={{0,1},{1,0},{2,3},{3,2},{4,5},{5,4},{6,7},{7,6},{8,9},{9,8},{10,11... | collective-permute-start | bytes 2752520 | tf_op jit(solution)/shard_map/ppermute | solution.py:251
  (28 other events, 201.8 us)

commit v10 on v9

--- a/solution.py
+++ b/solution.py
@@ -19,7 +19,7 @@
 PANEL = 48
 STEPS = 3
 KEPT = 12
-SPAN = 8 + STEPS - 1
+PIECES = 1
 HALF = STEPS * 128 + 16
 BLK = 128
 
@@ -75,42 +75,23 @@
     )(index, own, other, note)
 
 
-def split_kernel(index_ref, src_ref, note_ref, *outs):
-    for half, out in enumerate(outs):
-        for n in range(SPAN):
-            out[blk(n), :] = src_ref[index_ref[SPAN * half + n]]
-        out[pl.ds(SPAN * BLK, 16), :] = note_ref[...]
-
-
-def split(index, src, note):
-    return pl.pallas_call(
-        split_kernel,
-        out_shape=[rows_shape(SPAN * BLK + 16)] * 2,
-        in_specs=[SMEM_SPEC, VMEM_SPEC, VMEM_SPEC],
-        out_specs=[VMEM_SPEC] * 2,
-        compiler_params=LIMIT,
-        cost_estimate=moves(2 * SPAN),
-    )(index, src, note)
-
-
-def right_kernel(*refs):
-    sources, out = refs[:2], refs[-1]
-    for n in range(8):
-        for half, source in enumerate(sources):
-            out[n, pl.ds(half * HALF, STEPS * BLK), :] = source[pl.ds(n * BLK, STEPS * BLK), :]
-            note = source[pl.ds(SPAN * BLK, 16), :]
-            out[n, pl.ds(half * HALF + STEPS * BLK, 16), :] = note
-
-
-def right_packed(kept, other, after):
+def right_kernel(index_ref, src_ref, code_ref, after_ref, out):
+    del after_ref
+    for n in range(16):
+        for t in range(STEPS):
+            out[n, blk(t), :] = src_ref[index_ref[n + t]]
+        out[n, pl.ds(STEPS * BLK, 16), :] = code_ref[n]
+
+
+def right_packed(src, index, codes, after):
     return pl.pallas_call(
         right_kernel,
-        out_shape=jax.ShapeDtypeStruct((8, 2 * HALF, BLK), jnp.bfloat16),
-        in_specs=[VMEM_SPEC, VMEM_SPEC, ANY_SPEC],
+        out_shape=jax.ShapeDtypeStruct((16, HALF, BLK), jnp.bfloat16),
+        in_specs=[SMEM_SPEC, VMEM_SPEC, VMEM_SPEC, ANY_SPEC],
         out_specs=VMEM_SPEC,
         compiler_params=LIMIT,
         cost_estimate=moves(48),
-    )(kept, other, after)
+    )(index, src, codes, after)
 
 
 def turned(note, distance):
@@ -203,6 +184,11 @@
 
 
 def tables(order, notes, right_codes, c_code, start, core):
+    half = NQ // 4
+    order = [
+        (row, 1 - other, 1 - k, half, panel) if d == 3 * half else (row, other, k, d, panel)
+        for row, other, k, d, panel in order
+    ]
     order = np.array(order, np.int32)
     count = order.shape[0]
     row, other, k, distance, panel = (order[:, n] for n in range(5))
@@ -264,10 +250,6 @@
         digits = jnp.concatenate([code // 64, code % 64]).astype(jnp.bfloat16).reshape(1, 32)
         return jnp.pad(digits, ((0, 15), (0, BLK - 32)))
 
-    spans = 2 * q + core + 8 * lax.axis_index("xl") + jnp.arange(SPAN, dtype=jnp.int32)
-    b_kept, b_sent = split(jnp.concatenate([spans, spans + 8]) % 16, b_own, note_of(b_own_code))
-    b_other = lax.ppermute(b_sent, "xl", [(0, 1), (1, 0)])
-
     sources, at = [], {}
 
     def keep(array, names):
@@ -287,13 +269,22 @@
 
     note = note_of(a_own_code)
     a_other, note_other = from_other_core(a_own), from_other_core(note)
+
+    shift = (2 * q + core + jnp.arange(18, dtype=jnp.int32)) % 16
+    b_code = b_own_code.reshape(16) + 1
+    b_code = jnp.sum(jnp.where(shift[:, None] == jnp.arange(16)[None, :], b_code[None, :], 0), axis=1)
+    b_code = jnp.stack([b_code[t : t + 16] for t in range(STEPS)], axis=1)
+    b_code = jnp.concatenate([b_code // 16, b_code % 16], axis=1).astype(jnp.bfloat16)
+    b_code = jnp.broadcast_to(jnp.pad(b_code, ((0, 0), (0, BLK - 6)))[:, None, :], (16, 16, BLK))
+    right = right_packed(b_own, shift, b_code, note_other)
+    right = lax.all_to_all(right, ROW, 0, 0, tiled=True).reshape(16 * HALF, BLK)
     note = jnp.concatenate([note[:1], note_other[:1], note[2:]])
     a_index = jnp.arange(16, dtype=jnp.int32)
     a_index = (start + jnp.where(core == 0, a_index, 3 - a_index)) % 16
 
     starts = [
-        (items([(3, 0), (4, 0)]), 2),
-        (items([(7, 0), (0, 0)]), 14),
+        (items([(2, 0), (3, 0), (4, 0)]), 2),
+        (items([(6, 0), (7, 0), (0, 0)]), 14),
         (items([(1, 0), (2, 0)]), 1),
         (items([(5, 0), (6, 0)]), 13),
         ([(4, 0, 0), (5, 0, 0)], 12),
@@ -309,47 +300,46 @@
     for array, (names, distance) in zip(arrays[:4], starts[:4], strict=True):
         near.append((send(array, names, distance), 2 * len(names) * BLK, distance, True))
 
-    names = items([(2, 1), (6, 13), (3, 2), (7, 14), (0, 14), (4, 2)])
-    (up_in,) = packed([(blocks(names), True)], near, (b_other,))
-    sources.append(up_in)
-    up3 = send(up_in, names, 1)
-    right = lax.all_to_all(right_packed(b_kept, b_other, up_in), "y", 0, 0, tiled=True)
-    right = right.reshape(16 * HALF, BLK)
-    middle = [(up3 - 1, 24 * BLK, 0, False), (up3, 24 * BLK, 1, False)]
-
-    names = items([(1, 1), (5, 13), (2, 2), (6, 14)])
-    (up_in,) = packed([(blocks(names), True)], middle)
-    up6 = send(up_in, names, 15)
-    across, _ = lax.optimization_barrier((arrays[4], up_in))
-    middle.append((send(across, *starts[4]), 4 * BLK, starts[4][1], True))
-    far = middle + [(up6, 16 * BLK, 15, False)]
-
-    early = items([(1, 1), (5, 13), (2, 2), (6, 14), (3, 3), (7, 15)]) + [(4, 12, 0)]
-    early += items([(2, 1), (6, 13), (3, 2), (7, 14), (0, 15), (4, 3)]) + [(5, 12, 0)]
+    sources.append(moved(note, NQ // 4))
+    opposite = len(sources) - 1
+    long_names = items([(1, 1), (5, 13), (2, 2), (6, 14)])
+    names = items([(3, 2), (7, 14), (0, 14), (4, 2)])
+    long_in, up_in = packed([(blocks(long_names), True), (blocks(names), True)], near, (sources[opposite],))
+    far = [(len(sources), 16 * BLK, 0, False)]
+    sources.append(long_in)
+    far.append((send(long_in, long_names, 15), 16 * BLK, 15, False))
+    far.append((send(up_in, names, 1), 16 * BLK, 1, False))
+    across, _ = lax.optimization_barrier((arrays[4], long_in))
+    far.append((send(across, *starts[4]), 4 * BLK, starts[4][1], True))
+    far.append((opposite, 0, NQ // 4, True))
+
+    early = items([(1, 1), (5, 13), (2, 2), (6, 14), (2, 1), (6, 13), (3, 2), (7, 14)])
 
     def pass_on(names, pieces, kept=None, notes=(), after=()):
         entries = [(at[name][0], at[name][1] + b) for name in names for b, _ in passed_on(name)]
-        size = len(entries) // pieces
-        assert size * pieces == len(entries)
-        spec = [(entries[n * size : (n + 1) * size], bool(notes) and n == 0) for n in range(pieces)]
+        size = -(-len(entries) // pieces)
+        spec = [(entries[n * size : (n + 1) * size], bool(notes) and n == pieces - 1) for n in range(pieces)]
         if kept:
             spec.append(([(at[name][0], at[name][1] + b) for name in kept for b, _ in wanted(name)], False))
         arrays = packed(spec, notes, after)
         received = [from_other_core(array) for array in arrays[:pieces]]
-        end = size * BLK
-        return received, arrays[pieces:], (arrays[0][end:], received[0][end:])
+        end = (len(entries) - size * (pieces - 1)) * BLK
+        return received, arrays[pieces:], (arrays[pieces - 1][end:], received[-1][end:])
 
     mine = items([(0, 0), (1, 0)]) + early
-    early_other, early_own, early_notes = pass_on(early, 3, mine, middle, (up_in,))
+    early_other, early_own, early_notes = pass_on(early, PIECES, mine, near, (long_in,))
 
     names = items([(1, 16), (5, 4), (2, 17), (6, 5), (0, 15), (4, 3)])
-    up_in, notes = packed([(blocks(names), False), ((), True)], far)
+    (up_in,) = packed([(blocks(names), False)])
     send(up_in, names, 1)
-    notes, _ = lax.optimization_barrier((notes, early_other[2]))
-    notes = (notes, from_other_core(notes))
-
-    late = items([(1, 16), (5, 4), (2, 17), (6, 5)])
-    late += items([(1, 17), (5, 5), (2, 18), (6, 6), (0, 16), (4, 4)])
+
+    late = [(4, 12, 0), (5, 12, 0)] + items([(3, 3), (7, 15)]) + names
+    last = items([(1, 17), (5, 5), (2, 18), (6, 6), (0, 16), (4, 4)])
+    late_other, late_own, late_notes = pass_on(late, 3, late, far, (up_in,))
+
+    def kept_of(array, names):
+        found = [(name, panel) for name in names for _, panel in wanted(name)]
+        return [(array, [(m * BLK, 0, n[2], n[1], panel) for m, (n, panel) in enumerate(found)])]
 
     def part_of(names):
         by_source = {}
@@ -361,18 +351,14 @@
 
     def received_of(arrays, names):
         found = [(name, panel) for name in names for _, panel in passed_on(name)]
-        size = len(found) // len(arrays)
+        size = -(-len(found) // len(arrays))
         return [
             (array, [(m * BLK, 1, name[2], name[1], panel) for m, (name, panel) in enumerate(found[n * size : (n + 1) * size])])
             for n, array in enumerate(arrays)
         ]
 
-    panels = (start + core + jnp.arange(STEPS, dtype=jnp.int32)) % 16
-    digits = right.reshape(16, HALF, BLK)[:, STEPS * BLK, :32].astype(jnp.int32)
-    right_codes = (digits[:, :16] * 64 + digits[:, 16:] - 1)[:, None, :]
-    right_codes = jnp.sum(
-        jnp.where(panels[:, None] == jnp.arange(16)[None, :], right_codes, 0), axis=2
-    )
+    right_codes = right.reshape(16, HALF, BLK)[:, STEPS * BLK, :6].astype(jnp.int32)
+    right_codes = right_codes[:, :3] * 16 + right_codes[:, 3:] - 1
     c_code = c_code.reshape(KEPT)
 
     def table_of(parts, notes):
@@ -383,16 +369,15 @@
         lefts, counts = [array for array, _ in part], tuple(len(rows) for _, rows in part)
         return product(table, right, lefts, counts, base, before, last), base + sum(counts)
 
-    rows = []
-    for name in mine:
-        rows += [(len(rows) * BLK + n * BLK, 0, name[2], name[1], w) for n, (_, w) in enumerate(wanted(name))]
-    part = [(early_own[0], rows)] + received_of(early_other, early)
+    part = kept_of(early_own[0], mine) + received_of(early_other, early)
     sums, _ = product_of(table_of((part,), early_notes), part, 0)
-    parts = [part_of(late), received_of([None], late)]
-    table = table_of(parts, notes)
-    late_other, _, _ = pass_on(late, 1, None, (), (sums,))
-    sums, base = product_of(table, parts[0], 0, sums)
-    out, _ = product_of(table, received_of(late_other, late), base, sums, last=True)
+    part = kept_of(late_own[0], late) + received_of(late_other, late)
+    parts = [part, part_of(last), received_of([None], last)]
+    table = table_of(parts, late_notes)
+    sums, base = product_of(table, part, 0, sums)
+    last_other, _, _ = pass_on(last, 1, None, (), (sums,))
+    sums, base = product_of(table, parts[1], base, sums)
+    out, _ = product_of(table, received_of(last_other, last), base, sums, last=True)
     return out[None, None]
 
 

time: 129 us -> 145 us (1.12)
  other arithmetic: 3.48 us -> 17.7 us
  local copies, waits for them, and re-layouts: 18 us -> 11 us
  waiting for transfers between devices: 15.5 us -> 19.8 us
  starting transfers between devices: 72.8 us -> 75.9 us
    unnamed x70 -> x35, local copies, waits for them, and re-layouts: 17.7 us -> 6.93 us
    ppermute x8 -> x9, waiting for transfers between devices: 15.3 us -> 19.8 us  [moved(): return lax.ppermute(array, COL, route)]
    pallas_call x5, Pallas kernels: 5.98 us -> 2.35 us  [pack(): pl.pallas_call(functools.partial(pack_kernel, spec, notes, len(used)), ou...]
    pallas_call x3 -> x4, Pallas kernels: 8.49 us -> 11.2 us  [product(): pl.pallas_call(functools.partial(product_kernel, counts, base, before is...]
    eq x2, other arithmetic: 0.02 us -> 2.55 us  [tables(): step == 0]
    ppermute x7, starting transfers between devices: 29 us -> 31.4 us  [from_other_core(): return lax.ppermute(array, 'core', [(0, 1), (1, 0)])]
    another operation x2, other arithmetic: 0.04 us -> 1.96 us  [tables(): jnp.stack(rows + [jnp.array(row)]).astype(jnp.int32).reshape(5, count)]
    ppermute x1 -> x0, starting transfers between devices: 1.92 us -> none  [local(): b_other = lax.ppermute(b_sent, 'xl', [(0, 1), (1, 0)])]
  transfers between devices with their start and end apart: 17 -> 17, of which waited for: 8 -> 4; matrix products, arithmetic and copies ran while one was open for 2% -> 15% of each run, Pallas kernels for 9% -> 10%
where the time goes in v10:
time: 145 us; the launch traced here: 142 us
  starting transfers between devices  75.9 us (52%)
  waiting for transfers between devices  19.8 us (14%)
  other arithmetic  17.7 us (12%)
  Pallas kernels  16.9 us (12%)
  local copies, waits for them, and re-layouts  11 us (8%)
    ppermute x9, starting transfers between devices, moved(): return lax.ppermute(array, COL, route)  36.7 us
    ppermute x7, starting transfers between devices, from_other_core(): return lax.ppermute(array, 'core', [(0, 1), (1, 0)])  31.4 us
    ppermute x9, waiting for transfers between devices, moved(): return lax.ppermute(array, COL, route)  19.8 us
    pallas_call x4, Pallas kernels, product(): pl.pallas_call(functools.partial(product_kernel, counts, base, before is...  11.2 us
    all_to_all x1, starting transfers between devices, local(): right = lax.all_to_all(right, ROW, 0, 0, tiled=True).reshape(16 * HALF, BLK)  7.8 us
    unnamed x35, local copies, waits for them, and re-layouts  6.93 us
  transfers between devices with their start and end apart: 17, of which 4 were waited for; matrix products, arithmetic and copies ran while one was open for 15% of the time, Pallas kernels for 10%

profile of v10, /device:TPU:1, one launch (start us, length us, event | category | flops | bytes accessed | tf_op | source)
XLA Modules:
  0.0 141.8 jit_solution(8964190956138390934)
XLA Ops:
  0.8 12.4 %collective-permute-start = (bf16[16,128]{1,0:T(8,128)(2,1)S(1)}, bf16[16,128]{1,0:T(8,128)(2,1)S(1)}, u32[]{:S(2)}, u32[]{:S(2)}) collective-permute-start(bf16[16,128]{1,0:T(8,128)(2,1)S(1)} %fusion.31), channel_id=1, source_target_pairs={{0,1},{1,0},{2,3},{3,2},{4,5},{5,4},{6,7},{7,6},{8,9},{9,8},{10,11... | collective-permute-start | bytes 12296 | tf_op jit(solution)/shard_map/ppermute | solution.py:237
  13.2 1.9 %collective-permute-start.2 = (bf16[16,128,128]{2,1,0:T(8,128)(2,1)}, bf16[16,128,128]{2,1,0:T(8,128)(2,1)S(1)}, u32[]{:S(2)}, u32[]{:S(2)}) collective-permute-start(bf16[16,128,128]{2,1,0:T(8,128)(2,1)} %bitcast.67), channel_id=1, source_target_pairs={{0,1},{1,0},{2,3},{3,2},{4,5},{5,4},{6,7},{7,6},{8,9},{9,8},{10,11... | collective-permute-start | bytes 1572872 | tf_op jit(solution)/shard_map/ppermute | solution.py:237
  21.9 7.7 %collective-permute-start.3 = (bf16[1552,128]{1,0:T(8,128)(2,1)}, bf16[1552,128]{1,0:T(8,128)(2,1)S(1)}, u32[]{:S(2)}, u32[]{:S(2)}) collective-permute-start(bf16[1552,128]{1,0:T(8,128)(2,1)} %get-tuple-element.20), channel_id=1, source_target_pairs={{0,4},{1,45},{2,6},{3,47},{4,8},{5,1},{6,10},{7,3},{8,12},{9,5},{1... | collective-permute-start | bytes 1191944 | tf_op jit(solution)/shard_map/ppermute | solution.py:233
  29.7 1.9 %collective-permute-start.4 = (bf16[1552,128]{1,0:T(8,128)(2,1)}, bf16[1552,128]{1,0:T(8,128)(2,1)S(1)}, u32[]{:S(2)}, u32[]{:S(2)}) collective-permute-start(bf16[1552,128]{1,0:T(8,128)(2,1)} %get-tuple-element.21.refs_0_), channel_id=1, source_target_pairs={{0,28},{1,21},{2,30},{3,23},{4,32},{5,25},{6,34},{7,27},{8,36},{9,... | collective-permute-start | bytes 1191944 | tf_op jit(solution)/shard_map/ppermute | solution.py:233
  32.9 3.6 %collective-permute-start.5 = (bf16[1040,128]{1,0:T(8,128)(2,1)S(1)}, bf16[1040,128]{1,0:T(8,128)(2,1)S(1)}, u32[]{:S(2)}, u32[]{:S(2)}) collective-permute-start(bf16[1040,128]{1,0:T(8,128)(2,1)S(1)} %get-tuple-element.22.refs_1_), channel_id=1, source_target_pairs={{0,2},{1,47},{2,4},{3,1},{4,6},{5,3},{6,8},{7,5},{8,10},{9,7},{10,... | collective-permute-start | bytes 798728 | tf_op jit(solution)/shard_map/ppermute | solution.py:233
  36.5 2.0 %collective-permute-start.6 = (bf16[1040,128]{1,0:T(8,128)(2,1)S(1)}, bf16[1040,128]{1,0:T(8,128)(2,1)S(1)}, u32[]{:S(2)}, u32[]{:S(2)}) collective-permute-start(bf16[1040,128]{1,0:T(8,128)(2,1)S(1)} %get-tuple-element.19.refs_0_.refs_2_), channel_id=1, source_target_pairs={{0,26},{1,23},{2,28},{3,25},{4,30},{5,27},{6,32},{7,29},{8,34},{9,... | collective-permute-start | bytes 798728 | tf_op jit(solution)/shard_map/ppermute | solution.py:233
  38.5 1.9 %collective-permute-start.1 = (bf16[16,128]{1,0:T(8,128)(2,1)S(1)}, bf16[16,128]{1,0:T(8,128)(2,1)S(1)}, u32[]{:S(2)}, u32[]{:S(2)}) collective-permute-start(bf16[16,128]{1,0:T(8,128)(2,1)S(1)} %maximum_maximum_fusion.note_ref), channel_id=1, source_target_pairs={{0,12},{1,37},{2,14},{3,39},{4,16},{5,41},{6,18},{7,43},{8,20},{9,... | collective-permute-start | bytes 12296 | tf_op jit(solution)/shard_map/ppermute | solution.py:233
  40.6 1.9 %shard_map.145 = bf16[16,400,128]{2,1,0:T(8,128)(2,1)} custom-call(s32[18]{0:T(128)S(1)} %and_select_fusion.17.index_ref, bf16[16,128,128]{2,1,0:T(8,128)(2,1)S(1)} %bitcast.66, bf16[16,16,128]{2,1,0:T(8,128)(2,1)S(1)} %broadcast_in_dim.226.code_ref, bf16[16,128]{1,0:T(8,128)(2,1)S(1)} %collective-permute-done.after_ref), custom_call_target="tpu_custom_call" | custom-call | bytes 3145728 | tf_op jit(solution)/shard_map/pallas_call | solution.py:87
  42.4 7.8 %all-to-all-start = ((bf16[16,400,128]{2,1,0:T(8,128)(2,1)}), bf16[16,400,128]{2,1,0:T(8,128)(2,1)S(1)}, u32[]{:S(2)}, u32[]{:S(2)}) async-start(bf16[16,400,128]{2,1,0:T(8,128)(2,1)} %shard_map.145), calls=%async_computation | async-start | bytes 3276800 | tf_op jit(solution)/shard_map/all_to_all | solution.py:280
  51.1 2.9 %collective-permute-done.6.refs_4_.refs_6_ = bf16[1040,128]{1,0:T(8,128)(2,1)S(1)} collective-permute-done((bf16[1040,128]{1,0:T(8,128)(2,1)S(1)}, bf16[1040,128]{1,0:T(8,128)(2,1)S(1)}, u32[]{:S(2)}, u32[]{:S(2)}) %collective-permute-start.6) | collective-permute-done | bytes 266272 | tf_op jit(solution)/shard_map/ppermute | solution.py:233
  56.2 8.4 %collective-permute-start.14 = (bf16[3120,128]{1,0:T(8,128)(2,1)S(1)}, bf16[3120,128]{1,0:T(8,128)(2,1)S(1)}, u32[]{:S(2)}, u32[]{:S(2)}) collective-permute-start(bf16[3120,128]{1,0:T(8,128)(2,1)S(1)} %get-tuple-element.31), channel_id=1, source_target_pairs={{0,1},{1,0},{2,3},{3,2},{4,5},{5,4},{6,7},{7,6},{8,9},{9,8},{10,11... | collective-permute-start | bytes 2396168 | tf_op jit(solution)/shard_map/ppermute | solution.py:237
  65.1 2.3 %collective-permute-start.7 = (bf16[2096,128]{1,0:T(8,128)(2,1)S(1)}, bf16[2096,128]{1,0:T(8,128)(2,1)S(1)}, u32[]{:S(2)}, u32[]{:S(2)}) collective-permute-start(bf16[2096,128]{1,0:T(8,128)(2,1)S(1)} %get-tuple-element.23.refs_1_.refs_7_), channel_id=1, source_target_pairs={{0,30},{1,19},{2,32},{3,21},{4,34},{5,23},{6,36},{7,25},{8,38},{9,... | collective-permute-start | bytes 1609736 | tf_op jit(solution)/shard_map/ppermute | solution.py:233
  67.4 5.2 %collective-permute-start.8 = (bf16[2096,128]{1,0:T(8,128)(2,1)S(1)}, bf16[2096,128]{1,0:T(8,128)(2,1)S(1)}, u32[]{:S(2)}, u32[]{:S(2)}) collective-permute-start(bf16[2096,128]{1,0:T(8,128)(2,1)S(1)} %get-tuple-element.24), channel_id=1, source_target_pairs={{0,2},{1,47},{2,4},{3,1},{4,6},{5,3},{6,8},{7,5},{8,10},{9,7},{10,... | collective-permute-start | bytes 1609736 | tf_op jit(solution)/shard_map/ppermute | solution.py:233
  73.7 3.6 %collective-permute-start.9 = (bf16[528,128]{1,0:T(8,128)(2,1)S(1)}, bf16[528,128]{1,0:T(8,128)(2,1)S(1)}, u32[]{:S(2)}, u32[]{:S(2)}) collective-permute-start(bf16[528,128]{1,0:T(8,128)(2,1)S(1)} %copy-done.9), channel_id=1, source_target_pairs={{0,24},{1,25},{2,26},{3,27},{4,28},{5,29},{6,30},{7,31},{8,32},{9,... | collective-permute-start | bytes 405512 | tf_op jit(solution)/shard_map/ppermute | solution.py:233
  77.4 14.3 %collective-permute-done.7.refs_0_.refs_2_ = bf16[2096,128]{1,0:T(8,128)(2,1)S(1)} collective-permute-done((bf16[2096,128]{1,0:T(8,128)(2,1)S(1)}, bf16[2096,128]{1,0:T(8,128)(2,1)S(1)}, u32[]{:S(2)}, u32[]{:S(2)}) %collective-permute-start.7) | collective-permute-done | bytes 536608 | tf_op jit(solution)/shard_map/ppermute | solution.py:233
  91.7 1.8 %collective-permute-done.8.refs_1_.refs_3_ = bf16[2096,128]{1,0:T(8,128)(2,1)S(1)} collective-permute-done((bf16[2096,128]{1,0:T(8,128)(2,1)S(1)}, bf16[2096,128]{1,0:T(8,128)(2,1)S(1)}, u32[]{:S(2)}, u32[]{:S(2)}) %collective-permute-start.8) | collective-permute-done | bytes 536608 | tf_op jit(solution)/shard_map/ppermute | solution.py:233
  93.5 8.4 %collective-permute-start.11 = (bf16[3072,128]{1,0:T(8,128)(2,1)S(1)}, bf16[3072,128]{1,0:T(8,128)(2,1)S(1)}, u32[]{:S(2)}, u32[]{:S(2)}) collective-permute-start(bf16[3072,128]{1,0:T(8,128)(2,1)S(1)} %shard_map.148.refs_5_), channel_id=1, source_target_pairs={{0,2},{1,47},{2,4},{3,1},{4,6},{5,3},{6,8},{7,5},{8,10},{9,7},{10,... | collective-permute-start | bytes 2359304 | tf_op jit(solution)/shard_map/ppermute | solution.py:233
  104.0 1.9 %collective-permute-start.10 = (bf16[1200,128]{1,0:T(8,128)(2,1)}, bf16[1200,128]{1,0:T(8,128)(2,1)S(1)}, u32[]{:S(2)}, u32[]{:S(2)}) collective-permute-start(bf16[1200,128]{1,0:T(8,128)(2,1)} %get-tuple-element.27), channel_id=1, source_target_pairs={{0,1},{1,0},{2,3},{3,2},{4,5},{5,4},{6,7},{7,6},{8,9},{9,8},{10,11... | collective-permute-start | bytes 921608 | tf_op jit(solution)/shard_map/ppermute | solution.py:237
  105.9 2.4 %collective-permute-start.12 = (bf16[1408,128]{1,0:T(8,128)(2,1)}, bf16[1408,128]{1,0:T(8,128)(2,1)}, u32[]{:S(2)}, u32[]{:S(2)}) collective-permute-start(bf16[1408,128]{1,0:T(8,128)(2,1)} %get-tuple-element.29), channel_id=1, source_target_pairs={{0,1},{1,0},{2,3},{3,2},{4,5},{5,4},{6,7},{7,6},{8,9},{9,8},{10,11... | collective-permute-start | bytes 1081352 | tf_op jit(solution)/shard_map/ppermute | solution.py:237
  108.3 1.9 %collective-permute-start.13 = (bf16[1408,128]{1,0:T(8,128)(2,1)}, bf16[1408,128]{1,0:T(8,128)(2,1)}, u32[]{:S(2)}, u32[]{:S(2)}) collective-permute-start(bf16[1408,128]{1,0:T(8,128)(2,1)} %get-tuple-element.30), channel_id=1, source_target_pairs={{0,1},{1,0},{2,3},{3,2},{4,5},{5,4},{6,7},{7,6},{8,9},{9,8},{10,11... | collective-permute-start | bytes 1081352 | tf_op jit(solution)/shard_map/ppermute | solution.py:237
  128.2 2.3 %shard_map.151.rest_4_ = f32[13,128,128]{2,1,0:T(8,128)S(1)} custom-call(s32[5,54]{1,0:T(8,128)S(1)} %stack.75.table_ref, bf16[6400,128]{1,0:T(8,128)(2,1)S(1)} %bitcast.62, bf16[3840,128]{1,0:T(8,128)(2,1)S(1)} %copy-done.5, bf16[3120,128]{1,0:T(8,128)(2,1)S(1)} %copy-done.3), custom_call_target="tpu_custom_call" | custom-call | flops 1811939328 | bytes 1769472 | tf_op jit(solution)/shard_map/pallas_call | solution.py:173
  130.5 5.6 %shard_map.152.refs_1_.rest_1_ = f32[13,128,128]{2,1,0:T(8,128)S(1)} custom-call(s32[5,90]{1,0:T(8,128)S(1)} %stack.68.table_ref, bf16[6400,128]{1,0:T(8,128)(2,1)S(1)} %bitcast.63, bf16[2944,128]{1,0:T(8,128)(2,1)S(1)} %copy-done.7, bf16[1408,128]{1,0:T(8,128)(2,1)} %collective-permute-done.12.rest_1_, bf16[1408,128]{1,0:T(8,128)(2,1)} %collective-permute-done.13.rest_2_, ...), custom_call_target="tpu_custom_call" | custom-call | flops 1811939328 | bytes 1769472 | tf_op jit(solution)/shard_map/pallas_call | solution.py:173
  136.2 2.4 %collective-permute-start.15 = (bf16[1536,128]{1,0:T(8,128)(2,1)S(1)}, bf16[1536,128]{1,0:T(8,128)(2,1)S(1)}, u32[]{:S(2)}, u32[]{:S(2)}) collective-permute-start(bf16[1536,128]{1,0:T(8,128)(2,1)S(1)} %shard_map.153), channel_id=1, source_target_pairs={{0,1},{1,0},{2,3},{3,2},{4,5},{5,4},{6,7},{7,6},{8,9},{9,8},{10,11... | collective-permute-start | bytes 1179656 | tf_op jit(solution)/shard_map/ppermute | solution.py:237
  140.1 1.8 %shard_map.155 = bf16[12,128,128]{2,1,0:T(8,128)(2,1)} custom-call(s32[5,90]{1,0:T(8,128)S(1)} %stack.68.table_ref, bf16[6400,128]{1,0:T(8,128)(2,1)S(1)} %bitcast.65, bf16[1536,128]{1,0:T(8,128)(2,1)S(1)} %collective-permute-done.15.rest_0_, f32[13,128,128]{2,1,0:T(8,128)S(1)} %shard_map.154.rest_1_), custom_call_target="tpu_custom_call" | custom-call | flops 402653184 | bytes 393216 | tf_op jit(solution)/shard_map/pallas_call | solution.py:173
  (118 shorter events, 34.9 us)
Async XLA Ops:
  0.0 40.6 %copy-start = (bf16[1,1,16,1,128,128]{5,4,3,2,1,0:T(8,128)(2,1)S(1)}, bf16[1,1,16,1,128,128]{5,4,3,2,1,0:T(8,128)(2,1)}, u32[]{:S(2)}) copy-start(bf16[1,1,16,1,128,128]{5,4,3,2,1,0:T(8,128)(2,1)} %param.17) | copy-start | bytes 1572868
  0.8 17.8 %collective-permute-start = (bf16[16,128]{1,0:T(8,128)(2,1)S(1)}, bf16[16,128]{1,0:T(8,128)(2,1)S(1)}, u32[]{:S(2)}, u32[]{:S(2)}) collective-permute-start(bf16[16,128]{1,0:T(8,128)(2,1)S(1)} %fusion.31), channel_id=1, source_target_pairs={{0,1},{1,0},{2,3},{3,2},{4,5},{5,4},{6,7},{7,6},{8,9},{9,8},{10,11... | collective-permute-start | bytes 12296 | tf_op jit(solution)/shard_map/ppermute | solution.py:237
  13.2 5.5 %collective-permute-start.2 = (bf16[16,128,128]{2,1,0:T(8,128)(2,1)}, bf16[16,128,128]{2,1,0:T(8,128)(2,1)S(1)}, u32[]{:S(2)}, u32[]{:S(2)}) collective-permute-start(bf16[16,128,128]{2,1,0:T(8,128)(2,1)} %bitcast.67), channel_id=1, source_target_pairs={{0,1},{1,0},{2,3},{3,2},{4,5},{5,4},{6,7},{7,6},{8,9},{9,8},{10,11... | collective-permute-start | bytes 1572872 | tf_op jit(solution)/shard_map/ppermute | solution.py:237
  21.9 32.0 %collective-permute-start.3 = (bf16[1552,128]{1,0:T(8,128)(2,1)}, bf16[1552,128]{1,0:T(8,128)(2,1)S(1)}, u32[]{:S(2)}, u32[]{:S(2)}) collective-permute-start(bf16[1552,128]{1,0:T(8,128)(2,1)} %get-tuple-element.20), channel_id=1, source_target_pairs={{0,4},{1,45},{2,6},{3,47},{4,8},{5,1},{6,10},{7,3},{8,12},{9,5},{1... | collective-permute-start | bytes 1191944 | tf_op jit(solution)/shard_map/ppermute | solution.py:233
  29.7 24.3 %collective-permute-start.4 = (bf16[1552,128]{1,0:T(8,128)(2,1)}, bf16[1552,128]{1,0:T(8,128)(2,1)S(1)}, u32[]{:S(2)}, u32[]{:S(2)}) collective-permute-start(bf16[1552,128]{1,0:T(8,128)(2,1)} %get-tuple-element.21.refs_0_), channel_id=1, source_target_pairs={{0,28},{1,21},{2,30},{3,23},{4,32},{5,25},{6,34},{7,27},{8,36},{9,... | collective-permute-start | bytes 1191944 | tf_op jit(solution)/shard_map/ppermute | solution.py:233
  32.9 18.2 %collective-permute-start.5 = (bf16[1040,128]{1,0:T(8,128)(2,1)S(1)}, bf16[1040,128]{1,0:T(8,128)(2,1)S(1)}, u32[]{:S(2)}, u32[]{:S(2)}) collective-permute-start(bf16[1040,128]{1,0:T(8,128)(2,1)S(1)} %get-tuple-element.22.refs_1_), channel_id=1, source_target_pairs={{0,2},{1,47},{2,4},{3,1},{4,6},{5,3},{6,8},{7,5},{8,10},{9,7},{10,... | collective-permute-start | bytes 798728 | tf_op jit(solution)/shard_map/ppermute | solution.py:233
  36.5 17.5 %collective-permute-start.6 = (bf16[1040,128]{1,0:T(8,128)(2,1)S(1)}, bf16[1040,128]{1,0:T(8,128)(2,1)S(1)}, u32[]{:S(2)}, u32[]{:S(2)}) collective-permute-start(bf16[1040,128]{1,0:T(8,128)(2,1)S(1)} %get-tuple-element.19.refs_0_.refs_2_), channel_id=1, source_target_pairs={{0,26},{1,23},{2,28},{3,25},{4,30},{5,27},{6,32},{7,29},{8,34},{9,... | collective-permute-start | bytes 798728 | tf_op jit(solution)/shard_map/ppermute | solution.py:233
  38.5 11.8 %collective-permute-start.1 = (bf16[16,128]{1,0:T(8,128)(2,1)S(1)}, bf16[16,128]{1,0:T(8,128)(2,1)S(1)}, u32[]{:S(2)}, u32[]{:S(2)}) collective-permute-start(bf16[16,128]{1,0:T(8,128)(2,1)S(1)} %maximum_maximum_fusion.note_ref), channel_id=1, source_target_pairs={{0,12},{1,37},{2,14},{3,39},{4,16},{5,41},{6,18},{7,43},{8,20},{9,... | collective-permute-start | bytes 12296 | tf_op jit(solution)/shard_map/ppermute | solution.py:233
  42.4 76.5 %all-to-all-start = ((bf16[16,400,128]{2,1,0:T(8,128)(2,1)}), bf16[16,400,128]{2,1,0:T(8,128)(2,1)S(1)}, u32[]{:S(2)}, u32[]{:S(2)}) async-start(bf16[16,400,128]{2,1,0:T(8,128)(2,1)} %shard_map.145), calls=%async_computation | async-start | bytes 3276800 | tf_op jit(solution)/shard_map/all_to_all | solution.py:280
  54.0 19.1 %copy-start.10 = (s32[90]{0:T(128)S(1)}, s32[90]{0:T(128)}, u32[]{:S(2)}) copy-start(s32[90]{0:T(128)} %constant.372.clone) | copy-start | bytes 1084
  54.1 19.1 %copy-start.15 = (s32[90]{0:T(128)S(1)}, s32[90]{0:T(128)}, u32[]{:S(2)}) copy-start(s32[90]{0:T(128)} %constant.373.clone) | copy-start | bytes 1084
  54.1 19.1 %copy-start.16 = (s32[90]{0:T(128)S(1)}, s32[90]{0:T(128)}, u32[]{:S(2)}) copy-start(s32[90]{0:T(128)} %constant.374.clone) | copy-start | bytes 1084
  54.1 19.7 %copy-start.9 = (bf16[528,128]{1,0:T(8,128)(2,1)S(1)}, bf16[528,128]{1,0:T(8,128)(2,1)}, u32[]{:S(2)}) copy-start(bf16[528,128]{1,0:T(8,128)(2,1)} %copy-done.8) | copy-start | bytes 405508
  56.2 54.7 %collective-permute-start.14 = (bf16[3120,128]{1,0:T(8,128)(2,1)S(1)}, bf16[3120,128]{1,0:T(8,128)(2,1)S(1)}, u32[]{:S(2)}, u32[]{:S(2)}) collective-permute-start(bf16[3120,128]{1,0:T(8,128)(2,1)S(1)} %get-tuple-element.31), channel_id=1, source_target_pairs={{0,1},{1,0},{2,3},{3,2},{4,5},{5,4},{6,7},{7,6},{8,9},{9,8},{10,11... | collective-permute-start | bytes 2396168 | tf_op jit(solution)/shard_map/ppermute | solution.py:237
  65.1 26.6 %collective-permute-start.7 = (bf16[2096,128]{1,0:T(8,128)(2,1)S(1)}, bf16[2096,128]{1,0:T(8,128)(2,1)S(1)}, u32[]{:S(2)}, u32[]{:S(2)}) collective-permute-start(bf16[2096,128]{1,0:T(8,128)(2,1)S(1)} %get-tuple-element.23.refs_1_.refs_7_), channel_id=1, source_target_pairs={{0,30},{1,19},{2,32},{3,21},{4,34},{5,23},{6,36},{7,25},{8,38},{9,... | collective-permute-start | bytes 1609736 | tf_op jit(solution)/shard_map/ppermute | solution.py:233
  67.4 26.0 %collective-permute-start.8 = (bf16[2096,128]{1,0:T(8,128)(2,1)S(1)}, bf16[2096,128]{1,0:T(8,128)(2,1)S(1)}, u32[]{:S(2)}, u32[]{:S(2)}) collective-permute-start(bf16[2096,128]{1,0:T(8,128)(2,1)S(1)} %get-tuple-element.24), channel_id=1, source_target_pairs={{0,2},{1,47},{2,4},{3,1},{4,6},{5,3},{6,8},{7,5},{8,10},{9,7},{10,... | collective-permute-start | bytes 1609736 | tf_op jit(solution)/shard_map/ppermute | solution.py:233
  73.7 28.3 %collective-permute-start.9 = (bf16[528,128]{1,0:T(8,128)(2,1)S(1)}, bf16[528,128]{1,0:T(8,128)(2,1)S(1)}, u32[]{:S(2)}, u32[]{:S(2)}) collective-permute-start(bf16[528,128]{1,0:T(8,128)(2,1)S(1)} %copy-done.9), channel_id=1, source_target_pairs={{0,24},{1,25},{2,26},{3,27},{4,28},{5,29},{6,30},{7,31},{8,32},{9,... | collective-permute-start | bytes 405512 | tf_op jit(solution)/shard_map/ppermute | solution.py:233
  93.5 26.6 %copy-start.11 = (s32[54]{0:T(128)S(1)}, s32[54]{0:T(128)}, u32[]{:S(2)}) copy-start(s32[54]{0:T(128)} %constant.367.clone) | copy-start | bytes 652
  93.5 28.6 %copy-start.12 = (s32[90]{0:T(128)S(1)}, s32[90]{0:T(128)}, u32[]{:S(2)}) copy-start(s32[90]{0:T(128)} %constant.375.clone) | copy-start | bytes 1084
  93.5 42.6 %collective-permute-start.11 = (bf16[3072,128]{1,0:T(8,128)(2,1)S(1)}, bf16[3072,128]{1,0:T(8,128)(2,1)S(1)}, u32[]{:S(2)}, u32[]{:S(2)}) collective-permute-start(bf16[3072,128]{1,0:T(8,128)(2,1)S(1)} %shard_map.148.refs_5_), channel_id=1, source_target_pairs={{0,2},{1,47},{2,4},{3,1},{4,6},{5,3},{6,8},{7,5},{8,10},{9,7},{10,... | collective-permute-start | bytes 2359304 | tf_op jit(solution)/shard_map/ppermute | solution.py:233
  104.0 11.3 %collective-permute-start.10 = (bf16[1200,128]{1,0:T(8,128)(2,1)}, bf16[1200,128]{1,0:T(8,128)(2,1)S(1)}, u32[]{:S(2)}, u32[]{:S(2)}) collective-permute-start(bf16[1200,128]{1,0:T(8,128)(2,1)} %get-tuple-element.27), channel_id=1, source_target_pairs={{0,1},{1,0},{2,3},{3,2},{4,5},{5,4},{6,7},{7,6},{8,9},{9,8},{10,11... | collective-permute-start | bytes 921608 | tf_op jit(solution)/shard_map/ppermute | solution.py:237
  105.9 24.6 %collective-permute-start.12 = (bf16[1408,128]{1,0:T(8,128)(2,1)}, bf16[1408,128]{1,0:T(8,128)(2,1)}, u32[]{:S(2)}, u32[]{:S(2)}) collective-permute-start(bf16[1408,128]{1,0:T(8,128)(2,1)} %get-tuple-element.29), channel_id=1, source_target_pairs={{0,1},{1,0},{2,3},{3,2},{4,5},{5,4},{6,7},{7,6},{8,9},{9,8},{10,11... | collective-permute-start | bytes 1081352 | tf_op jit(solution)/shard_map/ppermute | solution.py:237
  108.3 22.2 %collective-permute-start.13 = (bf16[1408,128]{1,0:T(8,128)(2,1)}, bf16[1408,128]{1,0:T(8,128)(2,1)}, u32[]{:S(2)}, u32[]{:S(2)}) collective-permute-start(bf16[1408,128]{1,0:T(8,128)(2,1)} %get-tuple-element.30), channel_id=1, source_target_pairs={{0,1},{1,0},{2,3},{3,2},{4,5},{5,4},{6,7},{7,6},{8,9},{9,8},{10,11... | collective-permute-start | bytes 1081352 | tf_op jit(solution)/shard_map/ppermute | solution.py:237
  136.2 3.9 %collective-permute-start.15 = (bf16[1536,128]{1,0:T(8,128)(2,1)S(1)}, bf16[1536,128]{1,0:T(8,128)(2,1)S(1)}, u32[]{:S(2)}, u32[]{:S(2)}) collective-permute-start(bf16[1536,128]{1,0:T(8,128)(2,1)S(1)} %shard_map.153), channel_id=1, source_target_pairs={{0,1},{1,0},{2,3},{3,2},{4,5},{5,4},{6,7},{7,6},{8,9},{9,8},{10,11... | collective-permute-start | bytes 1179656 | tf_op jit(solution)/shard_map/ppermute | solution.py:237
  (10 other events, 11.3 us)

commit v11 on v10

--- a/solution.py
+++ b/solution.py
@@ -75,8 +75,8 @@
     )(index, own, other, note)
 
 
-def right_kernel(index_ref, src_ref, code_ref, after_ref, out):
-    del after_ref
+def right_kernel(index_ref, src_ref, code_ref, *rest):
+    out = rest[-1]
     for n in range(16):
         for t in range(STEPS):
             out[n, blk(t), :] = src_ref[index_ref[n + t]]
@@ -87,11 +87,11 @@
     return pl.pallas_call(
         right_kernel,
         out_shape=jax.ShapeDtypeStruct((16, HALF, BLK), jnp.bfloat16),
-        in_specs=[SMEM_SPEC, VMEM_SPEC, VMEM_SPEC, ANY_SPEC],
+        in_specs=[SMEM_SPEC, VMEM_SPEC, VMEM_SPEC] + [ANY_SPEC] * len(after),
         out_specs=VMEM_SPEC,
         compiler_params=LIMIT,
         cost_estimate=moves(48),
-    )(index, src, codes, after)
+    )(index, src, codes, *after)
 
 
 def turned(note, distance):
@@ -150,17 +150,17 @@
     for left, count in zip(lefts, counts, strict=True):
 
         def body(n, carry, left=left, base=base):
-            block = left[pl.ds(pl.multiple_of(table_ref[4, base + n], BLK), BLK), :]
+            block = left[pl.ds(pl.multiple_of(table_ref[base + n, 4], BLK), BLK), :]
             pair = []
             for rank in range(2):
-                row = pl.multiple_of(table_ref[2 * rank, base + n], 16)
+                row = pl.multiple_of(table_ref[base + n, 2 * rank], 16)
                 pair.append(right_ref[pl.ds(row, BLK), :])
             both = jnp.dot(block, jnp.concatenate(pair, axis=1), preferred_element_type=jnp.float32)
-            acc[table_ref[1, base + n]] += both[:, :BLK]
-            acc[table_ref[3, base + n]] += both[:, BLK:]
+            acc[table_ref[base + n, 1]] += both[:, :BLK]
+            acc[table_ref[base + n, 3]] += both[:, BLK:]
             return carry
 
-        unroll = max(n for n in range(1, 17) if count % n == 0)
+        unroll = count if count <= 24 else max(n for n in range(1, 17) if count % n == 0)
         lax.fori_loop(0, count, body, 0, unroll=unroll)
         base += count
     if last:
@@ -183,46 +183,100 @@
     )(table, right, *lefts, *(() if before is None else (before,)))
 
 
-def tables(order, notes, right_codes, c_code, start, core):
+def total(mask, value, axis):
+    return jnp.sum(jnp.where(mask, value, 0.0), axis=axis, keepdims=True)
+
+
+def table_kernel(note_rows, scalars, pick_ref, meta_ref, slots_ref, own, other, right, out, notes, tails, sems):
+    copies = [
+        pltpu.make_async_copy(
+            ref.at[pl.ds(row, NOTE)], notes.at[pl.ds(n * NOTE, NOTE)], sems.at[n]
+        )
+        for n, (ref, row) in enumerate(zip((own, other), note_rows, strict=True))
+    ]
+    copies += [
+        pltpu.make_async_copy(
+            right.at[pl.ds(n * HALF + STEPS * BLK, 16)], tails.at[pl.ds(n * 16, 16)], sems.at[2 + n]
+        )
+        for n in range(16)
+    ]
+    for copy in copies:
+        copy.start()
+    for copy in copies:
+        copy.wait()
+    start, core = scalars[0], scalars[1]
+    count = out.shape[0]
+    lane = lax.broadcasted_iota(jnp.int32, (count, BLK), 1)
+    panel = meta_ref[:, 0:1]
+    picked = jnp.dot(pick_ref[...], notes[...], preferred_element_type=jnp.float32)
+    at = (start + panel + core * (3 - 2 * panel)) & 15
+    code = total(lane == at, picked, 1) * 64.0 + total(lane == at + 16, picked, 1)
+    code = code.astype(jnp.int32) - 1
+    left_row = (jnp.maximum(code, 0) * 43691) >> 21
+    left_key = code - left_row * PANEL + (panel + core * (2 - 2 * panel)) * 64
+    left_key = jnp.where(code >= 0, left_key, -2)
+    rows = lax.broadcasted_iota(jnp.int32, (16, 256), 0)
+    firsts = (rows * 16 == lax.broadcasted_iota(jnp.int32, (16, 256), 1)).astype(jnp.bfloat16)
+    digits = jnp.dot(firsts, tails[...], preferred_element_type=jnp.float32).astype(jnp.bfloat16)
+    rows = lax.broadcasted_iota(jnp.int32, (BLK, BLK), 0)
+    cols = lax.broadcasted_iota(jnp.int32, (BLK, BLK), 1)
+    owner = lax.broadcasted_iota(jnp.int32, (16, BLK), 0) == (cols[:16] & 15)
+    values = []
+    for digit in range(2):
+        spread = (rows == (cols >> 4) + STEPS * digit).astype(jnp.bfloat16)
+        spread = jnp.dot(digits, spread, preferred_element_type=jnp.float32)
+        values.append(total(owner, spread, 0))
+    right_code = (values[0] * 16.0 + values[1]).astype(jnp.int32) - 1
+    line = cols[:1]
+    live = (right_code >= 0) & (line < 16 * STEPS)
+    key = jnp.where(live, (right_code >> 4) + (line >> 4) * 64, -1)
+    column = (right_code & 15).astype(jnp.float32)
+    keys = jnp.broadcast_to(key, (BLK, BLK)).astype(jnp.float32)
+    turned_keys = total(rows == cols, keys, 1)
+    rank = total((turned_keys == keys) & (rows < cols), 1.0, 0)
+    place = ((line & 15) * HALF + (line >> 4) * BLK + 1).astype(jnp.float32)
+    match = left_key == key
+    table = jnp.where(lane == 4, meta_ref[:, 1:2], 0)
+    for rank_number in range(2):
+        hit = match & (rank == rank_number)
+        found = total(hit, place, 1).astype(jnp.int32)
+        target = left_row * BC + total(hit, column, 1).astype(jnp.int32)
+        there = (slots_ref[...] == target) & (found > 0)
+        slot = total(there, (lane - KEPT).astype(jnp.float32), 1).astype(jnp.int32) + KEPT
+        table = jnp.where(lane == 2 * rank_number, jnp.maximum(found - 1, 0), table)
+        table = jnp.where(lane == 2 * rank_number + 1, slot, table)
+    out[...] = table
+
+
+def tables(order, notes, right, slots, scalars):
     half = NQ // 4
     order = [
         (row, 1 - other, 1 - k, half, panel) if d == 3 * half else (row, other, k, d, panel)
         for row, other, k, d, panel in order
     ]
     order = np.array(order, np.int32)
-    count = order.shape[0]
-    row, other, k, distance, panel = (order[:, n] for n in range(5))
-    notes = jnp.stack(notes)[:, :, :32].astype(jnp.int32)
-    flat = (notes[:, :, :16] * 64 + notes[:, :, 16:] - 1).reshape(1, 2 * NOTE * 16)
-    of = (start + panel + core * (3 - 2 * panel)) % 16
-    place = (other * NOTE + k * NQ + distance) * 16 + of
-    codes = jnp.sum(jnp.where(place[:, None] == jnp.arange(2 * NOTE * 16)[None, :], flat, 0), axis=1)
-    step = panel + core * (2 - 2 * panel)
-    right_live = right_codes >= 0
-    right_inner = jnp.where(right_live, right_codes // BC, -1)
-    owners = jnp.arange(16, dtype=jnp.int32)
-    earlier = owners[None, :] < owners[:, None]
-    rank = jnp.sum(
-        ((right_inner[:, None, :] == right_inner[None, :, :]) & earlier[:, :, None]).astype(jnp.int32),
-        axis=1,
-    )
-    packed = jnp.where(right_live, right_inner * 1024 + rank * 32 + right_codes % BC, -1)
-    right_n = jnp.where(
-        (step == 0)[:, None],
-        packed[None, :, 0],
-        jnp.where((step == 1)[:, None], packed[None, :, 1], packed[None, :, 2]),
-    )
-    match = (right_n >= 0) & (codes >= 0)[:, None] & ((right_n // 1024) == (codes % PANEL)[:, None])
-    rows = []
-    for rank_number in range(2):
-        hit = match & ((right_n // 32) % 32 == rank_number)
-        found = jnp.sum(jnp.where(hit, owners[None, :] * 32 + right_n % 32 + 1, 0), axis=1)
-        partner = jnp.maximum(found - 1, 0)
-        target = (codes // PANEL) * BC + partner % 32
-        there = (target[:, None] == c_code[None, :]) & (found > 0)[:, None]
-        slot = jnp.sum(jnp.where(there, jnp.arange(KEPT)[None, :] - KEPT, 0), axis=1) + KEPT
-        rows += [partner // 32 * HALF + step * BLK, slot]
-    return jnp.stack(rows + [jnp.array(row)]).astype(jnp.int32).reshape(5, count)
+    count = -(-order.shape[0] // 8) * 8
+    pick = np.zeros((count, 2 * NOTE), np.float32)
+    pick[np.arange(order.shape[0]), order[:, 1] * NOTE + order[:, 2] * NQ + order[:, 3]] = 1
+    meta = np.zeros((count, BLK), np.int32)
+    meta[: order.shape[0], 0] = order[:, 4]
+    meta[: order.shape[0], 1] = order[:, 0]
+    arrays, rows = zip(*notes, strict=True)
+    return pl.pallas_call(
+        functools.partial(table_kernel, rows),
+        out_shape=jax.ShapeDtypeStruct((count, BLK), jnp.int32),
+        in_specs=[SMEM_SPEC] + [VMEM_SPEC] * 3 + [ANY_SPEC] * 3,
+        out_specs=VMEM_SPEC,
+        scratch_shapes=[
+            VMEM((2 * NOTE, BLK), jnp.bfloat16),
+            VMEM((256, BLK), jnp.bfloat16),
+            pltpu.SemaphoreType.DMA((18,)),
+        ],
+        compiler_params=LIMIT,
+        cost_estimate=pl.CostEstimate(
+            flops=count * BLK * 200, bytes_accessed=count * BLK * 8, transcendentals=0
+        ),
+    )(scalars, jnp.asarray(pick, jnp.bfloat16), jnp.asarray(meta), slots, *arrays, right)
 
 
 def moved(array, distance):
@@ -276,7 +330,7 @@
     b_code = jnp.stack([b_code[t : t + 16] for t in range(STEPS)], axis=1)
     b_code = jnp.concatenate([b_code // 16, b_code % 16], axis=1).astype(jnp.bfloat16)
     b_code = jnp.broadcast_to(jnp.pad(b_code, ((0, 0), (0, BLK - 6)))[:, None, :], (16, 16, BLK))
-    right = right_packed(b_own, shift, b_code, note_other)
+    right = right_packed(b_own, shift, b_code, (note_other, a_other))
     right = lax.all_to_all(right, ROW, 0, 0, tiled=True).reshape(16 * HALF, BLK)
     note = jnp.concatenate([note[:1], note_other[:1], note[2:]])
     a_index = jnp.arange(16, dtype=jnp.int32)
@@ -300,18 +354,17 @@
     for array, (names, distance) in zip(arrays[:4], starts[:4], strict=True):
         near.append((send(array, names, distance), 2 * len(names) * BLK, distance, True))
 
-    sources.append(moved(note, NQ // 4))
-    opposite = len(sources) - 1
     long_names = items([(1, 1), (5, 13), (2, 2), (6, 14)])
     names = items([(3, 2), (7, 14), (0, 14), (4, 2)])
-    long_in, up_in = packed([(blocks(long_names), True), (blocks(names), True)], near, (sources[opposite],))
+    long_in, up_in = packed([(blocks(long_names), True), (blocks(names), True)], near)
     far = [(len(sources), 16 * BLK, 0, False)]
     sources.append(long_in)
     far.append((send(long_in, long_names, 15), 16 * BLK, 15, False))
     far.append((send(up_in, names, 1), 16 * BLK, 1, False))
-    across, _ = lax.optimization_barrier((arrays[4], long_in))
+    across, opposite, _ = lax.optimization_barrier((arrays[4], note, long_in))
     far.append((send(across, *starts[4]), 4 * BLK, starts[4][1], True))
-    far.append((opposite, 0, NQ // 4, True))
+    sources.append(moved(opposite, NQ // 4))
+    far.append((len(sources) - 1, 0, NQ // 4, True))
 
     early = items([(1, 1), (5, 13), (2, 2), (6, 14), (2, 1), (6, 13), (3, 2), (7, 14)])
 
@@ -324,13 +377,13 @@
         arrays = packed(spec, notes, after)
         received = [from_other_core(array) for array in arrays[:pieces]]
         end = (len(entries) - size * (pieces - 1)) * BLK
-        return received, arrays[pieces:], (arrays[pieces - 1][end:], received[-1][end:])
+        return received, arrays[pieces:], ((arrays[pieces - 1], end), (received[-1], end))
 
     mine = items([(0, 0), (1, 0)]) + early
     early_other, early_own, early_notes = pass_on(early, PIECES, mine, near, (long_in,))
 
     names = items([(1, 16), (5, 4), (2, 17), (6, 5), (0, 15), (4, 3)])
-    (up_in,) = packed([(blocks(names), False)])
+    (up_in,) = packed([(blocks(names), False)], (), [sources[note[0]] for note in far[-2:]])
     send(up_in, names, 1)
 
     late = [(4, 12, 0), (5, 12, 0)] + items([(3, 3), (7, 15)]) + names
@@ -357,13 +410,12 @@
             for n, array in enumerate(arrays)
         ]
 
-    right_codes = right.reshape(16, HALF, BLK)[:, STEPS * BLK, :6].astype(jnp.int32)
-    right_codes = right_codes[:, :3] * 16 + right_codes[:, 3:] - 1
-    c_code = c_code.reshape(KEPT)
+    slots = jnp.pad(c_code.reshape(1, KEPT), ((0, 0), (0, BLK - KEPT)), constant_values=-1)
+    scalars = jnp.stack([start, core]).astype(jnp.int32)
 
     def table_of(parts, notes):
         order = [row for part in parts for _, rows in part for row in rows]
-        return tables(order, notes, right_codes, c_code, start, core)
+        return tables(order, notes, right, slots, scalars)
 
     def product_of(table, part, base, before=None, last=False):
         lefts, counts = [array for array, _ in part], tuple(len(rows) for _, rows in part)

time: 145 us -> 135 us (0.931)
  other arithmetic: 17.7 us -> 1.71 us
  waiting for transfers between devices: 19.8 us -> 28.1 us
  local copies, waits for them, and re-layouts: 11 us -> 7.12 us
  starting transfers between devices: 75.9 us -> 78.7 us
    ppermute x9, starting transfers between devices: 36.7 us -> 48.2 us  [moved(): return lax.ppermute(array, COL, route)]
    ppermute x9, waiting for transfers between devices: 19.8 us -> 27 us  [moved(): return lax.ppermute(array, COL, route)]
    reduce_sum x7 -> x0, other arithmetic: 5.02 us -> none  [the longest x2 1.71 us: tables(): jnp.sum(jnp.where(place[:, None] == jnp.arange(2 * NOTE * 16)[None, :], f...]
    ppermute x7, starting transfers between devices: 31.4 us -> 26.6 us  [from_other_core(): return lax.ppermute(array, 'core', [(0, 1), (1, 0)])]
    all_to_all x1, starting transfers between devices: 7.8 us -> 3.84 us  [local(): right = lax.all_to_all(right, ROW, 0, 0, tiled=True).reshape(16 * HALF, BLK)]
    pallas_call x0 -> x2, Pallas kernels: none -> 3.47 us  [tables(): pl.pallas_call(functools.partial(table_kernel, rows), out_shape=jax.Shape...]
    eq x2 -> x0, other arithmetic: 2.55 us -> none  [tables(): step == 0]
    another operation x6 -> x0, local copies, waits for them, and re-layouts: 2.1 us -> none  [the longest x2 1.38 us: tables(): jnp.stack(rows + [jnp.array(row)]).astype(jnp.int32).reshape(5, count)]
  transfers between devices with their start and end apart: 17 -> 17, of which waited for: 4 -> 5; matrix products, arithmetic and copies ran while one was open for 15% -> 1% of each run, Pallas kernels for 10% -> 9%
where the time goes in v11:
time: 135 us; the launch traced here: 133 us
  starting transfers between devices  78.7 us (58%)
  waiting for transfers between devices  28.1 us (21%)
  Pallas kernels  17 us (13%)
  local copies, waits for them, and re-layouts  7.12 us (5%)
  other arithmetic  1.71 us (1%)
    ppermute x9, starting transfers between devices, moved(): return lax.ppermute(array, COL, route)  48.2 us
    ppermute x9, waiting for transfers between devices, moved(): return lax.ppermute(array, COL, route)  27 us
    ppermute x7, starting transfers between devices, from_other_core(): return lax.ppermute(array, 'core', [(0, 1), (1, 0)])  26.6 us
    pallas_call x4, Pallas kernels, product(): pl.pallas_call(functools.partial(product_kernel, counts, base, before is...  9.74 us
    unnamed x33, local copies, waits for them, and re-layouts  6.94 us
    all_to_all x1, starting transfers between devices, local(): right = lax.all_to_all(right, ROW, 0, 0, tiled=True).reshape(16 * HALF, BLK)  3.84 us
    pallas_call x2, Pallas kernels, tables(): pl.pallas_call(functools.partial(table_kernel, rows), out_shape=jax.Shape...  3.47 us
  transfers between devices with their start and end apart: 17, of which 5 were waited for; matrix products, arithmetic and copies ran while one was open for 1% of the time, Pallas kernels for 9%

profile of v11, /device:TPU:1, one launch (start us, length us, event | category | flops | bytes accessed | tf_op | source)
XLA Modules:
  0.0 133.1 jit_solution(17638273645219609859)
XLA Ops:
  0.8 12.4 %collective-permute-start.1 = (bf16[16,128]{1,0:T(8,128)(2,1)S(1)}, bf16[16,128]{1,0:T(8,128)(2,1)S(1)}, u32[]{:S(2)}, u32[]{:S(2)}) collective-permute-start(bf16[16,128]{1,0:T(8,128)(2,1)S(1)} %fusion.5), channel_id=1, source_target_pairs={{0,1},{1,0},{2,3},{3,2},{4,5},{5,4},{6,7},{7,6},{8,9},{9,8},{10,11... | collective-permute-start | bytes 12296 | tf_op jit(solution)/shard_map/ppermute | solution.py:291
  13.2 1.9 %collective-permute-start = (bf16[16,128,128]{2,1,0:T(8,128)(2,1)}, bf16[16,128,128]{2,1,0:T(8,128)(2,1)S(1)}, u32[]{:S(2)}, u32[]{:S(2)}) collective-permute-start(bf16[16,128,128]{2,1,0:T(8,128)(2,1)} %bitcast.39), channel_id=1, source_target_pairs={{0,1},{1,0},{2,3},{3,2},{4,5},{5,4},{6,7},{7,6},{8,9},{9,8},{10,11... | collective-permute-start | bytes 1572872 | tf_op jit(solution)/shard_map/ppermute | solution.py:291
  20.1 3.8 %all-to-all-start = ((bf16[16,400,128]{2,1,0:T(8,128)(2,1)}), bf16[16,400,128]{2,1,0:T(8,128)(2,1)S(1)}, u32[]{:S(2)}, u32[]{:S(2)}) async-start(bf16[16,400,128]{2,1,0:T(8,128)(2,1)} %shard_map.95), calls=%async_computation | async-start | bytes 3276800 | tf_op jit(solution)/shard_map/all_to_all | solution.py:334
  24.8 11.6 %collective-permute-start.2 = (bf16[1552,128]{1,0:T(8,128)(2,1)S(1)}, bf16[1552,128]{1,0:T(8,128)(2,1)S(1)}, u32[]{:S(2)}, u32[]{:S(2)}) collective-permute-start(bf16[1552,128]{1,0:T(8,128)(2,1)S(1)} %get-tuple-element.21), channel_id=1, source_target_pairs={{0,4},{1,45},{2,6},{3,47},{4,8},{5,1},{6,10},{7,3},{8,12},{9,5},{1... | collective-permute-start | bytes 1191944 | tf_op jit(solution)/shard_map/ppermute | solution.py:287
  36.4 1.9 %collective-permute-start.3 = (bf16[1552,128]{1,0:T(8,128)(2,1)S(1)}, bf16[1552,128]{1,0:T(8,128)(2,1)S(1)}, u32[]{:S(2)}, u32[]{:S(2)}) collective-permute-start(bf16[1552,128]{1,0:T(8,128)(2,1)S(1)} %get-tuple-element.22.refs_0_), channel_id=1, source_target_pairs={{0,28},{1,21},{2,30},{3,23},{4,32},{5,25},{6,34},{7,27},{8,36},{9,... | collective-permute-start | bytes 1191944 | tf_op jit(solution)/shard_map/ppermute | solution.py:287
  38.4 3.9 %collective-permute-start.4 = (bf16[1040,128]{1,0:T(8,128)(2,1)S(1)}, bf16[1040,128]{1,0:T(8,128)(2,1)S(1)}, u32[]{:S(2)}, u32[]{:S(2)}) collective-permute-start(bf16[1040,128]{1,0:T(8,128)(2,1)S(1)} %get-tuple-element.23.refs_1_), channel_id=1, source_target_pairs={{0,2},{1,47},{2,4},{3,1},{4,6},{5,3},{6,8},{7,5},{8,10},{9,7},{10,... | collective-permute-start | bytes 798728 | tf_op jit(solution)/shard_map/ppermute | solution.py:287
  42.2 1.9 %collective-permute-start.5 = (bf16[1040,128]{1,0:T(8,128)(2,1)S(1)}, bf16[1040,128]{1,0:T(8,128)(2,1)S(1)}, u32[]{:S(2)}, u32[]{:S(2)}) collective-permute-start(bf16[1040,128]{1,0:T(8,128)(2,1)S(1)} %get-tuple-element.20.refs_0_.refs_2_), channel_id=1, source_target_pairs={{0,26},{1,23},{2,28},{3,25},{4,30},{5,27},{6,32},{7,29},{8,34},{9,... | collective-permute-start | bytes 798728 | tf_op jit(solution)/shard_map/ppermute | solution.py:287
  44.2 14.1 %collective-permute-done.4.refs_3_.refs_5_ = bf16[1040,128]{1,0:T(8,128)(2,1)S(1)} collective-permute-done((bf16[1040,128]{1,0:T(8,128)(2,1)S(1)}, bf16[1040,128]{1,0:T(8,128)(2,1)S(1)}, u32[]{:S(2)}, u32[]{:S(2)}) %collective-permute-start.4) | collective-permute-done | bytes 266272 | tf_op jit(solution)/shard_map/ppermute | solution.py:287
  58.3 4.1 %collective-permute-done.5.refs_4_.refs_6_ = bf16[1040,128]{1,0:T(8,128)(2,1)S(1)} collective-permute-done((bf16[1040,128]{1,0:T(8,128)(2,1)S(1)}, bf16[1040,128]{1,0:T(8,128)(2,1)S(1)}, u32[]{:S(2)}, u32[]{:S(2)}) %collective-permute-start.5) | collective-permute-done | bytes 266272 | tf_op jit(solution)/shard_map/ppermute | solution.py:287
  62.5 10.5 %collective-permute-start.6 = (bf16[2096,128]{1,0:T(8,128)(2,1)S(1)}, bf16[2096,128]{1,0:T(8,128)(2,1)S(1)}, u32[]{:S(2)}, u32[]{:S(2)}) collective-permute-start(bf16[2096,128]{1,0:T(8,128)(2,1)S(1)} %get-tuple-element.24.refs_0_.refs_7_), channel_id=1, source_target_pairs={{0,30},{1,19},{2,32},{3,21},{4,34},{5,23},{6,36},{7,25},{8,38},{9,... | collective-permute-start | bytes 1609736 | tf_op jit(solution)/shard_map/ppermute | solution.py:287
  73.0 8.5 %collective-permute-start.7 = (bf16[2096,128]{1,0:T(8,128)(2,1)S(1)}, bf16[2096,128]{1,0:T(8,128)(2,1)S(1)}, u32[]{:S(2)}, u32[]{:S(2)}) collective-permute-start(bf16[2096,128]{1,0:T(8,128)(2,1)S(1)} %get-tuple-element.25), channel_id=1, source_target_pairs={{0,2},{1,47},{2,4},{3,1},{4,6},{5,3},{6,8},{7,5},{8,10},{9,7},{10,... | collective-permute-start | bytes 1609736 | tf_op jit(solution)/shard_map/ppermute | solution.py:287
  84.6 2.6 %collective-permute-start.8 = (bf16[528,128]{1,0:T(8,128)(2,1)S(1)}, bf16[528,128]{1,0:T(8,128)(2,1)S(1)}, u32[]{:S(2)}, u32[]{:S(2)}) collective-permute-start(bf16[528,128]{1,0:T(8,128)(2,1)S(1)} %get-tuple-element.27), channel_id=1, source_target_pairs={{0,24},{1,25},{2,26},{3,27},{4,28},{5,29},{6,30},{7,31},{8,32},{9,... | collective-permute-start | bytes 405512 | tf_op jit(solution)/shard_map/ppermute | solution.py:287
  87.2 2.6 %collective-permute-start.9 = (bf16[16,128]{1,0:T(8,128)(2,1)S(1)}, bf16[16,128]{1,0:T(8,128)(2,1)S(1)}, u32[]{:S(2)}, u32[]{:S(2)}) collective-permute-start(bf16[16,128]{1,0:T(8,128)(2,1)S(1)} %maximum_maximum_fusion.note_ref), channel_id=1, source_target_pairs={{0,12},{1,37},{2,14},{3,39},{4,16},{5,41},{6,18},{7,43},{8,20},{9,... | collective-permute-start | bytes 12296 | tf_op jit(solution)/shard_map/ppermute | solution.py:287
  89.8 8.2 %collective-permute-done.9.refs_3_.refs_4_ = bf16[16,128]{1,0:T(8,128)(2,1)S(1)} collective-permute-done((bf16[16,128]{1,0:T(8,128)(2,1)S(1)}, bf16[16,128]{1,0:T(8,128)(2,1)S(1)}, u32[]{:S(2)}, u32[]{:S(2)}) %collective-permute-start.9) | collective-permute-done | bytes 4128 | tf_op jit(solution)/shard_map/ppermute | solution.py:287
  98.6 4.7 %collective-permute-start.11 = (bf16[3072,128]{1,0:T(8,128)(2,1)S(1)}, bf16[3072,128]{1,0:T(8,128)(2,1)S(1)}, u32[]{:S(2)}, u32[]{:S(2)}) collective-permute-start(bf16[3072,128]{1,0:T(8,128)(2,1)S(1)} %shard_map.93.refs_5_), channel_id=1, source_target_pairs={{0,2},{1,47},{2,4},{3,1},{4,6},{5,3},{6,8},{7,5},{8,10},{9,7},{10,... | collective-permute-start | bytes 2359304 | tf_op jit(solution)/shard_map/ppermute | solution.py:287
  105.3 4.1 %collective-permute-start.10 = (bf16[1200,128]{1,0:T(8,128)(2,1)}, bf16[1200,128]{1,0:T(8,128)(2,1)S(1)}, u32[]{:S(2)}, u32[]{:S(2)}) collective-permute-start(bf16[1200,128]{1,0:T(8,128)(2,1)} %get-tuple-element.29.own), channel_id=1, source_target_pairs={{0,1},{1,0},{2,3},{3,2},{4,5},{5,4},{6,7},{7,6},{8,9},{9,8},{10,11... | collective-permute-start | bytes 921608 | tf_op jit(solution)/shard_map/ppermute | solution.py:291
  109.4 1.9 %collective-permute-start.12 = (bf16[1408,128]{1,0:T(8,128)(2,1)}, bf16[1408,128]{1,0:T(8,128)(2,1)}, u32[]{:S(2)}, u32[]{:S(2)}) collective-permute-start(bf16[1408,128]{1,0:T(8,128)(2,1)} %get-tuple-element.31), channel_id=1, source_target_pairs={{0,1},{1,0},{2,3},{3,2},{4,5},{5,4},{6,7},{7,6},{8,9},{9,8},{10,11... | collective-permute-start | bytes 1081352 | tf_op jit(solution)/shard_map/ppermute | solution.py:291
  111.3 2.4 %collective-permute-start.13 = (bf16[1408,128]{1,0:T(8,128)(2,1)}, bf16[1408,128]{1,0:T(8,128)(2,1)}, u32[]{:S(2)}, u32[]{:S(2)}) collective-permute-start(bf16[1408,128]{1,0:T(8,128)(2,1)} %get-tuple-element.32), channel_id=1, source_target_pairs={{0,1},{1,0},{2,3},{3,2},{4,5},{5,4},{6,7},{7,6},{8,9},{9,8},{10,11... | collective-permute-start | bytes 1081352 | tf_op jit(solution)/shard_map/ppermute | solution.py:291
  119.2 2.0 %shard_map.96.table_ref = s32[96,128]{1,0:T(8,128)S(1)} custom-call(s32[2]{0:T(128)S(1)} %pad_add_fusion.1.scalars, bf16[96,96]{1,0:T(8,128)(2,1)S(1)} %copy-done.9, s32[96,128]{1,0:T(8,128)S(1)} %copy-done.7, s32[1,128]{1,0:T(1,128)S(1)} %pad.12.slots_ref, bf16[1200,128]{1,0:T(8,128)(2,1)} %get-tuple-element.29.own, ...), custom_call_target="tpu_custom_call" | custom-call | flops 2457600 | bytes 98304 | tf_op jit(solution)/shard_map/pallas_call | solution.py:265
  121.3 2.6 %shard_map.99.rest_4_ = f32[13,128,128]{2,1,0:T(8,128)S(1)} custom-call(s32[56,128]{1,0:T(8,128)S(1)} %shard_map.98.table_ref, bf16[6400,128]{1,0:T(8,128)(2,1)S(1)} %bitcast.35, bf16[3840,128]{1,0:T(8,128)(2,1)S(1)} %copy-done.12, bf16[3120,128]{1,0:T(8,128)(2,1)S(1)} %copy-done.4), custom_call_target="tpu_custom_call" | custom-call | flops 1811939328 | bytes 1769472 | tf_op jit(solution)/shard_map/pallas_call | solution.py:173
  123.9 2.6 %shard_map.100.refs_1_.rest_1_ = f32[13,128,128]{2,1,0:T(8,128)S(1)} custom-call(s32[96,128]{1,0:T(8,128)S(1)} %shard_map.96.table_ref, bf16[6400,128]{1,0:T(8,128)(2,1)S(1)} %bitcast.36, bf16[2944,128]{1,0:T(8,128)(2,1)S(1)} %copy-done.14, bf16[1408,128]{1,0:T(8,128)(2,1)} %collective-permute-done.12.rest_1_, ...), custom_call_target="tpu_custom_call" | custom-call | flops 1811939328 | bytes 1769472 | tf_op jit(solution)/shard_map/pallas_call | solution.py:173
  126.6 1.9 %collective-permute-start.15 = (bf16[1536,128]{1,0:T(8,128)(2,1)S(1)}, bf16[1536,128]{1,0:T(8,128)(2,1)S(1)}, u32[]{:S(2)}, u32[]{:S(2)}) collective-permute-start(bf16[1536,128]{1,0:T(8,128)(2,1)S(1)} %shard_map.101), channel_id=1, source_target_pairs={{0,1},{1,0},{2,3},{3,2},{4,5},{5,4},{6,7},{7,6},{8,9},{9,8},{10,11... | collective-permute-start | bytes 1179656 | tf_op jit(solution)/shard_map/ppermute | solution.py:291
  128.5 2.0 %shard_map.102.rest_1_ = f32[13,128,128]{2,1,0:T(8,128)S(1)} custom-call(s32[96,128]{1,0:T(8,128)S(1)} %shard_map.96.table_ref, bf16[6400,128]{1,0:T(8,128)(2,1)S(1)} %bitcast.37, bf16[3072,128]{1,0:T(8,128)(2,1)S(1)} %collective-permute-done.11.refs_0_.rest_0_, f32[13,128,128]{2,1,0:T(8,128)S(1)} %shard_map.100.refs_1_.rest_1_), custom_call_target="tpu_custom_call" | custom-call | flops 805306368 | bytes 786432 | tf_op jit(solution)/shard_map/pallas_call | solution.py:173
  130.5 2.5 %shard_map.103 = bf16[12,128,128]{2,1,0:T(8,128)(2,1)} custom-call(s32[96,128]{1,0:T(8,128)S(1)} %shard_map.96.table_ref, bf16[6400,128]{1,0:T(8,128)(2,1)S(1)} %bitcast.38, bf16[1536,128]{1,0:T(8,128)(2,1)S(1)} %collective-permute-done.15.rest_0_, f32[13,128,128]{2,1,0:T(8,128)S(1)} %shard_map.102.rest_1_), custom_call_target="tpu_custom_call" | custom-call | flops 402653184 | bytes 393216 | tf_op jit(solution)/shard_map/pallas_call | solution.py:173
  (75 shorter events, 17.6 us)
Async XLA Ops:
  0.8 15.4 %collective-permute-start.1 = (bf16[16,128]{1,0:T(8,128)(2,1)S(1)}, bf16[16,128]{1,0:T(8,128)(2,1)S(1)}, u32[]{:S(2)}, u32[]{:S(2)}) collective-permute-start(bf16[16,128]{1,0:T(8,128)(2,1)S(1)} %fusion.5), channel_id=1, source_target_pairs={{0,1},{1,0},{2,3},{3,2},{4,5},{5,4},{6,7},{7,6},{8,9},{9,8},{10,11... | collective-permute-start | bytes 12296 | tf_op jit(solution)/shard_map/ppermute | solution.py:291
  13.2 4.0 %collective-permute-start = (bf16[16,128,128]{2,1,0:T(8,128)(2,1)}, bf16[16,128,128]{2,1,0:T(8,128)(2,1)S(1)}, u32[]{:S(2)}, u32[]{:S(2)}) collective-permute-start(bf16[16,128,128]{2,1,0:T(8,128)(2,1)} %bitcast.39), channel_id=1, source_target_pairs={{0,1},{1,0},{2,3},{3,2},{4,5},{5,4},{6,7},{7,6},{8,9},{9,8},{10,11... | collective-permute-start | bytes 1572872 | tf_op jit(solution)/shard_map/ppermute | solution.py:291
  20.1 4.1 %copy-start.5 = (bf16[1,1,16,1,128,128]{5,4,3,2,1,0:T(8,128)(2,1)S(1)}, bf16[1,1,16,1,128,128]{5,4,3,2,1,0:T(8,128)(2,1)}, u32[]{:S(2)}) copy-start(bf16[1,1,16,1,128,128]{5,4,3,2,1,0:T(8,128)(2,1)} %param.9) | copy-start | bytes 1572868
  20.1 94.6 %all-to-all-start = ((bf16[16,400,128]{2,1,0:T(8,128)(2,1)}), bf16[16,400,128]{2,1,0:T(8,128)(2,1)S(1)}, u32[]{:S(2)}, u32[]{:S(2)}) async-start(bf16[16,400,128]{2,1,0:T(8,128)(2,1)} %shard_map.95), calls=%async_computation | async-start | bytes 3276800 | tf_op jit(solution)/shard_map/all_to_all | solution.py:334
  24.8 37.6 %collective-permute-start.2 = (bf16[1552,128]{1,0:T(8,128)(2,1)S(1)}, bf16[1552,128]{1,0:T(8,128)(2,1)S(1)}, u32[]{:S(2)}, u32[]{:S(2)}) collective-permute-start(bf16[1552,128]{1,0:T(8,128)(2,1)S(1)} %get-tuple-element.21), channel_id=1, source_target_pairs={{0,4},{1,45},{2,6},{3,47},{4,8},{5,1},{6,10},{7,3},{8,12},{9,5},{1... | collective-permute-start | bytes 1191944 | tf_op jit(solution)/shard_map/ppermute | solution.py:287
  36.4 26.0 %collective-permute-start.3 = (bf16[1552,128]{1,0:T(8,128)(2,1)S(1)}, bf16[1552,128]{1,0:T(8,128)(2,1)S(1)}, u32[]{:S(2)}, u32[]{:S(2)}) collective-permute-start(bf16[1552,128]{1,0:T(8,128)(2,1)S(1)} %get-tuple-element.22.refs_0_), channel_id=1, source_target_pairs={{0,28},{1,21},{2,30},{3,23},{4,32},{5,25},{6,34},{7,27},{8,36},{9,... | collective-permute-start | bytes 1191944 | tf_op jit(solution)/shard_map/ppermute | solution.py:287
  38.4 19.9 %collective-permute-start.4 = (bf16[1040,128]{1,0:T(8,128)(2,1)S(1)}, bf16[1040,128]{1,0:T(8,128)(2,1)S(1)}, u32[]{:S(2)}, u32[]{:S(2)}) collective-permute-start(bf16[1040,128]{1,0:T(8,128)(2,1)S(1)} %get-tuple-element.23.refs_1_), channel_id=1, source_target_pairs={{0,2},{1,47},{2,4},{3,1},{4,6},{5,3},{6,8},{7,5},{8,10},{9,7},{10,... | collective-permute-start | bytes 798728 | tf_op jit(solution)/shard_map/ppermute | solution.py:287
  42.2 20.2 %collective-permute-start.5 = (bf16[1040,128]{1,0:T(8,128)(2,1)S(1)}, bf16[1040,128]{1,0:T(8,128)(2,1)S(1)}, u32[]{:S(2)}, u32[]{:S(2)}) collective-permute-start(bf16[1040,128]{1,0:T(8,128)(2,1)S(1)} %get-tuple-element.20.refs_0_.refs_2_), channel_id=1, source_target_pairs={{0,26},{1,23},{2,28},{3,25},{4,30},{5,27},{6,32},{7,29},{8,34},{9,... | collective-permute-start | bytes 798728 | tf_op jit(solution)/shard_map/ppermute | solution.py:287
  62.5 36.0 %collective-permute-start.6 = (bf16[2096,128]{1,0:T(8,128)(2,1)S(1)}, bf16[2096,128]{1,0:T(8,128)(2,1)S(1)}, u32[]{:S(2)}, u32[]{:S(2)}) collective-permute-start(bf16[2096,128]{1,0:T(8,128)(2,1)S(1)} %get-tuple-element.24.refs_0_.refs_7_), channel_id=1, source_target_pairs={{0,30},{1,19},{2,32},{3,21},{4,34},{5,23},{6,36},{7,25},{8,38},{9,... | collective-permute-start | bytes 1609736 | tf_op jit(solution)/shard_map/ppermute | solution.py:287
  73.0 25.5 %collective-permute-start.7 = (bf16[2096,128]{1,0:T(8,128)(2,1)S(1)}, bf16[2096,128]{1,0:T(8,128)(2,1)S(1)}, u32[]{:S(2)}, u32[]{:S(2)}) collective-permute-start(bf16[2096,128]{1,0:T(8,128)(2,1)S(1)} %get-tuple-element.25), channel_id=1, source_target_pairs={{0,2},{1,47},{2,4},{3,1},{4,6},{5,3},{6,8},{7,5},{8,10},{9,7},{10,... | collective-permute-start | bytes 1609736 | tf_op jit(solution)/shard_map/ppermute | solution.py:287
  82.7 21.7 %copy-start = (bf16[3120,128]{1,0:T(8,128)(2,1)}, bf16[3120,128]{1,0:T(8,128)(2,1)S(1)}, u32[]{:S(2)}) copy-start(bf16[3120,128]{1,0:T(8,128)(2,1)S(1)} %get-tuple-element.33.own) | copy-start | bytes 2396164
  82.7 31.1 %collective-permute-start.14 = (bf16[3120,128]{1,0:T(8,128)(2,1)S(1)}, bf16[3120,128]{1,0:T(8,128)(2,1)S(1)}, u32[]{:S(2)}, u32[]{:S(2)}) collective-permute-start(bf16[3120,128]{1,0:T(8,128)(2,1)S(1)} %get-tuple-element.33.own), channel_id=1, source_target_pairs={{0,1},{1,0},{2,3},{3,2},{4,5},{5,4},{6,7},{7,6},{8,9},{9,8},{10,11... | collective-permute-start | bytes 2396168 | tf_op jit(solution)/shard_map/ppermute | solution.py:291
  84.6 13.9 %collective-permute-start.8 = (bf16[528,128]{1,0:T(8,128)(2,1)S(1)}, bf16[528,128]{1,0:T(8,128)(2,1)S(1)}, u32[]{:S(2)}, u32[]{:S(2)}) collective-permute-start(bf16[528,128]{1,0:T(8,128)(2,1)S(1)} %get-tuple-element.27), channel_id=1, source_target_pairs={{0,24},{1,25},{2,26},{3,27},{4,28},{5,29},{6,30},{7,31},{8,32},{9,... | collective-permute-start | bytes 405512 | tf_op jit(solution)/shard_map/ppermute | solution.py:287
  87.2 10.8 %collective-permute-start.9 = (bf16[16,128]{1,0:T(8,128)(2,1)S(1)}, bf16[16,128]{1,0:T(8,128)(2,1)S(1)}, u32[]{:S(2)}, u32[]{:S(2)}) collective-permute-start(bf16[16,128]{1,0:T(8,128)(2,1)S(1)} %maximum_maximum_fusion.note_ref), channel_id=1, source_target_pairs={{0,12},{1,37},{2,14},{3,39},{4,16},{5,41},{6,18},{7,43},{8,20},{9,... | collective-permute-start | bytes 12296 | tf_op jit(solution)/shard_map/ppermute | solution.py:287
  98.6 15.1 %copy-start.15 = (s32[1,1,12]{2,1,0:T(1,128)S(1)}, s32[1,1,12]{2,1,0:T(1,128)}, u32[]{:S(2)}) copy-start(s32[1,1,12]{2,1,0:T(1,128)} %param.13) | copy-start | bytes 148
  98.6 16.1 %copy-start.8 = (s32[56,128]{1,0:T(8,128)S(1)}, s32[56,128]{1,0:T(8,128)}, u32[]{:S(2)}) copy-start(s32[56,128]{1,0:T(8,128)} %constant.114.clone.meta_ref) | copy-start | bytes 86020
  98.6 27.9 %collective-permute-start.11 = (bf16[3072,128]{1,0:T(8,128)(2,1)S(1)}, bf16[3072,128]{1,0:T(8,128)(2,1)S(1)}, u32[]{:S(2)}, u32[]{:S(2)}) collective-permute-start(bf16[3072,128]{1,0:T(8,128)(2,1)S(1)} %shard_map.93.refs_5_), channel_id=1, source_target_pairs={{0,2},{1,47},{2,4},{3,1},{4,6},{5,3},{6,8},{7,5},{8,10},{9,7},{10,... | collective-permute-start | bytes 2359304 | tf_op jit(solution)/shard_map/ppermute | solution.py:287
  105.3 14.0 %collective-permute-start.10 = (bf16[1200,128]{1,0:T(8,128)(2,1)}, bf16[1200,128]{1,0:T(8,128)(2,1)S(1)}, u32[]{:S(2)}, u32[]{:S(2)}) collective-permute-start(bf16[1200,128]{1,0:T(8,128)(2,1)} %get-tuple-element.29.own), channel_id=1, source_target_pairs={{0,1},{1,0},{2,3},{3,2},{4,5},{5,4},{6,7},{7,6},{8,9},{9,8},{10,11... | collective-permute-start | bytes 921608 | tf_op jit(solution)/shard_map/ppermute | solution.py:291
  109.4 14.5 %collective-permute-start.12 = (bf16[1408,128]{1,0:T(8,128)(2,1)}, bf16[1408,128]{1,0:T(8,128)(2,1)}, u32[]{:S(2)}, u32[]{:S(2)}) collective-permute-start(bf16[1408,128]{1,0:T(8,128)(2,1)} %get-tuple-element.31), channel_id=1, source_target_pairs={{0,1},{1,0},{2,3},{3,2},{4,5},{5,4},{6,7},{7,6},{8,9},{9,8},{10,11... | collective-permute-start | bytes 1081352 | tf_op jit(solution)/shard_map/ppermute | solution.py:291
  111.3 12.6 %collective-permute-start.13 = (bf16[1408,128]{1,0:T(8,128)(2,1)}, bf16[1408,128]{1,0:T(8,128)(2,1)}, u32[]{:S(2)}, u32[]{:S(2)}) collective-permute-start(bf16[1408,128]{1,0:T(8,128)(2,1)} %get-tuple-element.32), channel_id=1, source_target_pairs={{0,1},{1,0},{2,3},{3,2},{4,5},{5,4},{6,7},{7,6},{8,9},{9,8},{10,11... | collective-permute-start | bytes 1081352 | tf_op jit(solution)/shard_map/ppermute | solution.py:291
  119.2 2.1 %copy-start.4 = (bf16[3120,128]{1,0:T(8,128)(2,1)S(1)}, bf16[3120,128]{1,0:T(8,128)(2,1)}, u32[]{:S(2)}) copy-start(bf16[3120,128]{1,0:T(8,128)(2,1)} %copy-done.2) | copy-start | bytes 2396164
  119.2 2.1 %copy-start.12 = (bf16[3840,128]{1,0:T(8,128)(2,1)S(1)}, bf16[3840,128]{1,0:T(8,128)(2,1)}, u32[]{:S(2)}) copy-start(bf16[3840,128]{1,0:T(8,128)(2,1)} %copy-done.11) | copy-start | bytes 2949124
  121.3 2.6 %copy-start.14 = (bf16[2944,128]{1,0:T(8,128)(2,1)S(1)}, bf16[2944,128]{1,0:T(8,128)(2,1)}, u32[]{:S(2)}) copy-start(bf16[2944,128]{1,0:T(8,128)(2,1)} %copy-done.13) | copy-start | bytes 2260996
  126.6 3.9 %collective-permute-start.15 = (bf16[1536,128]{1,0:T(8,128)(2,1)S(1)}, bf16[1536,128]{1,0:T(8,128)(2,1)S(1)}, u32[]{:S(2)}, u32[]{:S(2)}) collective-permute-start(bf16[1536,128]{1,0:T(8,128)(2,1)S(1)} %shard_map.101), channel_id=1, source_target_pairs={{0,1},{1,0},{2,3},{3,2},{4,5},{5,4},{6,7},{7,6},{8,9},{9,8},{10,11... | collective-permute-start | bytes 1179656 | tf_op jit(solution)/shard_map/ppermute | solution.py:291
  (9 other events, 9.8 us)

commit v12 on v8

--- a/solution.py
+++ b/solution.py
@@ -179,7 +179,7 @@
             acc[table_ref[3, base + n]] += both[:, BLK:]
             return carry
 
-        unroll = max(n for n in (7, 6, 5, 4, 3, 2, 1) if count % n == 0)
+        unroll = count if count <= 24 else max(n for n in range(1, 17) if count % n == 0)
         lax.fori_loop(0, count, body, 0, unroll=unroll)
         base += count
     if last:
@@ -345,8 +345,8 @@
     send(up_in, names, 1)
     notes = (notes, from_other_core(notes))
 
-    late = items([(1, 16), (5, 4), (2, 17), (6, 5)])
-    late += items([(1, 17), (5, 5), (2, 18), (6, 6), (0, 16), (4, 4)])
+    middle = items([(1, 16), (5, 4), (2, 17), (6, 5)])
+    last = items([(1, 17), (5, 5), (2, 18), (6, 6), (0, 16), (4, 4)])
 
     def part_of(names):
         by_source = {}
@@ -384,11 +384,13 @@
         rows += [(len(rows) * BLK + n * BLK, 0, name[2], name[1], w) for n, (_, w) in enumerate(wanted(name))]
     part = [(early_own[0], rows)] + received_of(early_other, early)
     sums, _ = product_of(table_of((part,), early_notes), part, 0)
-    parts = [part_of(late), received_of(None, late)]
+    parts = [part_of(middle + last) + received_of(None, middle), received_of(None, last)]
     table = table_of(parts, notes)
-    late_other, _, _ = pass_on(late, None, (), (sums,))
+    middle_other, _, _ = pass_on(middle, None, (), (sums,))
+    last_other, _, _ = pass_on(last, None, (), (sums,))
+    parts[0] = part_of(middle + last) + received_of(middle_other, middle)
     sums, base = product_of(table, parts[0], 0, sums)
-    out, _ = product_of(table, received_of(late_other, late), base, sums, last=True)
+    out, _ = product_of(table, received_of(last_other, last), base, sums, last=True)
     return out[None, None]
 
 

time: 126 us -> 128 us (1.016)
  Pallas kernels: 18.7 us -> 14.4 us
  other arithmetic: 3.47 us -> 6.69 us
  starting transfers between devices: 71.1 us -> 73.3 us
    pallas_call x3, Pallas kernels: 12.7 us -> 8.61 us  [product(): pl.pallas_call(functools.partial(product_kernel, counts, base, before is...]
    ppermute x5 -> x6, starting transfers between devices: 28.7 us -> 30.9 us  [from_other_core(): return lax.ppermute(array, 'core', [(0, 1), (1, 0)])]
    unnamed x62 -> x96, local copies, waits for them, and re-layouts: 8.2 us -> 8.54 us
    pallas_call x5 -> x6, Pallas kernels: 4.53 us -> 4.32 us  [pack(): pl.pallas_call(functools.partial(pack_kernel, spec, notes, len(used)), ou...]
  transfers between devices with their start and end apart: 15 -> 16, of which waited for: 7 -> 6; matrix products, arithmetic and copies ran while one was open for 4% -> 7% of each run, Pallas kernels for 11% -> 10%
where the time goes in v12:
time: 128 us; the launch traced here: 127 us
  starting transfers between devices  73.3 us (57%)
  waiting for transfers between devices  20.3 us (16%)
  Pallas kernels  14.4 us (11%)
  local copies, waits for them, and re-layouts  10.9 us (9%)
  other arithmetic  6.69 us (5%)
    ppermute x8, starting transfers between devices, moved(): return lax.ppermute(array, COL, route)  33.6 us
    ppermute x6, starting transfers between devices, from_other_core(): return lax.ppermute(array, 'core', [(0, 1), (1, 0)])  30.9 us
    ppermute x8, waiting for transfers between devices, moved(): return lax.ppermute(array, COL, route)  15.5 us
    pallas_call x3, Pallas kernels, product(): pl.pallas_call(functools.partial(product_kernel, counts, base, before is...  8.61 us
    unnamed x96, local copies, waits for them, and re-layouts  8.54 us
    all_to_all x1, starting transfers between devices, local(): lax.all_to_all(right_packed(b_kept, b_other, up_in), 'y', 0, 0, tiled=True)  6.86 us
    all_to_all x1, waiting for transfers between devices, local(): lax.all_to_all(right_packed(b_kept, b_other, up_in), 'y', 0, 0, tiled=True)  4.76 us
    pallas_call x6, Pallas kernels, pack(): pl.pallas_call(functools.partial(pack_kernel, spec, notes, len(used)), ou...  4.32 us
  transfers between devices with their start and end apart: 16, of which 6 were waited for; matrix products, arithmetic and copies ran while one was open for 7% of the time, Pallas kernels for 10%

profile of v12, /device:TPU:1, one launch (start us, length us, event | category | flops | bytes accessed | tf_op | source)
XLA Modules:
  0.0 126.5 jit_solution(13402422033117674389)
XLA Ops:
  0.8 12.4 %collective-permute-start.2 = (bf16[16,128]{1,0:T(8,128)(2,1)S(1)}, bf16[16,128]{1,0:T(8,128)(2,1)S(1)}, u32[]{:S(2)}, u32[]{:S(2)}) collective-permute-start(bf16[16,128]{1,0:T(8,128)(2,1)S(1)} %fusion.37), channel_id=1, source_target_pairs={{0,1},{1,0},{2,3},{3,2},{4,5},{5,4},{6,7},{7,6},{8,9},{9,8},{10,11... | collective-permute-start | bytes 12296 | tf_op jit(solution)/shard_map/ppermute | solution.py:251
  13.2 1.9 %collective-permute-start.1 = (bf16[16,128,128]{2,1,0:T(8,128)(2,1)}, bf16[16,128,128]{2,1,0:T(8,128)(2,1)S(1)}, u32[]{:S(2)}, u32[]{:S(2)}) collective-permute-start(bf16[16,128,128]{2,1,0:T(8,128)(2,1)} %bitcast.76), channel_id=1, source_target_pairs={{0,1},{1,0},{2,3},{3,2},{4,5},{5,4},{6,7},{7,6},{8,9},{9,8},{10,11... | collective-permute-start | bytes 1572872 | tf_op jit(solution)/shard_map/ppermute | solution.py:251
  17.6 1.9 %collective-permute-start = (bf16[1296,128]{1,0:T(8,128)(2,1)S(1)}, bf16[1296,128]{1,0:T(8,128)(2,1)S(1)}, u32[]{:S(2)}, u32[]{:S(2)}) collective-permute-start(bf16[1296,128]{1,0:T(8,128)(2,1)S(1)} %get-tuple-element.18), channel_id=1, source_target_pairs={{0,384},{384,0},{1,385},{385,1},{2,386},{386,2},{3,387},{387,3},{4... | collective-permute-start | bytes 995336 | tf_op jit(solution)/shard_map/ppermute | solution.py:269
  22.2 8.8 %collective-permute-start.3 = (bf16[1040,128]{1,0:T(8,128)(2,1)S(1)}, bf16[1040,128]{1,0:T(8,128)(2,1)S(1)}, u32[]{:S(2)}, u32[]{:S(2)}) collective-permute-start(bf16[1040,128]{1,0:T(8,128)(2,1)S(1)} %get-tuple-element.20), channel_id=1, source_target_pairs={{0,4},{1,45},{2,6},{3,47},{4,8},{5,1},{6,10},{7,3},{8,12},{9,5},{1... | collective-permute-start | bytes 798728 | tf_op jit(solution)/shard_map/ppermute | solution.py:247
  31.0 1.9 %collective-permute-start.4 = (bf16[1040,128]{1,0:T(8,128)(2,1)S(1)}, bf16[1040,128]{1,0:T(8,128)(2,1)S(1)}, u32[]{:S(2)}, u32[]{:S(2)}) collective-permute-start(bf16[1040,128]{1,0:T(8,128)(2,1)S(1)} %get-tuple-element.21.refs_0_), channel_id=1, source_target_pairs={{0,28},{1,21},{2,30},{3,23},{4,32},{5,25},{6,34},{7,27},{8,36},{9,... | collective-permute-start | bytes 798728 | tf_op jit(solution)/shard_map/ppermute | solution.py:247
  32.9 3.9 %collective-permute-start.5 = (bf16[1040,128]{1,0:T(8,128)(2,1)S(1)}, bf16[1040,128]{1,0:T(8,128)(2,1)S(1)}, u32[]{:S(2)}, u32[]{:S(2)}) collective-permute-start(bf16[1040,128]{1,0:T(8,128)(2,1)S(1)} %get-tuple-element.22.refs_1_), channel_id=1, source_target_pairs={{0,2},{1,47},{2,4},{3,1},{4,6},{5,3},{6,8},{7,5},{8,10},{9,7},{10,... | collective-permute-start | bytes 798728 | tf_op jit(solution)/shard_map/ppermute | solution.py:247
  36.8 1.9 %collective-permute-start.6 = (bf16[1040,128]{1,0:T(8,128)(2,1)S(1)}, bf16[1040,128]{1,0:T(8,128)(2,1)S(1)}, u32[]{:S(2)}, u32[]{:S(2)}) collective-permute-start(bf16[1040,128]{1,0:T(8,128)(2,1)S(1)} %get-tuple-element.19.refs_0_), channel_id=1, source_target_pairs={{0,26},{1,23},{2,28},{3,25},{4,30},{5,27},{6,32},{7,29},{8,34},{9,... | collective-permute-start | bytes 798728 | tf_op jit(solution)/shard_map/ppermute | solution.py:247
  39.4 5.2 %collective-permute-done.4.refs_2_.refs_3_ = bf16[1040,128]{1,0:T(8,128)(2,1)S(1)} collective-permute-done((bf16[1040,128]{1,0:T(8,128)(2,1)S(1)}, bf16[1040,128]{1,0:T(8,128)(2,1)S(1)}, u32[]{:S(2)}, u32[]{:S(2)}) %collective-permute-start.4) | collective-permute-done | bytes 266272 | tf_op jit(solution)/shard_map/ppermute | solution.py:247
  46.3 3.7 %collective-permute-done.6.refs_4_.refs_1_.refs_5_ = bf16[1040,128]{1,0:T(8,128)(2,1)S(1)} collective-permute-done((bf16[1040,128]{1,0:T(8,128)(2,1)S(1)}, bf16[1040,128]{1,0:T(8,128)(2,1)S(1)}, u32[]{:S(2)}, u32[]{:S(2)}) %collective-permute-start.6) | collective-permute-done | bytes 266272 | tf_op jit(solution)/shard_map/ppermute | solution.py:247
  50.9 5.2 %collective-permute-start.7 = (bf16[3120,128]{1,0:T(8,128)(2,1)S(1)}, bf16[3120,128]{1,0:T(8,128)(2,1)S(1)}, u32[]{:S(2)}, u32[]{:S(2)}) collective-permute-start(bf16[3120,128]{1,0:T(8,128)(2,1)S(1)} %shard_map.147.refs_2_.refs_0_.refs_6_), channel_id=1, source_target_pairs={{0,2},{1,47},{2,4},{3,1},{4,6},{5,3},{6,8},{7,5},{8,10},{9,7},{10,... | collective-permute-start | bytes 2396168 | tf_op jit(solution)/shard_map/ppermute | solution.py:247
  58.2 6.9 %all-to-all-start = ((bf16[8,800,128]{2,1,0:T(8,128)(2,1)}), bf16[8,800,128]{2,1,0:T(8,128)(2,1)S(1)}, u32[]{:S(2)}, u32[]{:S(2)}) async-start(bf16[8,800,128]{2,1,0:T(8,128)(2,1)} %copy-done), calls=%async_computation | async-start | bytes 3276800 | tf_op jit(solution)/shard_map/all_to_all | solution.py:316
  66.1 2.8 %collective-permute-start.8 = (bf16[2096,128]{1,0:T(8,128)(2,1)S(1)}, bf16[2096,128]{1,0:T(8,128)(2,1)S(1)}, u32[]{:S(2)}, u32[]{:S(2)}) collective-permute-start(bf16[2096,128]{1,0:T(8,128)(2,1)S(1)} %shard_map.149.refs_9_), channel_id=1, source_target_pairs={{0,30},{1,19},{2,32},{3,21},{4,34},{5,23},{6,36},{7,25},{8,38},{9,... | collective-permute-start | bytes 1609736 | tf_op jit(solution)/shard_map/ppermute | solution.py:247
  68.9 4.8 %collective-permute-start.9 = (bf16[528,128]{1,0:T(8,128)(2,1)S(1)}, bf16[528,128]{1,0:T(8,128)(2,1)S(1)}, u32[]{:S(2)}, u32[]{:S(2)}) collective-permute-start(bf16[528,128]{1,0:T(8,128)(2,1)S(1)} %copy-done.19), channel_id=1, source_target_pairs={{0,24},{1,25},{2,26},{3,27},{4,28},{5,29},{6,30},{7,31},{8,32},{9,... | collective-permute-start | bytes 405512 | tf_op jit(solution)/shard_map/ppermute | solution.py:247
  73.8 4.1 %collective-permute-done.9.refs_3_.refs_8_ = bf16[528,128]{1,0:T(8,128)(2,1)S(1)} collective-permute-done((bf16[528,128]{1,0:T(8,128)(2,1)S(1)}, bf16[528,128]{1,0:T(8,128)(2,1)S(1)}, u32[]{:S(2)}, u32[]{:S(2)}) %collective-permute-start.9) | collective-permute-done | bytes 135200 | tf_op jit(solution)/shard_map/ppermute | solution.py:247
  80.4 7.0 %collective-permute-start.12 = (bf16[5040,128]{1,0:T(8,128)(2,1)}, bf16[5040,128]{1,0:T(8,128)(2,1)}, u32[]{:S(2)}, u32[]{:S(2)}) collective-permute-start(bf16[5040,128]{1,0:T(8,128)(2,1)} %get-tuple-element.27), channel_id=1, source_target_pairs={{0,1},{1,0},{2,3},{3,2},{4,5},{5,4},{6,7},{7,6},{8,9},{9,8},{10,11... | collective-permute-start | bytes 3870728 | tf_op jit(solution)/shard_map/ppermute | solution.py:251
  88.6 5.2 %collective-permute-start.10 = (bf16[48,128]{1,0:T(8,128)(2,1)S(1)}, bf16[48,128]{1,0:T(8,128)(2,1)S(1)}, u32[]{:S(2)}, u32[]{:S(2)}) collective-permute-start(bf16[48,128]{1,0:T(8,128)(2,1)S(1)} %get-tuple-element.25), channel_id=1, source_target_pairs={{0,1},{1,0},{2,3},{3,2},{4,5},{5,4},{6,7},{7,6},{8,9},{9,8},{10,11... | collective-permute-start | bytes 36872 | tf_op jit(solution)/shard_map/ppermute | solution.py:251
  94.5 4.4 %collective-permute-start.11 = (bf16[3072,128]{1,0:T(8,128)(2,1)}, bf16[3072,128]{1,0:T(8,128)(2,1)}, u32[]{:S(2)}, u32[]{:S(2)}) collective-permute-start(bf16[3072,128]{1,0:T(8,128)(2,1)} %get-tuple-element.26), channel_id=1, source_target_pairs={{0,2},{1,47},{2,4},{3,1},{4,6},{5,3},{6,8},{7,5},{8,10},{9,7},{10,... | collective-permute-start | bytes 2359304 | tf_op jit(solution)/shard_map/ppermute | solution.py:247
  101.5 4.8 %all-to-all-done = bf16[8,800,128]{2,1,0:T(8,128)(2,1)S(1)} async-done(((bf16[8,800,128]{2,1,0:T(8,128)(2,1)}), bf16[8,800,128]{2,1,0:T(8,128)(2,1)S(1)}, u32[]{:S(2)}, u32[]{:S(2)}) %all-to-all-start) | async-done | bytes 1638432 | tf_op jit(solution)/shard_map/all_to_all | solution.py:316
  108.8 4.0 %shard_map.152.refs_1_.rest_3_ = f32[13,128,128]{2,1,0:T(8,128)S(1)} custom-call(s32[5,84]{1,0:T(8,128)S(1)} %stack.59.table_ref, bf16[6400,128]{1,0:T(8,128)(2,1)S(1)} %bitcast.72, bf16[5760,128]{1,0:T(8,128)(2,1)S(1)} %copy-done.17, bf16[5040,128]{1,0:T(8,128)(2,1)} %collective-permute-done.12.rest_1_), custom_call_target="tpu_custom_call" | custom-call | flops 2818572288 | bytes 2752512 | tf_op jit(solution)/shard_map/pallas_call | solution.py:192
  113.0 2.1 %collective-permute-start.14 = (bf16[2048,128]{1,0:T(8,128)(2,1)S(1)}, bf16[2048,128]{1,0:T(8,128)(2,1)}, u32[]{:S(2)}, u32[]{:S(2)}) collective-permute-start(bf16[2048,128]{1,0:T(8,128)(2,1)S(1)} %shard_map.154), channel_id=1, source_target_pairs={{0,1},{1,0},{2,3},{3,2},{4,5},{5,4},{6,7},{7,6},{8,9},{9,8},{10,11... | collective-permute-start | bytes 1572872 | tf_op jit(solution)/shard_map/ppermute | solution.py:251
  115.9 1.9 %shard_map.153 = bf16[1536,128]{1,0:T(8,128)(2,1)} custom-call(bf16[3072,128]{1,0:T(8,128)(2,1)} %collective-permute-done.11.refs_0_.rest_1_, f32[13,128,128]{2,1,0:T(8,128)S(1)} %shard_map.152.refs_1_.rest_3_), custom_call_target="tpu_custom_call" | custom-call | bytes 786432 | tf_op jit(solution)/shard_map/pallas_call | solution.py:148
  117.8 2.2 %collective-permute-start.13 = (bf16[1536,128]{1,0:T(8,128)(2,1)}, bf16[1536,128]{1,0:T(8,128)(2,1)}, u32[]{:S(2)}, u32[]{:S(2)}) collective-permute-start(bf16[1536,128]{1,0:T(8,128)(2,1)} %shard_map.153), channel_id=1, source_target_pairs={{0,1},{1,0},{2,3},{3,2},{4,5},{5,4},{6,7},{7,6},{8,9},{9,8},{10,11... | collective-permute-start | bytes 1179656 | tf_op jit(solution)/shard_map/ppermute | solution.py:251
  121.9 2.4 %shard_map.155.rest_1_ = f32[13,128,128]{2,1,0:T(8,128)S(1)} custom-call(s32[5,60]{1,0:T(8,128)S(1)} %stack.52.table_ref, bf16[6400,128]{1,0:T(8,128)(2,1)S(1)} %bitcast.73, bf16[2096,128]{1,0:T(8,128)(2,1)S(1)} %copy-done.5, bf16[3072,128]{1,0:T(8,128)(2,1)} %collective-permute-done.11.refs_0_.rest_1_, bf16[2048,128]{1,0:T(8,128)(2,1)} %collective-permute-done.14.rest_2_, ...), custom_call_target="tpu_custom_call" | custom-call | flops 1610612736 | bytes 1572864 | tf_op jit(solution)/shard_map/pallas_call | solution.py:192
  124.3 2.2 %shard_map.156 = bf16[12,128,128]{2,1,0:T(8,128)(2,1)} custom-call(s32[5,60]{1,0:T(8,128)S(1)} %stack.52.table_ref, bf16[6400,128]{1,0:T(8,128)(2,1)S(1)} %bitcast.74, bf16[1536,128]{1,0:T(8,128)(2,1)} %collective-permute-done.13.rest_0_, f32[13,128,128]{2,1,0:T(8,128)S(1)} %shard_map.155.rest_1_), custom_call_target="tpu_custom_call" | custom-call | flops 402653184 | bytes 393216 | tf_op jit(solution)/shard_map/pallas_call | solution.py:192
  (178 shorter events, 23.9 us)
Async XLA Ops:
  0.8 18.9 %collective-permute-start.2 = (bf16[16,128]{1,0:T(8,128)(2,1)S(1)}, bf16[16,128]{1,0:T(8,128)(2,1)S(1)}, u32[]{:S(2)}, u32[]{:S(2)}) collective-permute-start(bf16[16,128]{1,0:T(8,128)(2,1)S(1)} %fusion.37), channel_id=1, source_target_pairs={{0,1},{1,0},{2,3},{3,2},{4,5},{5,4},{6,7},{7,6},{8,9},{9,8},{10,11... | collective-permute-start | bytes 12296 | tf_op jit(solution)/shard_map/ppermute | solution.py:251
  13.2 6.6 %collective-permute-start.1 = (bf16[16,128,128]{2,1,0:T(8,128)(2,1)}, bf16[16,128,128]{2,1,0:T(8,128)(2,1)S(1)}, u32[]{:S(2)}, u32[]{:S(2)}) collective-permute-start(bf16[16,128,128]{2,1,0:T(8,128)(2,1)} %bitcast.76), channel_id=1, source_target_pairs={{0,1},{1,0},{2,3},{3,2},{4,5},{5,4},{6,7},{7,6},{8,9},{9,8},{10,11... | collective-permute-start | bytes 1572872 | tf_op jit(solution)/shard_map/ppermute | solution.py:251
  17.6 21.1 %collective-permute-start = (bf16[1296,128]{1,0:T(8,128)(2,1)S(1)}, bf16[1296,128]{1,0:T(8,128)(2,1)S(1)}, u32[]{:S(2)}, u32[]{:S(2)}) collective-permute-start(bf16[1296,128]{1,0:T(8,128)(2,1)S(1)} %get-tuple-element.18), channel_id=1, source_target_pairs={{0,384},{384,0},{1,385},{385,1},{2,386},{386,2},{3,387},{387,3},{4... | collective-permute-start | bytes 995336 | tf_op jit(solution)/shard_map/ppermute | solution.py:269
  22.1 34.9 %copy-start.12 = (bf16[1040,128]{1,0:T(8,128)(2,1)}, bf16[1040,128]{1,0:T(8,128)(2,1)S(1)}, u32[]{:S(2)}) copy-start(bf16[1040,128]{1,0:T(8,128)(2,1)S(1)} %get-tuple-element.21.refs_0_) | copy-start | bytes 798724
  22.1 34.0 %copy-start.30 = (s32[84]{0:T(128)S(1)}, s32[84]{0:T(128)}, u32[]{:S(2)}) copy-start(s32[84]{0:T(128)} %constant.377.clone) | copy-start | bytes 1012
  22.1 34.0 %copy-start.45 = (s32[84]{0:T(128)S(1)}, s32[84]{0:T(128)}, u32[]{:S(2)}) copy-start(s32[84]{0:T(128)} %constant.375.clone) | copy-start | bytes 1012
  22.1 34.0 %copy-start.46 = (s32[84]{0:T(128)S(1)}, s32[84]{0:T(128)}, u32[]{:S(2)}) copy-start(s32[84]{0:T(128)} %constant.376.clone) | copy-start | bytes 1012
  22.1 34.0 %copy-start.20 = (s32[60]{0:T(128)S(1)}, s32[60]{0:T(128)}, u32[]{:S(2)}) copy-start(s32[60]{0:T(128)} %constant.379.clone) | copy-start | bytes 724
  22.1 34.0 %copy-start.28 = (s32[60]{0:T(128)S(1)}, s32[60]{0:T(128)}, u32[]{:S(2)}) copy-start(s32[60]{0:T(128)} %constant.382.clone) | copy-start | bytes 724
  22.1 34.6 %copy-start.43 = (s32[60]{0:T(128)S(1)}, s32[60]{0:T(128)}, u32[]{:S(2)}) copy-start(s32[60]{0:T(128)} %constant.380.clone) | copy-start | bytes 724
  22.2 34.6 %copy-start.44 = (s32[60]{0:T(128)S(1)}, s32[60]{0:T(128)}, u32[]{:S(2)}) copy-start(s32[60]{0:T(128)} %constant.381.clone) | copy-start | bytes 724
  22.2 17.2 %collective-permute-start.3 = (bf16[1040,128]{1,0:T(8,128)(2,1)S(1)}, bf16[1040,128]{1,0:T(8,128)(2,1)S(1)}, u32[]{:S(2)}, u32[]{:S(2)}) collective-permute-start(bf16[1040,128]{1,0:T(8,128)(2,1)S(1)} %get-tuple-element.20), channel_id=1, source_target_pairs={{0,4},{1,45},{2,6},{3,47},{4,8},{5,1},{6,10},{7,3},{8,12},{9,5},{1... | collective-permute-start | bytes 798728 | tf_op jit(solution)/shard_map/ppermute | solution.py:247
  31.0 13.7 %collective-permute-start.4 = (bf16[1040,128]{1,0:T(8,128)(2,1)S(1)}, bf16[1040,128]{1,0:T(8,128)(2,1)S(1)}, u32[]{:S(2)}, u32[]{:S(2)}) collective-permute-start(bf16[1040,128]{1,0:T(8,128)(2,1)S(1)} %get-tuple-element.21.refs_0_), channel_id=1, source_target_pairs={{0,28},{1,21},{2,30},{3,23},{4,32},{5,25},{6,34},{7,27},{8,36},{9,... | collective-permute-start | bytes 798728 | tf_op jit(solution)/shard_map/ppermute | solution.py:247
  32.9 13.4 %collective-permute-start.5 = (bf16[1040,128]{1,0:T(8,128)(2,1)S(1)}, bf16[1040,128]{1,0:T(8,128)(2,1)S(1)}, u32[]{:S(2)}, u32[]{:S(2)}) collective-permute-start(bf16[1040,128]{1,0:T(8,128)(2,1)S(1)} %get-tuple-element.22.refs_1_), channel_id=1, source_target_pairs={{0,2},{1,47},{2,4},{3,1},{4,6},{5,3},{6,8},{7,5},{8,10},{9,7},{10,... | collective-permute-start | bytes 798728 | tf_op jit(solution)/shard_map/ppermute | solution.py:247
  36.8 13.3 %collective-permute-start.6 = (bf16[1040,128]{1,0:T(8,128)(2,1)S(1)}, bf16[1040,128]{1,0:T(8,128)(2,1)S(1)}, u32[]{:S(2)}, u32[]{:S(2)}) collective-permute-start(bf16[1040,128]{1,0:T(8,128)(2,1)S(1)} %get-tuple-element.19.refs_0_), channel_id=1, source_target_pairs={{0,26},{1,23},{2,28},{3,25},{4,30},{5,27},{6,32},{7,29},{8,34},{9,... | collective-permute-start | bytes 798728 | tf_op jit(solution)/shard_map/ppermute | solution.py:247
  50.9 14.2 %collective-permute-start.7 = (bf16[3120,128]{1,0:T(8,128)(2,1)S(1)}, bf16[3120,128]{1,0:T(8,128)(2,1)S(1)}, u32[]{:S(2)}, u32[]{:S(2)}) collective-permute-start(bf16[3120,128]{1,0:T(8,128)(2,1)S(1)} %shard_map.147.refs_2_.refs_0_.refs_6_), channel_id=1, source_target_pairs={{0,2},{1,47},{2,4},{3,1},{4,6},{5,3},{6,8},{7,5},{8,10},{9,7},{10,... | collective-permute-start | bytes 2396168 | tf_op jit(solution)/shard_map/ppermute | solution.py:247
  58.2 48.0 %all-to-all-start = ((bf16[8,800,128]{2,1,0:T(8,128)(2,1)}), bf16[8,800,128]{2,1,0:T(8,128)(2,1)S(1)}, u32[]{:S(2)}, u32[]{:S(2)}) async-start(bf16[8,800,128]{2,1,0:T(8,128)(2,1)} %copy-done), calls=%async_computation | async-start | bytes 3276800 | tf_op jit(solution)/shard_map/all_to_all | solution.py:316
  66.1 21.3 %collective-permute-start.8 = (bf16[2096,128]{1,0:T(8,128)(2,1)S(1)}, bf16[2096,128]{1,0:T(8,128)(2,1)S(1)}, u32[]{:S(2)}, u32[]{:S(2)}) collective-permute-start(bf16[2096,128]{1,0:T(8,128)(2,1)S(1)} %shard_map.149.refs_9_), channel_id=1, source_target_pairs={{0,30},{1,19},{2,32},{3,21},{4,34},{5,23},{6,36},{7,25},{8,38},{9,... | collective-permute-start | bytes 1609736 | tf_op jit(solution)/shard_map/ppermute | solution.py:247
  68.9 9.0 %collective-permute-start.9 = (bf16[528,128]{1,0:T(8,128)(2,1)S(1)}, bf16[528,128]{1,0:T(8,128)(2,1)S(1)}, u32[]{:S(2)}, u32[]{:S(2)}) collective-permute-start(bf16[528,128]{1,0:T(8,128)(2,1)S(1)} %copy-done.19), channel_id=1, source_target_pairs={{0,24},{1,25},{2,26},{3,27},{4,28},{5,29},{6,30},{7,31},{8,32},{9,... | collective-permute-start | bytes 405512 | tf_op jit(solution)/shard_map/ppermute | solution.py:247
  80.4 20.0 %collective-permute-start.12 = (bf16[5040,128]{1,0:T(8,128)(2,1)}, bf16[5040,128]{1,0:T(8,128)(2,1)}, u32[]{:S(2)}, u32[]{:S(2)}) collective-permute-start(bf16[5040,128]{1,0:T(8,128)(2,1)} %get-tuple-element.27), channel_id=1, source_target_pairs={{0,1},{1,0},{2,3},{3,2},{4,5},{5,4},{6,7},{7,6},{8,9},{9,8},{10,11... | collective-permute-start | bytes 3870728 | tf_op jit(solution)/shard_map/ppermute | solution.py:251
  88.6 10.3 %collective-permute-start.10 = (bf16[48,128]{1,0:T(8,128)(2,1)S(1)}, bf16[48,128]{1,0:T(8,128)(2,1)S(1)}, u32[]{:S(2)}, u32[]{:S(2)}) collective-permute-start(bf16[48,128]{1,0:T(8,128)(2,1)S(1)} %get-tuple-element.25), channel_id=1, source_target_pairs={{0,1},{1,0},{2,3},{3,2},{4,5},{5,4},{6,7},{7,6},{8,9},{9,8},{10,11... | collective-permute-start | bytes 36872 | tf_op jit(solution)/shard_map/ppermute | solution.py:251
  94.5 21.4 %collective-permute-start.11 = (bf16[3072,128]{1,0:T(8,128)(2,1)}, bf16[3072,128]{1,0:T(8,128)(2,1)}, u32[]{:S(2)}, u32[]{:S(2)}) collective-permute-start(bf16[3072,128]{1,0:T(8,128)(2,1)} %get-tuple-element.26), channel_id=1, source_target_pairs={{0,2},{1,47},{2,4},{3,1},{4,6},{5,3},{6,8},{7,5},{8,10},{9,7},{10,... | collective-permute-start | bytes 2359304 | tf_op jit(solution)/shard_map/ppermute | solution.py:247
  113.0 9.0 %collective-permute-start.14 = (bf16[2048,128]{1,0:T(8,128)(2,1)S(1)}, bf16[2048,128]{1,0:T(8,128)(2,1)}, u32[]{:S(2)}, u32[]{:S(2)}) collective-permute-start(bf16[2048,128]{1,0:T(8,128)(2,1)S(1)} %shard_map.154), channel_id=1, source_target_pairs={{0,1},{1,0},{2,3},{3,2},{4,5},{5,4},{6,7},{7,6},{8,9},{9,8},{10,11... | collective-permute-start | bytes 1572872 | tf_op jit(solution)/shard_map/ppermute | solution.py:251
  117.8 6.5 %collective-permute-start.13 = (bf16[1536,128]{1,0:T(8,128)(2,1)}, bf16[1536,128]{1,0:T(8,128)(2,1)}, u32[]{:S(2)}, u32[]{:S(2)}) collective-permute-start(bf16[1536,128]{1,0:T(8,128)(2,1)} %shard_map.153), channel_id=1, source_target_pairs={{0,1},{1,0},{2,3},{3,2},{4,5},{5,4},{6,7},{7,6},{8,9},{9,8},{10,11... | collective-permute-start | bytes 1179656 | tf_op jit(solution)/shard_map/ppermute | solution.py:251
  (40 other events, 304.0 us)

commit v13 on v12

--- a/solution.py
+++ b/solution.py
@@ -310,10 +310,11 @@
         near.append((send(array, names, distance), 2 * len(names) * BLK, distance, True))
 
     names = items([(2, 1), (6, 13), (3, 2), (7, 14), (0, 14), (4, 2)])
-    (up_in,) = packed([(blocks(names), True)], near, (b_other,))
+    right_out = right_packed(b_kept, b_other, arrays[0])
+    (up_in,) = packed([(blocks(names), True)], near, (right_out,))
     sources.append(up_in)
     up3 = send(up_in, names, 1)
-    right = lax.all_to_all(right_packed(b_kept, b_other, up_in), "y", 0, 0, tiled=True)
+    right = lax.all_to_all(right_out, "y", 0, 0, tiled=True)
     right = right.reshape(16 * HALF, BLK)
     middle = [(up3 - 1, 24 * BLK, 0, False), (up3, 24 * BLK, 1, False)]
 
@@ -384,12 +385,12 @@
         rows += [(len(rows) * BLK + n * BLK, 0, name[2], name[1], w) for n, (_, w) in enumerate(wanted(name))]
     part = [(early_own[0], rows)] + received_of(early_other, early)
     sums, _ = product_of(table_of((part,), early_notes), part, 0)
-    parts = [part_of(middle + last) + received_of(None, middle), received_of(None, last)]
+    middle_other, _, _ = pass_on(middle, None, (), (early_other,))
+    parts = [part_of(middle) + received_of(middle_other, middle), part_of(last), received_of(None, last)]
     table = table_of(parts, notes)
-    middle_other, _, _ = pass_on(middle, None, (), (sums,))
+    sums, base = product_of(table, parts[0], 0, sums)
     last_other, _, _ = pass_on(last, None, (), (sums,))
-    parts[0] = part_of(middle + last) + received_of(middle_other, middle)
-    sums, base = product_of(table, parts[0], 0, sums)
+    sums, base = product_of(table, parts[1], base, sums)
     out, _ = product_of(table, received_of(last_other, last), base, sums, last=True)
     return out[None, None]
 

time: 128 us -> 124 us (0.969)
  waiting for transfers between devices: 20.3 us -> 16 us
  starting transfers between devices: 73.3 us -> 75 us
  other arithmetic: 6.69 us -> 5.13 us
    all_to_all x1, waiting for transfers between devices: 4.76 us -> 0.01 us  [local(): right = lax.all_to_all(right_out, 'y', 0, 0, tiled=True)]
    pallas_call x6, Pallas kernels: 4.32 us -> 2.51 us  [pack(): pl.pallas_call(functools.partial(pack_kernel, spec, notes, len(used)), ou...]
    ppermute x6, starting transfers between devices: 30.9 us -> 32.6 us  [from_other_core(): return lax.ppermute(array, 'core', [(0, 1), (1, 0)])]
    pallas_call x3 -> x4, Pallas kernels: 8.61 us -> 8.31 us  [product(): pl.pallas_call(functools.partial(product_kernel, counts, base, before is...]
    unnamed x96 -> x60, local copies, waits for them, and re-layouts: 8.54 us -> 8.33 us
  transfers between devices with their start and end apart: 16 -> 16, of which waited for: 6 -> 6; matrix products, arithmetic and copies ran while one was open for 7% -> 6% of each run, Pallas kernels for 10% -> 10%
where the time goes in v13:
time: 124 us; the launch traced here: 122 us
  starting transfers between devices  75 us (60%)
  waiting for transfers between devices  16 us (13%)
  Pallas kernels  13.4 us (11%)
  local copies, waits for them, and re-layouts  11.4 us (9%)
  other arithmetic  5.13 us (4%)
    ppermute x8, starting transfers between devices, moved(): return lax.ppermute(array, COL, route)  33.5 us
    ppermute x6, starting transfers between devices, from_other_core(): return lax.ppermute(array, 'core', [(0, 1), (1, 0)])  32.6 us
    ppermute x8, waiting for transfers between devices, moved(): return lax.ppermute(array, COL, route)  15.5 us
    unnamed x60, local copies, waits for them, and re-layouts  8.33 us
    pallas_call x4, Pallas kernels, product(): pl.pallas_call(functools.partial(product_kernel, counts, base, before is...  8.31 us
    all_to_all x1, starting transfers between devices, local(): right = lax.all_to_all(right_out, 'y', 0, 0, tiled=True)  6.88 us
    pallas_call x6, Pallas kernels, pack(): pl.pallas_call(functools.partial(pack_kernel, spec, notes, len(used)), ou...  2.51 us
  transfers between devices with their start and end apart: 16, of which 6 were waited for; matrix products, arithmetic and copies ran while one was open for 6% of the time, Pallas kernels for 10%

profile of v13, /device:TPU:1, one launch (start us, length us, event | category | flops | bytes accessed | tf_op | source)
XLA Modules:
  0.0 121.5 jit_solution(2499489684572957198)
XLA Ops:
  0.8 12.4 %collective-permute-start.2 = (bf16[16,128]{1,0:T(8,128)(2,1)S(1)}, bf16[16,128]{1,0:T(8,128)(2,1)S(1)}, u32[]{:S(2)}, u32[]{:S(2)}) collective-permute-start(bf16[16,128]{1,0:T(8,128)(2,1)S(1)} %fusion.37), channel_id=1, source_target_pairs={{0,1},{1,0},{2,3},{3,2},{4,5},{5,4},{6,7},{7,6},{8,9},{9,8},{10,11... | collective-permute-start | bytes 12296 | tf_op jit(solution)/shard_map/ppermute | solution.py:251
  13.2 1.9 %collective-permute-start.1 = (bf16[16,128,128]{2,1,0:T(8,128)(2,1)}, bf16[16,128,128]{2,1,0:T(8,128)(2,1)S(1)}, u32[]{:S(2)}, u32[]{:S(2)}) collective-permute-start(bf16[16,128,128]{2,1,0:T(8,128)(2,1)} %bitcast.77), channel_id=1, source_target_pairs={{0,1},{1,0},{2,3},{3,2},{4,5},{5,4},{6,7},{7,6},{8,9},{9,8},{10,11... | collective-permute-start | bytes 1572872 | tf_op jit(solution)/shard_map/ppermute | solution.py:251
  17.6 1.9 %collective-permute-start = (bf16[1296,128]{1,0:T(8,128)(2,1)S(1)}, bf16[1296,128]{1,0:T(8,128)(2,1)S(1)}, u32[]{:S(2)}, u32[]{:S(2)}) collective-permute-start(bf16[1296,128]{1,0:T(8,128)(2,1)S(1)} %get-tuple-element.18), channel_id=1, source_target_pairs={{0,384},{384,0},{1,385},{385,1},{2,386},{386,2},{3,387},{387,3},{4... | collective-permute-start | bytes 995336 | tf_op jit(solution)/shard_map/ppermute | solution.py:269
  22.1 8.6 %collective-permute-start.3 = (bf16[1040,128]{1,0:T(8,128)(2,1)S(1)}, bf16[1040,128]{1,0:T(8,128)(2,1)S(1)}, u32[]{:S(2)}, u32[]{:S(2)}) collective-permute-start(bf16[1040,128]{1,0:T(8,128)(2,1)S(1)} %get-tuple-element.19.refs_2_), channel_id=1, source_target_pairs={{0,4},{1,45},{2,6},{3,47},{4,8},{5,1},{6,10},{7,3},{8,12},{9,5},{1... | collective-permute-start | bytes 798728 | tf_op jit(solution)/shard_map/ppermute | solution.py:247
  30.7 1.9 %collective-permute-start.4 = (bf16[1040,128]{1,0:T(8,128)(2,1)S(1)}, bf16[1040,128]{1,0:T(8,128)(2,1)S(1)}, u32[]{:S(2)}, u32[]{:S(2)}) collective-permute-start(bf16[1040,128]{1,0:T(8,128)(2,1)S(1)} %get-tuple-element.21.refs_0_), channel_id=1, source_target_pairs={{0,28},{1,21},{2,30},{3,23},{4,32},{5,25},{6,34},{7,27},{8,36},{9,... | collective-permute-start | bytes 798728 | tf_op jit(solution)/shard_map/ppermute | solution.py:247
  32.7 3.9 %collective-permute-start.5 = (bf16[1040,128]{1,0:T(8,128)(2,1)S(1)}, bf16[1040,128]{1,0:T(8,128)(2,1)S(1)}, u32[]{:S(2)}, u32[]{:S(2)}) collective-permute-start(bf16[1040,128]{1,0:T(8,128)(2,1)S(1)} %get-tuple-element.22.refs_1_), channel_id=1, source_target_pairs={{0,2},{1,47},{2,4},{3,1},{4,6},{5,3},{6,8},{7,5},{8,10},{9,7},{10,... | collective-permute-start | bytes 798728 | tf_op jit(solution)/shard_map/ppermute | solution.py:247
  36.6 1.9 %collective-permute-start.6 = (bf16[1040,128]{1,0:T(8,128)(2,1)S(1)}, bf16[1040,128]{1,0:T(8,128)(2,1)S(1)}, u32[]{:S(2)}, u32[]{:S(2)}) collective-permute-start(bf16[1040,128]{1,0:T(8,128)(2,1)S(1)} %get-tuple-element.20.refs_0_), channel_id=1, source_target_pairs={{0,26},{1,23},{2,28},{3,25},{4,30},{5,27},{6,32},{7,29},{8,34},{9,... | collective-permute-start | bytes 798728 | tf_op jit(solution)/shard_map/ppermute | solution.py:247
  38.5 1.4 %shard_map.147.refs_5_ = bf16[8,800,128]{2,1,0:T(8,128)(2,1)} custom-call(bf16[1296,128]{1,0:T(8,128)(2,1)S(1)} %get-tuple-element.17.refs_0_, bf16[1296,128]{1,0:T(8,128)(2,1)S(1)} %collective-permute-done.refs_1_, bf16[1040,128]{1,0:T(8,128)(2,1)S(1)} %get-tuple-element.19.refs_2_), custom_call_target="tpu_custom_call" | custom-call | bytes 3145728 | tf_op jit(solution)/shard_map/pallas_call | solution.py:106
  40.0 4.4 %collective-permute-done.4.refs_2_.refs_3_ = bf16[1040,128]{1,0:T(8,128)(2,1)S(1)} collective-permute-done((bf16[1040,128]{1,0:T(8,128)(2,1)S(1)}, bf16[1040,128]{1,0:T(8,128)(2,1)S(1)}, u32[]{:S(2)}, u32[]{:S(2)}) %collective-permute-start.4) | collective-permute-done | bytes 266272 | tf_op jit(solution)/shard_map/ppermute | solution.py:247
  44.4 1.7 %collective-permute-done.5.refs_3_.refs_0_.refs_4_ = bf16[1040,128]{1,0:T(8,128)(2,1)S(1)} collective-permute-done((bf16[1040,128]{1,0:T(8,128)(2,1)S(1)}, bf16[1040,128]{1,0:T(8,128)(2,1)S(1)}, u32[]{:S(2)}, u32[]{:S(2)}) %collective-permute-start.5) | collective-permute-done | bytes 266272 | tf_op jit(solution)/shard_map/ppermute | solution.py:247
  46.1 3.7 %collective-permute-done.6.refs_4_.refs_1_.refs_5_ = bf16[1040,128]{1,0:T(8,128)(2,1)S(1)} collective-permute-done((bf16[1040,128]{1,0:T(8,128)(2,1)S(1)}, bf16[1040,128]{1,0:T(8,128)(2,1)S(1)}, u32[]{:S(2)}, u32[]{:S(2)}) %collective-permute-start.6) | collective-permute-done | bytes 266272 | tf_op jit(solution)/shard_map/ppermute | solution.py:247
  52.1 5.2 %collective-permute-start.7 = (bf16[3120,128]{1,0:T(8,128)(2,1)S(1)}, bf16[3120,128]{1,0:T(8,128)(2,1)S(1)}, u32[]{:S(2)}, u32[]{:S(2)}) collective-permute-start(bf16[3120,128]{1,0:T(8,128)(2,1)S(1)} %shard_map.148.refs_2_.refs_0_.refs_6_), channel_id=1, source_target_pairs={{0,2},{1,47},{2,4},{3,1},{4,6},{5,3},{6,8},{7,5},{8,10},{9,7},{10,... | collective-permute-start | bytes 2396168 | tf_op jit(solution)/shard_map/ppermute | solution.py:247
  57.4 6.9 %all-to-all-start = ((bf16[8,800,128]{2,1,0:T(8,128)(2,1)}), bf16[8,800,128]{2,1,0:T(8,128)(2,1)S(1)}, u32[]{:S(2)}, u32[]{:S(2)}) async-start(bf16[8,800,128]{2,1,0:T(8,128)(2,1)} %shard_map.147.refs_5_), calls=%async_computation | async-start | bytes 3276800 | tf_op jit(solution)/shard_map/all_to_all | solution.py:317
  64.3 2.0 %collective-permute-done.7.refs_3_.refs_1_.refs_7_ = bf16[3120,128]{1,0:T(8,128)(2,1)S(1)} collective-permute-done((bf16[3120,128]{1,0:T(8,128)(2,1)S(1)}, bf16[3120,128]{1,0:T(8,128)(2,1)S(1)}, u32[]{:S(2)}, u32[]{:S(2)}) %collective-permute-start.7) | collective-permute-done | bytes 798752 | tf_op jit(solution)/shard_map/ppermute | solution.py:247
  67.4 2.8 %collective-permute-start.8 = (bf16[2096,128]{1,0:T(8,128)(2,1)S(1)}, bf16[2096,128]{1,0:T(8,128)(2,1)S(1)}, u32[]{:S(2)}, u32[]{:S(2)}) collective-permute-start(bf16[2096,128]{1,0:T(8,128)(2,1)S(1)} %shard_map.149.refs_9_), channel_id=1, source_target_pairs={{0,30},{1,19},{2,32},{3,21},{4,34},{5,23},{6,36},{7,25},{8,38},{9,... | collective-permute-start | bytes 1609736 | tf_op jit(solution)/shard_map/ppermute | solution.py:247
  70.1 4.8 %collective-permute-start.9 = (bf16[528,128]{1,0:T(8,128)(2,1)S(1)}, bf16[528,128]{1,0:T(8,128)(2,1)S(1)}, u32[]{:S(2)}, u32[]{:S(2)}) collective-permute-start(bf16[528,128]{1,0:T(8,128)(2,1)S(1)} %copy-done.19), channel_id=1, source_target_pairs={{0,24},{1,25},{2,26},{3,27},{4,28},{5,29},{6,30},{7,31},{8,32},{9,... | collective-permute-start | bytes 405512 | tf_op jit(solution)/shard_map/ppermute | solution.py:247
  75.5 3.6 %collective-permute-done.9.refs_3_.refs_8_ = bf16[528,128]{1,0:T(8,128)(2,1)S(1)} collective-permute-done((bf16[528,128]{1,0:T(8,128)(2,1)S(1)}, bf16[528,128]{1,0:T(8,128)(2,1)S(1)}, u32[]{:S(2)}, u32[]{:S(2)}) %collective-permute-start.9) | collective-permute-done | bytes 135200 | tf_op jit(solution)/shard_map/ppermute | solution.py:247
  80.5 7.0 %collective-permute-start.12 = (bf16[5040,128]{1,0:T(8,128)(2,1)}, bf16[5040,128]{1,0:T(8,128)(2,1)}, u32[]{:S(2)}, u32[]{:S(2)}) collective-permute-start(bf16[5040,128]{1,0:T(8,128)(2,1)} %get-tuple-element.27), channel_id=1, source_target_pairs={{0,1},{1,0},{2,3},{3,2},{4,5},{5,4},{6,7},{7,6},{8,9},{9,8},{10,11... | collective-permute-start | bytes 3870728 | tf_op jit(solution)/shard_map/ppermute | solution.py:251
  88.6 6.4 %collective-permute-start.10 = (bf16[48,128]{1,0:T(8,128)(2,1)S(1)}, bf16[48,128]{1,0:T(8,128)(2,1)S(1)}, u32[]{:S(2)}, u32[]{:S(2)}) collective-permute-start(bf16[48,128]{1,0:T(8,128)(2,1)S(1)} %get-tuple-element.25), channel_id=1, source_target_pairs={{0,1},{1,0},{2,3},{3,2},{4,5},{5,4},{6,7},{7,6},{8,9},{9,8},{10,11... | collective-permute-start | bytes 36872 | tf_op jit(solution)/shard_map/ppermute | solution.py:251
  95.7 4.4 %collective-permute-start.11 = (bf16[3072,128]{1,0:T(8,128)(2,1)}, bf16[3072,128]{1,0:T(8,128)(2,1)S(1)}, u32[]{:S(2)}, u32[]{:S(2)}) collective-permute-start(bf16[3072,128]{1,0:T(8,128)(2,1)} %get-tuple-element.26), channel_id=1, source_target_pairs={{0,2},{1,47},{2,4},{3,1},{4,6},{5,3},{6,8},{7,5},{8,10},{9,7},{10,... | collective-permute-start | bytes 2359304 | tf_op jit(solution)/shard_map/ppermute | solution.py:247
  103.1 2.9 %collective-permute-start.13 = (bf16[2048,128]{1,0:T(8,128)(2,1)S(1)}, bf16[2048,128]{1,0:T(8,128)(2,1)S(1)}, u32[]{:S(2)}, u32[]{:S(2)}) collective-permute-start(bf16[2048,128]{1,0:T(8,128)(2,1)S(1)} %shard_map.152), channel_id=1, source_target_pairs={{0,1},{1,0},{2,3},{3,2},{4,5},{5,4},{6,7},{7,6},{8,9},{9,8},{10,11... | collective-permute-start | bytes 1572872 | tf_op jit(solution)/shard_map/ppermute | solution.py:251
  110.8 4.0 %shard_map.153.rest_2_ = f32[13,128,128]{2,1,0:T(8,128)S(1)} custom-call(s32[5,84]{1,0:T(8,128)S(1)} %stack.59.table_ref, bf16[6400,128]{1,0:T(8,128)(2,1)S(1)} %bitcast.72, bf16[5760,128]{1,0:T(8,128)(2,1)S(1)} %copy-done.17, bf16[5040,128]{1,0:T(8,128)(2,1)} %collective-permute-done.12.refs_1_.rest_1_), custom_call_target="tpu_custom_call" | custom-call | flops 2818572288 | bytes 2752512 | tf_op jit(solution)/shard_map/pallas_call | solution.py:192
  116.1 1.9 %collective-permute-start.14 = (bf16[1536,128]{1,0:T(8,128)(2,1)S(1)}, bf16[1536,128]{1,0:T(8,128)(2,1)S(1)}, u32[]{:S(2)}, u32[]{:S(2)}) collective-permute-start(bf16[1536,128]{1,0:T(8,128)(2,1)S(1)} %shard_map.155), channel_id=1, source_target_pairs={{0,1},{1,0},{2,3},{3,2},{4,5},{5,4},{6,7},{7,6},{8,9},{9,8},{10,11... | collective-permute-start | bytes 1179656 | tf_op jit(solution)/shard_map/ppermute | solution.py:251
  119.7 1.8 %shard_map.157 = bf16[12,128,128]{2,1,0:T(8,128)(2,1)} custom-call(s32[5,60]{1,0:T(8,128)S(1)} %stack.52.table_ref, bf16[6400,128]{1,0:T(8,128)(2,1)S(1)} %bitcast.75, bf16[1536,128]{1,0:T(8,128)(2,1)S(1)} %collective-permute-done.14.rest_0_, f32[13,128,128]{2,1,0:T(8,128)S(1)} %shard_map.156.rest_1_), custom_call_target="tpu_custom_call" | custom-call | flops 402653184 | bytes 393216 | tf_op jit(solution)/shard_map/pallas_call | solution.py:192
  (143 shorter events, 23.2 us)
Async XLA Ops:
  0.8 18.9 %collective-permute-start.2 = (bf16[16,128]{1,0:T(8,128)(2,1)S(1)}, bf16[16,128]{1,0:T(8,128)(2,1)S(1)}, u32[]{:S(2)}, u32[]{:S(2)}) collective-permute-start(bf16[16,128]{1,0:T(8,128)(2,1)S(1)} %fusion.37), channel_id=1, source_target_pairs={{0,1},{1,0},{2,3},{3,2},{4,5},{5,4},{6,7},{7,6},{8,9},{9,8},{10,11... | collective-permute-start | bytes 12296 | tf_op jit(solution)/shard_map/ppermute | solution.py:251
  13.2 6.6 %collective-permute-start.1 = (bf16[16,128,128]{2,1,0:T(8,128)(2,1)}, bf16[16,128,128]{2,1,0:T(8,128)(2,1)S(1)}, u32[]{:S(2)}, u32[]{:S(2)}) collective-permute-start(bf16[16,128,128]{2,1,0:T(8,128)(2,1)} %bitcast.77), channel_id=1, source_target_pairs={{0,1},{1,0},{2,3},{3,2},{4,5},{5,4},{6,7},{7,6},{8,9},{9,8},{10,11... | collective-permute-start | bytes 1572872 | tf_op jit(solution)/shard_map/ppermute | solution.py:251
  17.6 20.9 %collective-permute-start = (bf16[1296,128]{1,0:T(8,128)(2,1)S(1)}, bf16[1296,128]{1,0:T(8,128)(2,1)S(1)}, u32[]{:S(2)}, u32[]{:S(2)}) collective-permute-start(bf16[1296,128]{1,0:T(8,128)(2,1)S(1)} %get-tuple-element.18), channel_id=1, source_target_pairs={{0,384},{384,0},{1,385},{385,1},{2,386},{386,2},{3,387},{387,3},{4... | collective-permute-start | bytes 995336 | tf_op jit(solution)/shard_map/ppermute | solution.py:269
  22.1 24.0 %copy-start.12 = (bf16[1040,128]{1,0:T(8,128)(2,1)}, bf16[1040,128]{1,0:T(8,128)(2,1)S(1)}, u32[]{:S(2)}) copy-start(bf16[1040,128]{1,0:T(8,128)(2,1)S(1)} %get-tuple-element.21.refs_0_) | copy-start | bytes 798724
  22.1 24.0 %copy-start.14 = (bf16[1040,128]{1,0:T(8,128)(2,1)}, bf16[1040,128]{1,0:T(8,128)(2,1)S(1)}, u32[]{:S(2)}) copy-start(bf16[1040,128]{1,0:T(8,128)(2,1)S(1)} %get-tuple-element.22.refs_1_) | copy-start | bytes 798724
  22.1 17.9 %collective-permute-start.3 = (bf16[1040,128]{1,0:T(8,128)(2,1)S(1)}, bf16[1040,128]{1,0:T(8,128)(2,1)S(1)}, u32[]{:S(2)}, u32[]{:S(2)}) collective-permute-start(bf16[1040,128]{1,0:T(8,128)(2,1)S(1)} %get-tuple-element.19.refs_2_), channel_id=1, source_target_pairs={{0,4},{1,45},{2,6},{3,47},{4,8},{5,1},{6,10},{7,3},{8,12},{9,5},{1... | collective-permute-start | bytes 798728 | tf_op jit(solution)/shard_map/ppermute | solution.py:247
  30.7 13.7 %collective-permute-start.4 = (bf16[1040,128]{1,0:T(8,128)(2,1)S(1)}, bf16[1040,128]{1,0:T(8,128)(2,1)S(1)}, u32[]{:S(2)}, u32[]{:S(2)}) collective-permute-start(bf16[1040,128]{1,0:T(8,128)(2,1)S(1)} %get-tuple-element.21.refs_0_), channel_id=1, source_target_pairs={{0,28},{1,21},{2,30},{3,23},{4,32},{5,25},{6,34},{7,27},{8,36},{9,... | collective-permute-start | bytes 798728 | tf_op jit(solution)/shard_map/ppermute | solution.py:247
  32.7 13.4 %collective-permute-start.5 = (bf16[1040,128]{1,0:T(8,128)(2,1)S(1)}, bf16[1040,128]{1,0:T(8,128)(2,1)S(1)}, u32[]{:S(2)}, u32[]{:S(2)}) collective-permute-start(bf16[1040,128]{1,0:T(8,128)(2,1)S(1)} %get-tuple-element.22.refs_1_), channel_id=1, source_target_pairs={{0,2},{1,47},{2,4},{3,1},{4,6},{5,3},{6,8},{7,5},{8,10},{9,7},{10,... | collective-permute-start | bytes 798728 | tf_op jit(solution)/shard_map/ppermute | solution.py:247
  36.6 13.3 %collective-permute-start.6 = (bf16[1040,128]{1,0:T(8,128)(2,1)S(1)}, bf16[1040,128]{1,0:T(8,128)(2,1)S(1)}, u32[]{:S(2)}, u32[]{:S(2)}) collective-permute-start(bf16[1040,128]{1,0:T(8,128)(2,1)S(1)} %get-tuple-element.20.refs_0_), channel_id=1, source_target_pairs={{0,26},{1,23},{2,28},{3,25},{4,30},{5,27},{6,32},{7,29},{8,34},{9,... | collective-permute-start | bytes 798728 | tf_op jit(solution)/shard_map/ppermute | solution.py:247
  39.9 17.4 %copy-start.28 = (s32[84]{0:T(128)S(1)}, s32[84]{0:T(128)}, u32[]{:S(2)}) copy-start(s32[84]{0:T(128)} %constant.376.clone) | copy-start | bytes 1012
  39.9 17.4 %copy-start.20 = (s32[60]{0:T(128)S(1)}, s32[60]{0:T(128)}, u32[]{:S(2)}) copy-start(s32[60]{0:T(128)} %constant.379.clone) | copy-start | bytes 724
  39.9 17.4 %copy-start.22 = (s32[60]{0:T(128)S(1)}, s32[60]{0:T(128)}, u32[]{:S(2)}) copy-start(s32[60]{0:T(128)} %constant.382.clone) | copy-start | bytes 724
  39.9 17.4 %copy-start.25 = (s32[60]{0:T(128)S(1)}, s32[60]{0:T(128)}, u32[]{:S(2)}) copy-start(s32[60]{0:T(128)} %constant.380.clone) | copy-start | bytes 724
  40.0 17.4 %copy-start.26 = (s32[60]{0:T(128)S(1)}, s32[60]{0:T(128)}, u32[]{:S(2)}) copy-start(s32[60]{0:T(128)} %constant.381.clone) | copy-start | bytes 724
  52.1 14.3 %collective-permute-start.7 = (bf16[3120,128]{1,0:T(8,128)(2,1)S(1)}, bf16[3120,128]{1,0:T(8,128)(2,1)S(1)}, u32[]{:S(2)}, u32[]{:S(2)}) collective-permute-start(bf16[3120,128]{1,0:T(8,128)(2,1)S(1)} %shard_map.148.refs_2_.refs_0_.refs_6_), channel_id=1, source_target_pairs={{0,2},{1,47},{2,4},{3,1},{4,6},{5,3},{6,8},{7,5},{8,10},{9,7},{10,... | collective-permute-start | bytes 2396168 | tf_op jit(solution)/shard_map/ppermute | solution.py:247
  57.4 48.9 %all-to-all-start = ((bf16[8,800,128]{2,1,0:T(8,128)(2,1)}), bf16[8,800,128]{2,1,0:T(8,128)(2,1)S(1)}, u32[]{:S(2)}, u32[]{:S(2)}) async-start(bf16[8,800,128]{2,1,0:T(8,128)(2,1)} %shard_map.147.refs_5_), calls=%async_computation | async-start | bytes 3276800 | tf_op jit(solution)/shard_map/all_to_all | solution.py:317
  67.4 20.2 %collective-permute-start.8 = (bf16[2096,128]{1,0:T(8,128)(2,1)S(1)}, bf16[2096,128]{1,0:T(8,128)(2,1)S(1)}, u32[]{:S(2)}, u32[]{:S(2)}) collective-permute-start(bf16[2096,128]{1,0:T(8,128)(2,1)S(1)} %shard_map.149.refs_9_), channel_id=1, source_target_pairs={{0,30},{1,19},{2,32},{3,21},{4,34},{5,23},{6,36},{7,25},{8,38},{9,... | collective-permute-start | bytes 1609736 | tf_op jit(solution)/shard_map/ppermute | solution.py:247
  70.1 9.0 %collective-permute-start.9 = (bf16[528,128]{1,0:T(8,128)(2,1)S(1)}, bf16[528,128]{1,0:T(8,128)(2,1)S(1)}, u32[]{:S(2)}, u32[]{:S(2)}) collective-permute-start(bf16[528,128]{1,0:T(8,128)(2,1)S(1)} %copy-done.19), channel_id=1, source_target_pairs={{0,24},{1,25},{2,26},{3,27},{4,28},{5,29},{6,30},{7,31},{8,32},{9,... | collective-permute-start | bytes 405512 | tf_op jit(solution)/shard_map/ppermute | solution.py:247
  80.5 19.7 %copy-start.16 = (bf16[5760,128]{1,0:T(8,128)(2,1)}, bf16[5760,128]{1,0:T(8,128)(2,1)S(1)}, u32[]{:S(2)}) copy-start(bf16[5760,128]{1,0:T(8,128)(2,1)S(1)} %get-tuple-element.28.rest_0_) | copy-start | bytes 4423684
  80.5 20.7 %collective-permute-start.12 = (bf16[5040,128]{1,0:T(8,128)(2,1)}, bf16[5040,128]{1,0:T(8,128)(2,1)}, u32[]{:S(2)}, u32[]{:S(2)}) collective-permute-start(bf16[5040,128]{1,0:T(8,128)(2,1)} %get-tuple-element.27), channel_id=1, source_target_pairs={{0,1},{1,0},{2,3},{3,2},{4,5},{5,4},{6,7},{7,6},{8,9},{9,8},{10,11... | collective-permute-start | bytes 3870728 | tf_op jit(solution)/shard_map/ppermute | solution.py:251
  88.6 11.5 %collective-permute-start.10 = (bf16[48,128]{1,0:T(8,128)(2,1)S(1)}, bf16[48,128]{1,0:T(8,128)(2,1)S(1)}, u32[]{:S(2)}, u32[]{:S(2)}) collective-permute-start(bf16[48,128]{1,0:T(8,128)(2,1)S(1)} %get-tuple-element.25), channel_id=1, source_target_pairs={{0,1},{1,0},{2,3},{3,2},{4,5},{5,4},{6,7},{7,6},{8,9},{9,8},{10,11... | collective-permute-start | bytes 36872 | tf_op jit(solution)/shard_map/ppermute | solution.py:251
  95.7 20.4 %collective-permute-start.11 = (bf16[3072,128]{1,0:T(8,128)(2,1)}, bf16[3072,128]{1,0:T(8,128)(2,1)S(1)}, u32[]{:S(2)}, u32[]{:S(2)}) collective-permute-start(bf16[3072,128]{1,0:T(8,128)(2,1)} %get-tuple-element.26), channel_id=1, source_target_pairs={{0,2},{1,47},{2,4},{3,1},{4,6},{5,3},{6,8},{7,5},{8,10},{9,7},{10,... | collective-permute-start | bytes 2359304 | tf_op jit(solution)/shard_map/ppermute | solution.py:247
  103.1 11.7 %collective-permute-start.13 = (bf16[2048,128]{1,0:T(8,128)(2,1)S(1)}, bf16[2048,128]{1,0:T(8,128)(2,1)S(1)}, u32[]{:S(2)}, u32[]{:S(2)}) collective-permute-start(bf16[2048,128]{1,0:T(8,128)(2,1)S(1)} %shard_map.152), channel_id=1, source_target_pairs={{0,1},{1,0},{2,3},{3,2},{4,5},{5,4},{6,7},{7,6},{8,9},{9,8},{10,11... | collective-permute-start | bytes 1572872 | tf_op jit(solution)/shard_map/ppermute | solution.py:251
  116.1 3.6 %collective-permute-start.14 = (bf16[1536,128]{1,0:T(8,128)(2,1)S(1)}, bf16[1536,128]{1,0:T(8,128)(2,1)S(1)}, u32[]{:S(2)}, u32[]{:S(2)}) collective-permute-start(bf16[1536,128]{1,0:T(8,128)(2,1)S(1)} %shard_map.155), channel_id=1, source_target_pairs={{0,1},{1,0},{2,3},{3,2},{4,5},{5,4},{6,7},{7,6},{8,9},{9,8},{10,11... | collective-permute-start | bytes 1179656 | tf_op jit(solution)/shard_map/ppermute | solution.py:251
  (22 other events, 141.5 us)

commit v14 on v13

--- a/solution.py
+++ b/solution.py
@@ -57,37 +57,60 @@
     return pl.ds(n * BLK, BLK)
 
 
-def first_kernel(orders, index_ref, own_ref, other_ref, note_ref, *outs):
+def first_kernel(orders, index_ref, own_ref, other_ref, note_ref, *rest):
+    outs, sems = rest[:-1], rest[-1]
+    copies = []
     for out, order in zip(outs, orders, strict=True):
         for n, (other, place) in enumerate(order):
-            out[blk(n), :] = (other_ref if other else own_ref)[index_ref[place]]
+            if not other:
+                source = own_ref.at[index_ref[place]]
+                copies.append(pltpu.make_async_copy(source, out.at[blk(n)], sems.at[len(copies)]))
+    for copy in copies:
+        copy.start()
+    for out, order in zip(outs, orders, strict=True):
+        for n, (other, place) in enumerate(order):
+            if other:
+                out[blk(n), :] = other_ref[index_ref[place]]
         out[pl.ds(len(order) * BLK, 16), :] = note_ref[...]
+    for copy in copies:
+        copy.wait()
 
 
 def first_packed(index, own, other, note, orders):
+    count = sum(not k for order in orders for k, _ in order)
     return pl.pallas_call(
         functools.partial(first_kernel, orders),
         out_shape=[rows_shape(len(order) * BLK + 16) for order in orders],
-        in_specs=[SMEM_SPEC] + [VMEM_SPEC] * 3,
+        in_specs=[SMEM_SPEC, ANY_SPEC, VMEM_SPEC, VMEM_SPEC],
         out_specs=[VMEM_SPEC for _ in orders],
+        scratch_shapes=[pltpu.SemaphoreType.DMA((count,))],
         compiler_params=LIMIT,
         cost_estimate=moves(sum(len(order) for order in orders)),
     )(index, own, other, note)
 
 
-def split_kernel(index_ref, src_ref, note_ref, *outs):
+def split_kernel(index_ref, src_ref, note_ref, *rest):
+    outs, sems = rest[:2], rest[2]
+    copies = []
     for half, out in enumerate(outs):
         for n in range(SPAN):
-            out[blk(n), :] = src_ref[index_ref[SPAN * half + n]]
+            source = src_ref.at[index_ref[SPAN * half + n]]
+            copies.append(pltpu.make_async_copy(source, out.at[blk(n)], sems.at[len(copies)]))
+    for copy in copies:
+        copy.start()
+    for out in outs:
         out[pl.ds(SPAN * BLK, 16), :] = note_ref[...]
+    for copy in copies:
+        copy.wait()
 
 
 def split(index, src, note):
     return pl.pallas_call(
         split_kernel,
         out_shape=[rows_shape(SPAN * BLK + 16)] * 2,
-        in_specs=[SMEM_SPEC, VMEM_SPEC, VMEM_SPEC],
+        in_specs=[SMEM_SPEC, ANY_SPEC, VMEM_SPEC],
         out_specs=[VMEM_SPEC] * 2,
+        scratch_shapes=[pltpu.SemaphoreType.DMA((2 * SPAN,))],
         compiler_params=LIMIT,
         cost_estimate=moves(2 * SPAN),
     )(index, src, note)

time: 124 us -> 126 us (1.016)
  Pallas kernels: 13.4 us -> 15.6 us
  transfers between devices with their start and end apart: 16 -> 16, of which waited for: 6 -> 6; matrix products, arithmetic and copies ran while one was open for 6% -> 6% of each run, Pallas kernels for 10% -> 11%
where the time goes in v14:
time: 126 us; the launch traced here: 124 us
  starting transfers between devices  75 us (60%)
  waiting for transfers between devices  16 us (13%)
  Pallas kernels  15.6 us (12%)
  local copies, waits for them, and re-layouts  11.4 us (9%)
  other arithmetic  5.13 us (4%)
    ppermute x8, starting transfers between devices, moved(): return lax.ppermute(array, COL, route)  33.5 us
    ppermute x6, starting transfers between devices, from_other_core(): return lax.ppermute(array, 'core', [(0, 1), (1, 0)])  32.6 us
    ppermute x8, waiting for transfers between devices, moved(): return lax.ppermute(array, COL, route)  15.5 us
    unnamed x60, local copies, waits for them, and re-layouts  8.33 us
    pallas_call x4, Pallas kernels, product(): pl.pallas_call(functools.partial(product_kernel, counts, base, before is...  8.3 us
    all_to_all x1, starting transfers between devices, local(): right = lax.all_to_all(right_out, 'y', 0, 0, tiled=True)  6.88 us
  transfers between devices with their start and end apart: 16, of which 6 were waited for; matrix products, arithmetic and copies ran while one was open for 6% of the time, Pallas kernels for 11%

profile of v14, /device:TPU:1, one launch (start us, length us, event | category | flops | bytes accessed | tf_op | source)
XLA Modules:
  0.0 123.7 jit_solution(11530967012409472635)
XLA Ops:
  0.8 12.4 %collective-permute-start.2 = (bf16[16,128]{1,0:T(8,128)(2,1)S(1)}, bf16[16,128]{1,0:T(8,128)(2,1)S(1)}, u32[]{:S(2)}, u32[]{:S(2)}) collective-permute-start(bf16[16,128]{1,0:T(8,128)(2,1)S(1)} %fusion.37), channel_id=1, source_target_pairs={{0,1},{1,0},{2,3},{3,2},{4,5},{5,4},{6,7},{7,6},{8,9},{9,8},{10,11... | collective-permute-start | bytes 12296 | tf_op jit(solution)/shard_map/ppermute | solution.py:274
  13.2 1.9 %collective-permute-start.1 = (bf16[16,128,128]{2,1,0:T(8,128)(2,1)}, bf16[16,128,128]{2,1,0:T(8,128)(2,1)S(1)}, u32[]{:S(2)}, u32[]{:S(2)}) collective-permute-start(bf16[16,128,128]{2,1,0:T(8,128)(2,1)} %bitcast.77), channel_id=1, source_target_pairs={{0,1},{1,0},{2,3},{3,2},{4,5},{5,4},{6,7},{7,6},{8,9},{9,8},{10,11... | collective-permute-start | bytes 1572872 | tf_op jit(solution)/shard_map/ppermute | solution.py:274
  18.7 1.9 %collective-permute-start = (bf16[1296,128]{1,0:T(8,128)(2,1)S(1)}, bf16[1296,128]{1,0:T(8,128)(2,1)S(1)}, u32[]{:S(2)}, u32[]{:S(2)}) collective-permute-start(bf16[1296,128]{1,0:T(8,128)(2,1)S(1)} %get-tuple-element.18), channel_id=1, source_target_pairs={{0,384},{384,0},{1,385},{385,1},{2,386},{386,2},{3,387},{387,3},{4... | collective-permute-start | bytes 995336 | tf_op jit(solution)/shard_map/ppermute | solution.py:292
  21.9 1.7 %shard_map.146 = (bf16[1040,128]{1,0:T(8,128)(2,1)S(1)}, bf16[1040,128]{1,0:T(8,128)(2,1)S(1)}, bf16[1040,128]{1,0:T(8,128)(2,1)S(1)}, bf16[1040,128]{1,0:T(8,128)(2,1)S(1)}, bf16[528,128]{1,0:T(8,128)(2,1)S(1)}) custom-call(s32[16]{0:T(128)S(1)} %and_select_fusion.16.index_ref, bf16[16,128,128]{2,1,0:T(8,128)(2,1)S(1)} %bitcast.78, ...), custom_call_target="tpu_custom_call" | custom-call | bytes 2359296 | tf_op jit(solution)/shard_map/pallas_call | solution.py:81
  24.3 8.6 %collective-permute-start.3 = (bf16[1040,128]{1,0:T(8,128)(2,1)S(1)}, bf16[1040,128]{1,0:T(8,128)(2,1)S(1)}, u32[]{:S(2)}, u32[]{:S(2)}) collective-permute-start(bf16[1040,128]{1,0:T(8,128)(2,1)S(1)} %get-tuple-element.19.refs_2_), channel_id=1, source_target_pairs={{0,4},{1,45},{2,6},{3,47},{4,8},{5,1},{6,10},{7,3},{8,12},{9,5},{1... | collective-permute-start | bytes 798728 | tf_op jit(solution)/shard_map/ppermute | solution.py:270
  32.9 1.9 %collective-permute-start.4 = (bf16[1040,128]{1,0:T(8,128)(2,1)S(1)}, bf16[1040,128]{1,0:T(8,128)(2,1)S(1)}, u32[]{:S(2)}, u32[]{:S(2)}) collective-permute-start(bf16[1040,128]{1,0:T(8,128)(2,1)S(1)} %get-tuple-element.21.refs_0_), channel_id=1, source_target_pairs={{0,28},{1,21},{2,30},{3,23},{4,32},{5,25},{6,34},{7,27},{8,36},{9,... | collective-permute-start | bytes 798728 | tf_op jit(solution)/shard_map/ppermute | solution.py:270
  34.8 3.9 %collective-permute-start.5 = (bf16[1040,128]{1,0:T(8,128)(2,1)S(1)}, bf16[1040,128]{1,0:T(8,128)(2,1)S(1)}, u32[]{:S(2)}, u32[]{:S(2)}) collective-permute-start(bf16[1040,128]{1,0:T(8,128)(2,1)S(1)} %get-tuple-element.22.refs_1_), channel_id=1, source_target_pairs={{0,2},{1,47},{2,4},{3,1},{4,6},{5,3},{6,8},{7,5},{8,10},{9,7},{10,... | collective-permute-start | bytes 798728 | tf_op jit(solution)/shard_map/ppermute | solution.py:270
  38.7 1.9 %collective-permute-start.6 = (bf16[1040,128]{1,0:T(8,128)(2,1)S(1)}, bf16[1040,128]{1,0:T(8,128)(2,1)S(1)}, u32[]{:S(2)}, u32[]{:S(2)}) collective-permute-start(bf16[1040,128]{1,0:T(8,128)(2,1)S(1)} %get-tuple-element.20.refs_0_), channel_id=1, source_target_pairs={{0,26},{1,23},{2,28},{3,25},{4,30},{5,27},{6,32},{7,29},{8,34},{9,... | collective-permute-start | bytes 798728 | tf_op jit(solution)/shard_map/ppermute | solution.py:270
  42.2 4.4 %collective-permute-done.4.refs_2_.refs_3_ = bf16[1040,128]{1,0:T(8,128)(2,1)S(1)} collective-permute-done((bf16[1040,128]{1,0:T(8,128)(2,1)S(1)}, bf16[1040,128]{1,0:T(8,128)(2,1)S(1)}, u32[]{:S(2)}, u32[]{:S(2)}) %collective-permute-start.4) | collective-permute-done | bytes 266272 | tf_op jit(solution)/shard_map/ppermute | solution.py:270
  46.6 1.7 %collective-permute-done.5.refs_3_.refs_0_.refs_4_ = bf16[1040,128]{1,0:T(8,128)(2,1)S(1)} collective-permute-done((bf16[1040,128]{1,0:T(8,128)(2,1)S(1)}, bf16[1040,128]{1,0:T(8,128)(2,1)S(1)}, u32[]{:S(2)}, u32[]{:S(2)}) %collective-permute-start.5) | collective-permute-done | bytes 266272 | tf_op jit(solution)/shard_map/ppermute | solution.py:270
  48.3 3.7 %collective-permute-done.6.refs_4_.refs_1_.refs_5_ = bf16[1040,128]{1,0:T(8,128)(2,1)S(1)} collective-permute-done((bf16[1040,128]{1,0:T(8,128)(2,1)S(1)}, bf16[1040,128]{1,0:T(8,128)(2,1)S(1)}, u32[]{:S(2)}, u32[]{:S(2)}) %collective-permute-start.6) | collective-permute-done | bytes 266272 | tf_op jit(solution)/shard_map/ppermute | solution.py:270
  54.2 5.2 %collective-permute-start.7 = (bf16[3120,128]{1,0:T(8,128)(2,1)S(1)}, bf16[3120,128]{1,0:T(8,128)(2,1)S(1)}, u32[]{:S(2)}, u32[]{:S(2)}) collective-permute-start(bf16[3120,128]{1,0:T(8,128)(2,1)S(1)} %shard_map.148.refs_2_.refs_0_.refs_6_), channel_id=1, source_target_pairs={{0,2},{1,47},{2,4},{3,1},{4,6},{5,3},{6,8},{7,5},{8,10},{9,7},{10,... | collective-permute-start | bytes 2396168 | tf_op jit(solution)/shard_map/ppermute | solution.py:270
  59.6 6.9 %all-to-all-start = ((bf16[8,800,128]{2,1,0:T(8,128)(2,1)}), bf16[8,800,128]{2,1,0:T(8,128)(2,1)S(1)}, u32[]{:S(2)}, u32[]{:S(2)}) async-start(bf16[8,800,128]{2,1,0:T(8,128)(2,1)} %shard_map.147.refs_5_), calls=%async_computation | async-start | bytes 3276800 | tf_op jit(solution)/shard_map/all_to_all | solution.py:340
  66.5 2.0 %collective-permute-done.7.refs_3_.refs_1_.refs_7_ = bf16[3120,128]{1,0:T(8,128)(2,1)S(1)} collective-permute-done((bf16[3120,128]{1,0:T(8,128)(2,1)S(1)}, bf16[3120,128]{1,0:T(8,128)(2,1)S(1)}, u32[]{:S(2)}, u32[]{:S(2)}) %collective-permute-start.7) | collective-permute-done | bytes 798752 | tf_op jit(solution)/shard_map/ppermute | solution.py:270
  69.5 2.8 %collective-permute-start.8 = (bf16[2096,128]{1,0:T(8,128)(2,1)S(1)}, bf16[2096,128]{1,0:T(8,128)(2,1)S(1)}, u32[]{:S(2)}, u32[]{:S(2)}) collective-permute-start(bf16[2096,128]{1,0:T(8,128)(2,1)S(1)} %shard_map.149.refs_9_), channel_id=1, source_target_pairs={{0,30},{1,19},{2,32},{3,21},{4,34},{5,23},{6,36},{7,25},{8,38},{9,... | collective-permute-start | bytes 1609736 | tf_op jit(solution)/shard_map/ppermute | solution.py:270
  72.3 4.8 %collective-permute-start.9 = (bf16[528,128]{1,0:T(8,128)(2,1)S(1)}, bf16[528,128]{1,0:T(8,128)(2,1)S(1)}, u32[]{:S(2)}, u32[]{:S(2)}) collective-permute-start(bf16[528,128]{1,0:T(8,128)(2,1)S(1)} %copy-done.19), channel_id=1, source_target_pairs={{0,24},{1,25},{2,26},{3,27},{4,28},{5,29},{6,30},{7,31},{8,32},{9,... | collective-permute-start | bytes 405512 | tf_op jit(solution)/shard_map/ppermute | solution.py:270
  77.7 3.6 %collective-permute-done.9.refs_3_.refs_8_ = bf16[528,128]{1,0:T(8,128)(2,1)S(1)} collective-permute-done((bf16[528,128]{1,0:T(8,128)(2,1)S(1)}, bf16[528,128]{1,0:T(8,128)(2,1)S(1)}, u32[]{:S(2)}, u32[]{:S(2)}) %collective-permute-start.9) | collective-permute-done | bytes 135200 | tf_op jit(solution)/shard_map/ppermute | solution.py:270
  82.6 7.0 %collective-permute-start.12 = (bf16[5040,128]{1,0:T(8,128)(2,1)}, bf16[5040,128]{1,0:T(8,128)(2,1)}, u32[]{:S(2)}, u32[]{:S(2)}) collective-permute-start(bf16[5040,128]{1,0:T(8,128)(2,1)} %get-tuple-element.27), channel_id=1, source_target_pairs={{0,1},{1,0},{2,3},{3,2},{4,5},{5,4},{6,7},{7,6},{8,9},{9,8},{10,11... | collective-permute-start | bytes 3870728 | tf_op jit(solution)/shard_map/ppermute | solution.py:274
  90.8 6.4 %collective-permute-start.10 = (bf16[48,128]{1,0:T(8,128)(2,1)S(1)}, bf16[48,128]{1,0:T(8,128)(2,1)S(1)}, u32[]{:S(2)}, u32[]{:S(2)}) collective-permute-start(bf16[48,128]{1,0:T(8,128)(2,1)S(1)} %get-tuple-element.25), channel_id=1, source_target_pairs={{0,1},{1,0},{2,3},{3,2},{4,5},{5,4},{6,7},{7,6},{8,9},{9,8},{10,11... | collective-permute-start | bytes 36872 | tf_op jit(solution)/shard_map/ppermute | solution.py:274
  97.9 4.4 %collective-permute-start.11 = (bf16[3072,128]{1,0:T(8,128)(2,1)}, bf16[3072,128]{1,0:T(8,128)(2,1)S(1)}, u32[]{:S(2)}, u32[]{:S(2)}) collective-permute-start(bf16[3072,128]{1,0:T(8,128)(2,1)} %get-tuple-element.26), channel_id=1, source_target_pairs={{0,2},{1,47},{2,4},{3,1},{4,6},{5,3},{6,8},{7,5},{8,10},{9,7},{10,... | collective-permute-start | bytes 2359304 | tf_op jit(solution)/shard_map/ppermute | solution.py:270
  105.3 2.9 %collective-permute-start.13 = (bf16[2048,128]{1,0:T(8,128)(2,1)S(1)}, bf16[2048,128]{1,0:T(8,128)(2,1)S(1)}, u32[]{:S(2)}, u32[]{:S(2)}) collective-permute-start(bf16[2048,128]{1,0:T(8,128)(2,1)S(1)} %shard_map.152), channel_id=1, source_target_pairs={{0,1},{1,0},{2,3},{3,2},{4,5},{5,4},{6,7},{7,6},{8,9},{9,8},{10,11... | collective-permute-start | bytes 1572872 | tf_op jit(solution)/shard_map/ppermute | solution.py:274
  113.0 4.0 %shard_map.153.rest_2_ = f32[13,128,128]{2,1,0:T(8,128)S(1)} custom-call(s32[5,84]{1,0:T(8,128)S(1)} %stack.59.table_ref, bf16[6400,128]{1,0:T(8,128)(2,1)S(1)} %bitcast.72, bf16[5760,128]{1,0:T(8,128)(2,1)S(1)} %copy-done.17, bf16[5040,128]{1,0:T(8,128)(2,1)} %collective-permute-done.12.refs_1_.rest_1_), custom_call_target="tpu_custom_call" | custom-call | flops 2818572288 | bytes 2752512 | tf_op jit(solution)/shard_map/pallas_call | solution.py:215
  118.3 1.9 %collective-permute-start.14 = (bf16[1536,128]{1,0:T(8,128)(2,1)S(1)}, bf16[1536,128]{1,0:T(8,128)(2,1)S(1)}, u32[]{:S(2)}, u32[]{:S(2)}) collective-permute-start(bf16[1536,128]{1,0:T(8,128)(2,1)S(1)} %shard_map.155), channel_id=1, source_target_pairs={{0,1},{1,0},{2,3},{3,2},{4,5},{5,4},{6,7},{7,6},{8,9},{9,8},{10,11... | collective-permute-start | bytes 1179656 | tf_op jit(solution)/shard_map/ppermute | solution.py:274
  121.9 1.8 %shard_map.157 = bf16[12,128,128]{2,1,0:T(8,128)(2,1)} custom-call(s32[5,60]{1,0:T(8,128)S(1)} %stack.52.table_ref, bf16[6400,128]{1,0:T(8,128)(2,1)S(1)} %bitcast.75, bf16[1536,128]{1,0:T(8,128)(2,1)S(1)} %collective-permute-done.14.rest_0_, f32[13,128,128]{2,1,0:T(8,128)S(1)} %shard_map.156.rest_1_), custom_call_target="tpu_custom_call" | custom-call | flops 402653184 | bytes 393216 | tf_op jit(solution)/shard_map/pallas_call | solution.py:215
  (143 shorter events, 25.0 us)
Async XLA Ops:
  0.8 20.0 %collective-permute-start.2 = (bf16[16,128]{1,0:T(8,128)(2,1)S(1)}, bf16[16,128]{1,0:T(8,128)(2,1)S(1)}, u32[]{:S(2)}, u32[]{:S(2)}) collective-permute-start(bf16[16,128]{1,0:T(8,128)(2,1)S(1)} %fusion.37), channel_id=1, source_target_pairs={{0,1},{1,0},{2,3},{3,2},{4,5},{5,4},{6,7},{7,6},{8,9},{9,8},{10,11... | collective-permute-start | bytes 12296 | tf_op jit(solution)/shard_map/ppermute | solution.py:274
  13.2 7.7 %collective-permute-start.1 = (bf16[16,128,128]{2,1,0:T(8,128)(2,1)}, bf16[16,128,128]{2,1,0:T(8,128)(2,1)S(1)}, u32[]{:S(2)}, u32[]{:S(2)}) collective-permute-start(bf16[16,128,128]{2,1,0:T(8,128)(2,1)} %bitcast.77), channel_id=1, source_target_pairs={{0,1},{1,0},{2,3},{3,2},{4,5},{5,4},{6,7},{7,6},{8,9},{9,8},{10,11... | collective-permute-start | bytes 1572872 | tf_op jit(solution)/shard_map/ppermute | solution.py:274
  18.7 22.0 %collective-permute-start = (bf16[1296,128]{1,0:T(8,128)(2,1)S(1)}, bf16[1296,128]{1,0:T(8,128)(2,1)S(1)}, u32[]{:S(2)}, u32[]{:S(2)}) collective-permute-start(bf16[1296,128]{1,0:T(8,128)(2,1)S(1)} %get-tuple-element.18), channel_id=1, source_target_pairs={{0,384},{384,0},{1,385},{385,1},{2,386},{386,2},{3,387},{387,3},{4... | collective-permute-start | bytes 995336 | tf_op jit(solution)/shard_map/ppermute | solution.py:292
  24.3 24.0 %copy-start.12 = (bf16[1040,128]{1,0:T(8,128)(2,1)}, bf16[1040,128]{1,0:T(8,128)(2,1)S(1)}, u32[]{:S(2)}) copy-start(bf16[1040,128]{1,0:T(8,128)(2,1)S(1)} %get-tuple-element.21.refs_0_) | copy-start | bytes 798724
  24.3 24.0 %copy-start.14 = (bf16[1040,128]{1,0:T(8,128)(2,1)}, bf16[1040,128]{1,0:T(8,128)(2,1)S(1)}, u32[]{:S(2)}) copy-start(bf16[1040,128]{1,0:T(8,128)(2,1)S(1)} %get-tuple-element.22.refs_1_) | copy-start | bytes 798724
  24.3 17.9 %collective-permute-start.3 = (bf16[1040,128]{1,0:T(8,128)(2,1)S(1)}, bf16[1040,128]{1,0:T(8,128)(2,1)S(1)}, u32[]{:S(2)}, u32[]{:S(2)}) collective-permute-start(bf16[1040,128]{1,0:T(8,128)(2,1)S(1)} %get-tuple-element.19.refs_2_), channel_id=1, source_target_pairs={{0,4},{1,45},{2,6},{3,47},{4,8},{5,1},{6,10},{7,3},{8,12},{9,5},{1... | collective-permute-start | bytes 798728 | tf_op jit(solution)/shard_map/ppermute | solution.py:270
  32.9 13.7 %collective-permute-start.4 = (bf16[1040,128]{1,0:T(8,128)(2,1)S(1)}, bf16[1040,128]{1,0:T(8,128)(2,1)S(1)}, u32[]{:S(2)}, u32[]{:S(2)}) collective-permute-start(bf16[1040,128]{1,0:T(8,128)(2,1)S(1)} %get-tuple-element.21.refs_0_), channel_id=1, source_target_pairs={{0,28},{1,21},{2,30},{3,23},{4,32},{5,25},{6,34},{7,27},{8,36},{9,... | collective-permute-start | bytes 798728 | tf_op jit(solution)/shard_map/ppermute | solution.py:270
  34.8 13.4 %collective-permute-start.5 = (bf16[1040,128]{1,0:T(8,128)(2,1)S(1)}, bf16[1040,128]{1,0:T(8,128)(2,1)S(1)}, u32[]{:S(2)}, u32[]{:S(2)}) collective-permute-start(bf16[1040,128]{1,0:T(8,128)(2,1)S(1)} %get-tuple-element.22.refs_1_), channel_id=1, source_target_pairs={{0,2},{1,47},{2,4},{3,1},{4,6},{5,3},{6,8},{7,5},{8,10},{9,7},{10,... | collective-permute-start | bytes 798728 | tf_op jit(solution)/shard_map/ppermute | solution.py:270
  38.7 13.3 %collective-permute-start.6 = (bf16[1040,128]{1,0:T(8,128)(2,1)S(1)}, bf16[1040,128]{1,0:T(8,128)(2,1)S(1)}, u32[]{:S(2)}, u32[]{:S(2)}) collective-permute-start(bf16[1040,128]{1,0:T(8,128)(2,1)S(1)} %get-tuple-element.20.refs_0_), channel_id=1, source_target_pairs={{0,26},{1,23},{2,28},{3,25},{4,30},{5,27},{6,32},{7,29},{8,34},{9,... | collective-permute-start | bytes 798728 | tf_op jit(solution)/shard_map/ppermute | solution.py:270
  42.1 17.4 %copy-start.28 = (s32[84]{0:T(128)S(1)}, s32[84]{0:T(128)}, u32[]{:S(2)}) copy-start(s32[84]{0:T(128)} %constant.376.clone) | copy-start | bytes 1012
  42.1 17.4 %copy-start.20 = (s32[60]{0:T(128)S(1)}, s32[60]{0:T(128)}, u32[]{:S(2)}) copy-start(s32[60]{0:T(128)} %constant.379.clone) | copy-start | bytes 724
  42.1 17.4 %copy-start.22 = (s32[60]{0:T(128)S(1)}, s32[60]{0:T(128)}, u32[]{:S(2)}) copy-start(s32[60]{0:T(128)} %constant.382.clone) | copy-start | bytes 724
  42.1 17.4 %copy-start.25 = (s32[60]{0:T(128)S(1)}, s32[60]{0:T(128)}, u32[]{:S(2)}) copy-start(s32[60]{0:T(128)} %constant.380.clone) | copy-start | bytes 724
  42.1 17.4 %copy-start.26 = (s32[60]{0:T(128)S(1)}, s32[60]{0:T(128)}, u32[]{:S(2)}) copy-start(s32[60]{0:T(128)} %constant.381.clone) | copy-start | bytes 724
  54.2 14.3 %collective-permute-start.7 = (bf16[3120,128]{1,0:T(8,128)(2,1)S(1)}, bf16[3120,128]{1,0:T(8,128)(2,1)S(1)}, u32[]{:S(2)}, u32[]{:S(2)}) collective-permute-start(bf16[3120,128]{1,0:T(8,128)(2,1)S(1)} %shard_map.148.refs_2_.refs_0_.refs_6_), channel_id=1, source_target_pairs={{0,2},{1,47},{2,4},{3,1},{4,6},{5,3},{6,8},{7,5},{8,10},{9,7},{10,... | collective-permute-start | bytes 2396168 | tf_op jit(solution)/shard_map/ppermute | solution.py:270
  59.6 48.9 %all-to-all-start = ((bf16[8,800,128]{2,1,0:T(8,128)(2,1)}), bf16[8,800,128]{2,1,0:T(8,128)(2,1)S(1)}, u32[]{:S(2)}, u32[]{:S(2)}) async-start(bf16[8,800,128]{2,1,0:T(8,128)(2,1)} %shard_map.147.refs_5_), calls=%async_computation | async-start | bytes 3276800 | tf_op jit(solution)/shard_map/all_to_all | solution.py:340
  69.5 20.2 %collective-permute-start.8 = (bf16[2096,128]{1,0:T(8,128)(2,1)S(1)}, bf16[2096,128]{1,0:T(8,128)(2,1)S(1)}, u32[]{:S(2)}, u32[]{:S(2)}) collective-permute-start(bf16[2096,128]{1,0:T(8,128)(2,1)S(1)} %shard_map.149.refs_9_), channel_id=1, source_target_pairs={{0,30},{1,19},{2,32},{3,21},{4,34},{5,23},{6,36},{7,25},{8,38},{9,... | collective-permute-start | bytes 1609736 | tf_op jit(solution)/shard_map/ppermute | solution.py:270
  72.3 9.0 %collective-permute-start.9 = (bf16[528,128]{1,0:T(8,128)(2,1)S(1)}, bf16[528,128]{1,0:T(8,128)(2,1)S(1)}, u32[]{:S(2)}, u32[]{:S(2)}) collective-permute-start(bf16[528,128]{1,0:T(8,128)(2,1)S(1)} %copy-done.19), channel_id=1, source_target_pairs={{0,24},{1,25},{2,26},{3,27},{4,28},{5,29},{6,30},{7,31},{8,32},{9,... | collective-permute-start | bytes 405512 | tf_op jit(solution)/shard_map/ppermute | solution.py:270
  82.6 19.7 %copy-start.16 = (bf16[5760,128]{1,0:T(8,128)(2,1)}, bf16[5760,128]{1,0:T(8,128)(2,1)S(1)}, u32[]{:S(2)}) copy-start(bf16[5760,128]{1,0:T(8,128)(2,1)S(1)} %get-tuple-element.28.rest_0_) | copy-start | bytes 4423684
  82.6 20.7 %collective-permute-start.12 = (bf16[5040,128]{1,0:T(8,128)(2,1)}, bf16[5040,128]{1,0:T(8,128)(2,1)}, u32[]{:S(2)}, u32[]{:S(2)}) collective-permute-start(bf16[5040,128]{1,0:T(8,128)(2,1)} %get-tuple-element.27), channel_id=1, source_target_pairs={{0,1},{1,0},{2,3},{3,2},{4,5},{5,4},{6,7},{7,6},{8,9},{9,8},{10,11... | collective-permute-start | bytes 3870728 | tf_op jit(solution)/shard_map/ppermute | solution.py:274
  90.8 11.5 %collective-permute-start.10 = (bf16[48,128]{1,0:T(8,128)(2,1)S(1)}, bf16[48,128]{1,0:T(8,128)(2,1)S(1)}, u32[]{:S(2)}, u32[]{:S(2)}) collective-permute-start(bf16[48,128]{1,0:T(8,128)(2,1)S(1)} %get-tuple-element.25), channel_id=1, source_target_pairs={{0,1},{1,0},{2,3},{3,2},{4,5},{5,4},{6,7},{7,6},{8,9},{9,8},{10,11... | collective-permute-start | bytes 36872 | tf_op jit(solution)/shard_map/ppermute | solution.py:274
  97.9 20.3 %collective-permute-start.11 = (bf16[3072,128]{1,0:T(8,128)(2,1)}, bf16[3072,128]{1,0:T(8,128)(2,1)S(1)}, u32[]{:S(2)}, u32[]{:S(2)}) collective-permute-start(bf16[3072,128]{1,0:T(8,128)(2,1)} %get-tuple-element.26), channel_id=1, source_target_pairs={{0,2},{1,47},{2,4},{3,1},{4,6},{5,3},{6,8},{7,5},{8,10},{9,7},{10,... | collective-permute-start | bytes 2359304 | tf_op jit(solution)/shard_map/ppermute | solution.py:270
  105.3 11.7 %collective-permute-start.13 = (bf16[2048,128]{1,0:T(8,128)(2,1)S(1)}, bf16[2048,128]{1,0:T(8,128)(2,1)S(1)}, u32[]{:S(2)}, u32[]{:S(2)}) collective-permute-start(bf16[2048,128]{1,0:T(8,128)(2,1)S(1)} %shard_map.152), channel_id=1, source_target_pairs={{0,1},{1,0},{2,3},{3,2},{4,5},{5,4},{6,7},{7,6},{8,9},{9,8},{10,11... | collective-permute-start | bytes 1572872 | tf_op jit(solution)/shard_map/ppermute | solution.py:274
  118.3 3.6 %collective-permute-start.14 = (bf16[1536,128]{1,0:T(8,128)(2,1)S(1)}, bf16[1536,128]{1,0:T(8,128)(2,1)S(1)}, u32[]{:S(2)}, u32[]{:S(2)}) collective-permute-start(bf16[1536,128]{1,0:T(8,128)(2,1)S(1)} %shard_map.155), channel_id=1, source_target_pairs={{0,1},{1,0},{2,3},{3,2},{4,5},{5,4},{6,7},{7,6},{8,9},{9,8},{10,11... | collective-permute-start | bytes 1179656 | tf_op jit(solution)/shard_map/ppermute | solution.py:274
  (22 other events, 141.4 us)

commit v15 on v13

--- a/solution.py
+++ b/solution.py
@@ -310,11 +310,10 @@
         near.append((send(array, names, distance), 2 * len(names) * BLK, distance, True))
 
     names = items([(2, 1), (6, 13), (3, 2), (7, 14), (0, 14), (4, 2)])
-    right_out = right_packed(b_kept, b_other, arrays[0])
-    (up_in,) = packed([(blocks(names), True)], near, (right_out,))
+    (up_in,) = packed([(blocks(names), True)], near, (b_other,))
     sources.append(up_in)
     up3 = send(up_in, names, 1)
-    right = lax.all_to_all(right_out, "y", 0, 0, tiled=True)
+    right = lax.all_to_all(right_packed(b_kept, b_other, up_in), "y", 0, 0, tiled=True)
     right = right.reshape(16 * HALF, BLK)
     middle = [(up3 - 1, 24 * BLK, 0, False), (up3, 24 * BLK, 1, False)]
 

time: 124 us -> 122 us (0.984); the launches traced: 122 us -> 121 us
    unnamed x60 -> x62, local copies, waits for them, and re-layouts: 8.33 us -> 9.25 us
  transfers between devices with their start and end apart: 16 -> 16, of which waited for: 6 -> 8; matrix products, arithmetic and copies ran while one was open for 6% -> 6% of each run, Pallas kernels for 10% -> 9%
where the time goes in v15:
time: 122 us; the launch traced here: 121 us
  starting transfers between devices  74.3 us (61%)
  waiting for transfers between devices  16.1 us (13%)
  local copies, waits for them, and re-layouts  12.3 us (10%)
  Pallas kernels  12.2 us (10%)
  other arithmetic  5.2 us (4%)
    ppermute x8, starting transfers between devices, moved(): return lax.ppermute(array, COL, route)  33.6 us
    ppermute x6, starting transfers between devices, from_other_core(): return lax.ppermute(array, 'core', [(0, 1), (1, 0)])  31.9 us
    ppermute x8, waiting for transfers between devices, moved(): return lax.ppermute(array, COL, route)  15.5 us
    unnamed x62, local copies, waits for them, and re-layouts  9.25 us
    pallas_call x4, Pallas kernels, product(): pl.pallas_call(functools.partial(product_kernel, counts, base, before is...  8.29 us
    all_to_all x1, starting transfers between devices, local(): lax.all_to_all(right_packed(b_kept, b_other, up_in), 'y', 0, 0, tiled=True)  6.86 us
    pallas_call x6, Pallas kernels, pack(): pl.pallas_call(functools.partial(pack_kernel, spec, notes, len(used)), ou...  2.48 us
  transfers between devices with their start and end apart: 16, of which 8 were waited for; matrix products, arithmetic and copies ran while one was open for 6% of the time, Pallas kernels for 9%

profile of v15, /device:TPU:1, one launch (start us, length us, event | category | flops | bytes accessed | tf_op | source)
XLA Modules:
  0.0 120.8 jit_solution(6695509353517143322)
XLA Ops:
  0.8 12.4 %collective-permute-start.2 = (bf16[16,128]{1,0:T(8,128)(2,1)S(1)}, bf16[16,128]{1,0:T(8,128)(2,1)S(1)}, u32[]{:S(2)}, u32[]{:S(2)}) collective-permute-start(bf16[16,128]{1,0:T(8,128)(2,1)S(1)} %fusion.37), channel_id=1, source_target_pairs={{0,1},{1,0},{2,3},{3,2},{4,5},{5,4},{6,7},{7,6},{8,9},{9,8},{10,11... | collective-permute-start | bytes 12296 | tf_op jit(solution)/shard_map/ppermute | solution.py:251
  13.2 1.9 %collective-permute-start.1 = (bf16[16,128,128]{2,1,0:T(8,128)(2,1)}, bf16[16,128,128]{2,1,0:T(8,128)(2,1)S(1)}, u32[]{:S(2)}, u32[]{:S(2)}) collective-permute-start(bf16[16,128,128]{2,1,0:T(8,128)(2,1)} %bitcast.77), channel_id=1, source_target_pairs={{0,1},{1,0},{2,3},{3,2},{4,5},{5,4},{6,7},{7,6},{8,9},{9,8},{10,11... | collective-permute-start | bytes 1572872 | tf_op jit(solution)/shard_map/ppermute | solution.py:251
  17.6 1.9 %collective-permute-start = (bf16[1296,128]{1,0:T(8,128)(2,1)S(1)}, bf16[1296,128]{1,0:T(8,128)(2,1)S(1)}, u32[]{:S(2)}, u32[]{:S(2)}) collective-permute-start(bf16[1296,128]{1,0:T(8,128)(2,1)S(1)} %get-tuple-element.18), channel_id=1, source_target_pairs={{0,384},{384,0},{1,385},{385,1},{2,386},{386,2},{3,387},{387,3},{4... | collective-permute-start | bytes 995336 | tf_op jit(solution)/shard_map/ppermute | solution.py:269
  22.2 8.8 %collective-permute-start.3 = (bf16[1040,128]{1,0:T(8,128)(2,1)S(1)}, bf16[1040,128]{1,0:T(8,128)(2,1)S(1)}, u32[]{:S(2)}, u32[]{:S(2)}) collective-permute-start(bf16[1040,128]{1,0:T(8,128)(2,1)S(1)} %get-tuple-element.20), channel_id=1, source_target_pairs={{0,4},{1,45},{2,6},{3,47},{4,8},{5,1},{6,10},{7,3},{8,12},{9,5},{1... | collective-permute-start | bytes 798728 | tf_op jit(solution)/shard_map/ppermute | solution.py:247
  31.0 1.9 %collective-permute-start.4 = (bf16[1040,128]{1,0:T(8,128)(2,1)S(1)}, bf16[1040,128]{1,0:T(8,128)(2,1)S(1)}, u32[]{:S(2)}, u32[]{:S(2)}) collective-permute-start(bf16[1040,128]{1,0:T(8,128)(2,1)S(1)} %get-tuple-element.21.refs_0_), channel_id=1, source_target_pairs={{0,28},{1,21},{2,30},{3,23},{4,32},{5,25},{6,34},{7,27},{8,36},{9,... | collective-permute-start | bytes 798728 | tf_op jit(solution)/shard_map/ppermute | solution.py:247
  32.9 3.9 %collective-permute-start.5 = (bf16[1040,128]{1,0:T(8,128)(2,1)S(1)}, bf16[1040,128]{1,0:T(8,128)(2,1)S(1)}, u32[]{:S(2)}, u32[]{:S(2)}) collective-permute-start(bf16[1040,128]{1,0:T(8,128)(2,1)S(1)} %get-tuple-element.22.refs_1_), channel_id=1, source_target_pairs={{0,2},{1,47},{2,4},{3,1},{4,6},{5,3},{6,8},{7,5},{8,10},{9,7},{10,... | collective-permute-start | bytes 798728 | tf_op jit(solution)/shard_map/ppermute | solution.py:247
  36.8 1.9 %collective-permute-start.6 = (bf16[1040,128]{1,0:T(8,128)(2,1)S(1)}, bf16[1040,128]{1,0:T(8,128)(2,1)S(1)}, u32[]{:S(2)}, u32[]{:S(2)}) collective-permute-start(bf16[1040,128]{1,0:T(8,128)(2,1)S(1)} %get-tuple-element.19.refs_0_), channel_id=1, source_target_pairs={{0,26},{1,23},{2,28},{3,25},{4,30},{5,27},{6,32},{7,29},{8,34},{9,... | collective-permute-start | bytes 798728 | tf_op jit(solution)/shard_map/ppermute | solution.py:247
  39.4 5.2 %collective-permute-done.4.refs_2_.refs_3_ = bf16[1040,128]{1,0:T(8,128)(2,1)S(1)} collective-permute-done((bf16[1040,128]{1,0:T(8,128)(2,1)S(1)}, bf16[1040,128]{1,0:T(8,128)(2,1)S(1)}, u32[]{:S(2)}, u32[]{:S(2)}) %collective-permute-start.4) | collective-permute-done | bytes 266272 | tf_op jit(solution)/shard_map/ppermute | solution.py:247
  44.6 1.7 %collective-permute-done.5.refs_3_.refs_0_.refs_4_ = bf16[1040,128]{1,0:T(8,128)(2,1)S(1)} collective-permute-done((bf16[1040,128]{1,0:T(8,128)(2,1)S(1)}, bf16[1040,128]{1,0:T(8,128)(2,1)S(1)}, u32[]{:S(2)}, u32[]{:S(2)}) %collective-permute-start.5) | collective-permute-done | bytes 266272 | tf_op jit(solution)/shard_map/ppermute | solution.py:247
  46.4 3.7 %collective-permute-done.6.refs_4_.refs_1_.refs_5_ = bf16[1040,128]{1,0:T(8,128)(2,1)S(1)} collective-permute-done((bf16[1040,128]{1,0:T(8,128)(2,1)S(1)}, bf16[1040,128]{1,0:T(8,128)(2,1)S(1)}, u32[]{:S(2)}, u32[]{:S(2)}) %collective-permute-start.6) | collective-permute-done | bytes 266272 | tf_op jit(solution)/shard_map/ppermute | solution.py:247
  50.9 5.2 %collective-permute-start.7 = (bf16[3120,128]{1,0:T(8,128)(2,1)S(1)}, bf16[3120,128]{1,0:T(8,128)(2,1)S(1)}, u32[]{:S(2)}, u32[]{:S(2)}) collective-permute-start(bf16[3120,128]{1,0:T(8,128)(2,1)S(1)} %shard_map.147.refs_2_.refs_0_.refs_6_), channel_id=1, source_target_pairs={{0,2},{1,47},{2,4},{3,1},{4,6},{5,3},{6,8},{7,5},{8,10},{9,7},{10,... | collective-permute-start | bytes 2396168 | tf_op jit(solution)/shard_map/ppermute | solution.py:247
  57.7 6.9 %all-to-all-start = ((bf16[8,800,128]{2,1,0:T(8,128)(2,1)}), bf16[8,800,128]{2,1,0:T(8,128)(2,1)S(1)}, u32[]{:S(2)}, u32[]{:S(2)}) async-start(bf16[8,800,128]{2,1,0:T(8,128)(2,1)} %copy-done), calls=%async_computation | async-start | bytes 3276800 | tf_op jit(solution)/shard_map/all_to_all | solution.py:316
  66.2 2.8 %collective-permute-start.8 = (bf16[2096,128]{1,0:T(8,128)(2,1)S(1)}, bf16[2096,128]{1,0:T(8,128)(2,1)S(1)}, u32[]{:S(2)}, u32[]{:S(2)}) collective-permute-start(bf16[2096,128]{1,0:T(8,128)(2,1)S(1)} %shard_map.149.refs_9_), channel_id=1, source_target_pairs={{0,30},{1,19},{2,32},{3,21},{4,34},{5,23},{6,36},{7,25},{8,38},{9,... | collective-permute-start | bytes 1609736 | tf_op jit(solution)/shard_map/ppermute | solution.py:247
  69.0 4.8 %collective-permute-start.9 = (bf16[528,128]{1,0:T(8,128)(2,1)S(1)}, bf16[528,128]{1,0:T(8,128)(2,1)S(1)}, u32[]{:S(2)}, u32[]{:S(2)}) collective-permute-start(bf16[528,128]{1,0:T(8,128)(2,1)S(1)} %copy-done.20), channel_id=1, source_target_pairs={{0,24},{1,25},{2,26},{3,27},{4,28},{5,29},{6,30},{7,31},{8,32},{9,... | collective-permute-start | bytes 405512 | tf_op jit(solution)/shard_map/ppermute | solution.py:247
  74.4 3.6 %collective-permute-done.9.refs_3_.refs_8_ = bf16[528,128]{1,0:T(8,128)(2,1)S(1)} collective-permute-done((bf16[528,128]{1,0:T(8,128)(2,1)S(1)}, bf16[528,128]{1,0:T(8,128)(2,1)S(1)}, u32[]{:S(2)}, u32[]{:S(2)}) %collective-permute-start.9) | collective-permute-done | bytes 135200 | tf_op jit(solution)/shard_map/ppermute | solution.py:247
  78.0 1.3 %shard_map.151 = (bf16[5040,128]{1,0:T(8,128)(2,1)}, bf16[5760,128]{1,0:T(8,128)(2,1)S(1)}) custom-call(bf16[1040,128]{1,0:T(8,128)(2,1)S(1)} %copy-done.14, bf16[1040,128]{1,0:T(8,128)(2,1)S(1)} %copy-done.16, bf16[1040,128]{1,0:T(8,128)(2,1)S(1)} %copy-done.8, bf16[1040,128]{1,0:T(8,128)(2,1)S(1)} %copy-done.10, ...), custom_call_target="tpu_custom_call" | custom-call | bytes 5505024 | tf_op jit(solution)/shard_map/pallas_call | solution.py:148
  80.4 7.0 %collective-permute-start.12 = (bf16[5040,128]{1,0:T(8,128)(2,1)}, bf16[5040,128]{1,0:T(8,128)(2,1)}, u32[]{:S(2)}, u32[]{:S(2)}) collective-permute-start(bf16[5040,128]{1,0:T(8,128)(2,1)} %get-tuple-element.27), channel_id=1, source_target_pairs={{0,1},{1,0},{2,3},{3,2},{4,5},{5,4},{6,7},{7,6},{8,9},{9,8},{10,11... | collective-permute-start | bytes 3870728 | tf_op jit(solution)/shard_map/ppermute | solution.py:251
  88.5 5.3 %collective-permute-start.10 = (bf16[48,128]{1,0:T(8,128)(2,1)S(1)}, bf16[48,128]{1,0:T(8,128)(2,1)S(1)}, u32[]{:S(2)}, u32[]{:S(2)}) collective-permute-start(bf16[48,128]{1,0:T(8,128)(2,1)S(1)} %get-tuple-element.25), channel_id=1, source_target_pairs={{0,1},{1,0},{2,3},{3,2},{4,5},{5,4},{6,7},{7,6},{8,9},{9,8},{10,11... | collective-permute-start | bytes 36872 | tf_op jit(solution)/shard_map/ppermute | solution.py:251
  94.6 4.4 %collective-permute-start.11 = (bf16[3072,128]{1,0:T(8,128)(2,1)}, bf16[3072,128]{1,0:T(8,128)(2,1)S(1)}, u32[]{:S(2)}, u32[]{:S(2)}) collective-permute-start(bf16[3072,128]{1,0:T(8,128)(2,1)} %get-tuple-element.26), channel_id=1, source_target_pairs={{0,2},{1,47},{2,4},{3,1},{4,6},{5,3},{6,8},{7,5},{8,10},{9,7},{10,... | collective-permute-start | bytes 2359304 | tf_op jit(solution)/shard_map/ppermute | solution.py:247
  101.9 3.0 %collective-permute-start.13 = (bf16[2048,128]{1,0:T(8,128)(2,1)S(1)}, bf16[2048,128]{1,0:T(8,128)(2,1)S(1)}, u32[]{:S(2)}, u32[]{:S(2)}) collective-permute-start(bf16[2048,128]{1,0:T(8,128)(2,1)S(1)} %shard_map.152), channel_id=1, source_target_pairs={{0,1},{1,0},{2,3},{3,2},{4,5},{5,4},{6,7},{7,6},{8,9},{9,8},{10,11... | collective-permute-start | bytes 1572872 | tf_op jit(solution)/shard_map/ppermute | solution.py:251
  108.7 1.4 %copy-done.18 = bf16[5760,128]{1,0:T(8,128)(2,1)S(1)} copy-done((bf16[5760,128]{1,0:T(8,128)(2,1)S(1)}, bf16[5760,128]{1,0:T(8,128)(2,1)}, u32[]{:S(2)}) %copy-start.18) | copy-done | bytes 1474584
  110.1 4.0 %shard_map.153.rest_2_ = f32[13,128,128]{2,1,0:T(8,128)S(1)} custom-call(s32[5,84]{1,0:T(8,128)S(1)} %stack.59.table_ref, bf16[6400,128]{1,0:T(8,128)(2,1)S(1)} %bitcast.72, bf16[5760,128]{1,0:T(8,128)(2,1)S(1)} %copy-done.18, bf16[5040,128]{1,0:T(8,128)(2,1)} %collective-permute-done.12.refs_1_.rest_1_), custom_call_target="tpu_custom_call" | custom-call | flops 2818572288 | bytes 2752512 | tf_op jit(solution)/shard_map/pallas_call | solution.py:192
  115.4 2.2 %collective-permute-start.14 = (bf16[1536,128]{1,0:T(8,128)(2,1)S(1)}, bf16[1536,128]{1,0:T(8,128)(2,1)S(1)}, u32[]{:S(2)}, u32[]{:S(2)}) collective-permute-start(bf16[1536,128]{1,0:T(8,128)(2,1)S(1)} %shard_map.155), channel_id=1, source_target_pairs={{0,1},{1,0},{2,3},{3,2},{4,5},{5,4},{6,7},{7,6},{8,9},{9,8},{10,11... | collective-permute-start | bytes 1179656 | tf_op jit(solution)/shard_map/ppermute | solution.py:251
  119.0 1.8 %shard_map.157 = bf16[12,128,128]{2,1,0:T(8,128)(2,1)} custom-call(s32[5,60]{1,0:T(8,128)S(1)} %stack.52.table_ref, bf16[6400,128]{1,0:T(8,128)(2,1)S(1)} %bitcast.75, bf16[1536,128]{1,0:T(8,128)(2,1)S(1)} %collective-permute-done.14.rest_0_, f32[13,128,128]{2,1,0:T(8,128)S(1)} %shard_map.156.rest_1_), custom_call_target="tpu_custom_call" | custom-call | flops 402653184 | bytes 393216 | tf_op jit(solution)/shard_map/pallas_call | solution.py:192
  (145 shorter events, 23.1 us)
Async XLA Ops:
  0.8 18.9 %collective-permute-start.2 = (bf16[16,128]{1,0:T(8,128)(2,1)S(1)}, bf16[16,128]{1,0:T(8,128)(2,1)S(1)}, u32[]{:S(2)}, u32[]{:S(2)}) collective-permute-start(bf16[16,128]{1,0:T(8,128)(2,1)S(1)} %fusion.37), channel_id=1, source_target_pairs={{0,1},{1,0},{2,3},{3,2},{4,5},{5,4},{6,7},{7,6},{8,9},{9,8},{10,11... | collective-permute-start | bytes 12296 | tf_op jit(solution)/shard_map/ppermute | solution.py:251
  13.2 6.6 %collective-permute-start.1 = (bf16[16,128,128]{2,1,0:T(8,128)(2,1)}, bf16[16,128,128]{2,1,0:T(8,128)(2,1)S(1)}, u32[]{:S(2)}, u32[]{:S(2)}) collective-permute-start(bf16[16,128,128]{2,1,0:T(8,128)(2,1)} %bitcast.77), channel_id=1, source_target_pairs={{0,1},{1,0},{2,3},{3,2},{4,5},{5,4},{6,7},{7,6},{8,9},{9,8},{10,11... | collective-permute-start | bytes 1572872 | tf_op jit(solution)/shard_map/ppermute | solution.py:251
  17.6 21.1 %collective-permute-start = (bf16[1296,128]{1,0:T(8,128)(2,1)S(1)}, bf16[1296,128]{1,0:T(8,128)(2,1)S(1)}, u32[]{:S(2)}, u32[]{:S(2)}) collective-permute-start(bf16[1296,128]{1,0:T(8,128)(2,1)S(1)} %get-tuple-element.18), channel_id=1, source_target_pairs={{0,384},{384,0},{1,385},{385,1},{2,386},{386,2},{3,387},{387,3},{4... | collective-permute-start | bytes 995336 | tf_op jit(solution)/shard_map/ppermute | solution.py:269
  22.1 34.4 %copy-start.13 = (bf16[1040,128]{1,0:T(8,128)(2,1)}, bf16[1040,128]{1,0:T(8,128)(2,1)S(1)}, u32[]{:S(2)}) copy-start(bf16[1040,128]{1,0:T(8,128)(2,1)S(1)} %get-tuple-element.21.refs_0_) | copy-start | bytes 798724
  22.1 34.0 %copy-start.24 = (s32[84]{0:T(128)S(1)}, s32[84]{0:T(128)}, u32[]{:S(2)}) copy-start(s32[84]{0:T(128)} %constant.377.clone) | copy-start | bytes 1012
  22.1 34.0 %copy-start.28 = (s32[84]{0:T(128)S(1)}, s32[84]{0:T(128)}, u32[]{:S(2)}) copy-start(s32[84]{0:T(128)} %constant.375.clone) | copy-start | bytes 1012
  22.1 34.0 %copy-start.29 = (s32[84]{0:T(128)S(1)}, s32[84]{0:T(128)}, u32[]{:S(2)}) copy-start(s32[84]{0:T(128)} %constant.376.clone) | copy-start | bytes 1012
  22.1 34.0 %copy-start.21 = (s32[60]{0:T(128)S(1)}, s32[60]{0:T(128)}, u32[]{:S(2)}) copy-start(s32[60]{0:T(128)} %constant.379.clone) | copy-start | bytes 724
  22.1 34.0 %copy-start.23 = (s32[60]{0:T(128)S(1)}, s32[60]{0:T(128)}, u32[]{:S(2)}) copy-start(s32[60]{0:T(128)} %constant.382.clone) | copy-start | bytes 724
  22.2 34.1 %copy-start.26 = (s32[60]{0:T(128)S(1)}, s32[60]{0:T(128)}, u32[]{:S(2)}) copy-start(s32[60]{0:T(128)} %constant.380.clone) | copy-start | bytes 724
  22.2 34.0 %copy-start.27 = (s32[60]{0:T(128)S(1)}, s32[60]{0:T(128)}, u32[]{:S(2)}) copy-start(s32[60]{0:T(128)} %constant.381.clone) | copy-start | bytes 724
  22.2 17.2 %collective-permute-start.3 = (bf16[1040,128]{1,0:T(8,128)(2,1)S(1)}, bf16[1040,128]{1,0:T(8,128)(2,1)S(1)}, u32[]{:S(2)}, u32[]{:S(2)}) collective-permute-start(bf16[1040,128]{1,0:T(8,128)(2,1)S(1)} %get-tuple-element.20), channel_id=1, source_target_pairs={{0,4},{1,45},{2,6},{3,47},{4,8},{5,1},{6,10},{7,3},{8,12},{9,5},{1... | collective-permute-start | bytes 798728 | tf_op jit(solution)/shard_map/ppermute | solution.py:247
  31.0 13.7 %collective-permute-start.4 = (bf16[1040,128]{1,0:T(8,128)(2,1)S(1)}, bf16[1040,128]{1,0:T(8,128)(2,1)S(1)}, u32[]{:S(2)}, u32[]{:S(2)}) collective-permute-start(bf16[1040,128]{1,0:T(8,128)(2,1)S(1)} %get-tuple-element.21.refs_0_), channel_id=1, source_target_pairs={{0,28},{1,21},{2,30},{3,23},{4,32},{5,25},{6,34},{7,27},{8,36},{9,... | collective-permute-start | bytes 798728 | tf_op jit(solution)/shard_map/ppermute | solution.py:247
  32.9 13.4 %collective-permute-start.5 = (bf16[1040,128]{1,0:T(8,128)(2,1)S(1)}, bf16[1040,128]{1,0:T(8,128)(2,1)S(1)}, u32[]{:S(2)}, u32[]{:S(2)}) collective-permute-start(bf16[1040,128]{1,0:T(8,128)(2,1)S(1)} %get-tuple-element.22.refs_1_), channel_id=1, source_target_pairs={{0,2},{1,47},{2,4},{3,1},{4,6},{5,3},{6,8},{7,5},{8,10},{9,7},{10,... | collective-permute-start | bytes 798728 | tf_op jit(solution)/shard_map/ppermute | solution.py:247
  36.8 13.3 %collective-permute-start.6 = (bf16[1040,128]{1,0:T(8,128)(2,1)S(1)}, bf16[1040,128]{1,0:T(8,128)(2,1)S(1)}, u32[]{:S(2)}, u32[]{:S(2)}) collective-permute-start(bf16[1040,128]{1,0:T(8,128)(2,1)S(1)} %get-tuple-element.19.refs_0_), channel_id=1, source_target_pairs={{0,26},{1,23},{2,28},{3,25},{4,30},{5,27},{6,32},{7,29},{8,34},{9,... | collective-permute-start | bytes 798728 | tf_op jit(solution)/shard_map/ppermute | solution.py:247
  50.9 14.2 %collective-permute-start.7 = (bf16[3120,128]{1,0:T(8,128)(2,1)S(1)}, bf16[3120,128]{1,0:T(8,128)(2,1)S(1)}, u32[]{:S(2)}, u32[]{:S(2)}) collective-permute-start(bf16[3120,128]{1,0:T(8,128)(2,1)S(1)} %shard_map.147.refs_2_.refs_0_.refs_6_), channel_id=1, source_target_pairs={{0,2},{1,47},{2,4},{3,1},{4,6},{5,3},{6,8},{7,5},{8,10},{9,7},{10,... | collective-permute-start | bytes 2396168 | tf_op jit(solution)/shard_map/ppermute | solution.py:247
  57.7 47.9 %all-to-all-start = ((bf16[8,800,128]{2,1,0:T(8,128)(2,1)}), bf16[8,800,128]{2,1,0:T(8,128)(2,1)S(1)}, u32[]{:S(2)}, u32[]{:S(2)}) async-start(bf16[8,800,128]{2,1,0:T(8,128)(2,1)} %copy-done), calls=%async_computation | async-start | bytes 3276800 | tf_op jit(solution)/shard_map/all_to_all | solution.py:316
  66.2 21.3 %collective-permute-start.8 = (bf16[2096,128]{1,0:T(8,128)(2,1)S(1)}, bf16[2096,128]{1,0:T(8,128)(2,1)S(1)}, u32[]{:S(2)}, u32[]{:S(2)}) collective-permute-start(bf16[2096,128]{1,0:T(8,128)(2,1)S(1)} %shard_map.149.refs_9_), channel_id=1, source_target_pairs={{0,30},{1,19},{2,32},{3,21},{4,34},{5,23},{6,36},{7,25},{8,38},{9,... | collective-permute-start | bytes 1609736 | tf_op jit(solution)/shard_map/ppermute | solution.py:247
  69.0 9.0 %collective-permute-start.9 = (bf16[528,128]{1,0:T(8,128)(2,1)S(1)}, bf16[528,128]{1,0:T(8,128)(2,1)S(1)}, u32[]{:S(2)}, u32[]{:S(2)}) collective-permute-start(bf16[528,128]{1,0:T(8,128)(2,1)S(1)} %copy-done.20), channel_id=1, source_target_pairs={{0,24},{1,25},{2,26},{3,27},{4,28},{5,29},{6,30},{7,31},{8,32},{9,... | collective-permute-start | bytes 405512 | tf_op jit(solution)/shard_map/ppermute | solution.py:247
  80.4 19.5 %collective-permute-start.12 = (bf16[5040,128]{1,0:T(8,128)(2,1)}, bf16[5040,128]{1,0:T(8,128)(2,1)}, u32[]{:S(2)}, u32[]{:S(2)}) collective-permute-start(bf16[5040,128]{1,0:T(8,128)(2,1)} %get-tuple-element.27), channel_id=1, source_target_pairs={{0,1},{1,0},{2,3},{3,2},{4,5},{5,4},{6,7},{7,6},{8,9},{9,8},{10,11... | collective-permute-start | bytes 3870728 | tf_op jit(solution)/shard_map/ppermute | solution.py:251
  88.5 10.4 %collective-permute-start.10 = (bf16[48,128]{1,0:T(8,128)(2,1)S(1)}, bf16[48,128]{1,0:T(8,128)(2,1)S(1)}, u32[]{:S(2)}, u32[]{:S(2)}) collective-permute-start(bf16[48,128]{1,0:T(8,128)(2,1)S(1)} %get-tuple-element.25), channel_id=1, source_target_pairs={{0,1},{1,0},{2,3},{3,2},{4,5},{5,4},{6,7},{7,6},{8,9},{9,8},{10,11... | collective-permute-start | bytes 36872 | tf_op jit(solution)/shard_map/ppermute | solution.py:251
  94.6 20.8 %collective-permute-start.11 = (bf16[3072,128]{1,0:T(8,128)(2,1)}, bf16[3072,128]{1,0:T(8,128)(2,1)S(1)}, u32[]{:S(2)}, u32[]{:S(2)}) collective-permute-start(bf16[3072,128]{1,0:T(8,128)(2,1)} %get-tuple-element.26), channel_id=1, source_target_pairs={{0,2},{1,47},{2,4},{3,1},{4,6},{5,3},{6,8},{7,5},{8,10},{9,7},{10,... | collective-permute-start | bytes 2359304 | tf_op jit(solution)/shard_map/ppermute | solution.py:247
  101.9 12.2 %collective-permute-start.13 = (bf16[2048,128]{1,0:T(8,128)(2,1)S(1)}, bf16[2048,128]{1,0:T(8,128)(2,1)S(1)}, u32[]{:S(2)}, u32[]{:S(2)}) collective-permute-start(bf16[2048,128]{1,0:T(8,128)(2,1)S(1)} %shard_map.152), channel_id=1, source_target_pairs={{0,1},{1,0},{2,3},{3,2},{4,5},{5,4},{6,7},{7,6},{8,9},{9,8},{10,11... | collective-permute-start | bytes 1572872 | tf_op jit(solution)/shard_map/ppermute | solution.py:251
  115.4 3.6 %collective-permute-start.14 = (bf16[1536,128]{1,0:T(8,128)(2,1)S(1)}, bf16[1536,128]{1,0:T(8,128)(2,1)S(1)}, u32[]{:S(2)}, u32[]{:S(2)}) collective-permute-start(bf16[1536,128]{1,0:T(8,128)(2,1)S(1)} %shard_map.155), channel_id=1, source_target_pairs={{0,1},{1,0},{2,3},{3,2},{4,5},{5,4},{6,7},{7,6},{8,9},{9,8},{10,11... | collective-permute-start | bytes 1179656 | tf_op jit(solution)/shard_map/ppermute | solution.py:251
  (23 other events, 181.6 us)
